TPU v7x, 32 devices: a whole 2x2x4 slice. The times are simulated.
32 devices in a mesh: batch: 8 (over z, y), seq: 4 (over x, core).
Axes of the slice: x: 2, y: 2, z: 4, core: 2. Of those that a mesh axis runs over, the one named last changes fastest.
Arguments:
- tokens: bfloat16 [16, 2048, 768], P('batch', 'seq'), may hold values from -6 to 6
- lengths: int32 [16], P('batch'), may hold values from 1024 to 2048, as said below
- picks: int32 [16, 256], P('batch', 'seq'), may hold values from 0 to 2047, as said below
- w_router: bfloat16 [768], replicated, may hold values from -0.21875 to 0.21875
- gain_attn: float32 [768], replicated, may hold values from 0.1 to 1.9
- gain_mlp: float32 [768], replicated, may hold values from 0.1 to 1.9
- w_query: bfloat16 [768, 768], replicated, may hold values from -0.21875 to 0.21875
- w_key: bfloat16 [768, 768], replicated, may hold values from -0.21875 to 0.21875
- w_value: bfloat16 [768, 768], replicated, may hold values from -0.21875 to 0.21875
- w_out: bfloat16 [768, 768], replicated, may hold values from -1.75 to 1.75
- w_up: bfloat16 [768, 3072], P(None, 'seq'), may hold values from -0.21875 to 0.21875
- w_down: bfloat16 [3072, 768], P('seq'), may hold values from -0.21875 to 0.21875
- cotangent: bfloat16 [16, 2048, 768], P('batch', 'seq'), may hold values from -6 to 6
Outputs:
- output: bfloat16 [16, 2048, 768], P('batch', 'seq')
- grad_tokens: bfloat16 [16, 2048, 768], P('batch', 'seq')
- grad_router: float32 [768], replicated
- grad_gain_attn: float32 [768], replicated
- grad_gain_mlp: float32 [768], replicated
- grad_query: float32 [768, 768], replicated
- grad_key: float32 [768, 768], replicated
- grad_value: float32 [768, 768], replicated
- grad_out: float32 [768, 768], replicated
- grad_up: float32 [768, 3072], P(None, 'seq')
- grad_down: float32 [3072, 768], P('seq')
Inputs may be any that keep to these rules, and one draw needn't show every extreme that they name: `lengths`: a multiple of 8; among the 2 sequences of each index of batch at least one has length 2048. `picks`: each row rises strictly; its first lengths // 8 entries are positions below the sequence's length, the others positions at or beyond it.
All inputs are finite; a program needn't handle non-finite values.
Results may differ from a plain program's by a relative error of at most 0.012.
The roundings to bfloat16 on the way count: a program that leaves them out, or rounds other values in their place, can miss the bound.
Values may be sent and summed in bfloat16 or wider, within the bound.
No kernel may reach another device: no remote copies, remote signals or barrier semaphores. Data moves between devices by JAX's collectives and lax.ppermute only.
A program may use at most 128 MiB of HBM per device.

v0:
```python
import jax
import jax.numpy as jnp
from jax import lax
from jax.sharding import PartitionSpec as P

NH = 12


def norm_scale(values, gain):
    return values * lax.rsqrt(jnp.mean(values * values, axis=-1, keepdims=True) + 1e-06) * gain


def split_heads(values):
    return values.reshape(values.shape[0], values.shape[1], NH, values.shape[2] // NH)


def attend(query, keys_all, values_all, allowed):
    seqs, local_slots, width = query.shape
    scaling = (width // NH) ** (-0.5)
    logits = (
        jnp.einsum(
            "sihd,sjhd->shij",
            split_heads(query),
            split_heads(keys_all),
            preferred_element_type=jnp.float32,
        )
        * scaling
    )
    logits = jnp.where(allowed, logits, -1e30)
    highest_logit = jnp.max(logits, axis=-1, keepdims=True)
    expd = jnp.exp(logits - highest_logit)
    probs = expd / jnp.sum(expd, axis=-1, keepdims=True)
    probs_low = probs.astype(jnp.bfloat16)
    mixed = jnp.einsum(
        "shij,sjhd->sihd", probs_low, split_heads(values_all), preferred_element_type=jnp.float32
    )
    return (probs, probs_low, mixed.reshape(seqs, local_slots, width).astype(jnp.bfloat16))


def body(
    tokens,
    lengths,
    picks,
    w_router,
    gain_attn,
    gain_mlp,
    w_query,
    w_key,
    w_value,
    w_out,
    w_up,
    w_down,
    cotangent,
):
    groups = lax.axis_size("seq")
    place_index = lax.axis_index("seq")
    seqs, local_len, width = tokens.shape
    local_slots = picks.shape[1]
    slots = local_slots * groups
    scaling = (width // NH) ** (-0.5)
    all_picks = lax.all_gather(picks, "seq", axis=1, tiled=True)
    counts = lengths // 8
    slot_ids = place_index * local_slots + jnp.arange(local_slots)
    valid = (slot_ids[None, :] < counts[:, None]).astype(jnp.float32)
    key_order = jnp.arange(slots)
    allowed = (key_order[None, :] <= slot_ids[:, None])[None, None] & (
        key_order[None, :] < counts[:, None]
    )[:, None, None, :]
    positions = place_index * local_len + jnp.arange(local_len)
    placing = (all_picks[:, :, None] == positions[None, None, :]).astype(jnp.bfloat16)
    pieces = (
        lax.all_gather(tokens, "seq", axis=1, tiled=True),
        lax.all_gather(cotangent, "seq", axis=1, tiled=True),
    )
    rows = pieces[0].shape[1]
    match = (picks[:, :, None] == jnp.arange(rows)[None, None, :]).astype(jnp.bfloat16)
    chosen = jnp.einsum("sir,srd->sid", match, pieces[0], preferred_element_type=jnp.float32)
    seen = jnp.einsum("sir,srd->sid", match, pieces[1], preferred_element_type=jnp.float32)
    chosen_low = chosen.astype(jnp.bfloat16)
    rate = jax.nn.sigmoid(
        jnp.einsum("sid,d->si", chosen_low, w_router, preferred_element_type=jnp.float32)
    )
    normed = norm_scale(chosen, gain_attn).astype(jnp.bfloat16)
    query = jnp.einsum("sid,de->sie", normed, w_query, preferred_element_type=jnp.float32).astype(
        jnp.bfloat16
    )
    keys = jnp.einsum("sid,de->sie", normed, w_key, preferred_element_type=jnp.float32).astype(
        jnp.bfloat16
    )
    values = jnp.einsum("sid,de->sie", normed, w_value, preferred_element_type=jnp.float32).astype(
        jnp.bfloat16
    )
    keys_all, values_all = (
        lax.all_gather(keys, "seq", axis=1, tiled=True),
        lax.all_gather(values, "seq", axis=1, tiled=True),
    )
    probs, probs_low, mixed = attend(query, keys_all, values_all, allowed)
    attended = jnp.einsum("sid,de->sie", mixed, w_out, preferred_element_type=jnp.float32)
    hidden = chosen + attended
    normed_mlp = norm_scale(hidden, gain_mlp).astype(jnp.bfloat16)
    normed_all = lax.all_gather(normed_mlp, "seq", axis=1, tiled=True)
    up_proj = jnp.einsum("sjd,df->sjf", normed_all, w_up, preferred_element_type=jnp.float32)
    activated = jax.nn.gelu(up_proj).astype(jnp.bfloat16)
    partial_out = jnp.einsum("sjf,fd->sjd", activated, w_down, preferred_element_type=jnp.float32)
    moved = lax.psum_scatter(
        partial_out.astype(jnp.bfloat16), "seq", scatter_dimension=1, tiled=True
    ).astype(jnp.float32)
    delta = attended + moved
    update = ((rate * valid)[:, :, None] * delta).astype(jnp.bfloat16)
    update_all = lax.all_gather(update, "seq", axis=1, tiled=True)
    output = tokens.astype(jnp.float32) + jnp.einsum(
        "sjr,sjd->srd", placing, update_all, preferred_element_type=jnp.float32
    )
    grad_delta = (rate * valid)[:, :, None] * seen
    grad_moved = grad_delta.astype(jnp.bfloat16)
    grad_score = valid * rate * (1.0 - rate) * jnp.sum(seen * delta, axis=-1)
    grad_moved_all = lax.all_gather(grad_moved, "seq", axis=1, tiled=True)
    grad_active = jnp.einsum(
        "sjd,fd->sjf", grad_moved_all, w_down, preferred_element_type=jnp.float32
    )
    grad_down = jnp.einsum(
        "sjf,sjd->fd", activated, grad_moved_all, preferred_element_type=jnp.float32
    )
    gelu_value, gelu_back = jax.vjp(jax.nn.gelu, up_proj)
    grad_up_proj = gelu_back(grad_active)[0].astype(jnp.bfloat16)
    grad_up = jnp.einsum(
        "sjd,sjf->df", normed_all, grad_up_proj, preferred_element_type=jnp.float32
    )
    grad_normed_part = jnp.einsum(
        "sjf,df->sjd", grad_up_proj, w_up, preferred_element_type=jnp.float32
    )
    grad_normed_mlp = lax.psum_scatter(grad_normed_part, "seq", scatter_dimension=1, tiled=True)
    norm_value, norm_back = jax.vjp(norm_scale, hidden, gain_mlp)
    grad_hidden, grad_gain_mlp = norm_back(grad_normed_mlp)
    grad_attended = (grad_delta + grad_hidden).astype(jnp.bfloat16)
    grad_out = jnp.einsum("sid,sie->de", mixed, grad_attended, preferred_element_type=jnp.float32)
    grad_mixed = jnp.einsum(
        "sie,de->sid", grad_attended, w_out, preferred_element_type=jnp.float32
    ).astype(jnp.bfloat16)
    keys_back, values_back, probs_back, probs_low_back = (keys_all, values_all, probs, probs_low)
    mixed_heads = split_heads(grad_mixed)
    grad_probs = jnp.einsum(
        "sihd,sjhd->shij", mixed_heads, split_heads(values_back), preferred_element_type=jnp.float32
    )
    grad_value_part = jnp.einsum(
        "shij,sihd->sjhd", probs_low_back, mixed_heads, preferred_element_type=jnp.float32
    )
    grad_logits = probs_back * (
        grad_probs - jnp.sum(grad_probs * probs_back, axis=-1, keepdims=True)
    )
    grad_logits = grad_logits.astype(jnp.bfloat16)
    grad_query_rows = (
        jnp.einsum(
            "shij,sjhd->sihd",
            grad_logits,
            split_heads(keys_back),
            preferred_element_type=jnp.float32,
        )
        * scaling
    )
    grad_query_rows = grad_query_rows.reshape(seqs, local_slots, width).astype(jnp.bfloat16)
    grad_key_part = (
        jnp.einsum(
            "shij,sihd->sjhd", grad_logits, split_heads(query), preferred_element_type=jnp.float32
        )
        * scaling
    )
    grad_key_rows, grad_value_rows = (
        lax.psum_scatter(
            grad_key_part.reshape(seqs, slots, width), "seq", scatter_dimension=1, tiled=True
        ),
        lax.psum_scatter(
            grad_value_part.reshape(seqs, slots, width), "seq", scatter_dimension=1, tiled=True
        ),
    )
    grad_key_rows = grad_key_rows.astype(jnp.bfloat16)
    grad_value_rows = grad_value_rows.astype(jnp.bfloat16)
    grad_query = jnp.einsum(
        "sid,sie->de", normed, grad_query_rows, preferred_element_type=jnp.float32
    )
    grad_key = jnp.einsum("sid,sie->de", normed, grad_key_rows, preferred_element_type=jnp.float32)
    grad_value = jnp.einsum(
        "sid,sie->de", normed, grad_value_rows, preferred_element_type=jnp.float32
    )
    grad_normed = (
        jnp.einsum("sie,de->sid", grad_query_rows, w_query, preferred_element_type=jnp.float32)
        + jnp.einsum("sie,de->sid", grad_key_rows, w_key, preferred_element_type=jnp.float32)
        + jnp.einsum("sie,de->sid", grad_value_rows, w_value, preferred_element_type=jnp.float32)
    )
    first_value, first_back = jax.vjp(norm_scale, chosen, gain_attn)
    grad_chosen_norm, grad_gain_attn = first_back(grad_normed)
    grad_router = jnp.einsum("si,sid->d", grad_score, chosen, precision=lax.Precision.HIGHEST)
    grad_chosen = (
        grad_chosen_norm + grad_hidden + grad_score[:, :, None] * w_router.astype(jnp.float32)
    )
    grad_chosen_all = lax.all_gather(grad_chosen.astype(jnp.bfloat16), "seq", axis=1, tiled=True)
    grad_tokens = cotangent.astype(jnp.float32) + jnp.einsum(
        "sjr,sjd->srd", placing, grad_chosen_all, preferred_element_type=jnp.float32
    )
    summed = lax.psum(
        (grad_query, grad_key, grad_value, grad_out, grad_router, grad_gain_attn, grad_gain_mlp),
        ("batch", "seq"),
    )
    grad_up_sum, grad_down_sum = lax.psum((grad_up, grad_down), "batch")
    return (
        output.astype(jnp.bfloat16),
        grad_tokens.astype(jnp.bfloat16),
        summed[4],
        summed[5],
        summed[6],
        summed[0],
        summed[1],
        summed[2],
        summed[3],
        grad_up_sum,
        grad_down_sum,
    )


def solution(mesh):
    placed = (
        P("batch", "seq", None),
        P("batch"),
        P("batch", "seq"),
        P(),
        P(),
        P(),
        P(),
        P(),
        P(),
        P(),
        P(None, "seq"),
        P("seq", None),
        P("batch", "seq", None),
    )
    return jax.shard_map(
        body,
        mesh=mesh,
        in_specs=placed,
        out_specs=(
            P("batch", "seq", None),
            P("batch", "seq", None),
            P(),
            P(),
            P(),
            P(),
            P(),
            P(),
            P(),
            P(None, "seq"),
            P("seq", None),
        ),
        check_vma=False,
    )
```

profile of v0, /device:TPU:0, one launch (start us, length us, event | category | flops | bytes accessed | tf_op | source)
XLA Modules:
  0.0 652.9 jit_solution(1916861347080338620)
XLA Ops:
  7.3 0.7 all-gather.4.cloned.1.call-update
  8.0 0.7 all-gather.6.cloned.1.call-update
  10.7 48.0 %all-gather.4.cloned.1.call-done = bf16[2,2048,768]{2,1,0:T(8,128)(2,1)} async-done(((bf16[2,512,768]{2,1,0:T(8,128)(2,1)}), bf16[2,2048,768]{2,1,0:T(8,128)(2,1)}) %all-gather.4.cloned.1.call-update) | async-done | bytes 6291472 | tf_op jit(solution)/shard_map/all_gather | solution.py:72
  58.7 4.1 multiply_reduce_fusion.7
  63.3 9.1 %all_gather.30 = bf16[2,256,768]{2,1,0:T(8,128)(2,1)} all-gather(bf16[2,64,768]{2,1,0:T(8,128)(2,1)S(1)} %fusion.39), channel_id=1, replica_groups=mesh['batch'=8,'seq'=4] {'seq'}, dimensions={1}, use_global_device_ids=true | all-gather | bytes 983040 | tf_op jit(solution)/shard_map/all_gather | solution.py:94
  72.5 2.4 copy.55
  74.9 1.6 fusion.36
  77.1 13.9 %all_gather.29 = bf16[2,256,768]{2,1,0:T(8,128)(2,1)} all-gather(bf16[2,64,768]{2,1,0:T(8,128)(2,1)S(1)} %fusion.33), channel_id=1, replica_groups=mesh['batch'=8,'seq'=4] {'seq'}, dimensions={1}, use_global_device_ids=true | all-gather | bytes 983040 | tf_op jit(solution)/shard_map/all_gather | solution.py:95
  91.0 2.3 copy.54
  93.3 1.8 fusion.70
  95.1 2.2 convolution_convert_fusion.1
  97.3 1.1 multiply_reduce_fusion.6
  98.9 13.8 %all_gather.31 = bf16[2,256,768]{2,1,0:T(8,128)(2,1)} all-gather(bf16[2,64,768]{2,1,0:T(8,128)(2,1)S(1)} %multiply_convert_fusion.3), channel_id=1, replica_groups=mesh['batch'=8,'seq'=4] {'seq'}, dimensions={1}, use_global_device_ids=true | all-gather | bytes 983040 | tf_op jit(solution)/shard_map/all_gather | solution.py:101
  112.7 2.5 all-gather.6.cloned.1.call-done
  115.1 4.9 multiply_convert_fusion.5
  120.0 8.6 %all_gather.34 = bf16[2,256,768]{2,1,0:T(8,128)(2,1)S(1)} all-gather(bf16[2,64,768]{2,1,0:T(8,128)(2,1)S(1)} %get-tuple-element.34), channel_id=1, replica_groups=mesh['batch'=8,'seq'=4] {'seq'}, dimensions={1}, use_global_device_ids=true | all-gather | bytes 983040 | tf_op jit(solution)/shard_map/all_gather | solution.py:117
  128.6 0.8 fusion.17
  129.5 0.7 copy-done.67
  130.2 1.5 fusion.8
  131.7 0.9 copy-done.72
  132.6 2.0 fusion.15
  134.6 1.2 copy-done.68
  135.8 3.4 convolution_convert_fusion
  139.3 23.7 %reduce-scatter.7.cloned.1.call-done = f32[2,64,768]{2,1,0:T(8,128)} async-done(((f32[2,256,768]{2,1,0:T(8,128)}), f32[2,64,768]{2,1,0:T(8,128)}) %reduce-scatter.7.cloned.1.call-update) | async-done | bytes 393232 | tf_op jit(solution)/shard_map/reduce_scatter | solution.py:132
  162.9 1.7 multiply_reduce_fusion.1
  164.7 24.7 %reduce-scatter.5.cloned.1.call-done = bf16[2,64,768]{2,1,0:T(8,128)(2,1)} async-done(((bf16[2,256,768]{2,1,0:T(8,128)(2,1)}), bf16[2,64,768]{2,1,0:T(8,128)(2,1)}) %reduce-scatter.5.cloned.1.call-update) | async-done | bytes 196624 | tf_op jit(solution)/shard_map/reduce_scatter | solution.py:105
  189.4 1.9 multiply_reduce_fusion.3
  192.1 3.0 fusion.56
  195.1 3.0 copy.63
  198.3 0.9 copy-done.27
  199.2 2.2 multiply_reduce_fusion
  202.4 1.5 convolution_multiply_fusion
  203.9 3.0 copy.61
  207.0 1.1 copy-done.29
  208.1 3.5 convolution_bitcast_fusion.1
  211.6 2.3 convolution_bitcast_fusion
  214.1 0.9 copy-done.21
  215.0 1.9 convolution_bitcast_fusion.2
  217.3 1.9 convolution_bitcast_fusion.5
  219.2 7.2 %reduce-scatter.11.cloned.1.call-done = f32[2,64,768]{2,1,0:T(8,128)} async-done(((f32[2,256,768]{2,1,0:T(8,128)}), f32[2,64,768]{2,1,0:T(8,128)}) %reduce-scatter.11.cloned.1.call-update) | async-done | bytes 393232 | tf_op jit(solution)/shard_map/reduce_scatter | solution.py:172
  226.4 2.9 convolution_bitcast_fusion.3
  229.3 28.4 %reduce-scatter.9.cloned.1.call-done = f32[2,64,768]{2,1,0:T(8,128)} async-done(((f32[2,256,768]{2,1,0:T(8,128)}), f32[2,64,768]{2,1,0:T(8,128)}) %reduce-scatter.9.cloned.1.call-update) | async-done | bytes 393232 | tf_op jit(solution)/shard_map/reduce_scatter | solution.py:169
  257.7 2.9 convolution_bitcast_fusion.4
  261.9 5.1 all-gather
  267.2 0.9 convolution_reduce_fusion
  268.6 8.8 %all_gather.32 = bf16[2,256,768]{2,1,0:T(8,128)(2,1)S(1)} all-gather(bf16[2,64,768]{2,1,0:T(8,128)(2,1)S(1)} %get-tuple-element.27), channel_id=1, replica_groups=mesh['batch'=8,'seq'=4] {'seq'}, dimensions={1}, use_global_device_ids=true | all-gather | bytes 983040 | tf_op jit(solution)/shard_map/all_gather | solution.py:110
  277.5 1.8 add_convert_fusion.1
  279.8 0.7 copy-done.8
  280.7 0.6 multiply_reduce_fusion.2
  281.4 43.9 %all-reduce = (f32[768]{0:T(1024)}, f32[768]{0:T(1024)}, f32[768]{0:T(1024)}) all-reduce(f32[768]{0:T(1024)S(1)} %copy-done.47, f32[768]{0:T(1024)S(1)} %get-tuple-element.13, f32[768]{0:T(1024)S(1)} %copy-done.46), channel_id=1, replica_groups=mesh['batch'=8,'seq'=4] {'batch','seq'}, use_global_device_ids=true, to_apply=%region_12.13 | all-reduce | flops 2304 | bytes 18432 | tf_op jit(solution)/shard_map/psum | solution.py:200
  325.6 9.4 %all_gather.35 = bf16[2,256,768]{2,1,0:T(8,128)(2,1)S(1)} all-gather(bf16[2,64,768]{2,1,0:T(8,128)(2,1)S(1)} %fusion.55), channel_id=1, replica_groups=mesh['batch'=8,'seq'=4] {'seq'}, dimensions={1}, use_global_device_ids=true | all-gather | bytes 983040 | tf_op jit(solution)/shard_map/all_gather | solution.py:196
  335.0 1.8 add_convert_fusion
  336.8 96.1 %all-reduce.8.cloned.1.call-done = (f32[768,768]{1,0:T(8,128)}, f32[768,768]{1,0:T(8,128)}) async-done(((f32[768,768]{1,0:T(8,128)}, f32[768,768]{1,0:T(8,128)}), (f32[768,768]{1,0:T(8,128)}, f32[768,768]{1,0:T(8,128)})) %all-reduce.8.cloned.1.call-update) | async-done | bytes 4718608 | tf_op jit(solution)/shard_map/psum | solution.py:204
  432.9 198.3 %all-reduce.6.cloned.1.call-done = (f32[768,768]{1,0:T(8,128)}, f32[768,768]{1,0:T(8,128)}, f32[768,768]{1,0:T(8,128)}, f32[768,768]{1,0:T(8,128)}) async-done(((f32[768,768]{1,0:T(8,128)}, f32[768,768]{1,0:T(8,128)}, f32[768,768]{1,0:T(8,128)}, f32[768,768]{1,0:T(8,128)}), (f32[768,768]{1,0:T(8,128)}, f32[768,768]{1,0:T(8,128)}, f32[768,768]{1,0:T(8,128)}, ...) | async-done | bytes 9437200 | tf_op jit(solution)/shard_map/psum | solution.py:200
  631.2 3.4 copy.82
  634.6 1.4 copy.83
  636.0 1.1 copy-done.17
  637.1 1.4 copy.84
  638.5 1.1 copy-done.16
  639.7 1.4 copy.85
  641.1 1.1 copy-done.15
  642.2 1.4 copy.86
  643.6 1.1 copy-done.14
  644.7 1.4 copy.87
  (178 shorter events, 9.1 us)
Async XLA Ops:
  7.2 121.4 %copy-start = (bf16[768,768]{1,0:T(8,128)(2,1)S(1)}, bf16[768,768]{1,0:T(8,128)(2,1)}, u32[]{:S(2)}) copy-start(bf16[768,768]{1,0:T(8,128)(2,1)} %param.23) | copy-start | bytes 3538948
  7.2 1.6 copy-start.58
  7.2 2.2 copy-start.69
  7.2 51.5 %copy-start.33 = (s32[2,64]{1,0:T(2,128)S(1)}, s32[2,64]{1,0:T(2,128)}, u32[]{:S(2)}) copy-start(s32[2,64]{1,0:T(2,128)} %param.15) | copy-start | bytes 1540
  7.2 51.5 %all-gather.4.cloned.1.call-start = ((), (), s32[]{:S(2)}) async-start(), calls=%async_computation.4 | async-start | bytes 7864320 | tf_op jit(solution)/shard_map/all_gather | solution.py:72
  8.0 107.2 %all-gather.6.cloned.1.call-start = ((), (), s32[]{:S(2)}) async-start(), calls=%async_computation.6 | async-start | bytes 7864320 | tf_op jit(solution)/shard_map/all_gather | solution.py:73
  8.7 154.2 %reduce-scatter.7.cloned.1.call-start = ((), (), s32[]{:S(2)}) async-start(), calls=%async_computation.7 | async-start | bytes 1966080 | tf_op jit(solution)/shard_map/reduce_scatter | solution.py:132
  10.7 52.2 %copy-start.34 = (f32[768]{0:T(1024)S(1)}, f32[768]{0:T(1024)}, u32[]{:S(2)}) copy-start(f32[768]{0:T(1024)} %param.17) | copy-start | bytes 9220
  10.7 52.3 %copy-start.5 = (bf16[768,768]{1,0:T(8,128)(2,1)S(1)}, bf16[768,768]{1,0:T(8,128)(2,1)}, u32[]{:S(2)}) copy-start(bf16[768,768]{1,0:T(8,128)(2,1)} %param.20) | copy-start | bytes 3538948
  62.9 9.6 %copy-start.54 = (f32[2,64]{1,0:T(2,128)}, f32[2,64]{1,0:T(2,128)S(1)}, u32[]{:S(2)}) copy-start(f32[2,64]{1,0:T(2,128)S(1)} %get-tuple-element.29) | copy-start | bytes 1540
  62.9 9.6 %copy-start.43 = (f32[2,64]{1,0:T(2,128)}, f32[2,64]{1,0:T(2,128)S(1)}, u32[]{:S(2)}) copy-start(f32[2,64]{1,0:T(2,128)S(1)} %fusion.65) | copy-start | bytes 1540
  72.5 4.2 copy-start.7
  76.7 16.6 %copy-start.25 = (bf16[2,64,768]{1,2,0:T(8,128)(2,1)}, bf16[2,64,768]{1,2,0:T(8,128)(2,1)S(1)}, u32[]{:S(2)}) copy-start(bf16[2,64,768]{1,2,0:T(8,128)(2,1)S(1)} %copy.74) | copy-start | bytes 589828
  77.0 16.2 %copy-start.12 = (bf16[2,256,768]{1,2,0:T(8,128)(2,1)S(1)}, bf16[2,256,768]{1,2,0:T(8,128)(2,1)}, u32[]{:S(2)}) copy-start(bf16[2,256,768]{1,2,0:T(8,128)(2,1)} %copy.55) | copy-start | bytes 2359300
  77.0 16.2 %copy-start.35 = (pred[2,64,256]{2,1,0:T(8,128)(4,1)S(1)}, pred[2,64,256]{2,1,0:T(8,128)(4,1)}, u32[]{:S(2)}) copy-start(pred[2,64,256]{2,1,0:T(8,128)(4,1)} %broadcast_and_fusion) | copy-start | bytes 98308
  95.1 2.2 copy-start.38
  95.1 2.2 copy-start.4
  97.3 1.4 copy-start.61
  97.3 1.4 copy-start.65
  97.3 1.5 copy-start.32
  98.6 21.4 %copy-start.56 = (f32[1,2,64]{2,0,1:T(1,128)}, f32[1,2,64]{2,0,1:T(1,128)S(1)}, u32[]{:S(2)}) copy-start(f32[1,2,64]{2,0,1:T(1,128)S(1)} %fusion.59) | copy-start | bytes 1540
  98.8 21.2 %copy-start.41 = (f32[2,64]{1,0:T(2,128)}, f32[2,64]{1,0:T(2,128)S(1)}, u32[]{:S(2)}) copy-start(f32[2,64]{1,0:T(2,128)S(1)} %compare_select_fusion) | copy-start | bytes 1540
  115.1 13.5 %copy-start.28 = (bf16[2,256,768]{2,1,0:T(8,128)(2,1)S(1)}, bf16[2,256,768]{2,1,0:T(8,128)(2,1)}, u32[]{:S(2)}) copy-start(bf16[2,256,768]{2,1,0:T(8,128)(2,1)} %all_gather.31) | copy-start | bytes 2359300
  128.6 1.6 copy-start.67
  130.2 1.5 copy-start.70
  134.6 54.8 %reduce-scatter.5.cloned.1.call-start = ((), (), s32[]{:S(2)}) async-start(), calls=%async_computation.5 | async-start | bytes 983040 | tf_op jit(solution)/shard_map/reduce_scatter | solution.py:105
  139.2 50.2 %copy-start.10 = (f32[2,64,768]{2,1,0:T(8,128)S(1)}, f32[2,64,768]{2,1,0:T(8,128)}, u32[]{:S(2)}) copy-start(f32[2,64,768]{2,1,0:T(8,128)} %get-tuple-element.35) | copy-start | bytes 1179652
  139.2 50.2 %copy-start.24 = (f32[2,64,768]{2,1,0:T(8,128)S(1)}, f32[2,64,768]{2,1,0:T(8,128)}, u32[]{:S(2)}) copy-start(f32[2,64,768]{2,1,0:T(8,128)} %get-tuple-element.33) | copy-start | bytes 1179652
  139.2 50.2 %copy-start.42 = (f32[2,64]{1,0:T(2,128)S(1)}, f32[2,64]{1,0:T(2,128)}, u32[]{:S(2)}) copy-start(f32[2,64]{1,0:T(2,128)} %copy-done.41) | copy-start | bytes 1540
  139.2 87.2 %reduce-scatter.11.cloned.1.call-start = ((), (), s32[]{:S(2)}) async-start(), calls=%async_computation.9 | async-start | bytes 1966080 | tf_op jit(solution)/shard_map/reduce_scatter | solution.py:172
  164.7 26.6 %copy-start.50 = (f32[2,64]{1,0:T(2,128)}, f32[2,64]{1,0:T(2,128)S(1)}, u32[]{:S(2)}) copy-start(f32[2,64]{1,0:T(2,128)S(1)} %multiply_multiply_fusion.4) | copy-start | bytes 1540
  198.1 59.6 %reduce-scatter.9.cloned.1.call-start = ((), (), s32[]{:S(2)}) async-start(), calls=%async_computation.8 | async-start | bytes 1966080 | tf_op jit(solution)/shard_map/reduce_scatter | solution.py:169
  199.2 2.2 copy-start.19
  207.0 226.0 %all-reduce.8.cloned.1.call-start = ((), (), s32[]{:S(2)}) async-start(), calls=%async_computation.11 | async-start | bytes 9437184 | tf_op jit(solution)/shard_map/psum | solution.py:204
  208.1 3.5 copy-start.31
  208.1 3.5 copy-start.71
  214.0 2.9 copy-start.13
  214.0 417.2 %all-reduce.6.cloned.1.call-start = ((), (), s32[]{:S(2)}) async-start(), calls=%async_computation.10 | async-start | bytes 18874368 | tf_op jit(solution)/shard_map/psum | solution.py:200
  260.6 6.4 copy-start.57
  260.6 6.4 copy-start.62
  260.6 6.4 copy-start.63
  260.6 6.4 copy-start.66
  260.7 7.4 %copy-start.9 = (bf16[768,768]{1,0:T(8,128)(2,1)S(1)}, bf16[768,768]{1,0:T(8,128)(2,1)}, u32[]{:S(2)}) copy-start(bf16[768,768]{1,0:T(8,128)(2,1)} %param.19) | copy-start | bytes 3538948
  267.1 10.4 %copy-start.36 = (s32[512]{0:T(512)}, s32[512]{0:T(512)S(1)}, u32[]{:S(2)}) copy-start(s32[512]{0:T(512)S(1)} %iota_add_fusion) | copy-start | bytes 6148
  267.2 10.3 %copy-start.52 = (f32[2,64]{1,0:T(2,128)}, f32[2,64]{1,0:T(2,128)S(1)}, u32[]{:S(2)}) copy-start(f32[2,64]{1,0:T(2,128)S(1)} %multiply_multiply_fusion.2) | copy-start | bytes 1540
  268.1 9.3 %copy-start.2 = (bf16[2,512,768]{2,1,0:T(8,128)(2,1)S(1)}, bf16[2,512,768]{2,1,0:T(8,128)(2,1)}, u32[]{:S(2)}) copy-start(bf16[2,512,768]{2,1,0:T(8,128)(2,1)} %param.13) | copy-start | bytes 4718596
  277.5 1.8 copy-start.6
  277.5 1.8 copy-start.23
  279.3 1.3 copy-start.22
  279.3 1.3 copy-start.44
  280.6 44.7 %copy-start.55 = (f32[2,64]{1,0:T(2,128)S(1)}, f32[2,64]{1,0:T(2,128)}, u32[]{:S(2)}) copy-start(f32[2,64]{1,0:T(2,128)} %copy-done.54) | copy-start | bytes 1540
  280.6 44.7 %copy-start.11 = (f32[2,64,768]{2,1,0:T(8,128)S(1)}, f32[2,64,768]{2,1,0:T(8,128)}, u32[]{:S(2)}) copy-start(f32[2,64,768]{2,1,0:T(8,128)} %reduce-scatter.7.cloned.1.call-done) | copy-start | bytes 1179652
  280.7 44.7 %copy-start.45 = (f32[2,64]{1,0:T(2,128)S(1)}, f32[2,64]{1,0:T(2,128)}, u32[]{:S(2)}) copy-start(f32[2,64]{1,0:T(2,128)} %copy-done.43) | copy-start | bytes 1540
  280.7 44.7 %copy-start.48 = (f32[768]{0:T(1024)S(1)}, f32[768]{0:T(1024)}, u32[]{:S(2)}) copy-start(f32[768]{0:T(1024)} %convert_element_type.120) | copy-start | bytes 9220
  280.7 44.7 %copy-start.51 = (f32[2,64]{1,0:T(2,128)S(1)}, f32[2,64]{1,0:T(2,128)}, u32[]{:S(2)}) copy-start(f32[2,64]{1,0:T(2,128)} %copy-done.50) | copy-start | bytes 1540
  280.7 44.7 %copy-start.53 = (f32[2,64]{1,0:T(2,128)S(1)}, f32[2,64]{1,0:T(2,128)}, u32[]{:S(2)}) copy-start(f32[2,64]{1,0:T(2,128)} %copy-done.52) | copy-start | bytes 1540
  281.3 53.7 %copy-start.3 = (bf16[2,512,768]{2,1,0:T(8,128)(2,1)S(1)}, bf16[2,512,768]{2,1,0:T(8,128)(2,1)}, u32[]{:S(2)}) copy-start(bf16[2,512,768]{2,1,0:T(8,128)(2,1)} %param.25) | copy-start | bytes 4718596
  281.3 53.7 %copy-start.37 = (s32[512]{0:T(512)S(1)}, s32[512]{0:T(512)}, u32[]{:S(2)}) copy-start(s32[512]{0:T(512)} %copy-done.36) | copy-start | bytes 6148
  631.2 3.4 copy-start.18
  634.6 2.5 copy-start.17
  637.1 2.5 copy-start.16
  639.7 2.5 copy-start.15
  642.2 2.5 copy-start.14
  642.2 3.9 copy-start.1
  (17 other events, 16.4 us)
Sparse Core Ops, SparseCore 0:
  9.6 49.0 all-gather.3
  60.3 54.7 all-gather.5
  134.7 28.1 reduce-scatter.6
  166.1 23.2 reduce-scatter.4
  198.2 28.1 reduce-scatter.10
  229.5 28.1 reduce-scatter.8
  261.9 170.9 all-reduce.7
  440.3 190.8 all-reduce.5
where the time goes:
time: 654 us; the launch traced here: 653 us
  waiting for transfers between devices  430 us (66%)
  blocking collectives  113 us (17%)
  matrix products  53.4 us (8%)
  local copies, waits for them, and re-layouts  35.2 us (5%)
  between operations  14.8 us (2%)
    psum x1, waiting for transfers between devices, body(): lax.psum((grad_query, grad_key, grad_value, grad_out, grad_router, grad_g...  198 us
    psum x1, waiting for transfers between devices, body(): grad_up_sum, grad_down_sum = lax.psum((grad_up, grad_down), 'batch')  96.1 us
    all_gather x1, waiting for transfers between devices, body(): lax.all_gather(tokens, 'seq', axis=1, tiled=True)  48 us
    psum x1, blocking collectives, body(): lax.psum((grad_query, grad_key, grad_value, grad_out, grad_router, grad_g...  43.9 us
    reduce_scatter x1, waiting for transfers between devices, body(): lax.psum_scatter(grad_key_part.reshape(seqs, slots, width), 'seq', scatte...  28.4 us
    reduce_scatter x1, waiting for transfers between devices, body(): lax.psum_scatter(partial_out.astype(jnp.bfloat16), 'seq', scatter_dimensi...  24.7 us
    unnamed x154, local copies, waits for them, and re-layouts  24 us
    reduce_scatter x1, waiting for transfers between devices, body(): lax.psum_scatter(grad_normed_part, 'seq', scatter_dimension=1, tiled=True)  23.7 us
  transfers between devices with their start and end apart: 8, of which 8 were waited for; matrix products, arithmetic and copies ran while one was open for 8% of the time, Pallas kernels for 0%

commit v1 on v0

v1 whole, which is shorter than its diff:
```python
import functools

import jax
import jax.numpy as jnp
from jax import lax
from jax.experimental import pallas as pl
from jax.experimental.pallas import tpu as pltpu
from jax.sharding import PartitionSpec as P

NH = 12
EPS = 1e-06
F32 = jnp.float32
BF16 = jnp.bfloat16
VMEM = pl.BlockSpec(memory_space=pltpu.VMEM)
SMEM = pl.BlockSpec(memory_space=pltpu.SMEM)


def mm(a, b):
    return jnp.dot(a, b, preferred_element_type=F32)


def mm_nt(a, b):
    return lax.dot_general(a, b, (((1,), (1,)), ((), ())), preferred_element_type=F32)


def mm_tn(a, b):
    return lax.dot_general(a, b, (((0,), (0,)), ((), ())), preferred_element_type=F32)


def call(kernel, ins, outs, specs=None, scratch=(), vmem=40, flops=0):
    shapes = tuple(jax.ShapeDtypeStruct(shape, dtype) for shape, dtype in outs)
    moved = sum(v.size * v.dtype.itemsize for v in list(ins) + list(shapes))
    return pl.pallas_call(
        kernel,
        out_shape=shapes,
        in_specs=specs or [VMEM] * len(ins),
        out_specs=tuple(VMEM for _ in shapes),
        scratch_shapes=list(scratch),
        cost_estimate=pl.CostEstimate(flops=flops, bytes_accessed=moved, transcendentals=0),
        compiler_params=pltpu.CompilerParams(vmem_limit_bytes=vmem * 1024 * 1024),
    )(*ins)


def select_kernel(meta, p0, p1, p2, p3, rows, own, other, hot):
    core = meta[1]
    length = rows.shape[1]
    local = p0.shape[1]
    base = meta[0] * length
    down = lax.broadcasted_iota(jnp.int32, (local, local), 0)
    along = lax.broadcasted_iota(jnp.int32, (local, local), 1)
    places = lax.broadcasted_iota(jnp.int32, (local, length), 1)
    for seq, out in ((1 - core, other), (core, own)):
        for k, part in enumerate((p0, p1, p2, p3)):
            row = part[pl.ds(seq, 1), :]
            column = jnp.sum(jnp.where(down == along, row, 0), axis=1, keepdims=True)
            at = pl.multiple_of(meta[4 + k] * local, local)
            hot[pl.ds(at, local), :] = jnp.where(column - base == places, 1.0, 0.0).astype(BF16)
        out[...] = mm(hot[...], rows[seq]).astype(BF16)


def place_kernel(meta, picks, rows, own, other, out):
    core = meta[1]
    length = rows.shape[1]
    slots = picks.shape[1]
    base = meta[0] * length
    places = lax.broadcasted_iota(jnp.int32, (length, slots), 0) + base
    for seq, update in ((core, own), (1 - core, other)):
        hot = jnp.where(picks[pl.ds(seq, 1), :] == places, 1.0, 0.0).astype(BF16)
        out[seq] = (rows[seq].astype(F32) + mm(hot, update[...])).astype(BF16)


def attend_kernel(
    meta, here, there, w_router, gain_attn, gain_mlp, w_query, w_key, w_value, w_out,
    chosen_out, normed_out, query_out, key_out, value_out, probs_out, mixed_out, attended_out,
    normed_mlp_out, rate_out,
):
    count = meta[2]
    slots, width = here.shape
    chosen = here[...].astype(F32) + there[...].astype(F32)
    chosen_out[...] = chosen.astype(BF16)
    score = jnp.sum(chosen * w_router[...].astype(F32), axis=-1, keepdims=True)
    rate = jax.nn.sigmoid(score)
    valid = lax.broadcasted_iota(jnp.int32, (slots, 1), 0) < count
    rate_out[...] = jnp.broadcast_to(jnp.where(valid, rate, 0.0), rate_out.shape)
    scale = lax.rsqrt(jnp.mean(chosen * chosen, axis=-1, keepdims=True) + EPS)
    normed = (chosen * scale * gain_attn[...]).astype(BF16)
    normed_out[...] = normed
    query_out[...] = mm(normed, w_query[...]).astype(BF16)
    key_out[...] = mm(normed, w_key[...]).astype(BF16)
    value_out[...] = mm(normed, w_value[...]).astype(BF16)
    head = width // NH
    pair = 2 * head
    i = lax.broadcasted_iota(jnp.int32, (slots, slots), 0)
    j = lax.broadcasted_iota(jnp.int32, (slots, slots), 1)
    allowed = (j <= i) & (j < count)
    first = lax.broadcasted_iota(jnp.int32, (slots, pair), 1) < head
    for p in range(NH // 2):
        cols = slice(p * pair, (p + 1) * pair)
        query = query_out[:, cols]
        keys = key_out[:, cols]
        values = value_out[:, cols]
        halves = []
        for h in range(2):
            mine = first if h == 0 else ~first
            logits = mm_nt(jnp.where(mine, query, jnp.zeros_like(query)), keys) * (head ** -0.5)
            logits = jnp.where(allowed, logits, -1e30)
            expd = jnp.exp(logits - jnp.max(logits, axis=-1, keepdims=True))
            probs = expd / jnp.sum(expd, axis=-1, keepdims=True)
            probs_out[2 * p + h] = probs
            halves.append(mm(probs.astype(BF16), values))
        mixed_out[:, cols] = jnp.where(first, halves[0], halves[1]).astype(BF16)
    attended = mm(mixed_out[...], w_out[...])
    attended_out[...] = attended
    hidden = chosen + attended
    scale = lax.rsqrt(jnp.mean(hidden * hidden, axis=-1, keepdims=True) + EPS)
    normed_mlp_out[...] = (hidden * scale * gain_mlp[...]).astype(BF16)


def mlp_kernel(
    normed, rate, here, there, up_own, up_other, down_own, down_other,
    act_own, act_other, back_own, back_other, grad_moved, grad_normed,
):
    seen = here[...].astype(F32) + there[...].astype(F32)
    moved = (rate[:, :1] * seen).astype(BF16)
    grad_moved[...] = moved
    total = None
    for w_up, w_down, act, back in (
        (up_own, down_own, act_own, back_own),
        (up_other, down_other, act_other, back_other),
    ):
        up = mm(normed[...], w_up[...])
        square = up * up
        root = 0.7978845608028654
        t = jnp.tanh(root * (up + 0.044715 * (square * up)))
        act[...] = (0.5 * up * (1.0 + t)).astype(BF16)
        slope = 0.5 * (1.0 + t) + (0.5 * root) * up * (1.0 - t * t) * (1.0 + 0.134145 * square)
        grad_up = (mm_nt(moved, w_down[...]) * slope).astype(BF16)
        back[...] = grad_up
        part = mm_nt(grad_up, w_up[...])
        total = part if total is None else total + part
    grad_normed[...] = total.astype(BF16)


def mlp_grads_kernel(
    normed, grad_moved, act_own, act_other, back_own, back_other, down_own, down_other,
    gd_own, gd_other, gu_own, gu_other, moved,
):
    gd_other[...] = mm_tn(act_other[...], grad_moved[...]).astype(BF16)
    gd_own[...] = mm_tn(act_own[...], grad_moved[...])
    gu_other[...] = mm_tn(normed[...], back_other[...]).astype(BF16)
    gu_own[...] = mm_tn(normed[...], back_own[...])
    moved[...] = (mm(act_own[...], down_own[...]) + mm(act_other[...], down_other[...])).astype(BF16)


def norm_back(values, gain, grad):
    scale = lax.rsqrt(jnp.mean(values * values, axis=-1, keepdims=True) + EPS)
    scaled = grad * gain
    inner = jnp.mean(scaled * values, axis=-1, keepdims=True)
    back = scale * scaled - values * (scale * scale * scale * inner)
    return back, jnp.sum(grad * values * scale, axis=0, keepdims=True)


def attend_back_kernel(
    chosen_in, attended, gain_attn, gain_mlp, gn_here, gn_there, rate, seen_here, seen_there,
    query_in, key_in, value_in, probs_in, w_query, w_key, w_value, w_out,
    grad_attended_out, grad_query, grad_key, grad_value, grad_sum, small, mixed_back,
):
    slots, width = chosen_in.shape
    head = width // NH
    pair = 2 * head
    chosen = chosen_in[...].astype(F32)
    grad_normed_mlp = gn_here[...].astype(F32) + gn_there[...].astype(F32)
    grad_hidden, gain_grad = norm_back(chosen + attended[...], gain_mlp[...], grad_normed_mlp)
    small[1:2, :] = gain_grad
    seen = seen_here[...].astype(F32) + seen_there[...].astype(F32)
    grad_attended = (rate[:, :1] * seen + grad_hidden).astype(BF16)
    grad_attended_out[...] = grad_attended
    mixed_back[...] = mm_nt(grad_attended, w_out[...]).astype(BF16)
    first = lax.broadcasted_iota(jnp.int32, (slots, pair), 1) < head
    factor = head ** -0.5
    for p in range(NH // 2):
        cols = slice(p * pair, (p + 1) * pair)
        query = query_in[:, cols]
        keys = key_in[:, cols]
        values = value_in[:, cols]
        back = mixed_back[:, cols]
        parts = []
        for h in range(2):
            mine = first if h == 0 else ~first
            probs = probs_in[2 * p + h]
            grad_probs = mm_nt(jnp.where(mine, back, jnp.zeros_like(back)), values)
            gv = mm_tn(probs.astype(BF16), back)
            inner = jnp.sum(grad_probs * probs, axis=-1, keepdims=True)
            grad_logits = (probs * (grad_probs - inner)).astype(BF16)
            gq = mm(grad_logits, keys) * factor
            gk = mm_tn(grad_logits, query) * factor
            parts.append((gq, gk, gv))
        for out, a, b in zip((grad_query, grad_key, grad_value), parts[0], parts[1]):
            out[:, cols] = jnp.where(first, a, b).astype(BF16)
    grad_normed = (
        mm_nt(grad_query[...], w_query[...])
        + mm_nt(grad_key[...], w_key[...])
        + mm_nt(grad_value[...], w_value[...])
    )
    back, gain_grad = norm_back(chosen, gain_attn[...], grad_normed)
    small[0:1, :] = gain_grad
    grad_sum[...] = back + grad_hidden


def attend_grads_kernel(
    meta, normed, mixed, grad_query, grad_key, grad_value, grad_attended, own, other, full
):
    core = meta[1]
    width = normed.shape[1]
    half = width // 2
    quarter = half // 2
    cols = pl.ds(pl.multiple_of(meta[3] * half, 128), half)
    mine = pl.ds(pl.multiple_of(core * quarter, quarter), quarter)
    yours = pl.ds(pl.multiple_of((1 - core) * quarter, quarter), quarter)
    left = normed[:, cols]
    for m, grad in enumerate((grad_query, grad_key, grad_value, grad_attended)):
        if m == 3:
            left = mixed[:, cols]
        full[...] = mm_tn(left, grad[...])
        own[m * quarter : (m + 1) * quarter, :] = full[mine, :]
        other[m * quarter : (m + 1) * quarter, :] = full[yours, :].astype(BF16)


def slots_kernel(
    chosen_in, attended, rate_in, seen_here, seen_there, moved_here, moved_there, w_router, grad_sum,
    update, grad_chosen, grad_router,
):
    chosen = chosen_in[...].astype(F32)
    rate = rate_in[:, :1]
    seen = seen_here[...].astype(F32) + seen_there[...].astype(F32)
    delta = attended[...] + (moved_here[...].astype(F32) + moved_there[...].astype(F32))
    update[...] = (rate * delta).astype(BF16)
    score = rate * (1.0 - rate) * jnp.sum(seen * delta, axis=-1, keepdims=True)
    grad_chosen[...] = (grad_sum[...] + score * w_router[...].astype(F32)).astype(BF16)
    grad_router[...] = jnp.sum(score * chosen, axis=0, keepdims=True)


def swap(v, axis, size, bits):
    return lax.ppermute(v, axis, [(i, i ^ bits) for i in range(size)])


def pick(v, index):
    return lax.dynamic_index_in_dim(v, index, 0, keepdims=False)


def stages_of(size):
    stages, shift = [], 0
    while (1 << shift) < size:
        left = size >> shift
        radix = 4 if (shift > 0 and left >= 4) else 2
        stages.append((shift, radix))
        shift += radix.bit_length() - 1
    return stages


def scatter_sum(own, got, batch):
    index = lax.axis_index("batch")
    stages = stages_of(batch)
    shape = tuple(radix for _, radix in stages) + (own.shape[0] // batch, own.shape[1])
    current = (own.reshape(shape), got.reshape(shape))
    for shift, radix in stages:
        digit = (index >> shift) & (radix - 1)
        arrived = []
        for k in range(1, radix):
            piece = sum(pick(v, digit ^ k).astype(F32) for v in current).astype(BF16)
            arrived.append(swap(piece, "batch", batch, k << shift))
        current = (sum([pick(v, digit).astype(F32) for v in current] + [v.astype(F32) for v in arrived]),)
    return current[0].astype(BF16)


def gather_all(piece, batch):
    current = piece
    for shift, radix in reversed(stages_of(batch)):
        current = jnp.stack(
            [current] + [swap(current, "batch", batch, k << shift) for k in range(1, radix)]
        )
    return current


def digits_of(index, batch):
    return [(index >> shift) & (radix - 1) for shift, radix in stages_of(batch)]


def unscramble_kernel(index, *refs):
    half = len(refs) // 2
    for v, out in zip(refs[:half], refs[half:]):
        out[...] = v[...].reshape(out.shape).astype(F32)


def order_rows(gathered, batch):
    index = lax.axis_index("batch")
    stages = stages_of(batch)
    rows, width = gathered.shape[-2:]
    if batch != 8:
        for axis, digit in enumerate(digits_of(index, batch)):
            radix = gathered.shape[axis]
            gathered = jnp.take(gathered, jnp.arange(radix) ^ digit, axis=axis)
        return gathered.reshape(-1, width).astype(F32)
    meta = jnp.stack(digits_of(index, batch)).astype(jnp.int32)
    return pl.pallas_call(
        unscramble_kernel,
        grid_spec=pltpu.PrefetchScalarGridSpec(
            num_scalar_prefetch=1,
            grid=(2, 4),
            in_specs=[
                pl.BlockSpec((1, 1, rows, width), lambda i, j, m: (i ^ m[0], j ^ m[1], 0, 0))
            ],
            out_specs=[pl.BlockSpec((rows, width), lambda i, j, m: (i * 4 + j, 0))],
        ),
        out_shape=[jax.ShapeDtypeStruct((8 * rows, width), F32)],
    )(meta, gathered)[0]


def order_attention(gathered, batch, place):
    index = lax.axis_index("batch")
    rows, width = gathered.shape[-2:]
    core, side = place % 2, place // 2
    if batch != 8:
        for axis, digit in enumerate([core, side] + digits_of(index, batch)):
            radix = gathered.shape[axis]
            gathered = jnp.take(gathered, jnp.arange(radix) ^ digit, axis=axis)
        whole = gathered.astype(F32).reshape(2, 2, 4, -1, width).transpose(2, 1, 0, 3, 4)
        return [whole[m].reshape(-1, width) for m in range(4)]
    meta = jnp.stack([core, side] + digits_of(index, batch)).astype(jnp.int32)

    def source(m):
        def at(j, d):
            p = 2 * m + j % 2
            return (((j // 2) % 2) ^ d[0], (j // 4) ^ d[1], (p // 4) ^ d[2], (p % 4) ^ d[3], 0, 0)

        return pl.BlockSpec((1, 1, 1, 1, rows, width), at)

    return pl.pallas_call(
        unscramble_kernel,
        grid_spec=pltpu.PrefetchScalarGridSpec(
            num_scalar_prefetch=1,
            grid=(8,),
            in_specs=[source(m) for m in range(4)],
            out_specs=[pl.BlockSpec((rows, width), lambda j, d: (j, 0))] * 4,
        ),
        out_shape=[jax.ShapeDtypeStruct((8 * rows, width), F32)] * 4,
    )(meta, gathered, gathered, gathered, gathered)


def body(
    batch, tokens, lengths, picks, w_router, gain_attn, gain_mlp, w_query, w_key, w_value, w_out,
    w_up, w_down, cotangent,
):
    place = lax.axis_index("seq")
    core, side = place % 2, place // 2
    seqs, length, width = tokens.shape
    local = picks.shape[1]
    slots = 4 * local
    across = functools.partial(swap, axis="seq", size=4)
    row = lambda v: v.reshape(1, width)
    gain_attn, gain_mlp, w_router = row(gain_attn), row(gain_mlp), row(w_router)

    got = [picks] + [across(picks, bits=k) for k in (1, 2, 3)]
    up_other, down_other = across(w_up, bits=1), across(w_down, bits=1)
    count = pick(lengths, core) // 8
    meta = jnp.stack([place, core, count, side] + [place ^ k for k in range(4)]).astype(jnp.int32)
    stacked = jnp.stack(got)
    all_picks = jnp.concatenate([pick(stacked, place ^ a) for a in range(4)], axis=1)

    slot_shape = ((slots, width), BF16)
    wide = ((slots, width), F32)

    def select(rows):
        return call(
            select_kernel, [meta, *got, rows], [slot_shape, slot_shape],
            specs=[SMEM] + [VMEM] * 5, scratch=[pltpu.VMEM((slots, length), BF16)],
            flops=4 * slots * length * width,
        )

    own, other = select(tokens)
    here = own + across(other, bits=1)
    there = across(here, bits=2)
    own, other = select(cotangent)
    seen_here = own + across(other, bits=1)
    seen_there = across(seen_here, bits=2)

    (chosen, normed, query, keys, values, probs, mixed, attended, normed_mlp, rate) = call(
        attend_kernel,
        [meta, here, there, w_router, gain_attn, gain_mlp, w_query, w_key, w_value, w_out],
        [slot_shape] * 5 + [((NH, slots, slots), F32), slot_shape, wide, slot_shape, ((slots, 128), F32)],
        specs=[SMEM] + [VMEM] * 9,
        flops=8 * slots * width * width,
    )
    hidden_units = w_up.shape[1]
    act = ((slots, hidden_units), BF16)
    act_own, act_other, back_own, back_other, grad_moved, gn_here = call(
        mlp_kernel,
        [normed_mlp, rate, seen_here, seen_there, w_up, up_other, w_down, down_other],
        [act] * 4 + [slot_shape] * 2,
        flops=12 * slots * width * hidden_units,
    )
    gn_there = across(gn_here, bits=2)
    gd_own, gd_other, gu_own, gu_other, moved_here = call(
        mlp_grads_kernel,
        [normed_mlp, grad_moved, act_own, act_other, back_own, back_other, w_down, down_other],
        [
            ((hidden_units, width), F32), ((hidden_units, width), BF16),
            ((width, hidden_units), F32), ((width, hidden_units), BF16), slot_shape,
        ],
        flops=12 * slots * width * hidden_units,
    )
    moved_there = across(moved_here, bits=2)
    down_part = scatter_sum(gd_own, across(gd_other, bits=1), batch)
    up_part = scatter_sum(gu_own, across(gu_other, bits=1), batch)

    grad_attended, gq, gk, gv, grad_sum, small = call(
        attend_back_kernel,
        [
            chosen, attended, gain_attn, gain_mlp, gn_here, gn_there, rate, seen_here, seen_there,
            query, keys, values, probs, w_query, w_key, w_value, w_out,
        ],
        [slot_shape] * 4 + [wide, ((2, width), F32)],
        scratch=[pltpu.VMEM((slots, width), BF16)],
        flops=8 * slots * width * width,
    )
    ga_own, ga_other = call(
        attend_grads_kernel,
        [meta, normed, mixed, gq, gk, gv, grad_attended],
        [((width, width), F32), ((width, width), BF16)],
        specs=[SMEM] + [VMEM] * 6,
        scratch=[pltpu.VMEM((width // 2, width), F32)],
        flops=4 * slots * width * width,
    )
    attention_part = scatter_sum(ga_own, across(ga_other, bits=1), batch)
    update, grad_chosen, grad_router = call(
        slots_kernel,
        [chosen, attended, rate, seen_here, seen_there, moved_here, moved_there, w_router, grad_sum],
        [slot_shape, slot_shape, ((1, width), F32)],
    )

    def placed(rows, mine):
        return call(
            place_kernel, [meta, all_picks, rows, mine, across(mine, bits=1)],
            [(rows.shape, BF16)], specs=[SMEM] + [VMEM] * 4,
            flops=4 * slots * length * width,
        )[0]

    output = placed(tokens, update)
    grad_tokens = placed(cotangent, grad_chosen)

    vectors = jnp.concatenate([grad_router, small], axis=0)
    vectors = vectors + across(vectors, bits=1)
    for bit in range(batch.bit_length() - 1):
        vectors = vectors + swap(vectors, "batch", batch, 1 << bit)

    down_all = gather_all(down_part, batch)
    up_all = gather_all(up_part, batch)
    attention_all = gather_all(attention_part, batch)
    attention_all = jnp.stack([attention_all, across(attention_all, bits=2)])
    attention_all = jnp.stack([attention_all, across(attention_all, bits=1)])
    grad_query, grad_key, grad_value, grad_out = order_attention(attention_all, batch, place)
    return (
        output, grad_tokens, vectors[0], vectors[1], vectors[2],
        grad_query, grad_key, grad_value, grad_out,
        order_rows(up_all, batch), order_rows(down_all, batch),
    )


def solution(mesh):
    rows, whole = P("batch", "seq", None), P()
    return jax.shard_map(
        functools.partial(body, mesh.shape["batch"]),
        mesh=mesh,
        in_specs=(
            rows, P("batch"), P("batch", "seq"), whole, whole, whole, whole, whole, whole, whole,
            P(None, "seq"), P("seq", None), rows,
        ),
        out_specs=(
            rows, rows, whole, whole, whole, whole, whole, whole, whole,
            P(None, "seq"), P("seq", None),
        ),
        check_vma=False,
    )
```

time: 654 us -> 300 us (0.46)
  waiting for transfers between devices: 430 us -> 145 us
  blocking collectives: 113 us -> 0 us
  starting transfers between devices: 0.5 us -> 61.8 us
  matrix products: 53.4 us -> 0 us
  Pallas kernels: 0 us -> 49.5 us
  local copies, waits for them, and re-layouts: 35.2 us -> 17.4 us
  other arithmetic: 6.11 us -> 20.7 us
  between operations: 14.8 us -> 3.92 us
    psum x2 -> x0, waiting for transfers between devices: 294 us -> none  [the longest x1 198 us: body(): lax.psum((grad_query, grad_key, grad_value, grad_out, grad_router, grad_g...]
    ppermute x0 -> x46, waiting for transfers between devices: none -> 145 us  [swap(): return lax.ppermute(v, axis, [(i, i ^ bits) for i in range(size)])]
    reduce_scatter x4 -> x0, waiting for transfers between devices: 84 us -> none  [the longest x1 28.4 us: body(): lax.psum_scatter(grad_key_part.reshape(seqs, slots, width), 'seq', scatte...]
    all_gather x7 -> x0, blocking collectives: 68.7 us -> none  [the longest x1 13.9 us: body(): lax.all_gather(values, 'seq', axis=1, tiled=True)]
    ppermute x0 -> x46, starting transfers between devices: none -> 61.8 us  [swap(): return lax.ppermute(v, axis, [(i, i ^ bits) for i in range(size)])]
    dot_general x29 -> x0, matrix products: 51.6 us -> none  [the longest x1 4.86 us: body(): jnp.einsum('sir,srd->sid', match, pieces[1], preferred_element_type=jnp.f...]
    all_gather x2 -> x0, waiting for transfers between devices: 50.5 us -> none  [the longest x1 48 us: body(): lax.all_gather(tokens, 'seq', axis=1, tiled=True)]
    pallas_call x0 -> x13, Pallas kernels: none -> 49.5 us  [the longest x10 28.5 us: call(): pl.pallas_call(kernel, out_shape=shapes, in_specs=specs or [VMEM] * len(i...]
  transfers between devices with their start and end apart: 8 -> 46, of which waited for: 8 -> 23; matrix products, arithmetic and copies ran while one was open for 8% -> 4% of each run, Pallas kernels for 0% -> 9%
where the time goes in v1:
time: 300 us; the launch traced here: 299 us
  waiting for transfers between devices  145 us (48%)
  starting transfers between devices  61.8 us (21%)
  Pallas kernels  49.5 us (16%)
  other arithmetic  20.7 us (7%)
  local copies, waits for them, and re-layouts  17.4 us (6%)
  between operations  3.92 us (1%)
    ppermute x46, waiting for transfers between devices, swap(): return lax.ppermute(v, axis, [(i, i ^ bits) for i in range(size)])  145 us
    ppermute x46, starting transfers between devices, swap(): return lax.ppermute(v, axis, [(i, i ^ bits) for i in range(size)])  61.8 us
    pallas_call x10, Pallas kernels, call(): pl.pallas_call(kernel, out_shape=shapes, in_specs=specs or [VMEM] * len(i...  28.5 us
    unnamed x102, local copies, waits for them, and re-layouts  14.5 us
    pallas_call x2, Pallas kernels, order_rows(): pl.pallas_call(unscramble_kernel, grid_spec=pltpu.PrefetchScalarGridSpec(...  12.4 us
    pallas_call x1, Pallas kernels, order_attention(): pl.pallas_call(unscramble_kernel, grid_spec=pltpu.PrefetchScalarGridSpec(...  8.57 us
    another operation x2, other arithmetic, body(): attention_all = jnp.stack([attention_all, across(attention_all, bits=1)])  7.48 us
  transfers between devices with their start and end apart: 46, of which 23 were waited for; matrix products, arithmetic and copies ran while one was open for 4% of the time, Pallas kernels for 9%

profile of v1, /device:TPU:0, one launch (start us, length us, event | category | flops | bytes accessed | tf_op | source)
XLA Modules:
  0.0 298.6 jit_solution(16311601310310108691)
XLA Ops:
  1.3 2.6 collective-permute-start.2
  8.3 1.4 copy-done.1
  10.4 1.3 shard_map.212
  12.2 1.3 shard_map.214
  13.8 1.8 collective-permute-start.4
  15.7 1.4 collective-permute-start.6
  17.2 8.6 %collective-permute-done.4.there = bf16[256,768]{1,0:T(8,128)(2,1)S(1)} collective-permute-done((bf16[256,768]{1,0:T(8,128)(2,1)S(1)}, bf16[256,768]{1,0:T(8,128)(2,1)S(1)}, u32[]{:S(2)}, u32[]{:S(2)}) %collective-permute-start.4) | collective-permute-done | bytes 393248 | tf_op jit(solution)/shard_map/ppermute | solution.py:244
  25.8 1.3 copy-done.6
  27.1 4.2 %shard_map.213 = (bf16[256,768]{1,0:T(8,128)(2,1)S(1)}, bf16[256,768]{1,0:T(8,128)(2,1)S(1)}, bf16[256,768]{1,0:T(8,128)(2,1)S(1)}, bf16[256,768]{1,0:T(8,128)(2...) custom-call(s32[8]{0:T(128)S(1)} %stack.156.meta, ...), custom_call_target="tpu_custom_call" | custom-call | flops 1207959552 | bytes 12328480 | tf_op jit(solution)/shard_map/pallas_call | solution.py:33
  31.3 1.6 copy-done.8
  33.8 4.2 %shard_map.215 = (bf16[256,768]{1,0:T(8,128)(2,1)S(1)}, bf16[256,768]{1,0:T(8,128)(2,1)S(1)}, bf16[256,768]{1,0:T(8,128)(2,1)S(1)}, bf16[256,768]{1,0:T(8,128)(2...) custom-call(bf16[256,768]{1,0:T(8,128)(2,1)S(1)} %get-tuple-element.58.normed, ...), custom_call_target="tpu_custom_call" | custom-call | flops 1811939328 | bytes 8388608 | tf_op jit(solution)/shard_map/pallas_call | solution.py:33
  39.5 1.7 collective-permute-start.10
  41.2 9.0 %collective-permute-done.10.gn_there = bf16[256,768]{1,0:T(8,128)(2,1)S(1)} collective-permute-done((bf16[256,768]{1,0:T(8,128)(2,1)S(1)}, bf16[256,768]{1,0:T(8,128)(2,1)S(1)}, u32[]{:S(2)}, u32[]{:S(2)}) %collective-permute-start.10) | collective-permute-done | bytes 393248 | tf_op jit(solution)/shard_map/ppermute | solution.py:244
  50.2 1.9 copy-done.9
  52.1 6.4 %shard_map.217 = (bf16[256,768]{1,0:T(8,128)(2,1)S(1)}, bf16[256,768]{1,0:T(8,128)(2,1)S(1)}, bf16[256,768]{1,0:T(8,128)(2,1)S(1)}, bf16[256,768]{1,0:T(8,128)(2...) custom-call(bf16[256,768]{1,0:T(8,128)(2,1)S(1)} %get-tuple-element.53.chosen_in, ...), custom_call_target="tpu_custom_call" | custom-call | flops 1207959552 | bytes 14299136 | tf_op jit(solution)/shard_map/pallas_call | solution.py:33
  58.5 2.7 shard_map.221
  61.2 1.4 copy-done.10
  62.6 3.2 %collective-permute-done.17 = bf16[768,768]{1,0:T(8,128)(2,1)} collective-permute-done((bf16[768,768]{1,0:T(8,128)(2,1)}, bf16[768,768]{1,0:T(8,128)(2,1)}, u32[]{:S(2)}, u32[]{:S(2)}) %collective-permute-start.17) | collective-permute-done | bytes 1179680 | tf_op jit(solution)/shard_map/ppermute | solution.py:244
  65.8 2.3 fusion
  68.2 1.6 collective-permute-start.18
  69.8 14.1 %collective-permute-done.18 = bf16[4,96,768]{2,1,0:T(8,128)(2,1)} collective-permute-done((bf16[4,96,768]{2,1,0:T(8,128)(2,1)}, bf16[4,96,768]{2,1,0:T(8,128)(2,1)}, u32[]{:S(2)}, u32[]{:S(2)}) %collective-permute-start.18) | collective-permute-done | bytes 589856 | tf_op jit(solution)/shard_map/ppermute | solution.py:244
  83.9 1.8 bitcast_add_fusion.2
  87.4 1.6 collective-permute-start.19
  89.0 2.5 collective-permute-start.21
  91.6 1.5 collective-permute-done.19
  93.1 6.5 %collective-permute-done.21 = bf16[96,768]{1,0:T(8,128)(2,1)} collective-permute-done((bf16[96,768]{1,0:T(8,128)(2,1)}, bf16[96,768]{1,0:T(8,128)(2,1)}, u32[]{:S(2)}, u32[]{:S(2)}) %collective-permute-start.21) | collective-permute-done | bytes 147488 | tf_op jit(solution)/shard_map/ppermute | solution.py:244
  99.6 4.8 %collective-permute-done.20 = bf16[96,768]{1,0:T(8,128)(2,1)} collective-permute-done((bf16[96,768]{1,0:T(8,128)(2,1)}, bf16[96,768]{1,0:T(8,128)(2,1)}, u32[]{:S(2)}, u32[]{:S(2)}) %collective-permute-start.20) | collective-permute-done | bytes 147488 | tf_op jit(solution)/shard_map/ppermute | solution.py:244
  104.5 1.2 fusion.11
  105.7 2.7 collective-permute-start.24
  108.4 1.7 collective-permute-start.22
  110.2 4.2 %collective-permute-done.24 = bf16[96,768]{1,0:T(8,128)(2,1)S(1)} collective-permute-done((bf16[96,768]{1,0:T(8,128)(2,1)S(1)}, bf16[96,768]{1,0:T(8,128)(2,1)S(1)}, u32[]{:S(2)}, u32[]{:S(2)}) %collective-permute-start.24) | collective-permute-done | bytes 147488 | tf_op jit(solution)/shard_map/ppermute | solution.py:244
  114.4 5.3 %collective-permute-done.23 = bf16[96,768]{1,0:T(8,128)(2,1)S(1)} collective-permute-done((bf16[96,768]{1,0:T(8,128)(2,1)S(1)}, bf16[96,768]{1,0:T(8,128)(2,1)S(1)}, u32[]{:S(2)}, u32[]{:S(2)}) %collective-permute-start.23) | collective-permute-done | bytes 147488 | tf_op jit(solution)/shard_map/ppermute | solution.py:244
  119.8 1.6 collective-permute-start.25
  124.4 3.3 %shard_map.216 = (f32[768,768]{1,0:T(8,128)S(1)}, bf16[768,768]{1,0:T(8,128)(2,1)S(1)}, f32[768,768]{1,0:T(8,128)S(1)}, bf16[768,768]{1,0:T(8,128)(2,1)S(1)}, bf16[256,768]{1,0:T(8,128)(2,1)S(1)}) custom-call(bf16[256,768]{1,0:T(8,128)(2,1)S(1)} %copy-done.31, bf16[256,768]{1,0:T(8,128)(2,1)S(1)} %copy-done.41, bf16[256,768]{1,0:T(8,128)(2,1)S(1)} %copy-done.33, ...), custom_call_target="tpu_custom_call" | custom-call | flops 1811939328 | bytes 12189696 | tf_op jit(solution)/shard_map/pallas_call | solution.py:33
  128.3 5.8 %collective-permute-done.25 = bf16[4,96,768]{2,1,0:T(8,128)(2,1)S(1)} collective-permute-done((bf16[4,96,768]{2,1,0:T(8,128)(2,1)S(1)}, bf16[4,96,768]{2,1,0:T(8,128)(2,1)S(1)}, u32[]{:S(2)}, u32[]{:S(2)}) %collective-permute-start.25) | collective-permute-done | bytes 589856 | tf_op jit(solution)/shard_map/ppermute | solution.py:244
  134.2 1.6 collective-permute-start.26
  136.3 32.4 %collective-permute-done.9.moved_there = bf16[256,768]{1,0:T(8,128)(2,1)S(1)} collective-permute-done((bf16[256,768]{1,0:T(8,128)(2,1)S(1)}, bf16[256,768]{1,0:T(8,128)(2,1)S(1)}, u32[]{:S(2)}, u32[]{:S(2)}) %collective-permute-start.9) | collective-permute-done | bytes 393248 | tf_op jit(solution)/shard_map/ppermute | solution.py:244
  170.1 1.5 collective-permute-start.29
  172.4 1.6 collective-permute-start.38
  174.5 12.0 %collective-permute-done.14 = f32[3,768]{1,0:T(4,128)S(1)} collective-permute-done((f32[3,768]{1,0:T(4,128)S(1)}, f32[3,768]{1,0:T(4,128)S(1)}, u32[]{:S(2)}, u32[]{:S(2)}) %collective-permute-start.14) | collective-permute-done | bytes 9248 | tf_op jit(solution)/shard_map/ppermute | solution.py:244
  186.6 2.5 fusion.30
  189.3 2.1 collective-permute-start.30
  191.4 3.5 %collective-permute-start.32 = (bf16[96,768]{1,0:T(8,128)(2,1)S(1)}, bf16[96,768]{1,0:T(8,128)(2,1)S(1)}, u32[]{:S(2)}, u32[]{:S(2)}) collective-permute-start(bf16[96,768]{1,0:T(8,128)(2,1)S(1)} %get-tuple-element.100), channel_id=1, source_target_pairs={{0,24},{4,28},{8,16},{12,20},{16,8},{20,12},{24,0},{28,4},{1,25},{... | collective-permute-start | bytes 442376 | tf_op jit(solution)/shard_map/ppermute | solution.py:244
  194.9 3.3 %collective-permute-done.38 = bf16[4,96,768]{2,1,0:T(8,128)(2,1)S(1)} collective-permute-done((bf16[4,96,768]{2,1,0:T(8,128)(2,1)S(1)}, bf16[4,96,768]{2,1,0:T(8,128)(2,1)S(1)}, u32[]{:S(2)}, u32[]{:S(2)}) %collective-permute-start.38) | collective-permute-done | bytes 589856 | tf_op jit(solution)/shard_map/ppermute | solution.py:244
  198.5 4.1 %collective-permute-start.39 = (bf16[96,768]{1,0:T(8,128)(2,1)S(1)}, bf16[96,768]{1,0:T(8,128)(2,1)S(1)}, u32[]{:S(2)}, u32[]{:S(2)}) collective-permute-start(bf16[96,768]{1,0:T(8,128)(2,1)S(1)} %get-tuple-element.96), channel_id=1, source_target_pairs={{0,8},{4,12},{8,0},{12,4},{16,24},{20,28},{24,16},{28,20},{1,9},{5... | collective-permute-start | bytes 442376 | tf_op jit(solution)/shard_map/ppermute | solution.py:244
  203.4 6.3 %collective-permute-done.31 = bf16[96,768]{1,0:T(8,128)(2,1)S(1)} collective-permute-done((bf16[96,768]{1,0:T(8,128)(2,1)S(1)}, bf16[96,768]{1,0:T(8,128)(2,1)S(1)}, u32[]{:S(2)}, u32[]{:S(2)}) %collective-permute-start.31) | collective-permute-done | bytes 147488 | tf_op jit(solution)/shard_map/ppermute | solution.py:244
  209.9 4.0 %collective-permute-start.35 = (bf16[96,768]{1,0:T(8,128)(2,1)S(1)}, bf16[96,768]{1,0:T(8,128)(2,1)S(1)}, u32[]{:S(2)}, u32[]{:S(2)}) collective-permute-start(bf16[96,768]{1,0:T(8,128)(2,1)S(1)} %fusion.8), channel_id=1, source_target_pairs={{0,24},{4,28},{8,16},{12,20},{16,8},{20,12},{24,0},{28,4},{1,25},{... | collective-permute-start | bytes 442376 | tf_op jit(solution)/shard_map/ppermute | solution.py:244
  213.9 8.4 %collective-permute-start.34 = (bf16[96,768]{1,0:T(8,128)(2,1)S(1)}, bf16[96,768]{1,0:T(8,128)(2,1)S(1)}, u32[]{:S(2)}, u32[]{:S(2)}) collective-permute-start(bf16[96,768]{1,0:T(8,128)(2,1)S(1)} %fusion.8), channel_id=1, source_target_pairs={{0,16},{4,20},{8,24},{12,28},{16,0},{20,4},{24,8},{28,12},{1,17},{... | collective-permute-start | bytes 442376 | tf_op jit(solution)/shard_map/ppermute | solution.py:244
  222.3 2.2 collective-permute-done.40
  224.6 5.1 %collective-permute-start.44 = (bf16[96,768]{1,0:T(8,128)(2,1)S(1)}, bf16[96,768]{1,0:T(8,128)(2,1)S(1)}, u32[]{:S(2)}, u32[]{:S(2)}) collective-permute-start(bf16[96,768]{1,0:T(8,128)(2,1)S(1)} %fusion.5), channel_id=1, source_target_pairs={{0,24},{4,28},{8,16},{12,20},{16,8},{20,12},{24,0},{28,4},{1,25},{... | collective-permute-start | bytes 442376 | tf_op jit(solution)/shard_map/ppermute | solution.py:244
  229.7 3.7 %collective-permute-start.43 = (bf16[96,768]{1,0:T(8,128)(2,1)S(1)}, bf16[96,768]{1,0:T(8,128)(2,1)S(1)}, u32[]{:S(2)}, u32[]{:S(2)}) collective-permute-start(bf16[96,768]{1,0:T(8,128)(2,1)S(1)} %fusion.5), channel_id=1, source_target_pairs={{0,16},{4,20},{8,24},{12,28},{16,0},{20,4},{24,8},{28,12},{1,17},{... | collective-permute-start | bytes 442376 | tf_op jit(solution)/shard_map/ppermute | solution.py:244
  233.4 6.9 %collective-permute-done.34 = bf16[96,768]{1,0:T(8,128)(2,1)S(1)} collective-permute-done((bf16[96,768]{1,0:T(8,128)(2,1)S(1)}, bf16[96,768]{1,0:T(8,128)(2,1)S(1)}, u32[]{:S(2)}, u32[]{:S(2)}) %collective-permute-start.34) | collective-permute-done | bytes 147488 | tf_op jit(solution)/shard_map/ppermute | solution.py:244
  242.5 4.2 %collective-permute-done.43 = bf16[96,768]{1,0:T(8,128)(2,1)S(1)} collective-permute-done((bf16[96,768]{1,0:T(8,128)(2,1)S(1)}, bf16[96,768]{1,0:T(8,128)(2,1)S(1)}, u32[]{:S(2)}, u32[]{:S(2)}) %collective-permute-start.43) | collective-permute-done | bytes 147488 | tf_op jit(solution)/shard_map/ppermute | solution.py:244
  246.7 2.5 collective-permute-done.42
  249.2 1.5 collective-permute-start.36
  253.5 2.3 shard_map.220
  255.8 2.3 shard_map.219
  258.1 7.3 %collective-permute-done.36 = bf16[4,96,768]{2,1,0:T(8,128)(2,1)S(1)} collective-permute-done((bf16[4,96,768]{2,1,0:T(8,128)(2,1)S(1)}, bf16[4,96,768]{2,1,0:T(8,128)(2,1)S(1)}, u32[]{:S(2)}, u32[]{:S(2)}) %collective-permute-start.36) | collective-permute-done | bytes 589856 | tf_op jit(solution)/shard_map/ppermute | solution.py:244
  266.5 6.2 %shard_map.223 = f32[768,768]{1,0:T(8,128)} custom-call(s32[2]{0:T(128)} %pad_add_fusion.3.index, bf16[2,4,96,768]{3,2,1,0:T(8,128)(2,1)} %pad_maximum_fusion.3.refs_0_), custom_call_target="tpu_custom_call" | custom-call | tf_op jit(solution)/shard_map/pallas_call | solution.py:305
  272.7 3.9 %collective-permute-done.45 = bf16[4,96,768]{2,1,0:T(8,128)(2,1)} collective-permute-done((bf16[4,96,768]{2,1,0:T(8,128)(2,1)S(1)}, bf16[4,96,768]{2,1,0:T(8,128)(2,1)}, u32[]{:S(2)}, u32[]{:S(2)}) %collective-permute-start.45) | collective-permute-done | bytes 589856 | tf_op jit(solution)/shard_map/ppermute | solution.py:244
  276.6 2.2 pad_maximum_fusion.4.refs_0_
  278.8 6.2 %shard_map.224 = f32[768,768]{1,0:T(8,128)} custom-call(s32[2]{0:T(128)} %pad_add_fusion.3.index, bf16[2,4,96,768]{3,2,1,0:T(8,128)(2,1)} %pad_maximum_fusion.4.refs_0_), custom_call_target="tpu_custom_call" | custom-call | tf_op jit(solution)/shard_map/pallas_call | solution.py:305
  285.0 5.0 %pad_maximum_fusion.refs_0_.refs_1_.refs_2_.refs_3_ = bf16[2,2,2,4,96,768]{5,4,3,2,1,0:T(8,128)(2,1)} fusion(bf16[1,2,2,4,96,768]{5,4,3,2,1,0:T(8,128)(2,1)} %bitcast.35, bf16[1,2,2,4,96,768]{5,4,3,2,1,0:T(8,128)(2,1)} %get-tuple-element.94), kind=kLoop, calls=%fused_computation | loop fusion | flops 2359296 | bytes 9437184 | tf_op jit(solution)/shard_map/stack | solution.py:460
  290.0 8.6 %shard_map.222 = (f32[768,768]{1,0:T(8,128)}, f32[768,768]{1,0:T(8,128)}, f32[768,768]{1,0:T(8,128)}, f32[768,768]{1,0:T(8,128)}) custom-call(s32[4]{0:T(128)} %pad_add_fusion.2.index, bf16[2,2,2,4,96,768]{5,4,3,2,1,0:T(8,128)(2,1)} %pad_maximum_fusion.refs_0_.refs_1_.refs_2_.refs_3_, ...), custom_call_target="tpu_custom_call" | custom-call | tf_op jit(solution)/shard_map/pallas_call | solution.py:338
  (181 shorter events, 22.8 us)
Async XLA Ops:
  0.7 33.1 %collective-permute-start.7 = (bf16[768,768]{1,0:T(8,128)(2,1)}, bf16[768,768]{1,0:T(8,128)(2,1)}, u32[]{:S(2)}, u32[]{:S(2)}) collective-permute-start(bf16[768,768]{1,0:T(8,128)(2,1)} %up_own.1), channel_id=1, source_target_pairs={{0,1},{1,0},{2,3},{3,2},{4,5},{5,4},{6,7},{7,6},{8,9},{9,8},{10,11... | collective-permute-start | bytes 3538952 | tf_op jit(solution)/shard_map/ppermute | solution.py:244
  1.2 32.6 %collective-permute-start.8 = (bf16[768,768]{1,0:T(8,128)(2,1)}, bf16[768,768]{1,0:T(8,128)(2,1)}, u32[]{:S(2)}, u32[]{:S(2)}) collective-permute-start(bf16[768,768]{1,0:T(8,128)(2,1)} %down_own.3), channel_id=1, source_target_pairs={{0,1},{1,0},{2,3},{3,2},{4,5},{5,4},{6,7},{7,6},{8,9},{9,8},{10,11... | collective-permute-start | bytes 3538952 | tf_op jit(solution)/shard_map/ppermute | solution.py:244
  1.3 7.0 %collective-permute-start.2 = (s32[2,64]{1,0:T(2,128)}, s32[2,64]{1,0:T(2,128)S(1)}, u32[]{:S(2)}, u32[]{:S(2)}) collective-permute-start(s32[2,64]{1,0:T(2,128)} %p0.3), channel_id=1, source_target_pairs={{0,3},{1,2},{2,1},{3,0},{4,7},{5,6},{6,5},{7,4},{8,11},{9,10},{10,... | collective-permute-start | bytes 1544 | tf_op jit(solution)/shard_map/ppermute | solution.py:244
  3.9 4.4 %collective-permute-start.1 = (s32[2,64]{1,0:T(2,128)}, s32[2,64]{1,0:T(2,128)S(1)}, u32[]{:S(2)}, u32[]{:S(2)}) collective-permute-start(s32[2,64]{1,0:T(2,128)} %p0.3), channel_id=1, source_target_pairs={{0,2},{1,3},{2,0},{3,1},{4,6},{5,7},{6,4},{7,5},{8,10},{9,11},{10,... | collective-permute-start | bytes 1544 | tf_op jit(solution)/shard_map/ppermute | solution.py:244
  4.2 4.1 %collective-permute-start = (s32[2,64]{1,0:T(2,128)}, s32[2,64]{1,0:T(2,128)S(1)}, u32[]{:S(2)}, u32[]{:S(2)}) collective-permute-start(s32[2,64]{1,0:T(2,128)} %p0.3), channel_id=1, source_target_pairs={{0,1},{1,0},{2,3},{3,2},{4,5},{5,4},{6,7},{7,6},{8,9},{9,8},{10,11... | collective-permute-start | bytes 1544 | tf_op jit(solution)/shard_map/ppermute | solution.py:244
  11.7 2.0 collective-permute-start.3
  12.2 13.6 %copy-start.5 = (bf16[768,768]{1,0:T(8,128)(2,1)S(1)}, bf16[768,768]{1,0:T(8,128)(2,1)}, u32[]{:S(2)}) copy-start(bf16[768,768]{1,0:T(8,128)(2,1)} %w_value.3) | copy-start | bytes 3538948
  13.5 2.1 collective-permute-start.5
  13.7 12.1 %copy-start.3 = (bf16[768,768]{1,0:T(8,128)(2,1)S(1)}, bf16[768,768]{1,0:T(8,128)(2,1)}, u32[]{:S(2)}) copy-start(bf16[768,768]{1,0:T(8,128)(2,1)} %w_query.3) | copy-start | bytes 3538948
  13.7 12.1 %copy-start.4 = (bf16[768,768]{1,0:T(8,128)(2,1)S(1)}, bf16[768,768]{1,0:T(8,128)(2,1)}, u32[]{:S(2)}) copy-start(bf16[768,768]{1,0:T(8,128)(2,1)} %w_key.3) | copy-start | bytes 3538948
  13.8 12.0 %collective-permute-start.4 = (bf16[256,768]{1,0:T(8,128)(2,1)S(1)}, bf16[256,768]{1,0:T(8,128)(2,1)S(1)}, u32[]{:S(2)}, u32[]{:S(2)}) collective-permute-start(bf16[256,768]{1,0:T(8,128)(2,1)S(1)} %add.153.here), channel_id=1, source_target_pairs={{0,2},{1,3},{2,0},{3,1},{4,6},{5,7},{6,4},{7,5},{8,10},{9,11},{10,... | collective-permute-start | bytes 1179656 | tf_op jit(solution)/shard_map/ppermute | solution.py:244
  15.7 18.0 %collective-permute-start.6 = (bf16[256,768]{1,0:T(8,128)(2,1)S(1)}, bf16[256,768]{1,0:T(8,128)(2,1)S(1)}, u32[]{:S(2)}, u32[]{:S(2)}) collective-permute-start(bf16[256,768]{1,0:T(8,128)(2,1)S(1)} %add.154.here.seen_here), channel_id=1, source_target_pairs={{0,2},{1,3},{2,0},{3,1},{4,6},{5,7},{6,4},{7,5},{8,10},{9,11},{10,... | collective-permute-start | bytes 1179656 | tf_op jit(solution)/shard_map/ppermute | solution.py:244
  32.9 17.2 %copy-start.13 = (f32[256,128]{1,0:T(8,128)}, f32[256,128]{1,0:T(8,128)S(1)}, u32[]{:S(2)}) copy-start(f32[256,128]{1,0:T(8,128)S(1)} %get-tuple-element.55.rate.rate_in) | copy-start | bytes 393220
  33.8 16.4 %copy-start.7 = (bf16[768,768]{1,0:T(8,128)(2,1)S(1)}, bf16[768,768]{1,0:T(8,128)(2,1)}, u32[]{:S(2)}) copy-start(bf16[768,768]{1,0:T(8,128)(2,1)} %w_out.3) | copy-start | bytes 3538948
  39.5 19.0 %copy-start.36 = (bf16[256,768]{1,0:T(8,128)(2,1)}, bf16[256,768]{1,0:T(8,128)(2,1)S(1)}, u32[]{:S(2)}) copy-start(bf16[256,768]{1,0:T(8,128)(2,1)S(1)} %get-tuple-element.62.back_own) | copy-start | bytes 1179652
  39.5 19.0 %copy-start.38 = (bf16[256,768]{1,0:T(8,128)(2,1)}, bf16[256,768]{1,0:T(8,128)(2,1)S(1)}, u32[]{:S(2)}) copy-start(bf16[256,768]{1,0:T(8,128)(2,1)S(1)} %get-tuple-element.63.back_other) | copy-start | bytes 1179652
  39.5 19.0 %copy-start.40 = (bf16[256,768]{1,0:T(8,128)(2,1)}, bf16[256,768]{1,0:T(8,128)(2,1)S(1)}, u32[]{:S(2)}) copy-start(bf16[256,768]{1,0:T(8,128)(2,1)S(1)} %get-tuple-element.59.grad_moved) | copy-start | bytes 1179652
  39.5 10.7 %collective-permute-start.10 = (bf16[256,768]{1,0:T(8,128)(2,1)S(1)}, bf16[256,768]{1,0:T(8,128)(2,1)S(1)}, u32[]{:S(2)}, u32[]{:S(2)}) collective-permute-start(bf16[256,768]{1,0:T(8,128)(2,1)S(1)} %get-tuple-element.65.gn_here), channel_id=1, source_target_pairs={{0,2},{1,3},{2,0},{3,1},{4,6},{5,7},{6,4},{7,5},{8,10},{9,11},{10,... | collective-permute-start | bytes 1179656 | tf_op jit(solution)/shard_map/ppermute | solution.py:244
  62.6 3.2 %collective-permute-start.17 = (bf16[768,768]{1,0:T(8,128)(2,1)}, bf16[768,768]{1,0:T(8,128)(2,1)}, u32[]{:S(2)}, u32[]{:S(2)}) collective-permute-start(bf16[768,768]{1,0:T(8,128)(2,1)} %get-tuple-element.82), channel_id=1, source_target_pairs={{0,1},{1,0},{2,3},{3,2},{4,5},{5,4},{6,7},{7,6},{8,9},{9,8},{10,11... | collective-permute-start | bytes 3538952 | tf_op jit(solution)/shard_map/ppermute | solution.py:244
  68.2 15.7 %collective-permute-start.18 = (bf16[4,96,768]{2,1,0:T(8,128)(2,1)}, bf16[4,96,768]{2,1,0:T(8,128)(2,1)}, u32[]{:S(2)}, u32[]{:S(2)}) collective-permute-start(bf16[4,96,768]{2,1,0:T(8,128)(2,1)} %fusion), channel_id=1, source_target_pairs={{0,4},{4,0},{8,12},{12,8},{16,20},{20,16},{24,28},{28,24},{1,5},{5... | collective-permute-start | bytes 1769480 | tf_op jit(solution)/shard_map/ppermute | solution.py:244
  87.4 5.7 %collective-permute-start.19 = (bf16[96,768]{1,0:T(8,128)(2,1)}, bf16[96,768]{1,0:T(8,128)(2,1)}, u32[]{:S(2)}, u32[]{:S(2)}) collective-permute-start(bf16[96,768]{1,0:T(8,128)(2,1)} %get-tuple-element.104), channel_id=1, source_target_pairs={{0,8},{4,12},{8,0},{12,4},{16,24},{20,28},{24,16},{28,20},{1,9},{5... | collective-permute-start | bytes 442376 | tf_op jit(solution)/shard_map/ppermute | solution.py:244
  89.0 10.6 %collective-permute-start.21 = (bf16[96,768]{1,0:T(8,128)(2,1)}, bf16[96,768]{1,0:T(8,128)(2,1)}, u32[]{:S(2)}, u32[]{:S(2)}) collective-permute-start(bf16[96,768]{1,0:T(8,128)(2,1)} %get-tuple-element.105), channel_id=1, source_target_pairs={{0,24},{4,28},{8,16},{12,20},{16,8},{20,12},{24,0},{28,4},{1,25},{... | collective-permute-start | bytes 442376 | tf_op jit(solution)/shard_map/ppermute | solution.py:244
  91.5 12.9 %collective-permute-start.20 = (bf16[96,768]{1,0:T(8,128)(2,1)}, bf16[96,768]{1,0:T(8,128)(2,1)}, u32[]{:S(2)}, u32[]{:S(2)}) collective-permute-start(bf16[96,768]{1,0:T(8,128)(2,1)} %get-tuple-element.106), channel_id=1, source_target_pairs={{0,16},{4,20},{8,24},{12,28},{16,0},{20,4},{24,8},{28,12},{1,17},{... | collective-permute-start | bytes 442376 | tf_op jit(solution)/shard_map/ppermute | solution.py:244
  91.6 29.7 %copy-start.29 = (bf16[768,768]{1,0:T(8,128)(2,1)S(1)}, bf16[768,768]{1,0:T(8,128)(2,1)}, u32[]{:S(2)}) copy-start(bf16[768,768]{1,0:T(8,128)(2,1)} %down_own.3) | copy-start | bytes 3538948
  91.6 29.7 %copy-start.31 = (bf16[256,768]{1,0:T(8,128)(2,1)S(1)}, bf16[256,768]{1,0:T(8,128)(2,1)}, u32[]{:S(2)}) copy-start(bf16[256,768]{1,0:T(8,128)(2,1)} %copy-done.30) | copy-start | bytes 1179652
  91.6 29.7 %copy-start.33 = (bf16[256,768]{1,0:T(8,128)(2,1)S(1)}, bf16[256,768]{1,0:T(8,128)(2,1)}, u32[]{:S(2)}) copy-start(bf16[256,768]{1,0:T(8,128)(2,1)} %copy-done.32) | copy-start | bytes 1179652
  91.6 29.7 %copy-start.35 = (bf16[256,768]{1,0:T(8,128)(2,1)S(1)}, bf16[256,768]{1,0:T(8,128)(2,1)}, u32[]{:S(2)}) copy-start(bf16[256,768]{1,0:T(8,128)(2,1)} %copy-done.34) | copy-start | bytes 1179652
  105.7 8.7 %collective-permute-start.24 = (bf16[96,768]{1,0:T(8,128)(2,1)S(1)}, bf16[96,768]{1,0:T(8,128)(2,1)S(1)}, u32[]{:S(2)}, u32[]{:S(2)}) collective-permute-start(bf16[96,768]{1,0:T(8,128)(2,1)S(1)} %fusion.11), channel_id=1, source_target_pairs={{0,24},{4,28},{8,16},{12,20},{16,8},{20,12},{24,0},{28,4},{1,25},{... | collective-permute-start | bytes 442376 | tf_op jit(solution)/shard_map/ppermute | solution.py:244
  108.4 11.2 %collective-permute-start.23 = (bf16[96,768]{1,0:T(8,128)(2,1)S(1)}, bf16[96,768]{1,0:T(8,128)(2,1)S(1)}, u32[]{:S(2)}, u32[]{:S(2)}) collective-permute-start(bf16[96,768]{1,0:T(8,128)(2,1)S(1)} %fusion.11), channel_id=1, source_target_pairs={{0,16},{4,20},{8,24},{12,28},{16,0},{20,4},{24,8},{28,12},{1,17},{... | collective-permute-start | bytes 442376 | tf_op jit(solution)/shard_map/ppermute | solution.py:244
  108.4 11.2 %collective-permute-start.22 = (bf16[96,768]{1,0:T(8,128)(2,1)S(1)}, bf16[96,768]{1,0:T(8,128)(2,1)S(1)}, u32[]{:S(2)}, u32[]{:S(2)}) collective-permute-start(bf16[96,768]{1,0:T(8,128)(2,1)S(1)} %fusion.11), channel_id=1, source_target_pairs={{0,8},{4,12},{8,0},{12,4},{16,24},{20,28},{24,16},{28,20},{1,9},{5... | collective-permute-start | bytes 442376 | tf_op jit(solution)/shard_map/ppermute | solution.py:244
  119.8 14.3 %collective-permute-start.25 = (bf16[4,96,768]{2,1,0:T(8,128)(2,1)S(1)}, bf16[4,96,768]{2,1,0:T(8,128)(2,1)S(1)}, u32[]{:S(2)}, u32[]{:S(2)}) collective-permute-start(bf16[4,96,768]{2,1,0:T(8,128)(2,1)S(1)} %get-tuple-element.112), channel_id=1, source_target_pairs={{0,4},{4,0},{8,12},{12,8},{16,20},{20,16},{24,28},{28,24},{1,5},{5... | collective-permute-start | bytes 1769480 | tf_op jit(solution)/shard_map/ppermute | solution.py:244
  127.7 41.7 %collective-permute-start.28 = (bf16[768,768]{1,0:T(8,128)(2,1)S(1)}, bf16[768,768]{1,0:T(8,128)(2,1)S(1)}, u32[]{:S(2)}, u32[]{:S(2)}) collective-permute-start(bf16[768,768]{1,0:T(8,128)(2,1)S(1)} %get-tuple-element.88), channel_id=1, source_target_pairs={{0,1},{1,0},{2,3},{3,2},{4,5},{5,4},{6,7},{7,6},{8,9},{9,8},{10,11... | collective-permute-start | bytes 3538952 | tf_op jit(solution)/shard_map/ppermute | solution.py:244
  127.8 44.4 %collective-permute-start.37 = (bf16[768,768]{1,0:T(8,128)(2,1)S(1)}, bf16[768,768]{1,0:T(8,128)(2,1)S(1)}, u32[]{:S(2)}, u32[]{:S(2)}) collective-permute-start(bf16[768,768]{1,0:T(8,128)(2,1)S(1)} %get-tuple-element.90), channel_id=1, source_target_pairs={{0,1},{1,0},{2,3},{3,2},{4,5},{5,4},{6,7},{7,6},{8,9},{9,8},{10,11... | collective-permute-start | bytes 3538952 | tf_op jit(solution)/shard_map/ppermute | solution.py:244
  134.1 34.6 %copy-start.12 = (f32[256,768]{1,0:T(8,128)S(1)}, f32[256,768]{1,0:T(8,128)}, u32[]{:S(2)}) copy-start(f32[256,768]{1,0:T(8,128)} %copy-done.11) | copy-start | bytes 2359300
  134.1 34.6 %copy-start.14 = (f32[256,128]{1,0:T(8,128)S(1)}, f32[256,128]{1,0:T(8,128)}, u32[]{:S(2)}) copy-start(f32[256,128]{1,0:T(8,128)} %copy-done.13) | copy-start | bytes 393220
  134.2 52.3 %collective-permute-start.26 = (bf16[2,4,96,768]{3,2,1,0:T(8,128)(2,1)S(1)}, bf16[2,4,96,768]{3,2,1,0:T(8,128)(2,1)S(1)}, u32[]{:S(2)}, u32[]{:S(2)}) collective-permute-start(bf16[2,4,96,768]{3,2,1,0:T(8,128)(2,1)S(1)} %get-tuple-element.103), channel_id=1, source_target_pairs={{0,2},{1,3},{2,0},{3,1},{4,6},{5,7},{6,4},{7,5},{8,10},{9,11},{10,... | collective-permute-start | bytes 3538952 | tf_op jit(solution)/shard_map/ppermute | solution.py:244
  135.8 32.9 %collective-permute-start.9 = (bf16[256,768]{1,0:T(8,128)(2,1)S(1)}, bf16[256,768]{1,0:T(8,128)(2,1)S(1)}, u32[]{:S(2)}, u32[]{:S(2)}) collective-permute-start(bf16[256,768]{1,0:T(8,128)(2,1)S(1)} %get-tuple-element.64.moved_here), channel_id=1, source_target_pairs={{0,2},{1,3},{2,0},{3,1},{4,6},{5,7},{6,4},{7,5},{8,10},{9,11},{10,... | collective-permute-start | bytes 1179656 | tf_op jit(solution)/shard_map/ppermute | solution.py:244
  169.3 2.3 collective-permute-start.13
  170.1 19.0 %collective-permute-start.29 = (bf16[4,96,768]{2,1,0:T(8,128)(2,1)S(1)}, bf16[4,96,768]{2,1,0:T(8,128)(2,1)S(1)}, u32[]{:S(2)}, u32[]{:S(2)}) collective-permute-start(bf16[4,96,768]{2,1,0:T(8,128)(2,1)S(1)} %fusion.1), channel_id=1, source_target_pairs={{0,4},{4,0},{8,12},{12,8},{16,20},{20,16},{24,28},{28,24},{1,5},{5... | collective-permute-start | bytes 1769480 | tf_op jit(solution)/shard_map/ppermute | solution.py:244
  171.6 14.9 %collective-permute-start.14 = (f32[3,768]{1,0:T(4,128)S(1)}, f32[3,768]{1,0:T(4,128)S(1)}, u32[]{:S(2)}, u32[]{:S(2)}) collective-permute-start(f32[3,768]{1,0:T(4,128)S(1)} %fusion.25), channel_id=1, source_target_pairs={{0,4},{4,0},{8,12},{12,8},{16,20},{20,16},{24,28},{28,24},{1,5},{5... | collective-permute-start | bytes 27656 | tf_op jit(solution)/shard_map/ppermute | solution.py:244
  172.4 25.9 %collective-permute-start.38 = (bf16[4,96,768]{2,1,0:T(8,128)(2,1)S(1)}, bf16[4,96,768]{2,1,0:T(8,128)(2,1)S(1)}, u32[]{:S(2)}, u32[]{:S(2)}) collective-permute-start(bf16[4,96,768]{2,1,0:T(8,128)(2,1)S(1)} %fusion.2), channel_id=1, source_target_pairs={{0,4},{4,0},{8,12},{12,8},{16,20},{20,16},{24,28},{28,24},{1,5},{5... | collective-permute-start | bytes 1769480 | tf_op jit(solution)/shard_map/ppermute | solution.py:244
  186.6 38.0 %collective-permute-start.15 = (f32[3,768]{1,0:T(4,128)S(1)}, f32[3,768]{1,0:T(4,128)S(1)}, u32[]{:S(2)}, u32[]{:S(2)}) collective-permute-start(f32[3,768]{1,0:T(4,128)S(1)} %add.156), channel_id=1, source_target_pairs={{0,8},{4,12},{8,0},{12,4},{16,24},{20,28},{24,16},{28,20},{1,9},{5... | collective-permute-start | bytes 27656 | tf_op jit(solution)/shard_map/ppermute | solution.py:244
  189.1 95.9 %collective-permute-start.27 = (bf16[2,2,4,96,768]{4,3,2,1,0:T(8,128)(2,1)}, bf16[2,2,4,96,768]{4,3,2,1,0:T(8,128)(2,1)}, u32[]{:S(2)}, u32[]{:S(2)}) collective-permute-start(bf16[2,2,4,96,768]{4,3,2,1,0:T(8,128)(2,1)} %get-tuple-element.95), channel_id=1, source_target_pairs={{0,1},{1,0},{2,3},{3,2},{4,5},{5,4},{6,7},{7,6},{8,9},{9,8},{10,11... | collective-permute-start | bytes 7077896 | tf_op jit(solution)/shard_map/ppermute | solution.py:244
  189.3 9.1 %collective-permute-start.30 = (bf16[96,768]{1,0:T(8,128)(2,1)S(1)}, bf16[96,768]{1,0:T(8,128)(2,1)S(1)}, u32[]{:S(2)}, u32[]{:S(2)}) collective-permute-start(bf16[96,768]{1,0:T(8,128)(2,1)S(1)} %get-tuple-element.99), channel_id=1, source_target_pairs={{0,8},{4,12},{8,0},{12,4},{16,24},{20,28},{24,16},{28,20},{1,9},{5... | collective-permute-start | bytes 442376 | tf_op jit(solution)/shard_map/ppermute | solution.py:244
  191.4 11.3 %collective-permute-start.32 = (bf16[96,768]{1,0:T(8,128)(2,1)S(1)}, bf16[96,768]{1,0:T(8,128)(2,1)S(1)}, u32[]{:S(2)}, u32[]{:S(2)}) collective-permute-start(bf16[96,768]{1,0:T(8,128)(2,1)S(1)} %get-tuple-element.100), channel_id=1, source_target_pairs={{0,24},{4,28},{8,16},{12,20},{16,8},{20,12},{24,0},{28,4},{1,25},{... | collective-permute-start | bytes 442376 | tf_op jit(solution)/shard_map/ppermute | solution.py:244
  198.2 11.5 %collective-permute-start.31 = (bf16[96,768]{1,0:T(8,128)(2,1)S(1)}, bf16[96,768]{1,0:T(8,128)(2,1)S(1)}, u32[]{:S(2)}, u32[]{:S(2)}) collective-permute-start(bf16[96,768]{1,0:T(8,128)(2,1)S(1)} %get-tuple-element.101), channel_id=1, source_target_pairs={{0,16},{4,20},{8,24},{12,28},{16,0},{20,4},{24,8},{28,12},{1,17},{... | collective-permute-start | bytes 442376 | tf_op jit(solution)/shard_map/ppermute | solution.py:244
  198.4 43.3 %copy-start.16 = (bf16[256,768]{1,0:T(8,128)(2,1)S(1)}, bf16[256,768]{1,0:T(8,128)(2,1)}, u32[]{:S(2)}) copy-start(bf16[256,768]{1,0:T(8,128)(2,1)} %copy-done.15) | copy-start | bytes 1179652
  198.5 11.4 %collective-permute-start.39 = (bf16[96,768]{1,0:T(8,128)(2,1)S(1)}, bf16[96,768]{1,0:T(8,128)(2,1)S(1)}, u32[]{:S(2)}, u32[]{:S(2)}) collective-permute-start(bf16[96,768]{1,0:T(8,128)(2,1)S(1)} %get-tuple-element.96), channel_id=1, source_target_pairs={{0,8},{4,12},{8,0},{12,4},{16,24},{20,28},{24,16},{28,20},{1,9},{5... | collective-permute-start | bytes 442376 | tf_op jit(solution)/shard_map/ppermute | solution.py:244
  202.7 11.1 %collective-permute-start.41 = (bf16[96,768]{1,0:T(8,128)(2,1)S(1)}, bf16[96,768]{1,0:T(8,128)(2,1)S(1)}, u32[]{:S(2)}, u32[]{:S(2)}) collective-permute-start(bf16[96,768]{1,0:T(8,128)(2,1)S(1)} %get-tuple-element.97), channel_id=1, source_target_pairs={{0,24},{4,28},{8,16},{12,20},{16,8},{20,12},{24,0},{28,4},{1,25},{... | collective-permute-start | bytes 442376 | tf_op jit(solution)/shard_map/ppermute | solution.py:244
  209.7 14.8 %collective-permute-start.40 = (bf16[96,768]{1,0:T(8,128)(2,1)S(1)}, bf16[96,768]{1,0:T(8,128)(2,1)S(1)}, u32[]{:S(2)}, u32[]{:S(2)}) collective-permute-start(bf16[96,768]{1,0:T(8,128)(2,1)S(1)} %get-tuple-element.98), channel_id=1, source_target_pairs={{0,16},{4,20},{8,24},{12,28},{16,0},{20,4},{24,8},{28,12},{1,17},{... | collective-permute-start | bytes 442376 | tf_op jit(solution)/shard_map/ppermute | solution.py:244
  209.8 32.1 %copy-start.18 = (bf16[256,768]{1,0:T(8,128)(2,1)S(1)}, bf16[256,768]{1,0:T(8,128)(2,1)}, u32[]{:S(2)}) copy-start(bf16[256,768]{1,0:T(8,128)(2,1)} %copy-done.17) | copy-start | bytes 1179652
  209.9 19.8 %collective-permute-start.35 = (bf16[96,768]{1,0:T(8,128)(2,1)S(1)}, bf16[96,768]{1,0:T(8,128)(2,1)S(1)}, u32[]{:S(2)}, u32[]{:S(2)}) collective-permute-start(bf16[96,768]{1,0:T(8,128)(2,1)S(1)} %fusion.8), channel_id=1, source_target_pairs={{0,24},{4,28},{8,16},{12,20},{16,8},{20,12},{24,0},{28,4},{1,25},{... | collective-permute-start | bytes 442376 | tf_op jit(solution)/shard_map/ppermute | solution.py:244
  213.9 26.4 %collective-permute-start.34 = (bf16[96,768]{1,0:T(8,128)(2,1)S(1)}, bf16[96,768]{1,0:T(8,128)(2,1)S(1)}, u32[]{:S(2)}, u32[]{:S(2)}) collective-permute-start(bf16[96,768]{1,0:T(8,128)(2,1)S(1)} %fusion.8), channel_id=1, source_target_pairs={{0,16},{4,20},{8,24},{12,28},{16,0},{20,4},{24,8},{28,12},{1,17},{... | collective-permute-start | bytes 442376 | tf_op jit(solution)/shard_map/ppermute | solution.py:244
  224.5 17.1 %collective-permute-start.33 = (bf16[96,768]{1,0:T(8,128)(2,1)S(1)}, bf16[96,768]{1,0:T(8,128)(2,1)S(1)}, u32[]{:S(2)}, u32[]{:S(2)}) collective-permute-start(bf16[96,768]{1,0:T(8,128)(2,1)S(1)} %fusion.8), channel_id=1, source_target_pairs={{0,8},{4,12},{8,0},{12,4},{16,24},{20,28},{24,16},{28,20},{1,9},{5... | collective-permute-start | bytes 442376 | tf_op jit(solution)/shard_map/ppermute | solution.py:244
  224.6 26.1 %copy-start.43 = (bf16[96,768]{1,0:T(8,128)(2,1)}, bf16[96,768]{1,0:T(8,128)(2,1)S(1)}, u32[]{:S(2)}) copy-start(bf16[96,768]{1,0:T(8,128)(2,1)S(1)} %fusion.5) | copy-start | bytes 442372
  224.6 15.7 %copy-start.47 = (f32[3,768]{1,0:T(4,128)}, f32[3,768]{1,0:T(4,128)S(1)}, u32[]{:S(2)}) copy-start(f32[3,768]{1,0:T(4,128)S(1)} %collective-permute-done.15) | copy-start | bytes 27652
  224.6 17.2 %collective-permute-start.44 = (bf16[96,768]{1,0:T(8,128)(2,1)S(1)}, bf16[96,768]{1,0:T(8,128)(2,1)S(1)}, u32[]{:S(2)}, u32[]{:S(2)}) collective-permute-start(bf16[96,768]{1,0:T(8,128)(2,1)S(1)} %fusion.5), channel_id=1, source_target_pairs={{0,24},{4,28},{8,16},{12,20},{16,8},{20,12},{24,0},{28,4},{1,25},{... | collective-permute-start | bytes 442376 | tf_op jit(solution)/shard_map/ppermute | solution.py:244
  229.7 17.0 %collective-permute-start.43 = (bf16[96,768]{1,0:T(8,128)(2,1)S(1)}, bf16[96,768]{1,0:T(8,128)(2,1)S(1)}, u32[]{:S(2)}, u32[]{:S(2)}) collective-permute-start(bf16[96,768]{1,0:T(8,128)(2,1)S(1)} %fusion.5), channel_id=1, source_target_pairs={{0,16},{4,20},{8,24},{12,28},{16,0},{20,4},{24,8},{28,12},{1,17},{... | collective-permute-start | bytes 442376 | tf_op jit(solution)/shard_map/ppermute | solution.py:244
  240.3 8.8 %collective-permute-start.42 = (bf16[96,768]{1,0:T(8,128)(2,1)S(1)}, bf16[96,768]{1,0:T(8,128)(2,1)S(1)}, u32[]{:S(2)}, u32[]{:S(2)}) collective-permute-start(bf16[96,768]{1,0:T(8,128)(2,1)S(1)} %fusion.5), channel_id=1, source_target_pairs={{0,8},{4,12},{8,0},{12,4},{16,24},{20,28},{24,16},{28,20},{1,9},{5... | collective-permute-start | bytes 442376 | tf_op jit(solution)/shard_map/ppermute | solution.py:244
  241.6 14.2 %collective-permute-start.11 = (bf16[256,768]{1,0:T(8,128)(2,1)S(1)}, bf16[256,768]{1,0:T(8,128)(2,1)S(1)}, u32[]{:S(2)}, u32[]{:S(2)}) collective-permute-start(bf16[256,768]{1,0:T(8,128)(2,1)S(1)} %copy-done.16), channel_id=1, source_target_pairs={{0,1},{1,0},{2,3},{3,2},{4,5},{5,4},{6,7},{7,6},{8,9},{9,8},{10,11... | collective-permute-start | bytes 1179656 | tf_op jit(solution)/shard_map/ppermute | solution.py:244
  241.9 11.6 %collective-permute-start.12 = (bf16[256,768]{1,0:T(8,128)(2,1)S(1)}, bf16[256,768]{1,0:T(8,128)(2,1)S(1)}, u32[]{:S(2)}, u32[]{:S(2)}) collective-permute-start(bf16[256,768]{1,0:T(8,128)(2,1)S(1)} %copy-done.18), channel_id=1, source_target_pairs={{0,1},{1,0},{2,3},{3,2},{4,5},{5,4},{6,7},{7,6},{8,9},{9,8},{10,11... | collective-permute-start | bytes 1179656 | tf_op jit(solution)/shard_map/ppermute | solution.py:244
  246.7 5.2 %collective-permute-start.16 = (f32[3,768]{1,0:T(4,128)S(1)}, f32[3,768]{1,0:T(4,128)S(1)}, u32[]{:S(2)}, u32[]{:S(2)}) collective-permute-start(f32[3,768]{1,0:T(4,128)S(1)} %add.157), channel_id=1, source_target_pairs={{0,16},{4,20},{8,24},{12,28},{16,0},{20,4},{24,8},{28,12},{1,17},{... | collective-permute-start | bytes 27656 | tf_op jit(solution)/shard_map/ppermute | solution.py:244
  249.2 16.3 %collective-permute-start.36 = (bf16[4,96,768]{2,1,0:T(8,128)(2,1)S(1)}, bf16[4,96,768]{2,1,0:T(8,128)(2,1)S(1)}, u32[]{:S(2)}, u32[]{:S(2)}) collective-permute-start(bf16[4,96,768]{2,1,0:T(8,128)(2,1)S(1)} %get-tuple-element.110), channel_id=1, source_target_pairs={{0,4},{4,0},{8,12},{12,8},{16,20},{20,16},{24,28},{28,24},{1,5},{5... | collective-permute-start | bytes 1769480 | tf_op jit(solution)/shard_map/ppermute | solution.py:244
  251.9 24.7 %collective-permute-start.45 = (bf16[4,96,768]{2,1,0:T(8,128)(2,1)S(1)}, bf16[4,96,768]{2,1,0:T(8,128)(2,1)}, u32[]{:S(2)}, u32[]{:S(2)}) collective-permute-start(bf16[4,96,768]{2,1,0:T(8,128)(2,1)S(1)} %get-tuple-element.108), channel_id=1, source_target_pairs={{0,4},{4,0},{8,12},{12,8},{16,20},{20,16},{24,28},{28,24},{1,5},{5... | collective-permute-start | bytes 1769480 | tf_op jit(solution)/shard_map/ppermute | solution.py:244
  (33 other events, 132.5 us)

commit v2 on v1

--- a/solution.py
+++ b/solution.py
@@ -8,11 +8,13 @@
 from jax.sharding import PartitionSpec as P
 
 NH = 12
+Y, Z0, Z1 = 8, 9, 10
 EPS = 1e-06
 F32 = jnp.float32
 BF16 = jnp.bfloat16
 VMEM = pl.BlockSpec(memory_space=pltpu.VMEM)
 SMEM = pl.BlockSpec(memory_space=pltpu.SMEM)
+ANY = pl.BlockSpec(memory_space=pl.ANY)
 
 
 def mm(a, b):
@@ -27,21 +29,26 @@
     return lax.dot_general(a, b, (((0,), (0,)), ((), ())), preferred_element_type=F32)
 
 
-def call(kernel, ins, outs, specs=None, scratch=(), vmem=40, flops=0):
+def call(kernel, ins, outs, specs=None, scratch=(), vmem=12, flops=0, after=()):
     shapes = tuple(jax.ShapeDtypeStruct(shape, dtype) for shape, dtype in outs)
     moved = sum(v.size * v.dtype.itemsize for v in list(ins) + list(shapes))
+    count, extra = len(ins), len(after)
+
+    def run(*refs):
+        kernel(*refs[:count], *refs[count + extra :])
+
     return pl.pallas_call(
-        kernel,
+        run,
         out_shape=shapes,
-        in_specs=specs or [VMEM] * len(ins),
+        in_specs=(specs or [VMEM] * count) + [ANY] * extra,
         out_specs=tuple(VMEM for _ in shapes),
         scratch_shapes=list(scratch),
         cost_estimate=pl.CostEstimate(flops=flops, bytes_accessed=moved, transcendentals=0),
         compiler_params=pltpu.CompilerParams(vmem_limit_bytes=vmem * 1024 * 1024),
-    )(*ins)
-
-
-def select_kernel(meta, p0, p1, p2, p3, rows, own, other, hot):
+    )(*ins, *after)
+
+
+def select_kernel(meta, p0, p1, p2, p3, rows, own, other, hot_own, hot_other):
     core = meta[1]
     length = rows.shape[1]
     local = p0.shape[1]
@@ -49,7 +56,7 @@
     down = lax.broadcasted_iota(jnp.int32, (local, local), 0)
     along = lax.broadcasted_iota(jnp.int32, (local, local), 1)
     places = lax.broadcasted_iota(jnp.int32, (local, length), 1)
-    for seq, out in ((1 - core, other), (core, own)):
+    for seq, hot, out in ((1 - core, hot_other, other), (core, hot_own, own)):
         for k, part in enumerate((p0, p1, p2, p3)):
             row = part[pl.ds(seq, 1), :]
             column = jnp.sum(jnp.where(down == along, row, 0), axis=1, keepdims=True)
@@ -58,15 +65,16 @@
         out[...] = mm(hot[...], rows[seq]).astype(BF16)
 
 
-def place_kernel(meta, picks, rows, own, other, out):
+def select_again_kernel(meta, hot_own, hot_other, rows, own, other):
     core = meta[1]
-    length = rows.shape[1]
-    slots = picks.shape[1]
-    base = meta[0] * length
-    places = lax.broadcasted_iota(jnp.int32, (length, slots), 0) + base
-    for seq, update in ((core, own), (1 - core, other)):
-        hot = jnp.where(picks[pl.ds(seq, 1), :] == places, 1.0, 0.0).astype(BF16)
-        out[seq] = (rows[seq].astype(F32) + mm(hot, update[...])).astype(BF16)
+    other[...] = mm(hot_other[...], rows[1 - core]).astype(BF16)
+    own[...] = mm(hot_own[...], rows[core]).astype(BF16)
+
+
+def place_kernel(meta, hot_own, hot_other, rows, own, other, out):
+    core = meta[1]
+    for seq, hot, update in ((core, hot_own, own), (1 - core, hot_other, other)):
+        out[seq] = (rows[seq].astype(F32) + mm_tn(hot[...], update[...])).astype(BF16)
 
 
 def attend_kernel(
@@ -165,13 +173,14 @@
     query_in, key_in, value_in, probs_in, w_query, w_key, w_value, w_out,
     grad_attended_out, grad_query, grad_key, grad_value, grad_sum, small, mixed_back,
 ):
+    small[...] = jnp.zeros_like(small)
     slots, width = chosen_in.shape
     head = width // NH
     pair = 2 * head
     chosen = chosen_in[...].astype(F32)
     grad_normed_mlp = gn_here[...].astype(F32) + gn_there[...].astype(F32)
     grad_hidden, gain_grad = norm_back(chosen + attended[...], gain_mlp[...], grad_normed_mlp)
-    small[1:2, :] = gain_grad
+    small[2:3, :] = gain_grad
     seen = seen_here[...].astype(F32) + seen_there[...].astype(F32)
     grad_attended = (rate[:, :1] * seen + grad_hidden).astype(BF16)
     grad_attended_out[...] = grad_attended
@@ -203,7 +212,7 @@
         + mm_nt(grad_value[...], w_value[...])
     )
     back, gain_grad = norm_back(chosen, gain_attn[...], grad_normed)
-    small[0:1, :] = gain_grad
+    small[1:2, :] = gain_grad
     grad_sum[...] = back + grad_hidden
 
 
@@ -228,7 +237,7 @@
 
 def slots_kernel(
     chosen_in, attended, rate_in, seen_here, seen_there, moved_here, moved_there, w_router, grad_sum,
-    update, grad_chosen, grad_router,
+    small, update, grad_chosen, vectors,
 ):
     chosen = chosen_in[...].astype(F32)
     rate = rate_in[:, :1]
@@ -237,7 +246,108 @@
     update[...] = (rate * delta).astype(BF16)
     score = rate * (1.0 - rate) * jnp.sum(seen * delta, axis=-1, keepdims=True)
     grad_chosen[...] = (grad_sum[...] + score * w_router[...].astype(F32)).astype(BF16)
-    grad_router[...] = jnp.sum(score * chosen, axis=0, keepdims=True)
+    vectors[...] = jnp.zeros_like(vectors)
+    vectors[0:1, :] = jnp.sum(score * chosen, axis=0, keepdims=True)
+    vectors[1:3, :] = small[1:3, :]
+
+
+def reduce_kernel(plan, gots, sends, meta, *refs):
+    keeps, refs = refs[: len(plan)], refs[len(plan) :]
+    got, refs = refs[:gots], refs[gots:]
+    send, kept = refs[:sends], refs[sends:]
+    for keep, new, (rows, bit, g, g_row, t, t_row) in zip(keeps, kept, plan):
+        half = rows // 2
+        mine = pl.multiple_of(meta[bit] * half, half)
+        yours = pl.multiple_of((1 - meta[bit]) * half, half)
+        send[t][t_row : t_row + half, :] = (
+            keep[pl.ds(yours, half), :] + got[g][pl.ds(g_row + yours, half), :].astype(F32)
+        ).astype(BF16)
+        new[...] = keep[pl.ds(mine, half), :] + got[g][pl.ds(g_row + mine, half), :].astype(F32)
+
+
+def split_vectors(v):
+    high = v.astype(BF16).astype(F32)
+    return jnp.concatenate([high, (v - high).astype(BF16).astype(F32)], axis=0)
+
+
+def join_vectors(v):
+    return v[:8, :] + v[8:, :]
+
+
+def reduce_small_kernel(plan, gots, sends, meta, *refs):
+    vectors, refs = refs[0], refs[1:]
+    out = refs[-1]
+    reduce_kernel(plan, gots, sends, meta, *refs[:-1])
+    got = refs[len(plan)]
+    own = join_vectors(split_vectors(vectors[...])) + join_vectors(got[got.shape[0] - 16 :, :].astype(F32))
+    out[...] = own
+    send = refs[len(plan) + gots]
+    send[send.shape[0] - 16 :, :] = split_vectors(own).astype(BF16)
+
+
+def attention_first_kernel(plan, meta, vectors, own, got, send_a, send_b, keep_a, keep_b, out):
+    for n, (send, keep) in enumerate(((send_a, keep_a), (send_b, keep_b))):
+        rows, bit, _, row, _, _ = plan[n]
+        half = rows // 2
+        mine = pl.ds(pl.multiple_of(row + meta[bit] * half, half), half)
+        yours = pl.ds(pl.multiple_of(row + (1 - meta[bit]) * half, half), half)
+        send[:half, :] = (own[yours, :] + got[yours, :].astype(F32)).astype(BF16)
+        keep[...] = own[mine, :] + got[mine, :].astype(F32)
+    out[...] = vectors[...]
+    send_a[send_a.shape[0] - 16 :, :] = split_vectors(vectors[...]).astype(BF16)
+
+
+def finish_kernel(vectors, first, second, got, cur, out):
+    rows = first.shape[0]
+    cur[:rows, :] = (first[...] + got[:rows, :].astype(F32)).astype(BF16)
+    cur[rows:, :] = (second[...] + got[rows : 2 * rows, :].astype(F32)).astype(BF16)
+    if vectors is not None:
+        own = join_vectors(split_vectors(vectors[...]))
+        out[...] = own + join_vectors(got[2 * rows :, :].astype(F32))
+
+
+def join_kernel(plan, meta, *refs):
+    count = len(plan)
+    for (rows, bit, row, got_row), own, got, out in zip(
+        plan, refs[:count], refs[count : 2 * count], refs[2 * count :]
+    ):
+        mine = pl.multiple_of(meta[bit] * rows, rows)
+        yours = pl.multiple_of((1 - meta[bit]) * rows, rows)
+        out[pl.ds(mine, rows), :] = own[row : row + rows, :].astype(out.dtype)
+        out[pl.ds(yours, rows), :] = got[got_row : got_row + rows, :].astype(out.dtype)
+
+
+def join_both_kernel(meta, own_a, own_b, got_a, got_b, out_a, out_b, both):
+    rows = own_a.shape[0]
+    for at, bit, own, got, out in ((0, Z0, own_a, got_a, out_a), (2 * rows, Y, own_b, got_b, out_b)):
+        mine = pl.multiple_of(meta[bit] * rows, rows)
+        yours = pl.multiple_of((1 - meta[bit]) * rows, rows)
+        out[pl.ds(mine, rows), :] = own[...]
+        out[pl.ds(yours, rows), :] = got[...]
+        both[at : at + 2 * rows, :] = out[...]
+
+
+def stack_kernel(got_a, got_b, late):
+    rows = got_a.shape[0]
+    late[:rows, :] = got_a[...]
+    late[rows:, :] = got_b[...]
+
+
+def attention_kernel(meta, *refs):
+    pieces, outs = refs[:8], refs[8:]
+    core, side, y, z0 = meta[1], meta[3], meta[Y], meta[Z0]
+    part = outs[0].shape[0] // 4
+    for n in range(8):
+        other_core, other_side, late = n // 4, (n // 2) % 2, n % 2
+        quarter = 2 * (side ^ other_side) + (core ^ other_core)
+        for packet, bit in ((0, y), (1, z0)):
+            index = bit ^ late
+            block = pieces[n][packet * part : (packet + 1) * part, :].astype(F32)
+            at = pl.multiple_of(quarter * part, 8)
+            for which in range(2):
+                @pl.when(index == which)
+                def _(block=block, at=at, out=outs[2 * packet + which]):
+                    out[pl.ds(at, part), :] = block
 
 
 def swap(v, axis, size, bits):
@@ -360,27 +470,29 @@
     row = lambda v: v.reshape(1, width)
     gain_attn, gain_mlp, w_router = row(gain_attn), row(gain_mlp), row(w_router)
 
+    index = lax.axis_index("batch")
+    along = lambda v, bit: swap(v, "batch", batch, 1 << bit)
     got = [picks] + [across(picks, bits=k) for k in (1, 2, 3)]
     up_other, down_other = across(w_up, bits=1), across(w_down, bits=1)
     count = pick(lengths, core) // 8
-    meta = jnp.stack([place, core, count, side] + [place ^ k for k in range(4)]).astype(jnp.int32)
-    stacked = jnp.stack(got)
-    all_picks = jnp.concatenate([pick(stacked, place ^ a) for a in range(4)], axis=1)
+    meta = jnp.stack(
+        [place, core, count, side] + [place ^ k for k in range(4)] + [(index >> k) & 1 for k in range(3)]
+    ).astype(jnp.int32)
 
     slot_shape = ((slots, width), BF16)
     wide = ((slots, width), F32)
-
-    def select(rows):
-        return call(
-            select_kernel, [meta, *got, rows], [slot_shape, slot_shape],
-            specs=[SMEM] + [VMEM] * 5, scratch=[pltpu.VMEM((slots, length), BF16)],
-            flops=4 * slots * length * width,
-        )
-
-    own, other = select(tokens)
+    hot_shape = ((slots, length), BF16)
+
+    own, other, hot_own, hot_other = call(
+        select_kernel, [meta, *got, tokens], [slot_shape] * 2 + [hot_shape] * 2,
+        specs=[SMEM] + [VMEM] * 5, flops=4 * slots * length * width,
+    )
     here = own + across(other, bits=1)
     there = across(here, bits=2)
-    own, other = select(cotangent)
+    own, other = call(
+        select_again_kernel, [meta, hot_own, hot_other, cotangent], [slot_shape] * 2,
+        specs=[SMEM] + [VMEM] * 3, flops=4 * slots * length * width, after=[here],
+    )
     seen_here = own + across(other, bits=1)
     seen_there = across(seen_here, bits=2)
 
@@ -388,8 +500,7 @@
         attend_kernel,
         [meta, here, there, w_router, gain_attn, gain_mlp, w_query, w_key, w_value, w_out],
         [slot_shape] * 5 + [((NH, slots, slots), F32), slot_shape, wide, slot_shape, ((slots, 128), F32)],
-        specs=[SMEM] + [VMEM] * 9,
-        flops=8 * slots * width * width,
+        specs=[SMEM] + [VMEM] * 9, flops=8 * slots * width * width, after=[seen_here],
     )
     hidden_units = w_up.shape[1]
     act = ((slots, hidden_units), BF16)
@@ -409,61 +520,157 @@
         ],
         flops=12 * slots * width * hidden_units,
     )
+    gd_got, gu_got = across(gd_other, bits=1), across(gu_other, bits=1)
     moved_there = across(moved_here, bits=2)
-    down_part = scatter_sum(gd_own, across(gd_other, bits=1), batch)
-    up_part = scatter_sum(gu_own, across(gu_other, bits=1), batch)
-
-    grad_attended, gq, gk, gv, grad_sum, small = call(
-        attend_back_kernel,
-        [
-            chosen, attended, gain_attn, gain_mlp, gn_here, gn_there, rate, seen_here, seen_there,
-            query, keys, values, probs, w_query, w_key, w_value, w_out,
-        ],
-        [slot_shape] * 4 + [wide, ((2, width), F32)],
-        scratch=[pltpu.VMEM((slots, width), BF16)],
-        flops=8 * slots * width * width,
-    )
-    ga_own, ga_other = call(
-        attend_grads_kernel,
-        [meta, normed, mixed, gq, gk, gv, grad_attended],
-        [((width, width), F32), ((width, width), BF16)],
-        specs=[SMEM] + [VMEM] * 6,
-        scratch=[pltpu.VMEM((width // 2, width), F32)],
-        flops=4 * slots * width * width,
-    )
-    attention_part = scatter_sum(ga_own, across(ga_other, bits=1), batch)
-    update, grad_chosen, grad_router = call(
-        slots_kernel,
-        [chosen, attended, rate, seen_here, seen_there, moved_here, moved_there, w_router, grad_sum],
-        [slot_shape, slot_shape, ((1, width), F32)],
-    )
-
-    def placed(rows, mine):
+
+    def attend_back(after):
+        grad_attended, gq, gk, gv, grad_sum, small = call(
+            attend_back_kernel,
+            [
+                chosen, attended, gain_attn, gain_mlp, gn_here, gn_there, rate, seen_here, seen_there,
+                query, keys, values, probs, w_query, w_key, w_value, w_out,
+            ],
+            [slot_shape] * 4 + [wide, ((8, width), F32)],
+            scratch=[pltpu.VMEM((slots, width), BF16)],
+            flops=8 * slots * width * width, after=after,
+        )
+        ga_own, ga_other = call(
+            attend_grads_kernel,
+            [meta, normed, mixed, gq, gk, gv, grad_attended],
+            [((width, width), F32), ((width, width), BF16)],
+            specs=[SMEM] + [VMEM] * 6,
+            scratch=[pltpu.VMEM((width // 2, width), F32)],
+            flops=4 * slots * width * width,
+        )
+        ga_got = across(ga_other, bits=1)
+        update, grad_chosen, vectors = call(
+            slots_kernel,
+            [chosen, attended, rate, seen_here, seen_there, moved_here, moved_there, w_router, grad_sum, small],
+            [slot_shape, slot_shape, ((8, width), F32)], after=[ga_own],
+        )
+        vectors = vectors + across(vectors, bits=1)
+        return ga_own, ga_got, update, grad_chosen, vectors
+
+    def placed(rows, mine, after=()):
         return call(
-            place_kernel, [meta, all_picks, rows, mine, across(mine, bits=1)],
-            [(rows.shape, BF16)], specs=[SMEM] + [VMEM] * 4,
-            flops=4 * slots * length * width,
+            place_kernel, [meta, hot_own, hot_other, rows, mine, across(mine, bits=1)],
+            [(rows.shape, BF16)], specs=[SMEM] + [VMEM] * 5,
+            flops=4 * slots * length * width, after=after,
         )[0]
 
-    output = placed(tokens, update)
-    grad_tokens = placed(cotangent, grad_chosen)
-
-    vectors = jnp.concatenate([grad_router, small], axis=0)
-    vectors = vectors + across(vectors, bits=1)
-    for bit in range(batch.bit_length() - 1):
-        vectors = vectors + swap(vectors, "batch", batch, 1 << bit)
-
-    down_all = gather_all(down_part, batch)
-    up_all = gather_all(up_part, batch)
-    attention_all = gather_all(attention_part, batch)
-    attention_all = jnp.stack([attention_all, across(attention_all, bits=2)])
-    attention_all = jnp.stack([attention_all, across(attention_all, bits=1)])
-    grad_query, grad_key, grad_value, grad_out = order_attention(attention_all, batch, place)
-    return (
-        output, grad_tokens, vectors[0], vectors[1], vectors[2],
-        grad_query, grad_key, grad_value, grad_out,
-        order_rows(up_all, batch), order_rows(down_all, batch),
-    )
+    if batch != 8:
+        ga_own, ga_got, update, grad_chosen, vectors = attend_back([])
+        for bit in range(batch.bit_length() - 1):
+            vectors = vectors + along(vectors, bit)
+        down_all = gather_all(scatter_sum(gd_own, gd_got, batch), batch)
+        up_all = gather_all(scatter_sum(gu_own, gu_got, batch), batch)
+        attention_all = gather_all(scatter_sum(ga_own, ga_got, batch), batch)
+        attention_all = jnp.stack([attention_all, across(attention_all, bits=2)])
+        attention_all = jnp.stack([attention_all, across(attention_all, bits=1)])
+        return (
+            placed(tokens, update), placed(cotangent, grad_chosen), vectors[0], vectors[1], vectors[2],
+            *order_attention(attention_all, batch, place),
+            order_rows(up_all, batch), order_rows(down_all, batch),
+        )
+
+    def reduce(keeps, gots, plan, sends, after=(), vectors=None):
+        kernel = functools.partial(reduce_kernel, plan, len(gots), len(sends))
+        outs = [((n, width), BF16) for n in sends] + [((p[0] // 2, width), F32) for p in plan]
+        ins = [meta, *keeps, *gots]
+        if vectors is not None:
+            kernel = functools.partial(reduce_small_kernel, plan, len(gots), len(sends))
+            ins = [meta, vectors, *keeps, *gots]
+            outs.append(((8, width), F32))
+        return call(kernel, ins, outs, specs=[SMEM] + [VMEM] * (len(ins) - 1), after=after)
+
+    def join(plan, own, got, dtype, after=()):
+        return call(
+            functools.partial(join_kernel, plan), [meta, *own, *got],
+            [((2 * p[0], width), dtype) for p in plan], specs=[SMEM] + [VMEM] * (2 * len(plan)), after=after,
+        )
+
+    n = width
+    d_send, u_send, d_keep, u_keep = reduce(
+        [gd_own, gu_own], [gd_got, gu_got], [(n, Y, 0, 0, 0, 0), (n, Z0, 1, 0, 1, 0)], [n // 2] * 2
+    )
+    d_got, u_got = along(d_send, 0), along(u_send, 1)
+    ga_own, ga_got, update, grad_chosen, vectors = attend_back([d_keep])
+    d_send, u_send, d_keep, u_keep = reduce(
+        [d_keep, u_keep], [d_got, u_got], [(n // 2, Z0, 0, 0, 0, 0), (n // 2, Y, 1, 0, 1, 0)], [n // 4] * 2,
+        after=[update],
+    )
+    d_got, u_got = along(d_send, 1), along(u_send, 0)
+    half = n // 2
+    a_first = [(half, Y, 0, 0, 0, 0), (half, Z0, 0, half, 1, 0)]
+    a_send, b_send, a_keep, b_keep, vectors = call(
+        functools.partial(attention_first_kernel, a_first),
+        [meta, vectors, ga_own, ga_got],
+        [((half // 2 + 16, width), BF16), ((half // 2, width), BF16)] + [((half // 2, width), F32)] * 2
+        + [((8, width), F32)],
+        specs=[SMEM] + [VMEM] * 3, after=[d_keep],
+    )
+    a_got, b_got = along(a_send, 0), along(b_send, 1)
+    output = placed(tokens, update, after=[a_keep])
+    send, d_keep, u_keep = reduce(
+        [d_keep, u_keep], [d_got, u_got], [(n // 4, Z1, 0, 0, 0, 0), (n // 4, Z1, 1, 0, 0, n // 8)], [n // 4],
+        after=[output],
+    )
+    du_got = along(send, 2)
+    a_send, b_send, a_keep, b_keep, vectors = reduce(
+        [a_keep, b_keep], [a_got, b_got], [(half // 2, Z0, 0, 0, 0, 0), (half // 2, Y, 1, 0, 1, 0)],
+        [half // 4 + 16, half // 4], vectors=vectors, after=[d_keep],
+    )
+    a_got, b_got = along(a_send, 1), along(b_send, 0)
+    grad_tokens = placed(cotangent, grad_chosen, after=[a_keep])
+    cur = call(
+        lambda *r: finish_kernel(None, *r, None), [d_keep, u_keep, du_got], [((n // 4, width), BF16)],
+        after=[grad_tokens],
+    )[0]
+    du_got = along(cur, 2)
+    send, a_keep, b_keep, vectors = reduce(
+        [a_keep, b_keep], [a_got, b_got], [(half // 4, Z1, 0, 0, 0, 0), (half // 4, Z1, 1, 0, 0, half // 8)],
+        [half // 4 + 16], vectors=vectors, after=[cur],
+    )
+    ab_got = along(send, 2)
+    d_all, u_all = join(
+        [(n // 8, Z1, 0, 0), (n // 8, Z1, n // 8, n // 8)], [cur, cur], [du_got, du_got], BF16, after=[a_keep]
+    )
+    d_got, u_got = along(d_all, 1), along(u_all, 0)
+    ab, vectors = call(
+        finish_kernel, [vectors, a_keep, b_keep, ab_got], [((half // 4, width), BF16), ((8, width), F32)],
+        after=[d_all],
+    )
+    ab_got = along(ab, 2)
+    d_all, u_all = join(
+        [(n // 4, Z0, 0, 0), (n // 4, Y, 0, 0)], [d_all, u_all], [d_got, u_got], BF16, after=[ab]
+    )
+    d_got, u_got = along(d_all, 0), along(u_all, 1)
+    a_all, b_all = join(
+        [(half // 8, Z1, 0, 0), (half // 8, Z1, half // 8, half // 8)], [ab, ab], [ab_got, ab_got], BF16,
+        after=[d_all],
+    )
+    a_got, b_got = along(a_all, 1), along(b_all, 0)
+    a_all, b_all, early = call(
+        join_both_kernel, [meta, a_all, b_all, a_got, b_got],
+        [((half // 2, width), BF16)] * 2 + [((half, width), BF16)], specs=[SMEM] + [VMEM] * 4,
+    )
+    a_got, b_got = along(a_all, 0), along(b_all, 1)
+    early_side = across(early, bits=2)
+    early_core = across(early, bits=1)
+    grad_down, grad_up = join(
+        [(n // 2, Y, 0, 0), (n // 2, Z0, 0, 0)], [d_all, u_all], [d_got, u_got], F32, after=[early]
+    )
+    late = call(stack_kernel, [a_got, b_got], [((half, width), BF16)], after=[grad_down])[0]
+    late_side = across(late, bits=2)
+    late_core = across(late, bits=1)
+    early_far = across(early_side, bits=1)
+    late_far = across(late_side, bits=1)
+    grads = call(
+        attention_kernel,
+        [meta, early, late, early_side, late_side, early_core, late_core, early_far, late_far],
+        [((width, width), F32)] * 4, specs=[SMEM] + [VMEM] * 8,
+    )
+    return (output, grad_tokens, vectors[0], vectors[1], vectors[2], *grads, grad_up, grad_down)
 
 
 def solution(mesh):

time: 300 us -> 185 us (0.62)
  waiting for transfers between devices: 145 us -> 80.7 us
  other arithmetic: 20.7 us -> 0.22 us
  starting transfers between devices: 61.8 us -> 51.4 us
  Pallas kernels: 49.5 us -> 39.2 us
  local copies, waits for them, and re-layouts: 17.4 us -> 8.7 us
    ppermute x46 -> x43, waiting for transfers between devices: 145 us -> 80.7 us  [swap(): return lax.ppermute(v, axis, [(i, i ^ bits) for i in range(size)])]
    another operation x11 -> x0, other arithmetic: 13.6 us -> none  [the longest x2 7.48 us: body(): attention_all = jnp.stack([attention_all, across(attention_all, bits=1)])]
    ppermute x46 -> x43, starting transfers between devices: 61.8 us -> 51.4 us  [swap(): return lax.ppermute(v, axis, [(i, i ^ bits) for i in range(size)])]
    pallas_call x13 -> x25, Pallas kernels: 49.5 us -> 39.2 us  [call(): pl.pallas_call(run, out_shape=shapes, in_specs=(specs or [VMEM] * count)...]
    unnamed x102 -> x32, local copies, waits for them, and re-layouts: 14.5 us -> 6.74 us
    convert_element_type x6 -> x0, other arithmetic: 4 us -> none  [the longest x3 2.62 us: scatter_sum(): piece = sum((pick(v, digit ^ k).astype(F32) for v in current)).astype(BF16)]
  transfers between devices with their start and end apart: 46 -> 43, of which waited for: 23 -> 23; matrix products, arithmetic and copies ran while one was open for 4% -> 1% of each run, Pallas kernels for 9% -> 11%
where the time goes in v2:
time: 185 us; the launch traced here: 184 us
  waiting for transfers between devices  80.7 us (44%)
  starting transfers between devices  51.4 us (28%)
  Pallas kernels  39.2 us (21%)
  local copies, waits for them, and re-layouts  8.7 us (5%)
  between operations  3.68 us (2%)
    ppermute x43, waiting for transfers between devices, swap(): return lax.ppermute(v, axis, [(i, i ^ bits) for i in range(size)])  80.7 us
    ppermute x43, starting transfers between devices, swap(): return lax.ppermute(v, axis, [(i, i ^ bits) for i in range(size)])  51.4 us
    pallas_call x25, Pallas kernels, call(): pl.pallas_call(run, out_shape=shapes, in_specs=(specs or [VMEM] * count)...  39.2 us
    unnamed x32, local copies, waits for them, and re-layouts  6.74 us
  transfers between devices with their start and end apart: 43, of which 23 were waited for; matrix products, arithmetic and copies ran while one was open for 1% of the time, Pallas kernels for 11%

profile of v2, /device:TPU:0, one launch (start us, length us, event | category | flops | bytes accessed | tf_op | source)
XLA Modules:
  0.0 183.9 jit_solution(13758526828300392963)
XLA Ops:
  0.6 3.0 %collective-permute-start.1 = (s32[2,64]{1,0:T(2,128)}, s32[2,64]{1,0:T(2,128)S(1)}, u32[]{:S(2)}, u32[]{:S(2)}) collective-permute-start(s32[2,64]{1,0:T(2,128)} %refs_1_.1), channel_id=1, source_target_pairs={{0,2},{1,3},{2,0},{3,1},{4,6},{5,7},{6,4},{7,5},{8,10},{9,11},{10,... | collective-permute-start | bytes 1544 | tf_op jit(solution)/shard_map/ppermute | solution.py:354
  3.9 1.2 dynamic_slice.4
  7.9 1.5 copy-done.2
  9.4 0.7 copy-done.10
  10.1 1.3 shard_map.212
  12.2 0.9 collective-permute-done.3
  13.3 1.1 shard_map.213
  14.8 1.8 collective-permute-start.4
  17.2 2.0 %collective-permute-start.6 = (bf16[256,768]{1,0:T(8,128)(2,1)S(1)}, bf16[256,768]{1,0:T(8,128)(2,1)S(1)}, u32[]{:S(2)}, u32[]{:S(2)}) collective-permute-start(bf16[256,768]{1,0:T(8,128)(2,1)S(1)} %add.22.refs_10_.refs_2_.refs_7_.refs_3_), channel_id=1, source_target_pairs={{0,2},{1,3},{2,0},{3,1},{4,6},{5,7},{6,4},{7,5},{8,10},{9,11},{10,... | collective-permute-start | bytes 1179656 | tf_op jit(solution)/shard_map/ppermute | solution.py:354
  19.2 7.5 %collective-permute-done.4.refs_2_ = bf16[256,768]{1,0:T(8,128)(2,1)S(1)} collective-permute-done((bf16[256,768]{1,0:T(8,128)(2,1)S(1)}, bf16[256,768]{1,0:T(8,128)(2,1)S(1)}, u32[]{:S(2)}, u32[]{:S(2)}) %collective-permute-start.4) | collective-permute-done | bytes 393248 | tf_op jit(solution)/shard_map/ppermute | solution.py:354
  26.8 4.2 %shard_map.214 = (bf16[256,768]{1,0:T(8,128)(2,1)S(1)}, bf16[256,768]{1,0:T(8,128)(2,1)S(1)}, bf16[256,768]{1,0:T(8,128)(2,1)S(1)}, bf16[256,768]{1,0:T(8,128)(2...) custom-call(s32[11]{0:T(128)S(1)} %stack.44.refs_0_, ...), custom_call_target="tpu_custom_call" | custom-call | flops 1207959552 | bytes 12328492 | tf_op jit(solution)/shard_map/pallas_call | solution.py:40
  31.0 3.7 %collective-permute-done.6.refs_3_.refs_8_.refs_4_ = bf16[256,768]{1,0:T(8,128)(2,1)S(1)} collective-permute-done((bf16[256,768]{1,0:T(8,128)(2,1)S(1)}, bf16[256,768]{1,0:T(8,128)(2,1)S(1)}, u32[]{:S(2)}, u32[]{:S(2)}) %collective-permute-start.6) | collective-permute-done | bytes 393248 | tf_op jit(solution)/shard_map/ppermute | solution.py:354
  34.7 2.5 %shard_map.215 = (bf16[256,768]{1,0:T(8,128)(2,1)S(1)}, bf16[256,768]{1,0:T(8,128)(2,1)S(1)}, bf16[256,768]{1,0:T(8,128)(2,1)S(1)}, bf16[256,768]{1,0:T(8,128)(2...) custom-call(bf16[256,768]{1,0:T(8,128)(2,1)S(1)} %get-tuple-element.100.refs_0_, ...), custom_call_target="tpu_custom_call" | custom-call | flops 1811939328 | bytes 8388608 | tf_op jit(solution)/shard_map/pallas_call | solution.py:40
  37.1 2.0 %shard_map.216 = (f32[768,768]{1,0:T(8,128)S(1)}, bf16[768,768]{1,0:T(8,128)(2,1)S(1)}, f32[768,768]{1,0:T(8,128)S(1)}, bf16[768,768]{1,0:T(8,128)(2,1)S(1)}, bf16[256,768]{1,0:T(8,128)(2,1)S(1)}) custom-call(bf16[256,768]{1,0:T(8,128)(2,1)S(1)} %get-tuple-element.100.refs_0_, bf16[256,768]{1,0:T(8,128)(2,1)S(1)} %get-tuple-element.101.refs_1_, ...), custom_call_target="tpu_custom_call" | custom-call | flops 1811939328 | bytes 12189696 | tf_op jit(solution)/shard_map/pallas_call | solution.py:40
  39.8 1.7 collective-permute-start.10
  42.1 1.7 collective-permute-done.12.refs_4_
  43.8 1.1 shard_map.217
  44.9 6.0 %collective-permute-done.10.refs_5_ = bf16[256,768]{1,0:T(8,128)(2,1)S(1)} collective-permute-done((bf16[256,768]{1,0:T(8,128)(2,1)S(1)}, bf16[256,768]{1,0:T(8,128)(2,1)S(1)}, u32[]{:S(2)}, u32[]{:S(2)}) %collective-permute-start.10) | collective-permute-done | bytes 393248 | tf_op jit(solution)/shard_map/ppermute | solution.py:354
  50.9 6.2 %shard_map.218 = (bf16[256,768]{1,0:T(8,128)(2,1)S(1)}, bf16[256,768]{1,0:T(8,128)(2,1)S(1)}, bf16[256,768]{1,0:T(8,128)(2,1)S(1)}, bf16[256,768]{1,0:T(8,128)(2...) custom-call(bf16[256,768]{1,0:T(8,128)(2,1)S(1)} %get-tuple-element.97.refs_0_, ...), custom_call_target="tpu_custom_call" | custom-call | flops 1207959552 | bytes 14317568 | tf_op jit(solution)/shard_map/pallas_call | solution.py:40
  57.0 1.6 shard_map.219
  58.8 1.8 collective-permute-start.16
  60.6 1.6 collective-permute-start.17
  62.2 1.5 collective-permute-start.9
  63.7 9.4 %collective-permute-done.9.refs_6_ = bf16[256,768]{1,0:T(8,128)(2,1)S(1)} collective-permute-done((bf16[256,768]{1,0:T(8,128)(2,1)S(1)}, bf16[256,768]{1,0:T(8,128)(2,1)S(1)}, u32[]{:S(2)}, u32[]{:S(2)}) %collective-permute-start.9) | collective-permute-done | bytes 393248 | tf_op jit(solution)/shard_map/ppermute | solution.py:354
  73.7 0.8 collective-permute-done.16.refs_3_
  74.5 1.5 collective-permute-done.17.refs_4_
  76.0 0.8 shard_map.221
  76.8 1.6 collective-permute-start.21
  79.0 1.2 collective-permute-done.14
  80.4 0.7 shard_map.222
  81.1 1.6 collective-permute-start.19
  83.1 2.3 %shard_map.223.refs_5_ = bf16[2,512,768]{2,1,0:T(8,128)(2,1)} custom-call(s32[11]{0:T(128)S(1)} %stack.44.refs_0_, bf16[256,512]{1,0:T(8,128)(2,1)S(1)} %get-tuple-element.91.refs_1_, bf16[256,512]{1,0:T(8,128)(2,1)S(1)} %get-tuple-element.92.refs_2_, bf16[2,512,768]{2,1,0:T(8,128)(2,1)S(1)} %copy-done.3, ...), custom_call_target="tpu_custom_call" | custom-call | flops 402653184 | bytes 4456492 | tf_op jit(solution)/shard_map/pallas_call | solution.py:40
  85.5 2.9 %collective-permute-done.22.refs_4_ = bf16[192,768]{1,0:T(8,128)(2,1)S(1)} collective-permute-done((bf16[192,768]{1,0:T(8,128)(2,1)S(1)}, bf16[192,768]{1,0:T(8,128)(2,1)S(1)}, u32[]{:S(2)}, u32[]{:S(2)}) %collective-permute-start.22) | collective-permute-done | bytes 294944 | tf_op jit(solution)/shard_map/ppermute | solution.py:354
  88.4 1.4 copy-done.4
  89.8 0.6 shard_map.224
  90.5 2.7 %collective-permute-start.25 = (bf16[192,768]{1,0:T(8,128)(2,1)S(1)}, bf16[192,768]{1,0:T(8,128)(2,1)S(1)}, u32[]{:S(2)}, u32[]{:S(2)}) collective-permute-start(bf16[192,768]{1,0:T(8,128)(2,1)S(1)} %get-tuple-element.149), channel_id=1, source_target_pairs={{0,16},{4,20},{8,24},{12,28},{16,0},{20,4},{24,8},{28,12},{1,17},{... | collective-permute-start | bytes 884744 | tf_op jit(solution)/shard_map/ppermute | solution.py:354
  93.1 1.2 collective-permute-done.20.refs_5_
  94.3 0.7 shard_map.225
  95.0 2.3 %shard_map.226.refs_3_ = bf16[2,512,768]{2,1,0:T(8,128)(2,1)} custom-call(s32[11]{0:T(128)S(1)} %stack.44.refs_0_, bf16[256,512]{1,0:T(8,128)(2,1)S(1)} %get-tuple-element.91.refs_1_, bf16[256,512]{1,0:T(8,128)(2,1)S(1)} %get-tuple-element.92.refs_2_, bf16[2,512,768]{2,1,0:T(8,128)(2,1)S(1)} %copy-done, bf16[256,768]{1,0:T(8,128)(2,1)S(1)} %get-tuple-element.134.refs_4_, ...), custom_call_target="tpu_custom_call" | custom-call | flops 402653184 | bytes 4456492 | tf_op jit(solution)/shard_map/pallas_call | solution.py:40
  97.3 6.2 %collective-permute-done.25.refs_2_ = bf16[192,768]{1,0:T(8,128)(2,1)S(1)} collective-permute-done((bf16[192,768]{1,0:T(8,128)(2,1)S(1)}, bf16[192,768]{1,0:T(8,128)(2,1)S(1)}, u32[]{:S(2)}, u32[]{:S(2)}) %collective-permute-start.25) | collective-permute-done | bytes 294944 | tf_op jit(solution)/shard_map/ppermute | solution.py:354
  103.6 1.4 copy-done.1
  105.1 7.2 %collective-permute-start.23 = (bf16[112,768]{1,0:T(8,128)(2,1)S(1)}, bf16[112,768]{1,0:T(8,128)(2,1)S(1)}, u32[]{:S(2)}, u32[]{:S(2)}) collective-permute-start(bf16[112,768]{1,0:T(8,128)(2,1)S(1)} %get-tuple-element.146), channel_id=1, source_target_pairs={{0,8},{4,12},{8,0},{12,4},{16,24},{20,28},{24,16},{28,20},{1,9},{5... | collective-permute-start | bytes 516104 | tf_op jit(solution)/shard_map/ppermute | solution.py:354
  112.3 5.1 %collective-permute-done.24.refs_5_ = bf16[96,768]{1,0:T(8,128)(2,1)S(1)} collective-permute-done((bf16[96,768]{1,0:T(8,128)(2,1)S(1)}, bf16[96,768]{1,0:T(8,128)(2,1)S(1)}, u32[]{:S(2)}, u32[]{:S(2)}) %collective-permute-start.24) | collective-permute-done | bytes 147488 | tf_op jit(solution)/shard_map/ppermute | solution.py:354
  119.1 1.0 collective-permute-start.30
  120.1 3.6 %collective-permute-start.26 = (bf16[112,768]{1,0:T(8,128)(2,1)S(1)}, bf16[112,768]{1,0:T(8,128)(2,1)S(1)}, u32[]{:S(2)}, u32[]{:S(2)}) collective-permute-start(bf16[112,768]{1,0:T(8,128)(2,1)S(1)} %get-tuple-element.153), channel_id=1, source_target_pairs={{0,16},{4,20},{8,24},{12,28},{16,0},{20,4},{24,8},{28,12},{1,17},{... | collective-permute-start | bytes 516104 | tf_op jit(solution)/shard_map/ppermute | solution.py:354
  123.7 4.8 %collective-permute-done.26.refs_3_ = bf16[112,768]{1,0:T(8,128)(2,1)S(1)} collective-permute-done((bf16[112,768]{1,0:T(8,128)(2,1)S(1)}, bf16[112,768]{1,0:T(8,128)(2,1)S(1)}, u32[]{:S(2)}, u32[]{:S(2)}) %collective-permute-start.26) | collective-permute-done | bytes 172064 | tf_op jit(solution)/shard_map/ppermute | solution.py:354
  128.5 3.3 %collective-permute-start.28 = (bf16[96,768]{1,0:T(8,128)(2,1)S(1)}, bf16[96,768]{1,0:T(8,128)(2,1)S(1)}, u32[]{:S(2)}, u32[]{:S(2)}) collective-permute-start(bf16[96,768]{1,0:T(8,128)(2,1)S(1)} %get-tuple-element.156.refs_5_.refs_1_.refs_2_), channel_id=1, source_target_pairs={{0,16},{4,20},{8,24},{12,28},{16,0},{20,4},{24,8},{28,12},{1,17},{... | collective-permute-start | bytes 442376 | tf_op jit(solution)/shard_map/ppermute | solution.py:354
  131.9 0.6 shard_map.231
  132.5 1.1 collective-permute-start.36
  133.6 2.9 %collective-permute-start.35 = (bf16[384,768]{1,0:T(8,128)(2,1)S(1)}, bf16[384,768]{1,0:T(8,128)(2,1)S(1)}, u32[]{:S(2)}, u32[]{:S(2)}) collective-permute-start(bf16[384,768]{1,0:T(8,128)(2,1)S(1)} %get-tuple-element.158.refs_5_.refs_1_), channel_id=1, source_target_pairs={{0,4},{4,0},{8,12},{12,8},{16,20},{20,16},{24,28},{28,24},{1,5},{5... | collective-permute-start | bytes 1769480 | tf_op jit(solution)/shard_map/ppermute | solution.py:354
  137.1 4.1 %collective-permute-start.31 = (bf16[96,768]{1,0:T(8,128)(2,1)S(1)}, bf16[96,768]{1,0:T(8,128)(2,1)S(1)}, u32[]{:S(2)}, u32[]{:S(2)}) collective-permute-start(bf16[96,768]{1,0:T(8,128)(2,1)S(1)} %get-tuple-element.159.refs_1_), channel_id=1, source_target_pairs={{0,8},{4,12},{8,0},{12,4},{16,24},{20,28},{24,16},{28,20},{1,9},{5... | collective-permute-start | bytes 442376 | tf_op jit(solution)/shard_map/ppermute | solution.py:354
  141.2 1.2 collective-permute-start.32
  142.4 7.7 %collective-permute-done.31.refs_3_ = bf16[96,768]{1,0:T(8,128)(2,1)S(1)} collective-permute-done((bf16[96,768]{1,0:T(8,128)(2,1)S(1)}, bf16[96,768]{1,0:T(8,128)(2,1)S(1)}, u32[]{:S(2)}, u32[]{:S(2)}) %collective-permute-start.31) | collective-permute-done | bytes 147488 | tf_op jit(solution)/shard_map/ppermute | solution.py:354
  150.1 0.6 shard_map.233
  151.4 1.5 collective-permute-start.37
  152.9 3.0 %shard_map.234 = (f32[768,768]{1,0:T(8,128)}, f32[768,768]{1,0:T(8,128)}) custom-call(s32[11]{0:T(128)S(1)} %stack.44.refs_0_, bf16[384,768]{1,0:T(8,128)(2,1)S(1)} %get-tuple-element.158.refs_5_.refs_1_, bf16[384,768]{1,0:T(8,128)(2,1)S(1)} %get-tuple-element.164.refs_2_, bf16[384,768]{1,0:T(8,128)(2,1)S(1)} %collective-permute-done.35.refs_3_, ...), custom_call_target="tpu_custom_call" | custom-call | bytes 7077932 | tf_op jit(solution)/shard_map/pallas_call | solution.py:40
  155.9 1.8 collective-permute-done.33.refs_0_
  157.7 1.7 copy-done.9
  159.4 1.5 collective-permute-start.38
  161.5 6.2 %collective-permute-done.37.refs_3_ = bf16[384,768]{1,0:T(8,128)(2,1)S(1)} collective-permute-done((bf16[384,768]{1,0:T(8,128)(2,1)S(1)}, bf16[384,768]{1,0:T(8,128)(2,1)S(1)}, u32[]{:S(2)}, u32[]{:S(2)}) %collective-permute-start.37) | collective-permute-done | bytes 589856 | tf_op jit(solution)/shard_map/ppermute | solution.py:354
  167.7 9.1 %collective-permute-done.38.refs_4_ = bf16[384,768]{1,0:T(8,128)(2,1)S(1)} collective-permute-done((bf16[384,768]{1,0:T(8,128)(2,1)S(1)}, bf16[384,768]{1,0:T(8,128)(2,1)S(1)}, u32[]{:S(2)}, u32[]{:S(2)}) %collective-permute-start.38) | collective-permute-done | bytes 589856 | tf_op jit(solution)/shard_map/ppermute | solution.py:354
  176.8 0.6 slice_reduce_fusion
  177.4 1.4 collective-permute-done.42.refs_8_
  178.8 5.1 %shard_map.236 = (f32[768,768]{1,0:T(8,128)}, f32[768,768]{1,0:T(8,128)}, f32[768,768]{1,0:T(8,128)}, f32[768,768]{1,0:T(8,128)}) custom-call(s32[11]{0:T(128)S(1)} %stack.44.refs_0_, bf16[384,768]{1,0:T(8,128)(2,1)S(1)} %get-tuple-element.161.refs_5_.refs_1_, bf16[384,768]{1,0:T(8,128)(2,1)S(1)} %shard_map.235.refs_2_, ...), custom_call_target="tpu_custom_call" | custom-call | bytes 14155820 | tf_op jit(solution)/shard_map/pallas_call | solution.py:40
  (88 shorter events, 9.0 us)
Async XLA Ops:
  0.6 7.2 %collective-permute-start.1 = (s32[2,64]{1,0:T(2,128)}, s32[2,64]{1,0:T(2,128)S(1)}, u32[]{:S(2)}, u32[]{:S(2)}) collective-permute-start(s32[2,64]{1,0:T(2,128)} %refs_1_.1), channel_id=1, source_target_pairs={{0,2},{1,3},{2,0},{3,1},{4,6},{5,7},{6,4},{7,5},{8,10},{9,11},{10,... | collective-permute-start | bytes 1544 | tf_op jit(solution)/shard_map/ppermute | solution.py:354
  3.6 4.2 %collective-permute-start = (s32[2,64]{1,0:T(2,128)}, s32[2,64]{1,0:T(2,128)S(1)}, u32[]{:S(2)}, u32[]{:S(2)}) collective-permute-start(s32[2,64]{1,0:T(2,128)} %refs_1_.1), channel_id=1, source_target_pairs={{0,1},{1,0},{2,3},{3,2},{4,5},{5,4},{6,7},{7,6},{8,9},{9,8},{10,11... | collective-permute-start | bytes 1544 | tf_op jit(solution)/shard_map/ppermute | solution.py:354
  3.6 4.2 %collective-permute-start.2 = (s32[2,64]{1,0:T(2,128)}, s32[2,64]{1,0:T(2,128)S(1)}, u32[]{:S(2)}, u32[]{:S(2)}) collective-permute-start(s32[2,64]{1,0:T(2,128)} %refs_1_.1), channel_id=1, source_target_pairs={{0,3},{1,2},{2,1},{3,0},{4,7},{5,6},{6,5},{7,4},{8,11},{9,10},{10,... | collective-permute-start | bytes 1544 | tf_op jit(solution)/shard_map/ppermute | solution.py:354
  7.8 5.4 %copy-start = (bf16[2,512,768]{2,1,0:T(8,128)(2,1)S(1)}, bf16[2,512,768]{2,1,0:T(8,128)(2,1)}, u32[]{:S(2)}) copy-start(bf16[2,512,768]{2,1,0:T(8,128)(2,1)} %refs_3_.5) | copy-start | bytes 4718596
  7.8 1.5 copy-start.2
  9.4 0.7 copy-start.10
  11.3 1.8 collective-permute-start.3
  11.7 19.2 %collective-permute-start.7 = (bf16[768,768]{1,0:T(8,128)(2,1)}, bf16[768,768]{1,0:T(8,128)(2,1)S(1)}, u32[]{:S(2)}, u32[]{:S(2)}) collective-permute-start(bf16[768,768]{1,0:T(8,128)(2,1)} %refs_4_.1), channel_id=1, source_target_pairs={{0,1},{1,0},{2,3},{3,2},{4,5},{5,4},{6,7},{7,6},{8,9},{9,8},{10,11... | collective-permute-start | bytes 3538952 | tf_op jit(solution)/shard_map/ppermute | solution.py:354
  11.9 19.0 %collective-permute-start.8 = (bf16[768,768]{1,0:T(8,128)(2,1)}, bf16[768,768]{1,0:T(8,128)(2,1)S(1)}, u32[]{:S(2)}, u32[]{:S(2)}) collective-permute-start(bf16[768,768]{1,0:T(8,128)(2,1)} %refs_6_.5), channel_id=1, source_target_pairs={{0,1},{1,0},{2,3},{3,2},{4,5},{5,4},{6,7},{7,6},{8,9},{9,8},{10,11... | collective-permute-start | bytes 3538952 | tf_op jit(solution)/shard_map/ppermute | solution.py:354
  13.1 13.6 %copy-start.8 = (bf16[768,768]{1,0:T(8,128)(2,1)S(1)}, bf16[768,768]{1,0:T(8,128)(2,1)}, u32[]{:S(2)}) copy-start(bf16[768,768]{1,0:T(8,128)(2,1)} %refs_16_.1) | copy-start | bytes 3538948
  13.2 5.9 %copy-start.15 = (bf16[768]{0:T(1024)(128)(2,1)S(1)}, bf16[768]{0:T(1024)(128)(2,1)}, u32[]{:S(2)}) copy-start(bf16[768]{0:T(1024)(128)(2,1)} %param.16) | copy-start | bytes 4612
  13.3 13.5 %copy-start.6 = (bf16[768,768]{1,0:T(8,128)(2,1)S(1)}, bf16[768,768]{1,0:T(8,128)(2,1)}, u32[]{:S(2)}) copy-start(bf16[768,768]{1,0:T(8,128)(2,1)} %refs_14_.1) | copy-start | bytes 3538948
  13.3 13.5 %copy-start.7 = (bf16[768,768]{1,0:T(8,128)(2,1)S(1)}, bf16[768,768]{1,0:T(8,128)(2,1)}, u32[]{:S(2)}) copy-start(bf16[768,768]{1,0:T(8,128)(2,1)} %refs_15_.1) | copy-start | bytes 3538948
  14.4 4.8 %copy-start.13 = (f32[768]{0:T(1024)S(1)}, f32[768]{0:T(1024)}, u32[]{:S(2)}) copy-start(f32[768]{0:T(1024)} %param.17) | copy-start | bytes 9220
  14.4 4.8 %copy-start.14 = (f32[768]{0:T(1024)S(1)}, f32[768]{0:T(1024)}, u32[]{:S(2)}) copy-start(f32[768]{0:T(1024)} %param.18) | copy-start | bytes 9220
  14.4 12.3 %copy-start.5 = (bf16[768,768]{1,0:T(8,128)(2,1)S(1)}, bf16[768,768]{1,0:T(8,128)(2,1)}, u32[]{:S(2)}) copy-start(bf16[768,768]{1,0:T(8,128)(2,1)} %refs_13_.1) | copy-start | bytes 3538948
  14.4 2.6 %collective-permute-start.5 = (bf16[256,768]{1,0:T(8,128)(2,1)S(1)}, bf16[256,768]{1,0:T(8,128)(2,1)S(1)}, u32[]{:S(2)}, u32[]{:S(2)}) collective-permute-start(bf16[256,768]{1,0:T(8,128)(2,1)S(1)} %get-tuple-element.96), channel_id=1, source_target_pairs={{0,1},{1,0},{2,3},{3,2},{4,5},{5,4},{6,7},{7,6},{8,9},{9,8},{10,11... | collective-permute-start | bytes 1179656 | tf_op jit(solution)/shard_map/ppermute | solution.py:354
  14.8 11.9 %collective-permute-start.4 = (bf16[256,768]{1,0:T(8,128)(2,1)S(1)}, bf16[256,768]{1,0:T(8,128)(2,1)S(1)}, u32[]{:S(2)}, u32[]{:S(2)}) collective-permute-start(bf16[256,768]{1,0:T(8,128)(2,1)S(1)} %add.21.refs_4_.refs_1_), channel_id=1, source_target_pairs={{0,2},{1,3},{2,0},{3,1},{4,6},{5,7},{6,4},{7,5},{8,10},{9,11},{10,... | collective-permute-start | bytes 1179656 | tf_op jit(solution)/shard_map/ppermute | solution.py:354
  17.2 17.5 %collective-permute-start.6 = (bf16[256,768]{1,0:T(8,128)(2,1)S(1)}, bf16[256,768]{1,0:T(8,128)(2,1)S(1)}, u32[]{:S(2)}, u32[]{:S(2)}) collective-permute-start(bf16[256,768]{1,0:T(8,128)(2,1)S(1)} %add.22.refs_10_.refs_2_.refs_7_.refs_3_), channel_id=1, source_target_pairs={{0,2},{1,3},{2,0},{3,1},{4,6},{5,7},{6,4},{7,5},{8,10},{9,11},{10,... | collective-permute-start | bytes 1179656 | tf_op jit(solution)/shard_map/ppermute | solution.py:354
  19.2 15.4 %copy-start.11 = (bf16[768,768]{1,0:T(8,128)(2,1)S(1)}, bf16[768,768]{1,0:T(8,128)(2,1)}, u32[]{:S(2)}) copy-start(bf16[768,768]{1,0:T(8,128)(2,1)} %refs_4_.1) | copy-start | bytes 3538948
  19.2 15.4 %copy-start.12 = (bf16[768,768]{1,0:T(8,128)(2,1)S(1)}, bf16[768,768]{1,0:T(8,128)(2,1)}, u32[]{:S(2)}) copy-start(bf16[768,768]{1,0:T(8,128)(2,1)} %refs_6_.5) | copy-start | bytes 3538948
  39.2 2.9 %collective-permute-start.11 = (bf16[768,768]{1,0:T(8,128)(2,1)S(1)}, bf16[768,768]{1,0:T(8,128)(2,1)S(1)}, u32[]{:S(2)}, u32[]{:S(2)}) collective-permute-start(bf16[768,768]{1,0:T(8,128)(2,1)S(1)} %get-tuple-element.114), channel_id=1, source_target_pairs={{0,1},{1,0},{2,3},{3,2},{4,5},{5,4},{6,7},{7,6},{8,9},{9,8},{10,11... | collective-permute-start | bytes 3538952 | tf_op jit(solution)/shard_map/ppermute | solution.py:354
  39.3 4.5 %collective-permute-start.12 = (bf16[768,768]{1,0:T(8,128)(2,1)S(1)}, bf16[768,768]{1,0:T(8,128)(2,1)S(1)}, u32[]{:S(2)}, u32[]{:S(2)}) collective-permute-start(bf16[768,768]{1,0:T(8,128)(2,1)S(1)} %get-tuple-element.115), channel_id=1, source_target_pairs={{0,1},{1,0},{2,3},{3,2},{4,5},{5,4},{6,7},{7,6},{8,9},{9,8},{10,11... | collective-permute-start | bytes 3538952 | tf_op jit(solution)/shard_map/ppermute | solution.py:354
  39.8 11.1 %collective-permute-start.10 = (bf16[256,768]{1,0:T(8,128)(2,1)S(1)}, bf16[256,768]{1,0:T(8,128)(2,1)S(1)}, u32[]{:S(2)}, u32[]{:S(2)}) collective-permute-start(bf16[256,768]{1,0:T(8,128)(2,1)S(1)} %get-tuple-element.107.refs_4_), channel_id=1, source_target_pairs={{0,2},{1,3},{2,0},{3,1},{4,6},{5,7},{6,4},{7,5},{8,10},{9,11},{10,... | collective-permute-start | bytes 1179656 | tf_op jit(solution)/shard_map/ppermute | solution.py:354
  58.7 21.6 %collective-permute-start.15 = (bf16[768,768]{1,0:T(8,128)(2,1)S(1)}, bf16[768,768]{1,0:T(8,128)(2,1)S(1)}, u32[]{:S(2)}, u32[]{:S(2)}) collective-permute-start(bf16[768,768]{1,0:T(8,128)(2,1)S(1)} %get-tuple-element.128), channel_id=1, source_target_pairs={{0,1},{1,0},{2,3},{3,2},{4,5},{5,4},{6,7},{7,6},{8,9},{9,8},{10,11... | collective-permute-start | bytes 3538952 | tf_op jit(solution)/shard_map/ppermute | solution.py:354
  58.8 15.8 %collective-permute-start.16 = (bf16[384,768]{1,0:T(8,128)(2,1)S(1)}, bf16[384,768]{1,0:T(8,128)(2,1)S(1)}, u32[]{:S(2)}, u32[]{:S(2)}) collective-permute-start(bf16[384,768]{1,0:T(8,128)(2,1)S(1)} %get-tuple-element.130), channel_id=1, source_target_pairs={{0,4},{4,0},{8,12},{12,8},{16,20},{20,16},{24,28},{28,24},{1,5},{5... | collective-permute-start | bytes 1769480 | tf_op jit(solution)/shard_map/ppermute | solution.py:354
  60.6 15.4 %collective-permute-start.17 = (bf16[384,768]{1,0:T(8,128)(2,1)S(1)}, bf16[384,768]{1,0:T(8,128)(2,1)S(1)}, u32[]{:S(2)}, u32[]{:S(2)}) collective-permute-start(bf16[384,768]{1,0:T(8,128)(2,1)S(1)} %get-tuple-element.131), channel_id=1, source_target_pairs={{0,8},{4,12},{8,0},{12,4},{16,24},{20,28},{24,16},{28,20},{1,9},{5... | collective-permute-start | bytes 1769480 | tf_op jit(solution)/shard_map/ppermute | solution.py:354
  62.2 10.9 %collective-permute-start.9 = (bf16[256,768]{1,0:T(8,128)(2,1)S(1)}, bf16[256,768]{1,0:T(8,128)(2,1)S(1)}, u32[]{:S(2)}, u32[]{:S(2)}) collective-permute-start(bf16[256,768]{1,0:T(8,128)(2,1)S(1)} %get-tuple-element.106.refs_5_), channel_id=1, source_target_pairs={{0,2},{1,3},{2,0},{3,1},{4,6},{5,7},{6,4},{7,5},{8,10},{9,11},{10,... | collective-permute-start | bytes 1179656 | tf_op jit(solution)/shard_map/ppermute | solution.py:354
  73.6 9.1 %collective-permute-start.13 = (bf16[256,768]{1,0:T(8,128)(2,1)S(1)}, bf16[256,768]{1,0:T(8,128)(2,1)S(1)}, u32[]{:S(2)}, u32[]{:S(2)}) collective-permute-start(bf16[256,768]{1,0:T(8,128)(2,1)S(1)} %get-tuple-element.126.refs_5_.refs_4_), channel_id=1, source_target_pairs={{0,1},{1,0},{2,3},{3,2},{4,5},{5,4},{6,7},{7,6},{8,9},{9,8},{10,11... | collective-permute-start | bytes 1179656 | tf_op jit(solution)/shard_map/ppermute | solution.py:354
  76.8 8.6 %collective-permute-start.21 = (bf16[192,768]{1,0:T(8,128)(2,1)S(1)}, bf16[192,768]{1,0:T(8,128)(2,1)S(1)}, u32[]{:S(2)}, u32[]{:S(2)}) collective-permute-start(bf16[192,768]{1,0:T(8,128)(2,1)S(1)} %get-tuple-element.140), channel_id=1, source_target_pairs={{0,8},{4,12},{8,0},{12,4},{16,24},{20,28},{24,16},{28,20},{1,9},{5... | collective-permute-start | bytes 884744 | tf_op jit(solution)/shard_map/ppermute | solution.py:354
  78.5 9.9 %collective-permute-start.22 = (bf16[192,768]{1,0:T(8,128)(2,1)S(1)}, bf16[192,768]{1,0:T(8,128)(2,1)S(1)}, u32[]{:S(2)}, u32[]{:S(2)}) collective-permute-start(bf16[192,768]{1,0:T(8,128)(2,1)S(1)} %get-tuple-element.141), channel_id=1, source_target_pairs={{0,4},{4,0},{8,12},{12,8},{16,20},{20,16},{24,28},{28,24},{1,5},{5... | collective-permute-start | bytes 884744 | tf_op jit(solution)/shard_map/ppermute | solution.py:354
  79.0 1.2 collective-permute-start.14
  80.2 14.8 %collective-permute-start.18 = (bf16[256,768]{1,0:T(8,128)(2,1)S(1)}, bf16[256,768]{1,0:T(8,128)(2,1)S(1)}, u32[]{:S(2)}, u32[]{:S(2)}) collective-permute-start(bf16[256,768]{1,0:T(8,128)(2,1)S(1)} %get-tuple-element.134.refs_4_), channel_id=1, source_target_pairs={{0,1},{1,0},{2,3},{3,2},{4,5},{5,4},{6,7},{7,6},{8,9},{9,8},{10,11... | collective-permute-start | bytes 1179656 | tf_op jit(solution)/shard_map/ppermute | solution.py:354
  80.3 2.8 %copy-start.3 = (bf16[2,512,768]{2,1,0:T(8,128)(2,1)S(1)}, bf16[2,512,768]{2,1,0:T(8,128)(2,1)}, u32[]{:S(2)}) copy-start(bf16[2,512,768]{2,1,0:T(8,128)(2,1)} %refs_3_.4) | copy-start | bytes 4718596
  81.1 13.2 %collective-permute-start.19 = (bf16[208,768]{1,0:T(8,128)(2,1)S(1)}, bf16[208,768]{1,0:T(8,128)(2,1)S(1)}, u32[]{:S(2)}, u32[]{:S(2)}) collective-permute-start(bf16[208,768]{1,0:T(8,128)(2,1)S(1)} %get-tuple-element.137), channel_id=1, source_target_pairs={{0,4},{4,0},{8,12},{12,8},{16,20},{20,16},{24,28},{28,24},{1,5},{5... | collective-permute-start | bytes 958472 | tf_op jit(solution)/shard_map/ppermute | solution.py:354
  82.7 11.6 %collective-permute-start.20 = (bf16[192,768]{1,0:T(8,128)(2,1)S(1)}, bf16[192,768]{1,0:T(8,128)(2,1)S(1)}, u32[]{:S(2)}, u32[]{:S(2)}) collective-permute-start(bf16[192,768]{1,0:T(8,128)(2,1)S(1)} %get-tuple-element.138), channel_id=1, source_target_pairs={{0,8},{4,12},{8,0},{12,4},{16,24},{20,28},{24,16},{28,20},{1,9},{5... | collective-permute-start | bytes 884744 | tf_op jit(solution)/shard_map/ppermute | solution.py:354
  88.4 1.4 copy-start.4
  90.5 13.1 %collective-permute-start.25 = (bf16[192,768]{1,0:T(8,128)(2,1)S(1)}, bf16[192,768]{1,0:T(8,128)(2,1)S(1)}, u32[]{:S(2)}, u32[]{:S(2)}) collective-permute-start(bf16[192,768]{1,0:T(8,128)(2,1)S(1)} %get-tuple-element.149), channel_id=1, source_target_pairs={{0,16},{4,20},{8,24},{12,28},{16,0},{20,4},{24,8},{28,12},{1,17},{... | collective-permute-start | bytes 884744 | tf_op jit(solution)/shard_map/ppermute | solution.py:354
  103.6 1.4 copy-start.1
  105.0 13.5 %collective-permute-start.27 = (bf16[192,768]{1,0:T(8,128)(2,1)S(1)}, bf16[192,768]{1,0:T(8,128)(2,1)S(1)}, u32[]{:S(2)}, u32[]{:S(2)}) collective-permute-start(bf16[192,768]{1,0:T(8,128)(2,1)S(1)} %shard_map.227.refs_6_.refs_1_.refs_2_), channel_id=1, source_target_pairs={{0,16},{4,20},{8,24},{12,28},{16,0},{20,4},{24,8},{28,12},{1,17},{... | collective-permute-start | bytes 884744 | tf_op jit(solution)/shard_map/ppermute | solution.py:354
  105.1 12.4 %collective-permute-start.23 = (bf16[112,768]{1,0:T(8,128)(2,1)S(1)}, bf16[112,768]{1,0:T(8,128)(2,1)S(1)}, u32[]{:S(2)}, u32[]{:S(2)}) collective-permute-start(bf16[112,768]{1,0:T(8,128)(2,1)S(1)} %get-tuple-element.146), channel_id=1, source_target_pairs={{0,8},{4,12},{8,0},{12,4},{16,24},{20,28},{24,16},{28,20},{1,9},{5... | collective-permute-start | bytes 516104 | tf_op jit(solution)/shard_map/ppermute | solution.py:354
  112.3 5.1 %collective-permute-start.24 = (bf16[96,768]{1,0:T(8,128)(2,1)S(1)}, bf16[96,768]{1,0:T(8,128)(2,1)S(1)}, u32[]{:S(2)}, u32[]{:S(2)}) collective-permute-start(bf16[96,768]{1,0:T(8,128)(2,1)S(1)} %get-tuple-element.147), channel_id=1, source_target_pairs={{0,4},{4,0},{8,12},{12,8},{16,20},{20,16},{24,28},{28,24},{1,5},{5... | collective-permute-start | bytes 442376 | tf_op jit(solution)/shard_map/ppermute | solution.py:354
  119.1 12.7 %collective-permute-start.30 = (bf16[192,768]{1,0:T(8,128)(2,1)S(1)}, bf16[192,768]{1,0:T(8,128)(2,1)S(1)}, u32[]{:S(2)}, u32[]{:S(2)}) collective-permute-start(bf16[192,768]{1,0:T(8,128)(2,1)S(1)} %get-tuple-element.157.refs_2_), channel_id=1, source_target_pairs={{0,4},{4,0},{8,12},{12,8},{16,20},{20,16},{24,28},{28,24},{1,5},{5... | collective-permute-start | bytes 884744 | tf_op jit(solution)/shard_map/ppermute | solution.py:354
  120.1 11.8 %collective-permute-start.29 = (bf16[192,768]{1,0:T(8,128)(2,1)S(1)}, bf16[192,768]{1,0:T(8,128)(2,1)S(1)}, u32[]{:S(2)}, u32[]{:S(2)}) collective-permute-start(bf16[192,768]{1,0:T(8,128)(2,1)S(1)} %get-tuple-element.154.refs_4_.refs_1_), channel_id=1, source_target_pairs={{0,8},{4,12},{8,0},{12,4},{16,24},{20,28},{24,16},{28,20},{1,9},{5... | collective-permute-start | bytes 884744 | tf_op jit(solution)/shard_map/ppermute | solution.py:354
  120.1 8.4 %collective-permute-start.26 = (bf16[112,768]{1,0:T(8,128)(2,1)S(1)}, bf16[112,768]{1,0:T(8,128)(2,1)S(1)}, u32[]{:S(2)}, u32[]{:S(2)}) collective-permute-start(bf16[112,768]{1,0:T(8,128)(2,1)S(1)} %get-tuple-element.153), channel_id=1, source_target_pairs={{0,16},{4,20},{8,24},{12,28},{16,0},{20,4},{24,8},{28,12},{1,17},{... | collective-permute-start | bytes 516104 | tf_op jit(solution)/shard_map/ppermute | solution.py:354
  128.5 8.0 %collective-permute-start.28 = (bf16[96,768]{1,0:T(8,128)(2,1)S(1)}, bf16[96,768]{1,0:T(8,128)(2,1)S(1)}, u32[]{:S(2)}, u32[]{:S(2)}) collective-permute-start(bf16[96,768]{1,0:T(8,128)(2,1)S(1)} %get-tuple-element.156.refs_5_.refs_1_.refs_2_), channel_id=1, source_target_pairs={{0,16},{4,20},{8,24},{12,28},{16,0},{20,4},{24,8},{28,12},{1,17},{... | collective-permute-start | bytes 442376 | tf_op jit(solution)/shard_map/ppermute | solution.py:354
  132.5 20.4 %collective-permute-start.36 = (bf16[384,768]{1,0:T(8,128)(2,1)S(1)}, bf16[384,768]{1,0:T(8,128)(2,1)S(1)}, u32[]{:S(2)}, u32[]{:S(2)}) collective-permute-start(bf16[384,768]{1,0:T(8,128)(2,1)S(1)} %get-tuple-element.164.refs_2_), channel_id=1, source_target_pairs={{0,8},{4,12},{8,0},{12,4},{16,24},{20,28},{24,16},{28,20},{1,9},{5... | collective-permute-start | bytes 1769480 | tf_op jit(solution)/shard_map/ppermute | solution.py:354
  133.6 19.3 %collective-permute-start.35 = (bf16[384,768]{1,0:T(8,128)(2,1)S(1)}, bf16[384,768]{1,0:T(8,128)(2,1)S(1)}, u32[]{:S(2)}, u32[]{:S(2)}) collective-permute-start(bf16[384,768]{1,0:T(8,128)(2,1)S(1)} %get-tuple-element.158.refs_5_.refs_1_), channel_id=1, source_target_pairs={{0,4},{4,0},{8,12},{12,8},{16,20},{20,16},{24,28},{28,24},{1,5},{5... | collective-permute-start | bytes 1769480 | tf_op jit(solution)/shard_map/ppermute | solution.py:354
  137.1 13.0 %collective-permute-start.31 = (bf16[96,768]{1,0:T(8,128)(2,1)S(1)}, bf16[96,768]{1,0:T(8,128)(2,1)S(1)}, u32[]{:S(2)}, u32[]{:S(2)}) collective-permute-start(bf16[96,768]{1,0:T(8,128)(2,1)S(1)} %get-tuple-element.159.refs_1_), channel_id=1, source_target_pairs={{0,8},{4,12},{8,0},{12,4},{16,24},{20,28},{24,16},{28,20},{1,9},{5... | collective-permute-start | bytes 442376 | tf_op jit(solution)/shard_map/ppermute | solution.py:354
  141.2 8.9 %collective-permute-start.32 = (bf16[96,768]{1,0:T(8,128)(2,1)S(1)}, bf16[96,768]{1,0:T(8,128)(2,1)S(1)}, u32[]{:S(2)}, u32[]{:S(2)}) collective-permute-start(bf16[96,768]{1,0:T(8,128)(2,1)S(1)} %get-tuple-element.160.refs_2_), channel_id=1, source_target_pairs={{0,4},{4,0},{8,12},{12,8},{16,20},{20,16},{24,28},{28,24},{1,5},{5... | collective-permute-start | bytes 442376 | tf_op jit(solution)/shard_map/ppermute | solution.py:354
  150.7 7.0 %collective-permute-start.33 = (bf16[192,768]{1,0:T(8,128)(2,1)S(1)}, bf16[192,768]{1,0:T(8,128)(2,1)S(1)}, u32[]{:S(2)}, u32[]{:S(2)}) collective-permute-start(bf16[192,768]{1,0:T(8,128)(2,1)S(1)} %get-tuple-element.162), channel_id=1, source_target_pairs={{0,4},{4,0},{8,12},{12,8},{16,20},{20,16},{24,28},{28,24},{1,5},{5... | collective-permute-start | bytes 884744 | tf_op jit(solution)/shard_map/ppermute | solution.py:354
  150.8 7.0 %collective-permute-start.34 = (bf16[192,768]{1,0:T(8,128)(2,1)S(1)}, bf16[192,768]{1,0:T(8,128)(2,1)S(1)}, u32[]{:S(2)}, u32[]{:S(2)}) collective-permute-start(bf16[192,768]{1,0:T(8,128)(2,1)S(1)} %get-tuple-element.163), channel_id=1, source_target_pairs={{0,8},{4,12},{8,0},{12,4},{16,24},{20,28},{24,16},{28,20},{1,9},{5... | collective-permute-start | bytes 884744 | tf_op jit(solution)/shard_map/ppermute | solution.py:354
  151.4 16.3 %collective-permute-start.37 = (bf16[384,768]{1,0:T(8,128)(2,1)S(1)}, bf16[384,768]{1,0:T(8,128)(2,1)S(1)}, u32[]{:S(2)}, u32[]{:S(2)}) collective-permute-start(bf16[384,768]{1,0:T(8,128)(2,1)S(1)} %get-tuple-element.161.refs_5_.refs_1_), channel_id=1, source_target_pairs={{0,2},{1,3},{2,0},{3,1},{4,6},{5,7},{6,4},{7,5},{8,10},{9,11},{10,... | collective-permute-start | bytes 1769480 | tf_op jit(solution)/shard_map/ppermute | solution.py:354
  157.7 1.7 copy-start.9
  159.4 17.3 %collective-permute-start.38 = (bf16[384,768]{1,0:T(8,128)(2,1)S(1)}, bf16[384,768]{1,0:T(8,128)(2,1)S(1)}, u32[]{:S(2)}, u32[]{:S(2)}) collective-permute-start(bf16[384,768]{1,0:T(8,128)(2,1)S(1)} %shard_map.235.refs_2_), channel_id=1, source_target_pairs={{0,2},{1,3},{2,0},{3,1},{4,6},{5,7},{6,4},{7,5},{8,10},{9,11},{10,... | collective-permute-start | bytes 1769480 | tf_op jit(solution)/shard_map/ppermute | solution.py:354
  161.0 16.4 %collective-permute-start.39 = (bf16[384,768]{1,0:T(8,128)(2,1)S(1)}, bf16[384,768]{1,0:T(8,128)(2,1)S(1)}, u32[]{:S(2)}, u32[]{:S(2)}) collective-permute-start(bf16[384,768]{1,0:T(8,128)(2,1)S(1)} %get-tuple-element.161.refs_5_.refs_1_), channel_id=1, source_target_pairs={{0,1},{1,0},{2,3},{3,2},{4,5},{5,4},{6,7},{7,6},{8,9},{9,8},{10,11... | collective-permute-start | bytes 1769480 | tf_op jit(solution)/shard_map/ppermute | solution.py:354
  161.0 16.4 %collective-permute-start.40 = (bf16[384,768]{1,0:T(8,128)(2,1)S(1)}, bf16[384,768]{1,0:T(8,128)(2,1)S(1)}, u32[]{:S(2)}, u32[]{:S(2)}) collective-permute-start(bf16[384,768]{1,0:T(8,128)(2,1)S(1)} %shard_map.235.refs_2_), channel_id=1, source_target_pairs={{0,1},{1,0},{2,3},{3,2},{4,5},{5,4},{6,7},{7,6},{8,9},{9,8},{10,11... | collective-permute-start | bytes 1769480 | tf_op jit(solution)/shard_map/ppermute | solution.py:354
  167.7 9.8 %collective-permute-start.41 = (bf16[384,768]{1,0:T(8,128)(2,1)S(1)}, bf16[384,768]{1,0:T(8,128)(2,1)S(1)}, u32[]{:S(2)}, u32[]{:S(2)}) collective-permute-start(bf16[384,768]{1,0:T(8,128)(2,1)S(1)} %collective-permute-done.37.refs_3_), channel_id=1, source_target_pairs={{0,1},{1,0},{2,3},{3,2},{4,5},{5,4},{6,7},{7,6},{8,9},{9,8},{10,11... | collective-permute-start | bytes 1769480 | tf_op jit(solution)/shard_map/ppermute | solution.py:354
  176.8 2.0 %collective-permute-start.42 = (bf16[384,768]{1,0:T(8,128)(2,1)S(1)}, bf16[384,768]{1,0:T(8,128)(2,1)S(1)}, u32[]{:S(2)}, u32[]{:S(2)}) collective-permute-start(bf16[384,768]{1,0:T(8,128)(2,1)S(1)} %collective-permute-done.38.refs_4_), channel_id=1, source_target_pairs={{0,1},{1,0},{2,3},{3,2},{4,5},{5,4},{6,7},{7,6},{8,9},{9,8},{10,11... | collective-permute-start | bytes 1769480 | tf_op jit(solution)/shard_map/ppermute | solution.py:354

commit v3 on v1

v3 whole, which is shorter than its diff:
```python
import functools

import jax
import jax.numpy as jnp
from jax import lax
from jax.experimental import pallas as pl
from jax.experimental.pallas import tpu as pltpu
from jax.sharding import PartitionSpec as P

NH = 12
Y, Z0, Z1 = 8, 9, 10
ORDER = (
    "F AB SL R2 FA D3 A2 A3 P2 R2U U3 A4 D4 P1 A5 U4 A6 U5 D5 AT0 XC UU DU AT1"
).split()
WORK = {'P1': 2000, 'AB': 100, 'A5': 8000, 'D5': 4000, 'U5': 8000, 'U4': 2000, 'D3': 300, 'SL': 8000, 'UU': 300, 'DU': 1000, 'P2': 4000, 'R2': 4000, 'AT0': 2000, 'A6': 300, 'SA': 8000, 'A4': 4000, 'ML': 100, 'A2': 300, 'R2U': 600, 'A3': 1000}
HOLD = {'A2': ['u1'], 'P2': ['d3'], 'U5': ['x1'], 'U4': ['b6'], 'A3': ['up'], 'A6': ['ce'], 'UU': ['d6']}
EPS = 1e-06
F32 = jnp.float32
BF16 = jnp.bfloat16
VMEM = pl.BlockSpec(memory_space=pltpu.VMEM)
SMEM = pl.BlockSpec(memory_space=pltpu.SMEM)
ANY = pl.BlockSpec(memory_space=pl.ANY)
HBM = pl.BlockSpec(memory_space=pltpu.HBM)


def mm(a, b):
    return jnp.dot(a, b, preferred_element_type=F32)


def mm_nt(a, b):
    return lax.dot_general(a, b, (((1,), (1,)), ((), ())), preferred_element_type=F32)


def mm_tn(a, b):
    return lax.dot_general(a, b, (((0,), (0,)), ((), ())), preferred_element_type=F32)


def call(
    tag, kernel, ins, outs, specs=None, scratch=(), vmem=12, after=(), name=None, token=False,
    out_specs=None, aliases=None,
):
    shapes = [jax.ShapeDtypeStruct(shape, dtype) for shape, dtype in outs]
    results = len(shapes)
    out_specs = list(out_specs or [VMEM] * results)
    if token:
        shapes.append(jax.ShapeDtypeStruct((8, 128), F32))
        out_specs.append(VMEM)
    count, extra = len(ins), len(after)

    def run(*refs):
        rest = refs[count + extra :]
        if token:
            rest[results][...] = jnp.zeros((8, 128), F32)
            rest = rest[:results] + rest[results + 1 :]
        kernel(*refs[:count], *rest)

    return pl.pallas_call(
        run,
        out_shape=tuple(shapes),
        in_specs=(specs or [VMEM] * count) + [ANY] * extra,
        out_specs=tuple(out_specs),
        scratch_shapes=list(scratch),
        input_output_aliases=aliases or {},
        name=name or getattr(kernel, "func", kernel).__name__,
        cost_estimate=pl.CostEstimate(flops=1 + WORK.get(tag, 0) * 1_000_000, bytes_accessed=1, transcendentals=0),
        compiler_params=pltpu.CompilerParams(vmem_limit_bytes=vmem * 1024 * 1024),
    )(*ins, *after)


def select_kernel(meta, p1, p2, p3, picks, rows, own, other, hot_own, hot_other, local_rows, p0, sems):
    core = meta[1]
    copies = [
        pltpu.make_async_copy(picks, p0, sems.at[0]),
        pltpu.make_async_copy(rows.at[1 - core], local_rows.at[0], sems.at[1]),
        pltpu.make_async_copy(rows.at[core], local_rows.at[1], sems.at[2]),
    ]
    for copy in copies:
        copy.start()
    length = rows.shape[1]
    local = p1.shape[1]
    base = meta[0] * length
    down = lax.broadcasted_iota(jnp.int32, (local, local), 0)
    along = lax.broadcasted_iota(jnp.int32, (local, local), 1)
    places = lax.broadcasted_iota(jnp.int32, (local, length), 1)
    for k, part in ((1, p1), (2, p2), (3, p3), (0, p0)):
        if k == 0:
            copies[0].wait()
        at = pl.multiple_of(meta[4 + k] * local, local)
        for seq, hot in ((1 - core, hot_other), (core, hot_own)):
            row = part[pl.ds(seq, 1), :]
            column = jnp.sum(jnp.where(down == along, row, 0), axis=1, keepdims=True)
            hot[pl.ds(at, local), :] = jnp.where(column - base == places, 1.0, 0.0).astype(BF16)
    copies[1].wait()
    other[...] = mm(hot_other[...], local_rows[0]).astype(BF16)
    copies[2].wait()
    own[...] = mm(hot_own[...], local_rows[1]).astype(BF16)


def select_again_kernel(meta, hot_own, hot_other, rows, own, first, second):
    core = meta[1]
    half = first.shape[0]
    first[...] = mm(hot_other[:half, :], rows[1 - core]).astype(BF16)
    second[...] = mm(hot_other[half:, :], rows[1 - core]).astype(BF16)
    own[...] = mm(hot_own[...], rows[core]).astype(BF16)


def place_kernel(meta, hot_own, hot_other, rows, own, other, out):
    core = meta[1]
    for seq, hot, update in ((core, hot_own, own), (1 - core, hot_other, other)):
        out[seq] = (rows[seq].astype(F32) + mm_tn(hot[...], update[...])).astype(BF16)


def attend_kernel(
    meta, lengths, here, there, w_router, gain_attn, gain_mlp, w_query, w_key, w_value, w_out,
    up_own, up_other, chosen_out, normed_out, query_out, key_out, value_out, probs_out, mixed_out, attended_out,
    normed_mlp_out, rate_out, act_own, act_other, slope_own, slope_other, early_rows, late_rows, up_local, sem,
):
    copy = pltpu.make_async_copy(up_own, up_local, sem)
    copy.start()
    count = lengths[meta[1]] // 8
    slots, width = here.shape
    chosen = here[...].astype(F32) + there[...].astype(F32)
    chosen_out[...] = chosen.astype(BF16)
    score = jnp.sum(chosen * w_router[...].astype(F32), axis=-1, keepdims=True)
    rate = jax.nn.sigmoid(score)
    valid = lax.broadcasted_iota(jnp.int32, (slots, 1), 0) < count
    rate_out[...] = jnp.broadcast_to(jnp.where(valid, rate, 0.0), rate_out.shape)
    scale = lax.rsqrt(jnp.mean(chosen * chosen, axis=-1, keepdims=True) + EPS)
    normed = (chosen * scale * gain_attn[...]).astype(BF16)
    normed_out[...] = normed
    query_out[...] = mm(normed, w_query[...]).astype(BF16)
    key_out[...] = mm(normed, w_key[...]).astype(BF16)
    value_out[...] = mm(normed, w_value[...]).astype(BF16)
    head = width // NH
    pair = 2 * head
    i = lax.broadcasted_iota(jnp.int32, (slots, slots), 0)
    j = lax.broadcasted_iota(jnp.int32, (slots, slots), 1)
    allowed = (j <= i) & (j < count)
    first = lax.broadcasted_iota(jnp.int32, (slots, pair), 1) < head
    for p in range(NH // 2):
        cols = slice(p * pair, (p + 1) * pair)
        query = query_out[:, cols]
        keys = key_out[:, cols]
        values = value_out[:, cols]
        halves = []
        for h in range(2):
            mine = first if h == 0 else ~first
            logits = mm_nt(jnp.where(mine, query, jnp.zeros_like(query)), keys) * (head ** -0.5)
            logits = jnp.where(allowed, logits, -1e30)
            expd = jnp.exp(logits - jnp.max(logits, axis=-1, keepdims=True))
            probs = expd / jnp.sum(expd, axis=-1, keepdims=True)
            probs_out[2 * p + h] = probs
            halves.append(mm(probs.astype(BF16), values))
        mixed_out[:, cols] = jnp.where(first, halves[0], halves[1]).astype(BF16)
    attended = mm(mixed_out[...], w_out[...])
    attended_out[...] = attended
    hidden = chosen + attended
    scale = lax.rsqrt(jnp.mean(hidden * hidden, axis=-1, keepdims=True) + EPS)
    normed_mlp = (hidden * scale * gain_mlp[...]).astype(BF16)
    normed_mlp_out[...] = normed_mlp
    for w_up, act, slope in ((up_other, act_other, slope_other), (up_local, act_own, slope_own)):
        if w_up is up_local:
            copy.wait()
        up = mm(normed_mlp, w_up[...])
        square = up * up
        root = 0.7978845608028654
        t = jnp.tanh(root * (up + 0.044715 * (square * up)))
        act[...] = (0.5 * up * (1.0 + t)).astype(BF16)
        slope[...] = 0.5 * (1.0 + t) + (0.5 * root) * up * (1.0 - t * t) * (1.0 + 0.134145 * square)
    early_rows[:slots, :] = normed_out[...]
    early_rows[slots:, :] = mixed_out[...]
    late_rows[:slots, :] = normed_mlp
    late_rows[slots:, :] = act_other[...]


def mlp_kernel(
    rate, here, there, slope_own, slope_other, up_own, up_other, down_own, down_other,
    back_own, rows, grad_normed,
):
    seen = here[...].astype(F32) + there[...].astype(F32)
    moved = (rate[:, :1] * seen).astype(BF16)
    slots = moved.shape[0]
    rows[:slots, :] = moved
    total = None
    for w_up, w_down, slope, own in (
        (up_own, down_own, slope_own, True),
        (up_other, down_other, slope_other, False),
    ):
        grad_up = (mm_nt(moved, w_down[...]) * slope[...]).astype(BF16)
        if own:
            back_own[...] = grad_up
        else:
            rows[slots:, :] = grad_up
        part = mm_nt(grad_up, w_up[...])
        total = part if total is None else total + part
    grad_normed[...] = total.astype(BF16)


def moved_kernel(act_own, act_other, down_own, down_other, moved):
    moved[...] = (mm(act_own[...], down_own[...]) + mm(act_other[...], down_other[...])).astype(BF16)


def mlp_grads_kernel(whole, meta, act, back, late_rows, rows, late_got, got, *outs):
    slots, width = act.shape
    moved, moved_got = rows[:slots, :], got[:slots, :]
    back_got = got[slots:, :]
    if whole:
        outs[0][...] = mm_tn(act[...], moved) + mm_tn(late_got[slots:, :], moved_got)
        outs[1][...] = mm_tn(late_rows[:slots, :], back[...]) + mm_tn(late_got[:slots, :], back_got)
        return
    half = width // 2
    d_send, u_send, d_keep, u_keep = outs
    for bit, send in ((1, True), (0, False)):
        cols = pl.ds(pl.multiple_of((meta[Y] ^ bit) * half, 128), half)
        d = mm_tn(act[:, cols], moved) + mm_tn(late_got[slots:, cols], moved_got)
        cols = pl.ds(pl.multiple_of((meta[Z0] ^ bit) * half, 128), half)
        u = mm_tn(late_rows[:slots, cols], back[...]) + mm_tn(late_got[:slots, cols], back_got)
        if send:
            d_send[...] = d.astype(BF16)
            u_send[...] = u.astype(BF16)
        else:
            d_keep[...] = d
            u_keep[...] = u


def norm_back(values, gain, grad):
    scale = lax.rsqrt(jnp.mean(values * values, axis=-1, keepdims=True) + EPS)
    scaled = grad * gain
    inner = jnp.mean(scaled * values, axis=-1, keepdims=True)
    back = scale * scaled - values * (scale * scale * scale * inner)
    return back, jnp.sum(grad * values * scale, axis=0, keepdims=True)


def attend_back_kernel(
    chosen_in, attended, gain_attn, gain_mlp, gn_here, gn_there, rate, seen_here, seen_there,
    query_in, key_in, value_in, probs_in, w_query, w_key, w_value, w_out, meta,
    kept_rows, sent_rows, grad_sum, small, mixed_back, grad_query, grad_key, grad_value,
):
    small[...] = jnp.zeros_like(small)
    slots, width = chosen_in.shape
    head = width // NH
    pair = 2 * head
    chosen = chosen_in[...].astype(F32)
    grad_normed_mlp = gn_here[...].astype(F32) + gn_there[...].astype(F32)
    grad_hidden, gain_grad = norm_back(chosen + attended[...], gain_mlp[...], grad_normed_mlp)
    small[2:3, :] = gain_grad
    seen = seen_here[...].astype(F32) + seen_there[...].astype(F32)
    grad_attended = (rate[:, :1] * seen + grad_hidden).astype(BF16)
    mixed_back[...] = mm_nt(grad_attended, w_out[...]).astype(BF16)
    first = lax.broadcasted_iota(jnp.int32, (slots, pair), 1) < head
    factor = head ** -0.5
    for p in range(NH // 2):
        cols = slice(p * pair, (p + 1) * pair)
        query = query_in[:, cols]
        keys = key_in[:, cols]
        values = value_in[:, cols]
        back = mixed_back[:, cols]
        parts = []
        for h in range(2):
            mine = first if h == 0 else ~first
            probs = probs_in[2 * p + h]
            grad_probs = mm_nt(jnp.where(mine, back, jnp.zeros_like(back)), values)
            gv = mm_tn(probs.astype(BF16), back)
            inner = jnp.sum(grad_probs * probs, axis=-1, keepdims=True)
            grad_logits = (probs * (grad_probs - inner)).astype(BF16)
            gq = mm(grad_logits, keys) * factor
            gk = mm_tn(grad_logits, query) * factor
            parts.append((gq, gk, gv))
        for out, a, b in zip((grad_query, grad_key, grad_value), parts[0], parts[1]):
            out[:, cols] = jnp.where(first, a, b).astype(BF16)
    grad_normed = (
        mm_nt(grad_query[...], w_query[...])
        + mm_nt(grad_key[...], w_key[...])
        + mm_nt(grad_value[...], w_value[...])
    )
    back, gain_grad = norm_back(chosen, gain_attn[...], grad_normed)
    small[1:2, :] = gain_grad
    grad_sum[...] = back + grad_hidden
    for core, (low, high) in enumerate(((kept_rows, sent_rows), (sent_rows, kept_rows))):

        @pl.when(meta[1] == core)
        def _():
            low[:slots, :] = grad_query[...]
            low[slots:, :] = grad_key[...]
            high[:slots, :] = grad_value[...]
            high[slots:, :] = grad_attended


def attend_grads_kernel(whole, meta, *refs):
    if not whole:
        vectors, refs = refs[0], refs[1:]
    early_rows, early_got, mine, got, *outs, full = refs
    slots = mine.shape[0] // 2
    half = mine.shape[1] // 2
    cols = pl.ds(pl.multiple_of(meta[3] * half, 128), half)
    lower, upper = pl.ds(0, slots), pl.ds(slots, slots)
    second = pl.ds(pl.multiple_of(meta[1] * slots, slots), slots)
    full[:half, :] = mm_tn(early_rows[lower, cols], mine[lower, :]) + mm_tn(early_got[lower, cols], got[lower, :])
    full[half:, :] = mm_tn(early_rows[second, cols], mine[upper, :]) + mm_tn(early_got[second, cols], got[upper, :])
    if whole:
        outs[0][...] = full[...]
        return
    part = half // 2
    send_a, send_b, keep_a, keep_b, out = outs
    for at, bit, send, keep in ((0, Y, send_a, keep_a), (half, Z0, send_b, keep_b)):
        yours = pl.multiple_of(at + (1 - meta[bit]) * part, part)
        send[:part, :] = full[pl.ds(yours, part), :].astype(BF16)
        keep[...] = full[pl.ds(pl.multiple_of(at + meta[bit] * part, part), part), :]
    out[...] = vectors[...]
    send_a[part:, :] = split_vectors(vectors[...]).astype(BF16)


def slots_kernel(
    chosen_in, attended, rate_in, seen_here, seen_there, moved_here, moved_there, w_router, grad_sum,
    small, update, grad_chosen, vectors,
):
    chosen = chosen_in[...].astype(F32)
    rate = rate_in[:, :1]
    seen = seen_here[...].astype(F32) + seen_there[...].astype(F32)
    delta = attended[...] + (moved_here[...].astype(F32) + moved_there[...].astype(F32))
    update[...] = (rate * delta).astype(BF16)
    score = rate * (1.0 - rate) * jnp.sum(seen * delta, axis=-1, keepdims=True)
    grad_chosen[...] = (grad_sum[...] + score * w_router[...].astype(F32)).astype(BF16)
    vectors[...] = jnp.zeros_like(vectors)
    vectors[0:1, :] = jnp.sum(score * chosen, axis=0, keepdims=True)
    vectors[1:3, :] = small[1:3, :]


def reduce_kernel(plan, gots, sends, meta, *refs):
    keeps, refs = refs[: len(plan)], refs[len(plan) :]
    got, refs = refs[:gots], refs[gots:]
    send, kept = refs[:sends], refs[sends:]
    for keep, new, (rows, bit, g, g_row, t, t_row) in zip(keeps, kept, plan):
        half = rows // 2
        mine = pl.multiple_of(meta[bit] * half, half)
        yours = pl.multiple_of((1 - meta[bit]) * half, half)
        send[t][t_row : t_row + half, :] = (
            keep[pl.ds(yours, half), :] + got[g][pl.ds(g_row + yours, half), :].astype(F32)
        ).astype(BF16)
        new[...] = keep[pl.ds(mine, half), :] + got[g][pl.ds(g_row + mine, half), :].astype(F32)


def split_vectors(v):
    high = v.astype(BF16).astype(F32)
    return jnp.concatenate([high, (v - high).astype(BF16).astype(F32)], axis=0)


def join_vectors(v):
    return v[:8, :] + v[8:, :]


def reduce_small_kernel(plan, gots, sends, meta, *refs):
    vectors, refs = refs[0], refs[1:]
    out = refs[-1]
    reduce_kernel(plan, gots, sends, meta, *refs[:-1])
    got = refs[len(plan)]
    own = join_vectors(split_vectors(vectors[...])) + join_vectors(got[got.shape[0] - 16 :, :].astype(F32))
    out[...] = own
    send = refs[len(plan) + gots]
    send[send.shape[0] - 16 :, :] = split_vectors(own).astype(BF16)


def round_kernel(keep, got, cur):
    cur[...] = (keep[...] + got[...].astype(F32)).astype(BF16)


def round_both_kernel(vectors, first, second, got_first, got_second, cur, out):
    rows = first.shape[0]
    cur[:rows, :] = (first[...] + got_first[:rows, :].astype(F32)).astype(BF16)
    cur[rows : 2 * rows, :] = (second[...] + got_second[...].astype(F32)).astype(BF16)
    own = join_vectors(split_vectors(vectors[...])) + join_vectors(got_first[rows:, :].astype(F32))
    cur[2 * rows :, :] = split_vectors(own).astype(BF16)
    out[...] = own


def last_kernel(cur, got, out):
    out[...] = (cur[...].astype(F32) + got[...].astype(F32)).astype(BF16)


def last_both_kernel(vectors, cur, got, first, second, both, *outs):
    rows = first.shape[0]
    for at, out in ((0, first), (rows, second)):
        out[...] = (cur[at : at + rows, :].astype(F32) + got[at : at + rows, :].astype(F32)).astype(BF16)
        both[at : at + rows, :] = out[...]
    own = join_vectors(split_vectors(vectors[...])) + join_vectors(got[2 * rows :, :].astype(F32))
    for n, out in enumerate(outs):
        out[...] = own[n, :]


def join_kernel(plan, meta, *refs):
    count = len(plan)
    for (rows, bit, row, got_row), own, got, out in zip(
        plan, refs[:count], refs[count : 2 * count], refs[2 * count :]
    ):
        mine = pl.multiple_of(meta[bit] * rows, rows)
        yours = pl.multiple_of((1 - meta[bit]) * rows, rows)
        out[pl.ds(mine, rows), :] = own[row : row + rows, :].astype(out.dtype)
        out[pl.ds(yours, rows), :] = got[got_row : got_row + rows, :].astype(out.dtype)


def join_both_kernel(meta, own_a, own_b, got_a, got_b, out_a, out_b, both, far):
    rows = own_a.shape[0]
    for n, bit, own, got, out in ((0, Z0, own_a, got_a, out_a), (1, Y, own_b, got_b, out_b)):
        mine = pl.multiple_of(meta[bit] * rows, rows)
        yours = pl.multiple_of((1 - meta[bit]) * rows, rows)
        out[pl.ds(mine, rows), :] = own[...]
        out[pl.ds(yours, rows), :] = got[...]
        both[2 * n * rows : 2 * (n + 1) * rows, :] = out[...]
        far[n * rows : (n + 1) * rows, :] = got[...]


def stack_kernel(got_a, got_b, late):
    rows = got_a.shape[0]
    late[:rows, :] = got_a[...]
    late[rows:, :] = got_b[...]


def attention_kernel(far, meta, *refs):
    outs, (block, sems) = refs[-6:-2], refs[-2:]
    count = 3 if far else 2
    core, side = meta[1], meta[3] ^ far
    part = block.shape[1] // 2
    at = pl.multiple_of(side * 2 * part, 8)
    for other in range(2):
        pieces = refs[other * count : (other + 1) * count]
        for packet, bit, inner in ((0, meta[Y], meta[Z0]), (1, meta[Z0], meta[Y])):
            m = 2 * (core ^ other) + packet
            rows = slice(packet * part, (packet + 1) * part)
            if far:
                size = part // 2
                for n in range(2):
                    start = pl.multiple_of(bit * part + (inner ^ n) * size, 8)
                    block[m, pl.ds(start, size), :] = pieces[n][packet * size : (packet + 1) * size, :].astype(F32)
            else:
                block[m, pl.ds(pl.multiple_of(bit * part, 8), part), :] = pieces[0][rows, :].astype(F32)
            block[m, pl.ds(pl.multiple_of((1 - bit) * part, 8), part), :] = pieces[-1][rows, :].astype(F32)
            for n, out in enumerate(outs):

                @pl.when(m == n)
                def _():
                    pltpu.make_async_copy(block.at[n], out.at[pl.ds(at, 2 * part), :], sems.at[n]).start()

    for n, out in enumerate(outs):
        pltpu.make_async_copy(block.at[n], out.at[pl.ds(at, 2 * part), :], sems.at[n]).wait()


def attention_near_kernel(*refs):
    attention_kernel(0, *refs)


def attention_far_kernel(*refs):
    attention_kernel(1, *refs)


def swap(v, axis, size, bits):
    return lax.ppermute(v, axis, [(i, i ^ bits) for i in range(size)])


def body(
    batch, tokens, lengths, picks, w_router, gain_attn, gain_mlp, w_query, w_key, w_value, w_out,
    w_up, w_down, cotangent,
):
    place, index = lax.axis_index("seq"), lax.axis_index("batch")
    core, side = place % 2, place // 2
    seqs, length, width = tokens.shape
    local = picks.shape[1]
    slots = 4 * local
    n, half = width, width // 2
    hidden_units = w_up.shape[1]
    across = functools.partial(swap, axis="seq", size=4)
    along = lambda v, bit: swap(v, "batch", batch, 1 << bit)
    row = lambda v: v.reshape(1, width)
    gain_attn, gain_mlp, w_router = row(gain_attn), row(gain_mlp), row(w_router)
    meta = jnp.stack(
        [place, core, index, side] + [place ^ k for k in range(4)] + [(index >> k) & 1 for k in range(3)]
    ).astype(jnp.int32)
    rows = lambda count: ((count, width), BF16)
    wide = lambda count: ((count, width), F32)
    hot = ((slots, length), BF16)
    act = ((slots, hidden_units), BF16)
    slope = ((slots, hidden_units), F32)

    got = [across(picks, bits=k) for k in (1, 2, 3)]
    own, other, hot_own, hot_other = call(
        "SE", select_kernel, [meta, *got, picks, tokens], [rows(slots)] * 2 + [hot] * 2,
        specs=[SMEM] + [VMEM] * 3 + [HBM] * 2,
        scratch=[
            pltpu.VMEM((2, length, width), BF16), pltpu.VMEM(picks.shape, jnp.int32),
            pltpu.SemaphoreType.DMA((3,)),
        ],
        vmem=52,
    )
    up_other, down_other = across(w_up, bits=1), across(w_down, bits=1)
    here = own + across(other, bits=1)
    there = across(here, bits=2)
    own, *other = call(
        "SA", select_again_kernel, [meta, hot_own, hot_other, cotangent], [rows(slots)] + [rows(slots // 2)] * 2,
        specs=[SMEM] + [VMEM] * 3,
    )
    seen_here = own + jnp.concatenate([across(v, bits=1) for v in other], axis=0)
    seen_there = across(seen_here, bits=2)

    (
        chosen, normed, query, keys, values, probs, mixed, attended, normed_mlp, rate,
        act_own, act_other, slope_own, slope_other, early_rows, late_rows,
    ) = call(
        "AT", attend_kernel,
        [meta, lengths, here, there, w_router, gain_attn, gain_mlp, w_query, w_key, w_value, w_out, w_up, up_other],
        [rows(slots)] * 5 + [((NH, slots, slots), F32), rows(slots), wide(slots), rows(slots), ((slots, 128), F32)]
        + [act] * 2 + [slope] * 2 + [rows(2 * slots)] * 2,
        specs=[SMEM] * 2 + [VMEM] * 9 + [HBM, VMEM], after=[seen_here],
        scratch=[pltpu.VMEM(w_up.shape, BF16), pltpu.SemaphoreType.DMA],
    )
    early_got, late_got = across(early_rows, bits=1), across(late_rows, bits=1)
    back_own, moved_rows, gn_here = call(
        "ML", mlp_kernel,
        [rate, seen_here, seen_there, slope_own, slope_other, w_up, up_other, w_down, down_other],
        [act, rows(2 * slots), rows(slots)],
    )
    gn_there = across(gn_here, bits=2)
    moved_got = across(moved_rows, bits=1)
    moved_here = call("MV", moved_kernel, [act_own, act_other, w_down, down_other], [rows(slots)], after=[gn_here])[0]
    moved_there = across(moved_here, bits=2)

    def mlp_grads(outs, after):
        return call(
            "F", functools.partial(mlp_grads_kernel, len(outs) == 2),
            [meta, act_own, back_own, late_rows, moved_rows, late_got, moved_got], outs,
            specs=[SMEM] + [VMEM] * 6, after=after,
        )

    def attend_back(after):
        return call(
            "AB", attend_back_kernel,
            [
                chosen, attended, gain_attn, gain_mlp, gn_here, gn_there, rate, seen_here, seen_there,
                query, keys, values, probs, w_query, w_key, w_value, w_out, meta,
            ],
            [rows(2 * slots)] * 2 + [wide(slots), wide(8)], specs=[VMEM] * 17 + [SMEM],
            scratch=[pltpu.VMEM((slots, width), BF16)] * 4, after=after,
        )

    def attend_grads(mine, got, vectors, outs, after):
        more = [] if vectors is None else [vectors]
        return call(
            "FA", functools.partial(attend_grads_kernel, vectors is None),
            [meta, *more, early_rows, early_got, mine, got], outs,
            specs=[SMEM] + [VMEM] * (4 + len(more)), scratch=[pltpu.VMEM((width, width), F32)], after=after,
        )

    def slot_sums(grad_sum, small, after):
        update, grad_chosen, vectors = call(
            "SL", slots_kernel,
            [chosen, attended, rate, seen_here, seen_there, moved_here, moved_there, w_router, grad_sum, small],
            [rows(slots), rows(slots), wide(8)], after=after,
        )
        return update, grad_chosen, vectors + across(vectors, bits=1)

    def placed(tag, values, mine, core, after=()):
        return call(
            tag, place_kernel, [meta, hot_own, hot_other, values, mine, core],
            [(values.shape, BF16)], specs=[SMEM] + [VMEM] * 5, after=after, token=True,
        )

    if batch != 8:
        whole = ((width, width), F32)
        down, up = mlp_grads([whole] * 2, [])
        mine, theirs, grad_sum, small = attend_back([])
        update, grad_chosen, vectors = slot_sums(grad_sum, small, [])
        attention = attend_grads(mine, across(theirs, bits=1), None, [whole], [])[0]
        down, up, attention, vectors = lax.psum((down, up, attention, vectors), "batch")
        attention = lax.all_gather(attention, "seq").reshape(2, 2, 2, half, width)
        return (
            placed("P1", tokens, update, across(update, bits=1))[0],
            placed("P2", cotangent, grad_chosen, across(grad_chosen, bits=1))[0],
            vectors[0], vectors[1], vectors[2],
            *(attention[:, m // 2, m % 2].reshape(width, width) for m in range(4)), up, down,
        )

    def reduce(tag, keeps, gots, plan, sends, after=(), vectors=None):
        kernel = functools.partial(reduce_kernel, plan, len(gots), len(sends))
        outs = [rows(count) for count in sends] + [wide(p[0] // 2) for p in plan]
        ins = [meta, *keeps, *gots]
        if vectors is not None:
            kernel = functools.partial(reduce_small_kernel, plan, len(gots), len(sends))
            ins = [meta, vectors, *keeps, *gots]
            outs.append(wide(8))
        return call(tag, kernel, ins, outs, specs=[SMEM] + [VMEM] * (len(ins) - 1), after=after)

    def join(tag, bit, own, got, dtype=BF16, after=(), token=False):
        count = own.shape[0]
        return call(
            tag, functools.partial(join_kernel, [(count, bit, 0, 0)]), [meta, own, got],
            [((2 * count, width), dtype)], specs=[SMEM] + [VMEM] * 2, after=after, token=token,
        )

    def attention(tag, kernel, pieces, outs=(), after=()):
        return call(
            tag, kernel, [meta, *pieces, *outs], [wide(width)] * 4,
            specs=[SMEM] + [VMEM] * len(pieces) + [HBM] * len(outs), out_specs=[HBM] * 4,
            scratch=[pltpu.VMEM((4, half, width), F32), pltpu.SemaphoreType.DMA((4,))],
            aliases={1 + len(pieces) + m: m for m in range(len(outs))}, after=after, token=True,
        )

    v, moved = {}, {}

    def kept(name, value):
        moved[name] = value
        return value

    moved["M"] = moved_there

    def step_f(after):
        d, u, v["d_keep"], v["u_keep"] = mlp_grads([rows(half)] * 2 + [wide(half)] * 2, after)
        v["d"], v["u"] = kept("d1", along(d, 0)), kept("u1", along(u, 1))
        return v["d_keep"]

    def step_ab(after):
        v["mine"], theirs, v["sum"], v["small"] = attend_back(after)
        v["got"] = kept("th", across(theirs, bits=1))
        return v["small"]

    def step_sl(after):
        v["update"], v["grad_chosen"], v["vectors"] = slot_sums(v["sum"], v["small"], after)
        v["update_core"] = kept("up", across(v["update"], bits=1))
        v["chosen_core"] = kept("gc", across(v["grad_chosen"], bits=1))
        return v["update"]

    def step_fa(after):
        a, b, v["a_keep"], v["b_keep"], v["vectors"] = attend_grads(
            v["mine"], v["got"], v["vectors"],
            [rows(half // 2 + 16), rows(half // 2), wide(half // 2), wide(half // 2), wide(8)], after,
        )
        v["a"], v["b"] = kept("a1", along(a, 0)), kept("b1", along(b, 1))
        return v["a_keep"]

    def step_r2(after):
        send, v["d_keep"] = reduce("R2", [v["d_keep"]], [v["d"]], [(n // 2, Z0, 0, 0, 0, 0)], [n // 4], after)
        v["d"] = kept("d2", along(send, 1))
        return v["d_keep"]

    def step_r2u(after):
        send, v["u_keep"] = reduce("R2U", [v["u_keep"]], [v["u"]], [(n // 2, Y, 0, 0, 0, 0)], [n // 4], after)
        v["u"] = kept("u2", along(send, 0))
        return v["u_keep"]

    def step_a2(after):
        a, b, v["a_keep"], v["b_keep"], v["vectors"] = reduce(
            "A2", [v["a_keep"], v["b_keep"]], [v["a"], v["b"]],
            [(half // 2, Z0, 0, 0, 0, 0), (half // 2, Y, 1, 0, 1, 0)],
            [half // 4 + 16, half // 4], after, v["vectors"],
        )
        v["a"], v["b"] = kept("a2", along(a, 1)), kept("b2", along(b, 0))
        return v["a_keep"]

    def third(tag, key):
        def step(after):
            v[key + "_cur"] = call(tag, round_kernel, [v[key + "_keep"], v[key]], [rows(n // 4)], after=after)[0]
            v[key] = kept(key + "3", along(v[key + "_cur"], 2))
            return v[key + "_cur"]

        return step

    def step_a3(after):
        v["ab_cur"], v["vectors"] = call(
            "A3", round_both_kernel, [v["vectors"], v["a_keep"], v["b_keep"], v["a"], v["b"]],
            [rows(half // 2 + 16), wide(8)], after=after,
        )
        v["ab"] = kept("ab3", along(v["ab_cur"], 2))
        return v["vectors"]

    def fourth(tag, key, bit):
        def step(after):
            v[key + "_all"] = call(tag, last_kernel, [v[key + "_cur"], v[key]], [rows(n // 4)], after=after)[0]
            v[key] = kept(key + "5", along(v[key + "_all"], bit))
            return v[key + "_all"]

        return step

    def step_a4(after):
        v["a_all"], v["b_all"], near, *v["vectors"] = call(
            "A4", last_both_kernel, [v["vectors"], v["ab_cur"], v["ab"]],
            [rows(half // 4)] * 2 + [rows(half // 2)] + [((width,), F32)] * 3, after=after,
        )
        v["a"], v["b"] = kept("a5", along(v["a_all"], 1)), kept("b5", along(v["b_all"], 0))
        v["near"] = kept("x1", across(near, bits=2))
        return v["a_all"]

    def step_a5(after):
        a, b, v["early"], far = call(
            "A5", join_both_kernel, [meta, v["a_all"], v["b_all"], v["a"], v["b"]],
            [rows(half // 2)] * 2 + [rows(half), rows(half // 2)], specs=[SMEM] + [VMEM] * 4, after=after,
        )
        v["a"], v["b"] = kept("a6", along(a, 0)), kept("b6", along(b, 1))
        v["far"] = kept("x2", across(far, bits=2))
        v["early_core"] = kept("ce", across(v["early"], bits=1))
        return v["early"]

    def step_a6(after):
        v["late"] = call("A6", stack_kernel, [v["a"], v["b"]], [rows(half)], after=after)[0]
        v["side"] = kept("xl", across(v["late"], bits=2))
        v["late_core"] = kept("cl", across(v["late"], bits=1))
        return v["late"]

    def fifth(tag, key, bit, along_bit):
        def step(after):
            v[key + "_all"] = join(tag, bit, v[key + "_all"], v[key], after=after)[0]
            v[key] = kept(key + "6", along(v[key + "_all"], along_bit))
            return v[key + "_all"]

        return step

    def sixth(tag, key, bit):
        def step(after):
            v["grad_" + key], token = join(tag, bit, v[key + "_all"], v[key], F32, after, token=True)
            return token

        return step

    def place(tag, name, values, mine, core):
        def step(after):
            v[name], token = placed(tag, values, v[mine], v[core], after)
            return token

        return step

    def step_at0(after):
        *v["grads"], token = attention(
            "AT0", attention_near_kernel, [v["early"], v["late"], v["early_core"], v["late_core"]], after=after
        )
        return token

    def step_xc(after):
        side, *_ = lax.optimization_barrier((v["side"], *after))
        v["pieces"] = [v["near"], v["far"], side]
        v["pieces"] += [across(piece, bits=1) for piece in v["pieces"]]
        return after[0]

    def step_at1(after):
        *v["grads"], token = attention("AT1", attention_far_kernel, v["pieces"], v["grads"], after)
        return token

    steps = dict(
        F=step_f, AB=step_ab, SL=step_sl, FA=step_fa, R2=step_r2, R2U=step_r2u, A2=step_a2, A3=step_a3,
        D3=third("D3", "d"), U3=third("U3", "u"), D4=fourth("D4", "d", 1), U4=fourth("U4", "u", 0), A4=step_a4,
        A5=step_a5, A6=step_a6, D5=fifth("D5", "d", Z0, 0), U5=fifth("U5", "u", Y, 1), DU=sixth("DU", "d", Y),
        UU=sixth("UU", "u", Z0), P1=place("P1", "output", tokens, "update", "update_core"),
        P2=place("P2", "grad_tokens", cotangent, "grad_chosen", "chosen_core"), AT0=step_at0, XC=step_xc, AT1=step_at1,
    )
    after = [moved_here]
    for name in ORDER:
        after = [steps[name](after + [moved[key] for key in HOLD.get(name, ())])]
    return (
        v["output"], v["grad_tokens"], *v["vectors"], *v["grads"], v["grad_u"], v["grad_d"],
    )


def solution(mesh):
    rows, whole = P("batch", "seq", None), P()
    return jax.shard_map(
        functools.partial(body, mesh.shape["batch"]),
        mesh=mesh,
        in_specs=(
            rows, P("batch"), P("batch", "seq"), whole, whole, whole, whole, whole, whole, whole,
            P(None, "seq"), P("seq", None), rows,
        ),
        out_specs=(
            rows, rows, whole, whole, whole, whole, whole, whole, whole,
            P(None, "seq"), P("seq", None),
        ),
        check_vma=False,
    )
```

time: 300 us -> 157 us (0.52)
  waiting for transfers between devices: 145 us -> 72.2 us
  starting transfers between devices: 61.8 us -> 38.1 us
  other arithmetic: 20.7 us -> 0.21 us
  local copies, waits for them, and re-layouts: 17.4 us -> 0.84 us
  Pallas kernels: 49.5 us -> 43.9 us
    ppermute x46, waiting for transfers between devices: 145 us -> 72.2 us  [swap(): return lax.ppermute(v, axis, [(i, i ^ bits) for i in range(size)])]
    ppermute x46, starting transfers between devices: 61.8 us -> 38.1 us  [swap(): return lax.ppermute(v, axis, [(i, i ^ bits) for i in range(size)])]
    unnamed x102 -> x26, local copies, waits for them, and re-layouts: 14.5 us -> 0.74 us
    another operation x11 -> x0, other arithmetic: 13.6 us -> none  [the longest x2 7.48 us: body(): attention_all = jnp.stack([attention_all, across(attention_all, bits=1)])]
    pallas_call x13 -> x28, Pallas kernels: 49.5 us -> 43.9 us  [call(): pl.pallas_call(run, out_shape=tuple(shapes), in_specs=(specs or [VMEM] *...]
    convert_element_type x6 -> x0, other arithmetic: 4 us -> none  [the longest x3 2.62 us: scatter_sum(): piece = sum((pick(v, digit ^ k).astype(F32) for v in current)).astype(BF16)]
  transfers between devices with their start and end apart: 46 -> 46, of which waited for: 23 -> 22; matrix products, arithmetic and copies ran while one was open for 4% -> 0% of each run, Pallas kernels for 9% -> 25%
where the time goes in v3:
time: 157 us; the launch traced here: 156 us
  waiting for transfers between devices  72.2 us (46%)
  Pallas kernels  43.9 us (28%)
  starting transfers between devices  38.1 us (24%)
    ppermute x46, waiting for transfers between devices, swap(): return lax.ppermute(v, axis, [(i, i ^ bits) for i in range(size)])  72.2 us
    pallas_call x28, Pallas kernels, call(): pl.pallas_call(run, out_shape=tuple(shapes), in_specs=(specs or [VMEM] *...  43.9 us
    ppermute x46, starting transfers between devices, swap(): return lax.ppermute(v, axis, [(i, i ^ bits) for i in range(size)])  38.1 us
  transfers between devices with their start and end apart: 46, of which 22 were waited for; matrix products, arithmetic and copies ran while one was open for 0% of the time, Pallas kernels for 25%

profile of v3, /device:TPU:0, one launch (start us, length us, event | category | flops | bytes accessed | tf_op | source)
XLA Modules:
  0.0 156.4 jit_solution(18256282492542597550)
XLA Ops:
  0.6 3.0 %collective-permute-start.1 = (s32[2,64]{1,0:T(2,128)}, s32[2,64]{1,0:T(2,128)S(1)}, u32[]{:S(2)}, u32[]{:S(2)}) collective-permute-start(s32[2,64]{1,0:T(2,128)} %refs_4_.1), channel_id=1, source_target_pairs={{0,2},{1,3},{2,0},{3,1},{4,6},{5,7},{6,4},{7,5},{8,10},{9,11},{10,... | collective-permute-start | bytes 1544 | tf_op jit(solution)/shard_map/ppermute | solution.py:456
  4.5 1.0 collective-permute-done.1.refs_2_
  5.4 1.4 collective-permute-done.2.refs_3_
  6.9 0.7 copy-done.7
  7.5 2.6 %select_kernel.1 = (bf16[256,768]{1,0:T(8,128)(2,1)S(1)}, bf16[256,768]{1,0:T(8,128)(2,1)S(1)}, bf16[256,512]{1,0:T(8,128)(2,1)S(1)}, bf16[256,512]{1,0:T(8,128)(2,1)S(1)}) custom-call(s32[11]{0:T(128)S(1)} %stack.44.refs_0_.refs_17_, s32[2,64]{1,0:T(2,128)S(1)} %collective-permute-done.refs_1_, s32[2,64]{1,0:T(2,128)S(1)} %collective-permute-done.1.refs_2_, ...), custom_call_target="tpu_custom_call" | custom-call | flops 1 | bytes 1 | tf_op jit(solution)/shard_map/select_kernel/pallas_call | solution.py:57
  10.1 0.6 collective-permute-start.3
  10.7 1.1 select_again_kernel.1
  12.8 0.6 collective-permute-done.6
  13.8 1.1 collective-permute-start.8
  14.9 9.7 %collective-permute-done.4.refs_3_ = bf16[256,768]{1,0:T(8,128)(2,1)S(1)} collective-permute-done((bf16[256,768]{1,0:T(8,128)(2,1)S(1)}, bf16[256,768]{1,0:T(8,128)(2,1)S(1)}, u32[]{:S(2)}, u32[]{:S(2)}) %collective-permute-start.4) | collective-permute-done | bytes 393248 | tf_op jit(solution)/shard_map/ppermute | solution.py:456
  24.7 6.6 %attend_kernel.1 = (bf16[256,768]{1,0:T(8,128)(2,1)S(1)}, bf16[256,768]{1,0:T(8,128)(2,1)}, bf16[256,768]{1,0:T(8,128)(2,1)S(1)}, bf16[256,768]{1,0:T(8,128)(2,1...) custom-call(s32[11]{0:T(128)S(1)} %stack.44.refs_0_.refs_17_, ...), custom_call_target="tpu_custom_call" | custom-call | flops 1 | bytes 1 | tf_op jit(solution)/shard_map/attend_kernel/pallas_call | solution.py:57
  31.3 0.9 collective-permute-done.8.refs_2_.refs_8_.refs_4_
  32.2 1.8 %mlp_kernel.1 = (bf16[256,768]{1,0:T(8,128)(2,1)S(1)}, bf16[512,768]{1,0:T(8,128)(2,1)S(1)}, bf16[256,768]{1,0:T(8,128)(2,1)S(1)}) custom-call(f32[256,128]{1,0:T(8,128)S(1)} %get-tuple-element.98.refs_0_.refs_6_.refs_2_, bf16[256,768]{1,0:T(8,128)(2,1)S(1)} %maximum_add_fusion.refs_13_.refs_1_.refs_7_.refs_3_, ...), custom_call_target="tpu_custom_call" | custom-call | flops 100000000 | bytes 1 | tf_op jit(solution)/shard_map/mlp_kernel/pallas_call | solution.py:57
  34.6 0.5 collective-permute-start.11
  35.1 0.8 moved_kernel.1.refs_7_.refs_5_
  35.9 1.6 collective-permute-start.10
  37.5 2.0 %mlp_grads_kernel.1 = (bf16[384,768]{1,0:T(8,128)(2,1)S(1)}, bf16[384,768]{1,0:T(8,128)(2,1)S(1)}, f32[384,768]{1,0:T(8,128)S(1)}, f32[384,768]{1,0:T(8,128)S(1)}) custom-call(s32[11]{0:T(128)S(1)} %stack.44.refs_0_.refs_17_, bf16[256,768]{1,0:T(8,128)(2,1)S(1)} %get-tuple-element.99.refs_0_.refs_1_, bf16[256,768]{1,0:T(8,128)(2,1)S(1)} %get-tuple-element.108.refs_2_, ...), custom_call_target="tpu_custom_call" | custom-call | flops 1 | bytes 1 | tf_op jit(solution)/shard_map/mlp_grads_kernel/pallas_call | solution.py:57
  39.4 1.6 %collective-permute-start.15 = (bf16[384,768]{1,0:T(8,128)(2,1)S(1)}, bf16[384,768]{1,0:T(8,128)(2,1)S(1)}, u32[]{:S(2)}, u32[]{:S(2)}) collective-permute-start(bf16[384,768]{1,0:T(8,128)(2,1)S(1)} %get-tuple-element.115), channel_id=1, source_target_pairs={{0,4},{4,0},{8,12},{12,8},{16,20},{20,16},{24,28},{28,24},{1,5},{5... | collective-permute-start | bytes 1769480 | tf_op jit(solution)/shard_map/ppermute | solution.py:456
  41.0 1.6 %collective-permute-start.23 = (bf16[384,768]{1,0:T(8,128)(2,1)S(1)}, bf16[384,768]{1,0:T(8,128)(2,1)S(1)}, u32[]{:S(2)}, u32[]{:S(2)}) collective-permute-start(bf16[384,768]{1,0:T(8,128)(2,1)S(1)} %get-tuple-element.127), channel_id=1, source_target_pairs={{0,8},{4,12},{8,0},{12,4},{16,24},{20,28},{24,16},{28,20},{1,9},{5... | collective-permute-start | bytes 1769480 | tf_op jit(solution)/shard_map/ppermute | solution.py:456
  42.6 3.9 %collective-permute-done.11.refs_5_ = bf16[256,768]{1,0:T(8,128)(2,1)S(1)} collective-permute-done((bf16[256,768]{1,0:T(8,128)(2,1)S(1)}, bf16[256,768]{1,0:T(8,128)(2,1)S(1)}, u32[]{:S(2)}, u32[]{:S(2)}) %collective-permute-start.11) | collective-permute-done | bytes 393248 | tf_op jit(solution)/shard_map/ppermute | solution.py:456
  46.5 7.1 %attend_back_kernel.1 = (bf16[512,768]{1,0:T(8,128)(2,1)S(1)}, bf16[512,768]{1,0:T(8,128)(2,1)S(1)}, f32[256,768]{1,0:T(8,128)S(1)}, f32[8,768]{1,0:T(8,128)S(1)}) custom-call(bf16[256,768]{1,0:T(8,128)(2,1)S(1)} %get-tuple-element.96.refs_0_, f32[256,768]{1,0:T(8,128)S(1)} %get-tuple-element.97.refs_1_, f32[1,768]{1,0:T(1,128)S(1)} %reshape.32.refs_5_.refs_2_, ...), custom_call_target="tpu_custom_call" | custom-call | flops 100000000 | bytes 1 | tf_op jit(solution)/shard_map/attend_back_kernel/pallas_call | solution.py:57
  54.1 0.5 slots_kernel.1
  54.6 0.6 collective-permute-done.15.refs_2_
  55.2 0.6 reduce_kernel.2
  55.9 1.6 %collective-permute-start.16 = (bf16[192,768]{1,0:T(8,128)(2,1)S(1)}, bf16[192,768]{1,0:T(8,128)(2,1)S(1)}, u32[]{:S(2)}, u32[]{:S(2)}) collective-permute-start(bf16[192,768]{1,0:T(8,128)(2,1)S(1)} %get-tuple-element.117), channel_id=1, source_target_pairs={{0,8},{4,12},{8,0},{12,4},{16,24},{20,28},{24,16},{28,20},{1,9},{5... | collective-permute-start | bytes 884744 | tf_op jit(solution)/shard_map/ppermute | solution.py:456
  57.5 1.2 collective-permute-done.17
  58.7 1.5 attend_grads_kernel.1
  60.2 1.6 %collective-permute-start.21 = (bf16[208,768]{1,0:T(8,128)(2,1)S(1)}, bf16[208,768]{1,0:T(8,128)(2,1)S(1)}, u32[]{:S(2)}, u32[]{:S(2)}) collective-permute-start(bf16[208,768]{1,0:T(8,128)(2,1)S(1)} %get-tuple-element.125), channel_id=1, source_target_pairs={{0,4},{4,0},{8,12},{12,8},{16,20},{20,16},{24,28},{28,24},{1,5},{5... | collective-permute-start | bytes 958472 | tf_op jit(solution)/shard_map/ppermute | solution.py:456
  62.3 2.7 %collective-permute-done.16.refs_1_ = bf16[192,768]{1,0:T(8,128)(2,1)S(1)} collective-permute-done((bf16[192,768]{1,0:T(8,128)(2,1)S(1)}, bf16[192,768]{1,0:T(8,128)(2,1)S(1)}, u32[]{:S(2)}, u32[]{:S(2)}) %collective-permute-start.16) | collective-permute-done | bytes 294944 | tf_op jit(solution)/shard_map/ppermute | solution.py:456
  65.1 2.7 %collective-permute-start.20 = (bf16[192,768]{1,0:T(8,128)(2,1)S(1)}, bf16[192,768]{1,0:T(8,128)(2,1)S(1)}, u32[]{:S(2)}, u32[]{:S(2)}) collective-permute-start(bf16[192,768]{1,0:T(8,128)(2,1)S(1)} %round_kernel.2.refs_6_.refs_0_), channel_id=1, source_target_pairs={{0,16},{4,20},{8,24},{12,28},{16,0},{20,4},{24,8},{28,12},{1,17},{... | collective-permute-start | bytes 884744 | tf_op jit(solution)/shard_map/ppermute | solution.py:456
  67.7 7.0 %collective-permute-done.22.refs_5_ = bf16[192,768]{1,0:T(8,128)(2,1)S(1)} collective-permute-done((bf16[192,768]{1,0:T(8,128)(2,1)S(1)}, bf16[192,768]{1,0:T(8,128)(2,1)S(1)}, u32[]{:S(2)}, u32[]{:S(2)}) %collective-permute-start.22) | collective-permute-done | bytes 294944 | tf_op jit(solution)/shard_map/ppermute | solution.py:456
  74.8 0.7 reduce_small_kernel.1
  75.5 0.6 collective-permute-start.25
  76.2 4.6 %collective-permute-done.25.refs_4_ = bf16[96,768]{1,0:T(8,128)(2,1)S(1)} collective-permute-done((bf16[96,768]{1,0:T(8,128)(2,1)S(1)}, bf16[96,768]{1,0:T(8,128)(2,1)S(1)}, u32[]{:S(2)}, u32[]{:S(2)}) %collective-permute-start.25) | collective-permute-done | bytes 147488 | tf_op jit(solution)/shard_map/ppermute | solution.py:456
  80.7 2.8 %collective-permute-done.24.refs_3_ = bf16[112,768]{1,0:T(8,128)(2,1)S(1)} collective-permute-done((bf16[112,768]{1,0:T(8,128)(2,1)S(1)}, bf16[112,768]{1,0:T(8,128)(2,1)S(1)}, u32[]{:S(2)}, u32[]{:S(2)}) %collective-permute-start.24) | collective-permute-done | bytes 172064 | tf_op jit(solution)/shard_map/ppermute | solution.py:456
  83.6 2.8 %collective-permute-start.26 = (bf16[208,768]{1,0:T(8,128)(2,1)S(1)}, bf16[208,768]{1,0:T(8,128)(2,1)S(1)}, u32[]{:S(2)}, u32[]{:S(2)}) collective-permute-start(bf16[208,768]{1,0:T(8,128)(2,1)S(1)} %get-tuple-element.134.refs_1_), channel_id=1, source_target_pairs={{0,16},{4,20},{8,24},{12,28},{16,0},{20,4},{24,8},{28,12},{1,17},{... | collective-permute-start | bytes 958472 | tf_op jit(solution)/shard_map/ppermute | solution.py:456
  86.4 2.3 %place_kernel.2 = (bf16[2,512,768]{2,1,0:T(8,128)(2,1)}, f32[8,128]{1,0:T(8,128)S(1)}) custom-call(s32[11]{0:T(128)S(1)} %stack.44.refs_0_.refs_17_, bf16[256,512]{1,0:T(8,128)(2,1)S(1)} %get-tuple-element.89.refs_1_, bf16[256,512]{1,0:T(8,128)(2,1)S(1)} %get-tuple-element.90.refs_2_, bf16[2,512,768]{2,1,0:T(8,128)(2,1)S(1)} %copy-done.9, ...), custom_call_target="tpu_custom_call" | custom-call | flops 4000000000 | bytes 1 | tf_op jit(solution)/shard_map/place_kernel/pallas_call | solution.py:57
  88.7 0.7 reduce_kernel.3
  89.4 1.2 collective-permute-start.28
  90.6 5.6 %collective-permute-done.28.refs_1_ = bf16[192,768]{1,0:T(8,128)(2,1)S(1)} collective-permute-done((bf16[192,768]{1,0:T(8,128)(2,1)S(1)}, bf16[192,768]{1,0:T(8,128)(2,1)S(1)}, u32[]{:S(2)}, u32[]{:S(2)}) %collective-permute-start.28) | collective-permute-done | bytes 294944 | tf_op jit(solution)/shard_map/ppermute | solution.py:456
  96.3 0.8 collective-permute-start.35
  97.0 4.5 %collective-permute-done.26.refs_2_ = bf16[208,768]{1,0:T(8,128)(2,1)S(1)} collective-permute-done((bf16[208,768]{1,0:T(8,128)(2,1)S(1)}, bf16[208,768]{1,0:T(8,128)(2,1)S(1)}, u32[]{:S(2)}, u32[]{:S(2)}) %collective-permute-start.26) | collective-permute-done | bytes 319520 | tf_op jit(solution)/shard_map/ppermute | solution.py:456
  101.6 0.7 last_both_kernel.1
  102.3 1.9 %collective-permute-start.31 = (bf16[96,768]{1,0:T(8,128)(2,1)S(1)}, bf16[96,768]{1,0:T(8,128)(2,1)S(1)}, u32[]{:S(2)}, u32[]{:S(2)}) collective-permute-start(bf16[96,768]{1,0:T(8,128)(2,1)S(1)} %get-tuple-element.147.refs_2_), channel_id=1, source_target_pairs={{0,4},{4,0},{8,12},{12,8},{16,20},{20,16},{24,28},{28,24},{1,5},{5... | collective-permute-start | bytes 442376 | tf_op jit(solution)/shard_map/ppermute | solution.py:456
  104.2 3.4 %collective-permute-start.30 = (bf16[96,768]{1,0:T(8,128)(2,1)S(1)}, bf16[96,768]{1,0:T(8,128)(2,1)S(1)}, u32[]{:S(2)}, u32[]{:S(2)}) collective-permute-start(bf16[96,768]{1,0:T(8,128)(2,1)S(1)} %get-tuple-element.140.refs_2_.refs_1_), channel_id=1, source_target_pairs={{0,8},{4,12},{8,0},{12,4},{16,24},{20,28},{24,16},{28,20},{1,9},{5... | collective-permute-start | bytes 442376 | tf_op jit(solution)/shard_map/ppermute | solution.py:456
  107.7 2.3 %place_kernel.3 = (bf16[2,512,768]{2,1,0:T(8,128)(2,1)}, f32[8,128]{1,0:T(8,128)S(1)}) custom-call(s32[11]{0:T(128)S(1)} %stack.44.refs_0_.refs_17_, bf16[256,512]{1,0:T(8,128)(2,1)S(1)} %get-tuple-element.89.refs_1_, bf16[256,512]{1,0:T(8,128)(2,1)S(1)} %get-tuple-element.90.refs_2_, bf16[2,512,768]{2,1,0:T(8,128)(2,1)S(1)} %copy-done.6, ...), custom_call_target="tpu_custom_call" | custom-call | flops 2000000000 | bytes 1 | tf_op jit(solution)/shard_map/place_kernel/pallas_call | solution.py:57
  110.0 2.6 %collective-permute-done.30.refs_3_ = bf16[96,768]{1,0:T(8,128)(2,1)S(1)} collective-permute-done((bf16[96,768]{1,0:T(8,128)(2,1)S(1)}, bf16[96,768]{1,0:T(8,128)(2,1)S(1)}, u32[]{:S(2)}, u32[]{:S(2)}) %collective-permute-start.30) | collective-permute-done | bytes 147488 | tf_op jit(solution)/shard_map/ppermute | solution.py:456
  112.6 0.6 join_both_kernel.1
  113.4 2.1 %collective-permute-start.29 = (bf16[192,768]{1,0:T(8,128)(2,1)S(1)}, bf16[192,768]{1,0:T(8,128)(2,1)S(1)}, u32[]{:S(2)}, u32[]{:S(2)}) collective-permute-start(bf16[192,768]{1,0:T(8,128)(2,1)S(1)} %get-tuple-element.146), channel_id=1, source_target_pairs={{0,2},{1,3},{2,0},{3,1},{4,6},{5,7},{6,4},{7,5},{8,10},{9,11},{10,... | collective-permute-start | bytes 884744 | tf_op jit(solution)/shard_map/ppermute | solution.py:456
  115.5 5.2 %collective-permute-done.34.refs_3_.refs_1_ = bf16[192,768]{1,0:T(8,128)(2,1)S(1)} collective-permute-done((bf16[192,768]{1,0:T(8,128)(2,1)S(1)}, bf16[192,768]{1,0:T(8,128)(2,1)S(1)}, u32[]{:S(2)}, u32[]{:S(2)}) %collective-permute-start.34) | collective-permute-done | bytes 294944 | tf_op jit(solution)/shard_map/ppermute | solution.py:456
  120.8 1.3 collective-permute-start.40
  122.4 3.0 %collective-permute-done.33.refs_0_ = bf16[192,768]{1,0:T(8,128)(2,1)S(1)} collective-permute-done((bf16[192,768]{1,0:T(8,128)(2,1)S(1)}, bf16[192,768]{1,0:T(8,128)(2,1)S(1)}, u32[]{:S(2)}, u32[]{:S(2)}) %collective-permute-start.33) | collective-permute-done | bytes 294944 | tf_op jit(solution)/shard_map/ppermute | solution.py:456
  125.6 2.0 %collective-permute-start.37 = (bf16[384,768]{1,0:T(8,128)(2,1)S(1)}, bf16[384,768]{1,0:T(8,128)(2,1)S(1)}, u32[]{:S(2)}, u32[]{:S(2)}) collective-permute-start(bf16[384,768]{1,0:T(8,128)(2,1)S(1)} %stack_kernel.1.refs_3_.refs_2_), channel_id=1, source_target_pairs={{0,2},{1,3},{2,0},{3,1},{4,6},{5,7},{6,4},{7,5},{8,10},{9,11},{10,... | collective-permute-start | bytes 1769480 | tf_op jit(solution)/shard_map/ppermute | solution.py:456
  127.6 3.3 %collective-permute-done.40.refs_2_ = bf16[192,768]{1,0:T(8,128)(2,1)S(1)} collective-permute-done((bf16[192,768]{1,0:T(8,128)(2,1)S(1)}, bf16[192,768]{1,0:T(8,128)(2,1)S(1)}, u32[]{:S(2)}, u32[]{:S(2)}) %collective-permute-start.40) | collective-permute-done | bytes 294944 | tf_op jit(solution)/shard_map/ppermute | solution.py:456
  130.9 0.6 join_kernel.4.refs_3_.refs_1_
  131.5 2.0 %collective-permute-start.45 = (bf16[384,768]{1,0:T(8,128)(2,1)S(1)}, bf16[384,768]{1,0:T(8,128)(2,1)S(1)}, u32[]{:S(2)}, u32[]{:S(2)}) collective-permute-start(bf16[384,768]{1,0:T(8,128)(2,1)S(1)} %join_kernel.4.refs_3_.refs_1_), channel_id=1, source_target_pairs={{0,8},{4,12},{8,0},{12,4},{16,24},{20,28},{24,16},{28,20},{1,9},{5... | collective-permute-start | bytes 1769480 | tf_op jit(solution)/shard_map/ppermute | solution.py:456
  133.5 0.6 join_kernel.5.refs_5_.refs_1_
  134.5 2.8 %attention_near_kernel.1 = (f32[768,768]{1,0:T(8,128)}, f32[768,768]{1,0:T(8,128)}, f32[768,768]{1,0:T(8,128)}, f32[768,768]{1,0:T(8,128)}, f32[8,128]{1,0:T(8,128)S(1)}) custom-call(s32[11]{0:T(128)S(1)} %stack.44.refs_0_.refs_17_, bf16[384,768]{1,0:T(8,128)(2,1)S(1)} %get-tuple-element.152.refs_2_.refs_1_, ...), custom_call_target="tpu_custom_call" | custom-call | flops 2000000000 | bytes 1 | tf_op jit(solution)/shard_map/attention_near_kernel/pallas_call | solution.py:57
  137.3 8.2 %collective-permute-done.37.refs_3_ = bf16[384,768]{1,0:T(8,128)(2,1)S(1)} collective-permute-done((bf16[384,768]{1,0:T(8,128)(2,1)S(1)}, bf16[384,768]{1,0:T(8,128)(2,1)S(1)}, u32[]{:S(2)}, u32[]{:S(2)}) %collective-permute-start.37) | collective-permute-done | bytes 589856 | tf_op jit(solution)/shard_map/ppermute | solution.py:456
  145.5 0.5 collective-permute-start.41
  146.0 2.5 %collective-permute-done.44.refs_4_.refs_2_ = bf16[384,768]{1,0:T(8,128)(2,1)S(1)} collective-permute-done((bf16[384,768]{1,0:T(8,128)(2,1)S(1)}, bf16[384,768]{1,0:T(8,128)(2,1)S(1)}, u32[]{:S(2)}, u32[]{:S(2)}) %collective-permute-start.44) | collective-permute-done | bytes 589856 | tf_op jit(solution)/shard_map/ppermute | solution.py:456
  148.5 2.1 %join_kernel.6 = (f32[768,768]{1,0:T(8,128)}, f32[8,128]{1,0:T(8,128)S(1)}) custom-call(s32[11]{0:T(128)S(1)} %stack.44.refs_0_.refs_17_, bf16[384,768]{1,0:T(8,128)(2,1)S(1)} %join_kernel.4.refs_3_.refs_1_, bf16[384,768]{1,0:T(8,128)(2,1)S(1)} %collective-permute-done.45.refs_2_, f32[8,128]{1,0:T(8,128)S(1)} %get-tuple-element.153.refs_3_, ...), custom_call_target="tpu_custom_call" | custom-call | flops 300000000 | bytes 1 | tf_op jit(solution)/shard_map/join_kernel/pallas_call | solution.py:57
  150.6 2.1 %join_kernel.7 = (f32[768,768]{1,0:T(8,128)}, f32[8,128]{1,0:T(8,128)S(1)}) custom-call(s32[11]{0:T(128)S(1)} %stack.44.refs_0_.refs_17_, bf16[384,768]{1,0:T(8,128)(2,1)S(1)} %join_kernel.5.refs_5_.refs_1_, bf16[384,768]{1,0:T(8,128)(2,1)S(1)} %collective-permute-done.44.refs_4_.refs_2_, f32[8,128]{1,0:T(8,128)S(1)} %get-tuple-element.159.refs_3_), custom_call_target="tpu_custom_call" | custom-call | flops 1000000000 | bytes 1 | tf_op jit(solution)/shard_map/join_kernel/pallas_call | solution.py:57
  152.8 3.4 %attention_far_kernel.1 = (f32[768,768]{1,0:T(8,128)}, f32[768,768]{1,0:T(8,128)}, f32[768,768]{1,0:T(8,128)}, f32[768,768]{1,0:T(8,128)}, f32[8,128]{1,0:T(8,128)}) custom-call(s32[11]{0:T(128)S(1)} %stack.44.refs_0_.refs_17_, ...), custom_call_target="tpu_custom_call", output_to_operand_aliasing={{0}: (7, {}), {1}: (8, {}), {2}: (9, {}), {3}: (10, {})} | custom-call | flops 1 | bytes 1 | tf_op jit(solution)/shard_map/attention_far_kernel/pallas_call | solution.py:57
  (89 shorter events, 5.2 us)
Async XLA Ops:
  0.6 4.8 %collective-permute-start.1 = (s32[2,64]{1,0:T(2,128)}, s32[2,64]{1,0:T(2,128)S(1)}, u32[]{:S(2)}, u32[]{:S(2)}) collective-permute-start(s32[2,64]{1,0:T(2,128)} %refs_4_.1), channel_id=1, source_target_pairs={{0,2},{1,3},{2,0},{3,1},{4,6},{5,7},{6,4},{7,5},{8,10},{9,11},{10,... | collective-permute-start | bytes 1544 | tf_op jit(solution)/shard_map/ppermute | solution.py:456
  3.6 1.8 %collective-permute-start = (s32[2,64]{1,0:T(2,128)}, s32[2,64]{1,0:T(2,128)S(1)}, u32[]{:S(2)}, u32[]{:S(2)}) collective-permute-start(s32[2,64]{1,0:T(2,128)} %refs_4_.1), channel_id=1, source_target_pairs={{0,1},{1,0},{2,3},{3,2},{4,5},{5,4},{6,7},{7,6},{8,9},{9,8},{10,11... | collective-permute-start | bytes 1544 | tf_op jit(solution)/shard_map/ppermute | solution.py:456
  3.6 3.2 %collective-permute-start.2 = (s32[2,64]{1,0:T(2,128)}, s32[2,64]{1,0:T(2,128)S(1)}, u32[]{:S(2)}, u32[]{:S(2)}) collective-permute-start(s32[2,64]{1,0:T(2,128)} %refs_4_.1), channel_id=1, source_target_pairs={{0,3},{1,2},{2,1},{3,0},{4,7},{5,6},{6,5},{7,4},{8,11},{9,10},{10,... | collective-permute-start | bytes 1544 | tf_op jit(solution)/shard_map/ppermute | solution.py:456
  3.9 20.8 %collective-permute-start.5 = (bf16[768,768]{1,0:T(8,128)(2,1)}, bf16[768,768]{1,0:T(8,128)(2,1)S(1)}, u32[]{:S(2)}, u32[]{:S(2)}) collective-permute-start(bf16[768,768]{1,0:T(8,128)(2,1)} %refs_5_.3), channel_id=1, source_target_pairs={{0,1},{1,0},{2,3},{3,2},{4,5},{5,4},{6,7},{7,6},{8,9},{9,8},{10,11... | collective-permute-start | bytes 3538952 | tf_op jit(solution)/shard_map/ppermute | solution.py:456
  4.2 28.0 %collective-permute-start.9 = (bf16[768,768]{1,0:T(8,128)(2,1)}, bf16[768,768]{1,0:T(8,128)(2,1)S(1)}, u32[]{:S(2)}, u32[]{:S(2)}) collective-permute-start(bf16[768,768]{1,0:T(8,128)(2,1)} %refs_2_.1), channel_id=1, source_target_pairs={{0,1},{1,0},{2,3},{3,2},{4,5},{5,4},{6,7},{7,6},{8,9},{9,8},{10,11... | collective-permute-start | bytes 3538952 | tf_op jit(solution)/shard_map/ppermute | solution.py:456
  6.9 0.7 copy-start.7
  7.5 3.2 %copy-start.9 = (bf16[2,512,768]{2,1,0:T(8,128)(2,1)S(1)}, bf16[2,512,768]{2,1,0:T(8,128)(2,1)}, u32[]{:S(2)}) copy-start(bf16[2,512,768]{2,1,0:T(8,128)(2,1)} %refs_3_.4) | copy-start | bytes 4718596
  10.1 2.4 %collective-permute-start.3 = (bf16[256,768]{1,0:T(8,128)(2,1)S(1)}, bf16[256,768]{1,0:T(8,128)(2,1)S(1)}, u32[]{:S(2)}, u32[]{:S(2)}) collective-permute-start(bf16[256,768]{1,0:T(8,128)(2,1)S(1)} %get-tuple-element.92), channel_id=1, source_target_pairs={{0,1},{1,0},{2,3},{3,2},{4,5},{5,4},{6,7},{7,6},{8,9},{9,8},{10,11... | collective-permute-start | bytes 1179656 | tf_op jit(solution)/shard_map/ppermute | solution.py:456
  10.7 4.2 %copy-start.12 = (bf16[768]{0:T(1024)(128)(2,1)S(1)}, bf16[768]{0:T(1024)(128)(2,1)}, u32[]{:S(2)}) copy-start(bf16[768]{0:T(1024)(128)(2,1)} %param.16) | copy-start | bytes 4612
  10.7 13.9 %copy-start.3 = (bf16[768,768]{1,0:T(8,128)(2,1)S(1)}, bf16[768,768]{1,0:T(8,128)(2,1)}, u32[]{:S(2)}) copy-start(bf16[768,768]{1,0:T(8,128)(2,1)} %refs_14_.1) | copy-start | bytes 3538948
  10.7 13.9 %copy-start.4 = (bf16[768,768]{1,0:T(8,128)(2,1)S(1)}, bf16[768,768]{1,0:T(8,128)(2,1)}, u32[]{:S(2)}) copy-start(bf16[768,768]{1,0:T(8,128)(2,1)} %refs_15_.1) | copy-start | bytes 3538948
  10.7 13.9 %copy-start.5 = (bf16[768,768]{1,0:T(8,128)(2,1)S(1)}, bf16[768,768]{1,0:T(8,128)(2,1)}, u32[]{:S(2)}) copy-start(bf16[768,768]{1,0:T(8,128)(2,1)} %refs_16_.1) | copy-start | bytes 3538948
  11.9 3.0 %copy-start.10 = (f32[768]{0:T(1024)S(1)}, f32[768]{0:T(1024)}, u32[]{:S(2)}) copy-start(f32[768]{0:T(1024)} %param.17) | copy-start | bytes 9220
  11.9 3.0 %copy-start.11 = (f32[768]{0:T(1024)S(1)}, f32[768]{0:T(1024)}, u32[]{:S(2)}) copy-start(f32[768]{0:T(1024)} %param.18) | copy-start | bytes 9220
  11.9 12.8 %copy-start = (bf16[768,768]{1,0:T(8,128)(2,1)S(1)}, bf16[768,768]{1,0:T(8,128)(2,1)}, u32[]{:S(2)}) copy-start(bf16[768,768]{1,0:T(8,128)(2,1)} %refs_5_.3) | copy-start | bytes 3538948
  11.9 12.8 %copy-start.2 = (bf16[768,768]{1,0:T(8,128)(2,1)S(1)}, bf16[768,768]{1,0:T(8,128)(2,1)}, u32[]{:S(2)}) copy-start(bf16[768,768]{1,0:T(8,128)(2,1)} %refs_13_.1) | copy-start | bytes 3538948
  11.9 12.8 %copy-start.8 = (s32[2]{0:T(128)S(1)}, s32[2]{0:T(128)}, u32[]{:S(2)}) copy-start(s32[2]{0:T(128)} %refs_1_.1) | copy-start | bytes 28
  11.9 1.5 collective-permute-start.6
  12.0 1.7 %collective-permute-start.7 = (bf16[128,768]{1,0:T(8,128)(2,1)S(1)}, bf16[128,768]{1,0:T(8,128)(2,1)S(1)}, u32[]{:S(2)}, u32[]{:S(2)}) collective-permute-start(bf16[128,768]{1,0:T(8,128)(2,1)S(1)} %get-tuple-element.95), channel_id=1, source_target_pairs={{0,1},{1,0},{2,3},{3,2},{4,5},{5,4},{6,7},{7,6},{8,9},{9,8},{10,11... | collective-permute-start | bytes 589832 | tf_op jit(solution)/shard_map/ppermute | solution.py:456
  12.6 12.0 %collective-permute-start.4 = (bf16[256,768]{1,0:T(8,128)(2,1)S(1)}, bf16[256,768]{1,0:T(8,128)(2,1)S(1)}, u32[]{:S(2)}, u32[]{:S(2)}) collective-permute-start(bf16[256,768]{1,0:T(8,128)(2,1)S(1)} %add.15.refs_2_), channel_id=1, source_target_pairs={{0,2},{1,3},{2,0},{3,1},{4,6},{5,7},{6,4},{7,5},{8,10},{9,11},{10,... | collective-permute-start | bytes 1179656 | tf_op jit(solution)/shard_map/ppermute | solution.py:456
  13.8 18.4 %collective-permute-start.8 = (bf16[256,768]{1,0:T(8,128)(2,1)S(1)}, bf16[256,768]{1,0:T(8,128)(2,1)S(1)}, u32[]{:S(2)}, u32[]{:S(2)}) collective-permute-start(bf16[256,768]{1,0:T(8,128)(2,1)S(1)} %maximum_add_fusion.refs_13_.refs_1_.refs_7_.refs_3_), channel_id=1, source_target_pairs={{0,2},{1,3},{2,0},{3,1},{4,6},{5,7},{6,4},{7,5},{8,10},{9,11},{10,... | collective-permute-start | bytes 1179656 | tf_op jit(solution)/shard_map/ppermute | solution.py:456
  14.9 17.3 %copy-start.1 = (bf16[768,768]{1,0:T(8,128)(2,1)S(1)}, bf16[768,768]{1,0:T(8,128)(2,1)}, u32[]{:S(2)}) copy-start(bf16[768,768]{1,0:T(8,128)(2,1)} %refs_2_.1) | copy-start | bytes 3538948
  34.0 3.5 %collective-permute-start.13 = (bf16[512,768]{1,0:T(8,128)(2,1)S(1)}, bf16[512,768]{1,0:T(8,128)(2,1)S(1)}, u32[]{:S(2)}, u32[]{:S(2)}) collective-permute-start(bf16[512,768]{1,0:T(8,128)(2,1)S(1)} %get-tuple-element.110.refs_4_), channel_id=1, source_target_pairs={{0,1},{1,0},{2,3},{3,2},{4,5},{5,4},{6,7},{7,6},{8,9},{9,8},{10,11... | collective-permute-start | bytes 2359304 | tf_op jit(solution)/shard_map/ppermute | solution.py:456
  34.1 3.4 %collective-permute-start.12 = (bf16[512,768]{1,0:T(8,128)(2,1)S(1)}, bf16[512,768]{1,0:T(8,128)(2,1)S(1)}, u32[]{:S(2)}, u32[]{:S(2)}) collective-permute-start(bf16[512,768]{1,0:T(8,128)(2,1)S(1)} %get-tuple-element.109.refs_3_), channel_id=1, source_target_pairs={{0,1},{1,0},{2,3},{3,2},{4,5},{5,4},{6,7},{7,6},{8,9},{9,8},{10,11... | collective-permute-start | bytes 2359304 | tf_op jit(solution)/shard_map/ppermute | solution.py:456
  34.6 12.0 %collective-permute-start.11 = (bf16[256,768]{1,0:T(8,128)(2,1)S(1)}, bf16[256,768]{1,0:T(8,128)(2,1)S(1)}, u32[]{:S(2)}, u32[]{:S(2)}) collective-permute-start(bf16[256,768]{1,0:T(8,128)(2,1)S(1)} %get-tuple-element.103.refs_4_), channel_id=1, source_target_pairs={{0,2},{1,3},{2,0},{3,1},{4,6},{5,7},{6,4},{7,5},{8,10},{9,11},{10,... | collective-permute-start | bytes 1179656 | tf_op jit(solution)/shard_map/ppermute | solution.py:456
  35.9 18.2 %collective-permute-start.10 = (bf16[256,768]{1,0:T(8,128)(2,1)S(1)}, bf16[256,768]{1,0:T(8,128)(2,1)S(1)}, u32[]{:S(2)}, u32[]{:S(2)}) collective-permute-start(bf16[256,768]{1,0:T(8,128)(2,1)S(1)} %moved_kernel.1.refs_7_.refs_5_), channel_id=1, source_target_pairs={{0,2},{1,3},{2,0},{3,1},{4,6},{5,7},{6,4},{7,5},{8,10},{9,11},{10,... | collective-permute-start | bytes 1179656 | tf_op jit(solution)/shard_map/ppermute | solution.py:456
  37.4 21.3 %collective-permute-start.18 = (bf16[512,768]{1,0:T(8,128)(2,1)S(1)}, bf16[512,768]{1,0:T(8,128)(2,1)S(1)}, u32[]{:S(2)}, u32[]{:S(2)}) collective-permute-start(bf16[512,768]{1,0:T(8,128)(2,1)S(1)} %get-tuple-element.119.refs_2_), channel_id=1, source_target_pairs={{0,1},{1,0},{2,3},{3,2},{4,5},{5,4},{6,7},{7,6},{8,9},{9,8},{10,11... | collective-permute-start | bytes 2359304 | tf_op jit(solution)/shard_map/ppermute | solution.py:456
  39.4 15.8 %collective-permute-start.15 = (bf16[384,768]{1,0:T(8,128)(2,1)S(1)}, bf16[384,768]{1,0:T(8,128)(2,1)S(1)}, u32[]{:S(2)}, u32[]{:S(2)}) collective-permute-start(bf16[384,768]{1,0:T(8,128)(2,1)S(1)} %get-tuple-element.115), channel_id=1, source_target_pairs={{0,4},{4,0},{8,12},{12,8},{16,20},{20,16},{24,28},{28,24},{1,5},{5... | collective-permute-start | bytes 1769480 | tf_op jit(solution)/shard_map/ppermute | solution.py:456
  41.0 24.0 %collective-permute-start.23 = (bf16[384,768]{1,0:T(8,128)(2,1)S(1)}, bf16[384,768]{1,0:T(8,128)(2,1)S(1)}, u32[]{:S(2)}, u32[]{:S(2)}) collective-permute-start(bf16[384,768]{1,0:T(8,128)(2,1)S(1)} %get-tuple-element.127), channel_id=1, source_target_pairs={{0,8},{4,12},{8,0},{12,4},{16,24},{20,28},{24,16},{28,20},{1,9},{5... | collective-permute-start | bytes 1769480 | tf_op jit(solution)/shard_map/ppermute | solution.py:456
  53.6 5.1 %collective-permute-start.19 = (bf16[512,768]{1,0:T(8,128)(2,1)S(1)}, bf16[512,768]{1,0:T(8,128)(2,1)S(1)}, u32[]{:S(2)}, u32[]{:S(2)}) collective-permute-start(bf16[512,768]{1,0:T(8,128)(2,1)S(1)} %get-tuple-element.121), channel_id=1, source_target_pairs={{0,1},{1,0},{2,3},{3,2},{4,5},{5,4},{6,7},{7,6},{8,9},{9,8},{10,11... | collective-permute-start | bytes 2359304 | tf_op jit(solution)/shard_map/ppermute | solution.py:456
  55.9 9.1 %collective-permute-start.16 = (bf16[192,768]{1,0:T(8,128)(2,1)S(1)}, bf16[192,768]{1,0:T(8,128)(2,1)S(1)}, u32[]{:S(2)}, u32[]{:S(2)}) collective-permute-start(bf16[192,768]{1,0:T(8,128)(2,1)S(1)} %get-tuple-element.117), channel_id=1, source_target_pairs={{0,8},{4,12},{8,0},{12,4},{16,24},{20,28},{24,16},{28,20},{1,9},{5... | collective-permute-start | bytes 884744 | tf_op jit(solution)/shard_map/ppermute | solution.py:456
  57.5 1.2 collective-permute-start.17
  60.2 14.5 %collective-permute-start.21 = (bf16[208,768]{1,0:T(8,128)(2,1)S(1)}, bf16[208,768]{1,0:T(8,128)(2,1)S(1)}, u32[]{:S(2)}, u32[]{:S(2)}) collective-permute-start(bf16[208,768]{1,0:T(8,128)(2,1)S(1)} %get-tuple-element.125), channel_id=1, source_target_pairs={{0,4},{4,0},{8,12},{12,8},{16,20},{20,16},{24,28},{28,24},{1,5},{5... | collective-permute-start | bytes 958472 | tf_op jit(solution)/shard_map/ppermute | solution.py:456
  61.8 12.9 %collective-permute-start.22 = (bf16[192,768]{1,0:T(8,128)(2,1)S(1)}, bf16[192,768]{1,0:T(8,128)(2,1)S(1)}, u32[]{:S(2)}, u32[]{:S(2)}) collective-permute-start(bf16[192,768]{1,0:T(8,128)(2,1)S(1)} %get-tuple-element.126), channel_id=1, source_target_pairs={{0,8},{4,12},{8,0},{12,4},{16,24},{20,28},{24,16},{28,20},{1,9},{5... | collective-permute-start | bytes 884744 | tf_op jit(solution)/shard_map/ppermute | solution.py:456
  62.3 13.9 %collective-permute-start.14 = (bf16[256,768]{1,0:T(8,128)(2,1)S(1)}, bf16[256,768]{1,0:T(8,128)(2,1)S(1)}, u32[]{:S(2)}, u32[]{:S(2)}) collective-permute-start(bf16[256,768]{1,0:T(8,128)(2,1)S(1)} %get-tuple-element.114.refs_3_.refs_4_), channel_id=1, source_target_pairs={{0,1},{1,0},{2,3},{3,2},{4,5},{5,4},{6,7},{7,6},{8,9},{9,8},{10,11... | collective-permute-start | bytes 1179656 | tf_op jit(solution)/shard_map/ppermute | solution.py:456
  65.0 21.5 %collective-permute-start.27 = (bf16[256,768]{1,0:T(8,128)(2,1)S(1)}, bf16[256,768]{1,0:T(8,128)(2,1)S(1)}, u32[]{:S(2)}, u32[]{:S(2)}) collective-permute-start(bf16[256,768]{1,0:T(8,128)(2,1)S(1)} %get-tuple-element.136.refs_4_), channel_id=1, source_target_pairs={{0,1},{1,0},{2,3},{3,2},{4,5},{5,4},{6,7},{7,6},{8,9},{9,8},{10,11... | collective-permute-start | bytes 1179656 | tf_op jit(solution)/shard_map/ppermute | solution.py:456
  65.1 21.4 %collective-permute-start.20 = (bf16[192,768]{1,0:T(8,128)(2,1)S(1)}, bf16[192,768]{1,0:T(8,128)(2,1)S(1)}, u32[]{:S(2)}, u32[]{:S(2)}) collective-permute-start(bf16[192,768]{1,0:T(8,128)(2,1)S(1)} %round_kernel.2.refs_6_.refs_0_), channel_id=1, source_target_pairs={{0,16},{4,20},{8,24},{12,28},{16,0},{20,4},{24,8},{28,12},{1,17},{... | collective-permute-start | bytes 884744 | tf_op jit(solution)/shard_map/ppermute | solution.py:456
  75.4 8.1 %collective-permute-start.24 = (bf16[112,768]{1,0:T(8,128)(2,1)S(1)}, bf16[112,768]{1,0:T(8,128)(2,1)S(1)}, u32[]{:S(2)}, u32[]{:S(2)}) collective-permute-start(bf16[112,768]{1,0:T(8,128)(2,1)S(1)} %get-tuple-element.131), channel_id=1, source_target_pairs={{0,8},{4,12},{8,0},{12,4},{16,24},{20,28},{24,16},{28,20},{1,9},{5... | collective-permute-start | bytes 516104 | tf_op jit(solution)/shard_map/ppermute | solution.py:456
  75.5 5.2 %collective-permute-start.25 = (bf16[96,768]{1,0:T(8,128)(2,1)S(1)}, bf16[96,768]{1,0:T(8,128)(2,1)S(1)}, u32[]{:S(2)}, u32[]{:S(2)}) collective-permute-start(bf16[96,768]{1,0:T(8,128)(2,1)S(1)} %get-tuple-element.132), channel_id=1, source_target_pairs={{0,4},{4,0},{8,12},{12,8},{16,20},{20,16},{24,28},{28,24},{1,5},{5... | collective-permute-start | bytes 442376 | tf_op jit(solution)/shard_map/ppermute | solution.py:456
  83.6 18.0 %collective-permute-start.26 = (bf16[208,768]{1,0:T(8,128)(2,1)S(1)}, bf16[208,768]{1,0:T(8,128)(2,1)S(1)}, u32[]{:S(2)}, u32[]{:S(2)}) collective-permute-start(bf16[208,768]{1,0:T(8,128)(2,1)S(1)} %get-tuple-element.134.refs_1_), channel_id=1, source_target_pairs={{0,16},{4,20},{8,24},{12,28},{16,0},{20,4},{24,8},{28,12},{1,17},{... | collective-permute-start | bytes 958472 | tf_op jit(solution)/shard_map/ppermute | solution.py:456
  89.4 6.8 %collective-permute-start.28 = (bf16[192,768]{1,0:T(8,128)(2,1)S(1)}, bf16[192,768]{1,0:T(8,128)(2,1)S(1)}, u32[]{:S(2)}, u32[]{:S(2)}) collective-permute-start(bf16[192,768]{1,0:T(8,128)(2,1)S(1)} %get-tuple-element.139), channel_id=1, source_target_pairs={{0,4},{4,0},{8,12},{12,8},{16,20},{20,16},{24,28},{28,24},{1,5},{5... | collective-permute-start | bytes 884744 | tf_op jit(solution)/shard_map/ppermute | solution.py:456
  96.3 11.4 %copy-start.6 = (bf16[2,512,768]{2,1,0:T(8,128)(2,1)S(1)}, bf16[2,512,768]{2,1,0:T(8,128)(2,1)}, u32[]{:S(2)}) copy-start(bf16[2,512,768]{2,1,0:T(8,128)(2,1)} %refs_3_.5) | copy-start | bytes 4718596
  96.3 19.3 %collective-permute-start.35 = (bf16[192,768]{1,0:T(8,128)(2,1)S(1)}, bf16[192,768]{1,0:T(8,128)(2,1)S(1)}, u32[]{:S(2)}, u32[]{:S(2)}) collective-permute-start(bf16[192,768]{1,0:T(8,128)(2,1)S(1)} %round_kernel.3.refs_3_.refs_0_), channel_id=1, source_target_pairs={{0,16},{4,20},{8,24},{12,28},{16,0},{20,4},{24,8},{28,12},{1,17},{... | collective-permute-start | bytes 884744 | tf_op jit(solution)/shard_map/ppermute | solution.py:456
  102.3 7.7 %collective-permute-start.31 = (bf16[96,768]{1,0:T(8,128)(2,1)S(1)}, bf16[96,768]{1,0:T(8,128)(2,1)S(1)}, u32[]{:S(2)}, u32[]{:S(2)}) collective-permute-start(bf16[96,768]{1,0:T(8,128)(2,1)S(1)} %get-tuple-element.147.refs_2_), channel_id=1, source_target_pairs={{0,4},{4,0},{8,12},{12,8},{16,20},{20,16},{24,28},{28,24},{1,5},{5... | collective-permute-start | bytes 442376 | tf_op jit(solution)/shard_map/ppermute | solution.py:456
  104.2 8.5 %collective-permute-start.30 = (bf16[96,768]{1,0:T(8,128)(2,1)S(1)}, bf16[96,768]{1,0:T(8,128)(2,1)S(1)}, u32[]{:S(2)}, u32[]{:S(2)}) collective-permute-start(bf16[96,768]{1,0:T(8,128)(2,1)S(1)} %get-tuple-element.140.refs_2_.refs_1_), channel_id=1, source_target_pairs={{0,8},{4,12},{8,0},{12,4},{16,24},{20,28},{24,16},{28,20},{1,9},{5... | collective-permute-start | bytes 442376 | tf_op jit(solution)/shard_map/ppermute | solution.py:456
  113.3 7.4 %collective-permute-start.34 = (bf16[192,768]{1,0:T(8,128)(2,1)S(1)}, bf16[192,768]{1,0:T(8,128)(2,1)S(1)}, u32[]{:S(2)}, u32[]{:S(2)}) collective-permute-start(bf16[192,768]{1,0:T(8,128)(2,1)S(1)} %get-tuple-element.151), channel_id=1, source_target_pairs={{0,8},{4,12},{8,0},{12,4},{16,24},{20,28},{24,16},{28,20},{1,9},{5... | collective-permute-start | bytes 884744 | tf_op jit(solution)/shard_map/ppermute | solution.py:456
  113.4 12.0 %collective-permute-start.36 = (bf16[384,768]{1,0:T(8,128)(2,1)S(1)}, bf16[384,768]{1,0:T(8,128)(2,1)S(1)}, u32[]{:S(2)}, u32[]{:S(2)}) collective-permute-start(bf16[384,768]{1,0:T(8,128)(2,1)S(1)} %get-tuple-element.152.refs_2_.refs_1_), channel_id=1, source_target_pairs={{0,1},{1,0},{2,3},{3,2},{4,5},{5,4},{6,7},{7,6},{8,9},{9,8},{10,11... | collective-permute-start | bytes 1769480 | tf_op jit(solution)/shard_map/ppermute | solution.py:456
  113.4 12.1 %collective-permute-start.29 = (bf16[192,768]{1,0:T(8,128)(2,1)S(1)}, bf16[192,768]{1,0:T(8,128)(2,1)S(1)}, u32[]{:S(2)}, u32[]{:S(2)}) collective-permute-start(bf16[192,768]{1,0:T(8,128)(2,1)S(1)} %get-tuple-element.146), channel_id=1, source_target_pairs={{0,2},{1,3},{2,0},{3,1},{4,6},{5,7},{6,4},{7,5},{8,10},{9,11},{10,... | collective-permute-start | bytes 884744 | tf_op jit(solution)/shard_map/ppermute | solution.py:456
  115.5 9.9 %collective-permute-start.33 = (bf16[192,768]{1,0:T(8,128)(2,1)S(1)}, bf16[192,768]{1,0:T(8,128)(2,1)S(1)}, u32[]{:S(2)}, u32[]{:S(2)}) collective-permute-start(bf16[192,768]{1,0:T(8,128)(2,1)S(1)} %get-tuple-element.150), channel_id=1, source_target_pairs={{0,4},{4,0},{8,12},{12,8},{16,20},{20,16},{24,28},{28,24},{1,5},{5... | collective-permute-start | bytes 884744 | tf_op jit(solution)/shard_map/ppermute | solution.py:456
  120.8 10.1 %collective-permute-start.40 = (bf16[192,768]{1,0:T(8,128)(2,1)S(1)}, bf16[192,768]{1,0:T(8,128)(2,1)S(1)}, u32[]{:S(2)}, u32[]{:S(2)}) collective-permute-start(bf16[192,768]{1,0:T(8,128)(2,1)S(1)} %last_kernel.3.refs_2_.refs_1_), channel_id=1, source_target_pairs={{0,4},{4,0},{8,12},{12,8},{16,20},{20,16},{24,28},{28,24},{1,5},{5... | collective-permute-start | bytes 884744 | tf_op jit(solution)/shard_map/ppermute | solution.py:456
  122.1 11.4 %collective-permute-start.39 = (bf16[192,768]{1,0:T(8,128)(2,1)S(1)}, bf16[192,768]{1,0:T(8,128)(2,1)S(1)}, u32[]{:S(2)}, u32[]{:S(2)}) collective-permute-start(bf16[192,768]{1,0:T(8,128)(2,1)S(1)} %last_kernel.2.refs_6_.refs_1_), channel_id=1, source_target_pairs={{0,8},{4,12},{8,0},{12,4},{16,24},{20,28},{24,16},{28,20},{1,9},{5... | collective-permute-start | bytes 884744 | tf_op jit(solution)/shard_map/ppermute | solution.py:456
  125.4 20.6 %collective-permute-start.32 = (bf16[192,768]{1,0:T(8,128)(2,1)S(1)}, bf16[192,768]{1,0:T(8,128)(2,1)S(1)}, u32[]{:S(2)}, u32[]{:S(2)}) collective-permute-start(bf16[192,768]{1,0:T(8,128)(2,1)S(1)} %get-tuple-element.149), channel_id=1, source_target_pairs={{0,2},{1,3},{2,0},{3,1},{4,6},{5,7},{6,4},{7,5},{8,10},{9,11},{10,... | collective-permute-start | bytes 884744 | tf_op jit(solution)/shard_map/ppermute | solution.py:456
  125.5 9.0 %collective-permute-start.38 = (bf16[384,768]{1,0:T(8,128)(2,1)S(1)}, bf16[384,768]{1,0:T(8,128)(2,1)S(1)}, u32[]{:S(2)}, u32[]{:S(2)}) collective-permute-start(bf16[384,768]{1,0:T(8,128)(2,1)S(1)} %stack_kernel.1.refs_3_.refs_2_), channel_id=1, source_target_pairs={{0,1},{1,0},{2,3},{3,2},{4,5},{5,4},{6,7},{7,6},{8,9},{9,8},{10,11... | collective-permute-start | bytes 1769480 | tf_op jit(solution)/shard_map/ppermute | solution.py:456
  125.6 19.9 %collective-permute-start.37 = (bf16[384,768]{1,0:T(8,128)(2,1)S(1)}, bf16[384,768]{1,0:T(8,128)(2,1)S(1)}, u32[]{:S(2)}, u32[]{:S(2)}) collective-permute-start(bf16[384,768]{1,0:T(8,128)(2,1)S(1)} %stack_kernel.1.refs_3_.refs_2_), channel_id=1, source_target_pairs={{0,2},{1,3},{2,0},{3,1},{4,6},{5,7},{6,4},{7,5},{8,10},{9,11},{10,... | collective-permute-start | bytes 1769480 | tf_op jit(solution)/shard_map/ppermute | solution.py:456
  131.5 17.0 %collective-permute-start.45 = (bf16[384,768]{1,0:T(8,128)(2,1)S(1)}, bf16[384,768]{1,0:T(8,128)(2,1)S(1)}, u32[]{:S(2)}, u32[]{:S(2)}) collective-permute-start(bf16[384,768]{1,0:T(8,128)(2,1)S(1)} %join_kernel.4.refs_3_.refs_1_), channel_id=1, source_target_pairs={{0,8},{4,12},{8,0},{12,4},{16,24},{20,28},{24,16},{28,20},{1,9},{5... | collective-permute-start | bytes 1769480 | tf_op jit(solution)/shard_map/ppermute | solution.py:456
  134.1 14.4 %collective-permute-start.44 = (bf16[384,768]{1,0:T(8,128)(2,1)S(1)}, bf16[384,768]{1,0:T(8,128)(2,1)S(1)}, u32[]{:S(2)}, u32[]{:S(2)}) collective-permute-start(bf16[384,768]{1,0:T(8,128)(2,1)S(1)} %join_kernel.5.refs_5_.refs_1_), channel_id=1, source_target_pairs={{0,4},{4,0},{8,12},{12,8},{16,20},{20,16},{24,28},{28,24},{1,5},{5... | collective-permute-start | bytes 1769480 | tf_op jit(solution)/shard_map/ppermute | solution.py:456
  145.5 7.3 %collective-permute-start.43 = (bf16[384,768]{1,0:T(8,128)(2,1)S(1)}, bf16[384,768]{1,0:T(8,128)(2,1)S(1)}, u32[]{:S(2)}, u32[]{:S(2)}) collective-permute-start(bf16[384,768]{1,0:T(8,128)(2,1)S(1)} %collective-permute-done.37.refs_3_), channel_id=1, source_target_pairs={{0,1},{1,0},{2,3},{3,2},{4,5},{5,4},{6,7},{7,6},{8,9},{9,8},{10,11... | collective-permute-start | bytes 1769480 | tf_op jit(solution)/shard_map/ppermute | solution.py:456
  145.5 7.3 %collective-permute-start.41 = (bf16[192,768]{1,0:T(8,128)(2,1)S(1)}, bf16[192,768]{1,0:T(8,128)(2,1)S(1)}, u32[]{:S(2)}, u32[]{:S(2)}) collective-permute-start(bf16[192,768]{1,0:T(8,128)(2,1)S(1)} %collective-permute-done.29.refs_4_.refs_1_), channel_id=1, source_target_pairs={{0,1},{1,0},{2,3},{3,2},{4,5},{5,4},{6,7},{7,6},{8,9},{9,8},{10,11... | collective-permute-start | bytes 884744 | tf_op jit(solution)/shard_map/ppermute | solution.py:456
  146.0 6.7 %collective-permute-start.42 = (bf16[192,768]{1,0:T(8,128)(2,1)S(1)}, bf16[192,768]{1,0:T(8,128)(2,1)S(1)}, u32[]{:S(2)}, u32[]{:S(2)}) collective-permute-start(bf16[192,768]{1,0:T(8,128)(2,1)S(1)} %collective-permute-done.32.refs_2_), channel_id=1, source_target_pairs={{0,1},{1,0},{2,3},{3,2},{4,5},{5,4},{6,7},{7,6},{8,9},{9,8},{10,11... | collective-permute-start | bytes 884744 | tf_op jit(solution)/shard_map/ppermute | solution.py:456

commit v4 on v3

--- a/solution.py
+++ b/solution.py
@@ -9,11 +9,9 @@
 
 NH = 12
 Y, Z0, Z1 = 8, 9, 10
-ORDER = (
-    "F AB SL R2 FA D3 A2 A3 P2 R2U U3 A4 D4 P1 A5 U4 A6 U5 D5 AT0 XC UU DU AT1"
-).split()
-WORK = {'P1': 2000, 'AB': 100, 'A5': 8000, 'D5': 4000, 'U5': 8000, 'U4': 2000, 'D3': 300, 'SL': 8000, 'UU': 300, 'DU': 1000, 'P2': 4000, 'R2': 4000, 'AT0': 2000, 'A6': 300, 'SA': 8000, 'A4': 4000, 'ML': 100, 'A2': 300, 'R2U': 600, 'A3': 1000}
-HOLD = {'A2': ['u1'], 'P2': ['d3'], 'U5': ['x1'], 'U4': ['b6'], 'A3': ['up'], 'A6': ['ce'], 'UU': ['d6']}
+ORDER = ("F", "AB", "MV", "R2", "FA", "SL", "D3", "A2", "A3", "D4", "R2U", "P2", "U3", "A4", "P1", "A5", "U4", "A6", "U5", "D5", "AT0", "UH", "XE", "DH", "ATE", "XC", "UU", "DU", "ATL")
+WORK = {"P1": 1000, "D5": 600, "U5": 8000, "U4": 2000, "D3": 100, "SL": 1000, "UU": 100, "DU": 4000, "P2": 100, "R2": 4000, "AT0": 4000, "A6": 300, "A4": 1000, "A2": 300, "A3": 1000, "AT": 600, "ATE": 100, "R2U": 600, "ATL": 8000, "ML": 4000, "F": 300, "A5": 100, "D4": 300, "SE": 8000, "MV": 4000, "SA": 300}
+HOLD = {"U5": ["x1"], "U3": ["d5"], "R2": ["u1"], "D4": ["up"]}
 EPS = 1e-06
 F32 = jnp.float32
 BF16 = jnp.bfloat16
@@ -232,9 +230,9 @@
 
 
 def attend_back_kernel(
-    chosen_in, attended, gain_attn, gain_mlp, gn_here, gn_there, rate, seen_here, seen_there,
-    query_in, key_in, value_in, probs_in, w_query, w_key, w_value, w_out, meta,
-    kept_rows, sent_rows, grad_sum, small, mixed_back, grad_query, grad_key, grad_value,
+    chosen_in, attended, gain_mlp, gn_here, gn_there, rate, seen_here, seen_there,
+    query_in, key_in, value_in, probs_in, w_out, meta,
+    kept_rows, sent_rows, grad_query, grad_key, grad_value, hidden_out, small, mixed_back,
 ):
     small[...] = jnp.zeros_like(small)
     slots, width = chosen_in.shape
@@ -244,6 +242,7 @@
     grad_normed_mlp = gn_here[...].astype(F32) + gn_there[...].astype(F32)
     grad_hidden, gain_grad = norm_back(chosen + attended[...], gain_mlp[...], grad_normed_mlp)
     small[2:3, :] = gain_grad
+    hidden_out[...] = grad_hidden
     seen = seen_here[...].astype(F32) + seen_there[...].astype(F32)
     grad_attended = (rate[:, :1] * seen + grad_hidden).astype(BF16)
     mixed_back[...] = mm_nt(grad_attended, w_out[...]).astype(BF16)
@@ -255,27 +254,21 @@
         keys = key_in[:, cols]
         values = value_in[:, cols]
         back = mixed_back[:, cols]
-        parts = []
+        back_turned, query_turned = back.T, query.T
+        for_query, for_key, for_value = [], [], []
         for h in range(2):
             mine = first if h == 0 else ~first
+            rows = slice(h * head, (h + 1) * head)
             probs = probs_in[2 * p + h]
             grad_probs = mm_nt(jnp.where(mine, back, jnp.zeros_like(back)), values)
-            gv = mm_tn(probs.astype(BF16), back)
+            for_value.append(mm(back_turned[rows, :], probs.astype(BF16)))
             inner = jnp.sum(grad_probs * probs, axis=-1, keepdims=True)
             grad_logits = (probs * (grad_probs - inner)).astype(BF16)
-            gq = mm(grad_logits, keys) * factor
-            gk = mm_tn(grad_logits, query) * factor
-            parts.append((gq, gk, gv))
-        for out, a, b in zip((grad_query, grad_key, grad_value), parts[0], parts[1]):
-            out[:, cols] = jnp.where(first, a, b).astype(BF16)
-    grad_normed = (
-        mm_nt(grad_query[...], w_query[...])
-        + mm_nt(grad_key[...], w_key[...])
-        + mm_nt(grad_value[...], w_value[...])
-    )
-    back, gain_grad = norm_back(chosen, gain_attn[...], grad_normed)
-    small[1:2, :] = gain_grad
-    grad_sum[...] = back + grad_hidden
+            for_query.append(mm(grad_logits, keys) * factor)
+            for_key.append(mm(query_turned[rows, :], grad_logits) * factor)
+        grad_query[:, cols] = jnp.where(first, for_query[0], for_query[1]).astype(BF16)
+        grad_key[:, cols] = jnp.concatenate(for_key, axis=0).astype(BF16).T
+        grad_value[:, cols] = jnp.concatenate(for_value, axis=0).astype(BF16).T
     for core, (low, high) in enumerate(((kept_rows, sent_rows), (sent_rows, kept_rows))):
 
         @pl.when(meta[1] == core)
@@ -287,8 +280,6 @@
 
 
 def attend_grads_kernel(whole, meta, *refs):
-    if not whole:
-        vectors, refs = refs[0], refs[1:]
     early_rows, early_got, mine, got, *outs, full = refs
     slots = mine.shape[0] // 2
     half = mine.shape[1] // 2
@@ -301,18 +292,17 @@
         outs[0][...] = full[...]
         return
     part = half // 2
-    send_a, send_b, keep_a, keep_b, out = outs
+    send_a, send_b, keep_a, keep_b = outs
     for at, bit, send, keep in ((0, Y, send_a, keep_a), (half, Z0, send_b, keep_b)):
         yours = pl.multiple_of(at + (1 - meta[bit]) * part, part)
-        send[:part, :] = full[pl.ds(yours, part), :].astype(BF16)
+        send[...] = full[pl.ds(yours, part), :].astype(BF16)
         keep[...] = full[pl.ds(pl.multiple_of(at + meta[bit] * part, part), part), :]
-    out[...] = vectors[...]
-    send_a[part:, :] = split_vectors(vectors[...]).astype(BF16)
 
 
 def slots_kernel(
-    chosen_in, attended, rate_in, seen_here, seen_there, moved_here, moved_there, w_router, grad_sum,
-    small, update, grad_chosen, vectors,
+    chosen_in, attended, rate_in, seen_here, seen_there, moved_here, moved_there, w_router, gain_attn,
+    grad_query, grad_key, grad_value, w_query, w_key, w_value, grad_hidden, small,
+    update, grad_chosen, vectors,
 ):
     chosen = chosen_in[...].astype(F32)
     rate = rate_in[:, :1]
@@ -320,10 +310,16 @@
     delta = attended[...] + (moved_here[...].astype(F32) + moved_there[...].astype(F32))
     update[...] = (rate * delta).astype(BF16)
     score = rate * (1.0 - rate) * jnp.sum(seen * delta, axis=-1, keepdims=True)
-    grad_chosen[...] = (grad_sum[...] + score * w_router[...].astype(F32)).astype(BF16)
-    vectors[...] = jnp.zeros_like(vectors)
+    grad_normed = (
+        mm_nt(grad_query[...], w_query[...])
+        + mm_nt(grad_key[...], w_key[...])
+        + mm_nt(grad_value[...], w_value[...])
+    )
+    back, gain_grad = norm_back(chosen, gain_attn[...], grad_normed)
+    grad_chosen[...] = (back + grad_hidden[...] + score * w_router[...].astype(F32)).astype(BF16)
+    vectors[...] = small[...]
     vectors[0:1, :] = jnp.sum(score * chosen, axis=0, keepdims=True)
-    vectors[1:3, :] = small[1:3, :]
+    vectors[1:2, :] = gain_grad
 
 
 def reduce_kernel(plan, gots, sends, meta, *refs):
@@ -349,15 +345,10 @@
     return v[:8, :] + v[8:, :]
 
 
-def reduce_small_kernel(plan, gots, sends, meta, *refs):
-    vectors, refs = refs[0], refs[1:]
-    out = refs[-1]
-    reduce_kernel(plan, gots, sends, meta, *refs[:-1])
-    got = refs[len(plan)]
-    own = join_vectors(split_vectors(vectors[...])) + join_vectors(got[got.shape[0] - 16 :, :].astype(F32))
-    out[...] = own
-    send = refs[len(plan) + gots]
-    send[send.shape[0] - 16 :, :] = split_vectors(own).astype(BF16)
+def reduce_small_kernel(plan, gots, sends, meta, vectors, *refs):
+    reduce_kernel(plan, gots, sends, meta, *refs)
+    send = refs[len(plan) + gots + sends - 1]
+    send[send.shape[0] - 16 :, :] = split_vectors(vectors[...]).astype(BF16)
 
 
 def round_kernel(keep, got, cur):
@@ -366,9 +357,9 @@
 
 def round_both_kernel(vectors, first, second, got_first, got_second, cur, out):
     rows = first.shape[0]
-    cur[:rows, :] = (first[...] + got_first[:rows, :].astype(F32)).astype(BF16)
-    cur[rows : 2 * rows, :] = (second[...] + got_second[...].astype(F32)).astype(BF16)
-    own = join_vectors(split_vectors(vectors[...])) + join_vectors(got_first[rows:, :].astype(F32))
+    cur[:rows, :] = (first[...] + got_first[...].astype(F32)).astype(BF16)
+    cur[rows : 2 * rows, :] = (second[...] + got_second[:rows, :].astype(F32)).astype(BF16)
+    own = join_vectors(split_vectors(vectors[...])) + join_vectors(got_second[rows:, :].astype(F32))
     cur[2 * rows :, :] = split_vectors(own).astype(BF16)
     out[...] = own
 
@@ -377,14 +368,14 @@
     out[...] = (cur[...].astype(F32) + got[...].astype(F32)).astype(BF16)
 
 
-def last_both_kernel(vectors, cur, got, first, second, both, *outs):
-    rows = first.shape[0]
-    for at, out in ((0, first), (rows, second)):
-        out[...] = (cur[at : at + rows, :].astype(F32) + got[at : at + rows, :].astype(F32)).astype(BF16)
-        both[at : at + rows, :] = out[...]
+def last_both_kernel(vectors, cur, got, first, second, both, out):
+    rows = second.shape[0]
+    for at, piece in ((0, first), (rows, second)):
+        piece[:rows, :] = (cur[at : at + rows, :].astype(F32) + got[at : at + rows, :].astype(F32)).astype(BF16)
+        both[at : at + rows, :] = piece[:rows, :]
     own = join_vectors(split_vectors(vectors[...])) + join_vectors(got[2 * rows :, :].astype(F32))
-    for n, out in enumerate(outs):
-        out[...] = own[n, :]
+    first[rows:, :] = split_vectors(own).astype(BF16)
+    out[...] = own
 
 
 def join_kernel(plan, meta, *refs):
@@ -398,15 +389,18 @@
         out[pl.ds(yours, rows), :] = got[got_row : got_row + rows, :].astype(out.dtype)
 
 
-def join_both_kernel(meta, own_a, own_b, got_a, got_b, out_a, out_b, both, far):
-    rows = own_a.shape[0]
+def join_both_kernel(meta, vectors, own_a, own_b, got_a, got_b, out_a, out_b, both, far, *sums):
+    rows = own_b.shape[0]
     for n, bit, own, got, out in ((0, Z0, own_a, got_a, out_a), (1, Y, own_b, got_b, out_b)):
         mine = pl.multiple_of(meta[bit] * rows, rows)
         yours = pl.multiple_of((1 - meta[bit]) * rows, rows)
-        out[pl.ds(mine, rows), :] = own[...]
-        out[pl.ds(yours, rows), :] = got[...]
+        out[pl.ds(mine, rows), :] = own[:rows, :]
+        out[pl.ds(yours, rows), :] = got[:rows, :]
         both[2 * n * rows : 2 * (n + 1) * rows, :] = out[...]
-        far[n * rows : (n + 1) * rows, :] = got[...]
+        far[n * rows : (n + 1) * rows, :] = got[:rows, :]
+    total = join_vectors(split_vectors(vectors[...])) + join_vectors(got_a[rows:, :].astype(F32))
+    for n, out in enumerate(sums):
+        out[...] = total[n, :]
 
 
 def stack_kernel(got_a, got_b, late):
@@ -415,41 +409,42 @@
     late[rows:, :] = got_b[...]
 
 
-def attention_kernel(far, meta, *refs):
+def attention_kernel(far, parts, meta, *refs):
     outs, (block, sems) = refs[-6:-2], refs[-2:]
-    count = 3 if far else 2
     core, side = meta[1], meta[3] ^ far
-    part = block.shape[1] // 2
-    at = pl.multiple_of(side * 2 * part, 8)
+    rows = block.shape[1]
+    count = sum(n for _, n in parts)
+    copies = []
     for other in range(2):
-        pieces = refs[other * count : (other + 1) * count]
-        for packet, bit, inner in ((0, meta[Y], meta[Z0]), (1, meta[Z0], meta[Y])):
-            m = 2 * (core ^ other) + packet
-            rows = slice(packet * part, (packet + 1) * part)
-            if far:
-                size = part // 2
-                for n in range(2):
-                    start = pl.multiple_of(bit * part + (inner ^ n) * size, 8)
-                    block[m, pl.ds(start, size), :] = pieces[n][packet * size : (packet + 1) * size, :].astype(F32)
-            else:
-                block[m, pl.ds(pl.multiple_of(bit * part, 8), part), :] = pieces[0][rows, :].astype(F32)
-            block[m, pl.ds(pl.multiple_of((1 - bit) * part, 8), part), :] = pieces[-1][rows, :].astype(F32)
-            for n, out in enumerate(outs):
-
-                @pl.when(m == n)
-                def _():
-                    pltpu.make_async_copy(block.at[n], out.at[pl.ds(at, 2 * part), :], sems.at[n]).start()
-
-    for n, out in enumerate(outs):
-        pltpu.make_async_copy(block.at[n], out.at[pl.ds(at, 2 * part), :], sems.at[n]).wait()
-
-
-def attention_near_kernel(*refs):
-    attention_kernel(0, *refs)
-
-
-def attention_far_kernel(*refs):
-    attention_kernel(1, *refs)
+        pieces = list(refs[other * count : (other + 1) * count])
+        for late, arrays in parts:
+            here, pieces = pieces[:arrays], pieces[arrays:]
+            size = rows // arrays
+            for packet, bit, inner in ((0, meta[Y], meta[Z0]), (1, meta[Z0], meta[Y])):
+                slot = len(copies)
+                for n, piece in enumerate(here):
+                    at = pl.multiple_of((inner ^ n) * size, 8) if arrays == 2 else 0
+                    block[slot, pl.ds(at, size), :] = piece[packet * size : (packet + 1) * size, :].astype(F32)
+                at = pl.ds(pl.multiple_of((side * 2 + (bit ^ late)) * rows, 8), rows)
+                for m, out in enumerate(outs):
+
+                    @pl.when(2 * (core ^ other) + packet == m)
+                    def _():
+                        pltpu.make_async_copy(block.at[slot], out.at[at, :], sems.at[slot]).start()
+
+                copies.append(pltpu.make_async_copy(block.at[slot], outs[0].at[at, :], sems.at[slot]))
+    for copy in copies:
+        copy.wait()
+
+
+def half_kernel(bit, theirs, meta, piece, *refs):
+    out, block, sem = refs[-3:]
+    rows = piece.shape[0]
+    block[...] = piece[...].astype(F32)
+    at = pl.multiple_of((meta[bit] ^ theirs) * rows, rows)
+    copy = pltpu.make_async_copy(block, out.at[pl.ds(at, rows), :], sem)
+    copy.start()
+    copy.wait()
 
 
 def swap(v, axis, size, bits):
@@ -519,8 +514,10 @@
     )
     gn_there = across(gn_here, bits=2)
     moved_got = across(moved_rows, bits=1)
-    moved_here = call("MV", moved_kernel, [act_own, act_other, w_down, down_other], [rows(slots)], after=[gn_here])[0]
-    moved_there = across(moved_here, bits=2)
+
+    def moved_part(after):
+        moved = call("MV", moved_kernel, [act_own, act_other, w_down, down_other], [rows(slots)], after=after)[0]
+        return moved, across(moved, bits=2)
 
     def mlp_grads(outs, after):
         return call(
@@ -533,25 +530,27 @@
         return call(
             "AB", attend_back_kernel,
             [
-                chosen, attended, gain_attn, gain_mlp, gn_here, gn_there, rate, seen_here, seen_there,
-                query, keys, values, probs, w_query, w_key, w_value, w_out, meta,
+                chosen, attended, gain_mlp, gn_here, gn_there, rate, seen_here, seen_there,
+                query, keys, values, probs, w_out, meta,
             ],
-            [rows(2 * slots)] * 2 + [wide(slots), wide(8)], specs=[VMEM] * 17 + [SMEM],
-            scratch=[pltpu.VMEM((slots, width), BF16)] * 4, after=after,
-        )
-
-    def attend_grads(mine, got, vectors, outs, after):
-        more = [] if vectors is None else [vectors]
+            [rows(2 * slots)] * 2 + [rows(slots)] * 3 + [wide(slots), wide(8)], specs=[VMEM] * 13 + [SMEM],
+            scratch=[pltpu.VMEM((slots, width), BF16)], after=after,
+        )
+
+    def attend_grads(mine, got, outs, after):
         return call(
-            "FA", functools.partial(attend_grads_kernel, vectors is None),
-            [meta, *more, early_rows, early_got, mine, got], outs,
-            specs=[SMEM] + [VMEM] * (4 + len(more)), scratch=[pltpu.VMEM((width, width), F32)], after=after,
-        )
-
-    def slot_sums(grad_sum, small, after):
+            "FA", functools.partial(attend_grads_kernel, len(outs) == 1),
+            [meta, early_rows, early_got, mine, got], outs,
+            specs=[SMEM] + [VMEM] * 4, scratch=[pltpu.VMEM((width, width), F32)], after=after,
+        )
+
+    def slot_sums(back, moved_here, moved_there, after):
         update, grad_chosen, vectors = call(
             "SL", slots_kernel,
-            [chosen, attended, rate, seen_here, seen_there, moved_here, moved_there, w_router, grad_sum, small],
+            [
+                chosen, attended, rate, seen_here, seen_there, moved_here, moved_there, w_router, gain_attn,
+                *back[:3], w_query, w_key, w_value, *back[3:],
+            ],
             [rows(slots), rows(slots), wide(8)], after=after,
         )
         return update, grad_chosen, vectors + across(vectors, bits=1)
@@ -565,9 +564,9 @@
     if batch != 8:
         whole = ((width, width), F32)
         down, up = mlp_grads([whole] * 2, [])
-        mine, theirs, grad_sum, small = attend_back([])
-        update, grad_chosen, vectors = slot_sums(grad_sum, small, [])
-        attention = attend_grads(mine, across(theirs, bits=1), None, [whole], [])[0]
+        mine, theirs, *back = attend_back([])
+        update, grad_chosen, vectors = slot_sums(back, *moved_part([]), [])
+        attention = attend_grads(mine, across(theirs, bits=1), [whole], [])[0]
         down, up, attention, vectors = lax.psum((down, up, attention, vectors), "batch")
         attention = lax.all_gather(attention, "seq").reshape(2, 2, 2, half, width)
         return (
@@ -584,7 +583,6 @@
         if vectors is not None:
             kernel = functools.partial(reduce_small_kernel, plan, len(gots), len(sends))
             ins = [meta, vectors, *keeps, *gots]
-            outs.append(wide(8))
         return call(tag, kernel, ins, outs, specs=[SMEM] + [VMEM] * (len(ins) - 1), after=after)
 
     def join(tag, bit, own, got, dtype=BF16, after=(), token=False):
@@ -594,12 +592,20 @@
             [((2 * count, width), dtype)], specs=[SMEM] + [VMEM] * 2, after=after, token=token,
         )
 
-    def attention(tag, kernel, pieces, outs=(), after=()):
+    def attention(tag, far, parts, pieces, outs=(), after=()):
         return call(
-            tag, kernel, [meta, *pieces, *outs], [wide(width)] * 4,
+            tag, functools.partial(attention_kernel, far, parts), [meta, *pieces, *outs], [wide(width)] * 4,
             specs=[SMEM] + [VMEM] * len(pieces) + [HBM] * len(outs), out_specs=[HBM] * 4,
-            scratch=[pltpu.VMEM((4, half, width), F32), pltpu.SemaphoreType.DMA((4,))],
-            aliases={1 + len(pieces) + m: m for m in range(len(outs))}, after=after, token=True,
+            scratch=[pltpu.VMEM((4 * len(parts), half // 2, width), F32), pltpu.SemaphoreType.DMA((4 * len(parts),))],
+            aliases={1 + len(pieces) + m: m for m in range(len(outs))}, after=after, token=True, name=tag,
+        )
+
+    def write_half(tag, bit, theirs, piece, outs=(), after=()):
+        return call(
+            tag, functools.partial(half_kernel, bit, theirs), [meta, piece, *outs], [wide(width)],
+            specs=[SMEM, VMEM] + [HBM] * len(outs), out_specs=[HBM],
+            scratch=[pltpu.VMEM(piece.shape, F32), pltpu.SemaphoreType.DMA],
+            aliases={2: 0} if outs else {}, after=after, token=True,
         )
 
     v, moved = {}, {}
@@ -608,7 +614,9 @@
         moved[name] = value
         return value
 
-    moved["M"] = moved_there
+    def step_mv(after):
+        v["moved"], moved["M"] = moved_part(after)
+        return v["moved"]
 
     def step_f(after):
         d, u, v["d_keep"], v["u_keep"] = mlp_grads([rows(half)] * 2 + [wide(half)] * 2, after)
@@ -616,20 +624,21 @@
         return v["d_keep"]
 
     def step_ab(after):
-        v["mine"], theirs, v["sum"], v["small"] = attend_back(after)
+        v["mine"], theirs, *v["back"] = attend_back(after)
         v["got"] = kept("th", across(theirs, bits=1))
-        return v["small"]
+        return v["back"][-1]
 
     def step_sl(after):
-        v["update"], v["grad_chosen"], v["vectors"] = slot_sums(v["sum"], v["small"], after)
+        v["update"], v["grad_chosen"], v["vectors"] = slot_sums(
+            v["back"], v["moved"], moved["M"], after
+        )
         v["update_core"] = kept("up", across(v["update"], bits=1))
         v["chosen_core"] = kept("gc", across(v["grad_chosen"], bits=1))
         return v["update"]
 
     def step_fa(after):
-        a, b, v["a_keep"], v["b_keep"], v["vectors"] = attend_grads(
-            v["mine"], v["got"], v["vectors"],
-            [rows(half // 2 + 16), rows(half // 2), wide(half // 2), wide(half // 2), wide(8)], after,
+        a, b, v["a_keep"], v["b_keep"] = attend_grads(
+            v["mine"], v["got"], [rows(half // 2)] * 2 + [wide(half // 2)] * 2, after
         )
         v["a"], v["b"] = kept("a1", along(a, 0)), kept("b1", along(b, 1))
         return v["a_keep"]
@@ -645,10 +654,10 @@
         return v["u_keep"]
 
     def step_a2(after):
-        a, b, v["a_keep"], v["b_keep"], v["vectors"] = reduce(
+        a, b, v["a_keep"], v["b_keep"] = reduce(
             "A2", [v["a_keep"], v["b_keep"]], [v["a"], v["b"]],
             [(half // 2, Z0, 0, 0, 0, 0), (half // 2, Y, 1, 0, 1, 0)],
-            [half // 4 + 16, half // 4], after, v["vectors"],
+            [half // 4, half // 4 + 16], after, v["vectors"],
         )
         v["a"], v["b"] = kept("a2", along(a, 1)), kept("b2", along(b, 0))
         return v["a_keep"]
@@ -678,18 +687,19 @@
         return step
 
     def step_a4(after):
-        v["a_all"], v["b_all"], near, *v["vectors"] = call(
+        v["a_all"], v["b_all"], near, v["vectors"] = call(
             "A4", last_both_kernel, [v["vectors"], v["ab_cur"], v["ab"]],
-            [rows(half // 4)] * 2 + [rows(half // 2)] + [((width,), F32)] * 3, after=after,
+            [rows(half // 4 + 16), rows(half // 4), rows(half // 2), wide(8)], after=after,
         )
         v["a"], v["b"] = kept("a5", along(v["a_all"], 1)), kept("b5", along(v["b_all"], 0))
         v["near"] = kept("x1", across(near, bits=2))
         return v["a_all"]
 
     def step_a5(after):
-        a, b, v["early"], far = call(
-            "A5", join_both_kernel, [meta, v["a_all"], v["b_all"], v["a"], v["b"]],
-            [rows(half // 2)] * 2 + [rows(half), rows(half // 2)], specs=[SMEM] + [VMEM] * 4, after=after,
+        a, b, v["early"], far, *v["vectors"] = call(
+            "A5", join_both_kernel, [meta, v["vectors"], v["a_all"], v["b_all"], v["a"], v["b"]],
+            [rows(half // 2)] * 2 + [rows(half), rows(half // 2)] + [((width,), F32)] * 3,
+            specs=[SMEM] + [VMEM] * 5, after=after,
         )
         v["a"], v["b"] = kept("a6", along(a, 0)), kept("b6", along(b, 1))
         v["far"] = kept("x2", across(far, bits=2))
@@ -710,9 +720,11 @@
 
         return step
 
-    def sixth(tag, key, bit):
+    def halves(tag, key, bit, theirs):
         def step(after):
-            v["grad_" + key], token = join(tag, bit, v[key + "_all"], v[key], F32, after, token=True)
+            outs = [v["grad_" + key]] if theirs else []
+            piece = v[key] if theirs else v[key + "_all"]
+            v["grad_" + key], token = write_half(tag, bit, theirs, piece, outs, after)
             return token
 
         return step
@@ -725,29 +737,37 @@
         return step
 
     def step_at0(after):
-        *v["grads"], token = attention(
-            "AT0", attention_near_kernel, [v["early"], v["late"], v["early_core"], v["late_core"]], after=after
-        )
+        pieces = [v["early"], v["late"], v["early_core"], v["late_core"]]
+        *v["grads"], token = attention("AT0", 0, ((0, 1), (1, 1)), pieces, after=after)
+        return token
+
+    def step_xe(after):
+        near, far, *_ = lax.optimization_barrier((v["near"], v["far"], *after))
+        v["side_early"] = [near, far, kept("g1", across(near, bits=1)), kept("g2", across(far, bits=1))]
+        return after[0]
+
+    def step_ate(after):
+        *v["grads"], token = attention("ATE", 1, ((0, 2),), v["side_early"], v["grads"], after)
         return token
 
     def step_xc(after):
         side, *_ = lax.optimization_barrier((v["side"], *after))
-        v["pieces"] = [v["near"], v["far"], side]
-        v["pieces"] += [across(piece, bits=1) for piece in v["pieces"]]
+        v["side_late"] = [side, across(side, bits=1)]
         return after[0]
 
-    def step_at1(after):
-        *v["grads"], token = attention("AT1", attention_far_kernel, v["pieces"], v["grads"], after)
+    def step_atl(after):
+        *v["grads"], token = attention("ATL", 1, ((1, 1),), v["side_late"], v["grads"], after)
         return token
 
     steps = dict(
         F=step_f, AB=step_ab, SL=step_sl, FA=step_fa, R2=step_r2, R2U=step_r2u, A2=step_a2, A3=step_a3,
         D3=third("D3", "d"), U3=third("U3", "u"), D4=fourth("D4", "d", 1), U4=fourth("U4", "u", 0), A4=step_a4,
-        A5=step_a5, A6=step_a6, D5=fifth("D5", "d", Z0, 0), U5=fifth("U5", "u", Y, 1), DU=sixth("DU", "d", Y),
-        UU=sixth("UU", "u", Z0), P1=place("P1", "output", tokens, "update", "update_core"),
-        P2=place("P2", "grad_tokens", cotangent, "grad_chosen", "chosen_core"), AT0=step_at0, XC=step_xc, AT1=step_at1,
+        A5=step_a5, A6=step_a6, D5=fifth("D5", "d", Z0, 0), U5=fifth("U5", "u", Y, 1), DH=halves("DH", "d", Y, 0),
+        DU=halves("DU", "d", Y, 1), UH=halves("UH", "u", Z0, 0), UU=halves("UU", "u", Z0, 1), MV=step_mv, XE=step_xe,
+        ATE=step_ate, ATL=step_atl, P1=place("P1", "output", tokens, "update", "update_core"),
+        P2=place("P2", "grad_tokens", cotangent, "grad_chosen", "chosen_core"), AT0=step_at0, XC=step_xc,
     )
-    after = [moved_here]
+    after = []
     for name in ORDER:
         after = [steps[name](after + [moved[key] for key in HOLD.get(name, ())])]
     return (

time: 157 us -> 148 us (0.943)
  waiting for transfers between devices: 72.2 us -> 57.7 us
  Pallas kernels: 43.9 us -> 47 us
  starting transfers between devices: 38.1 us -> 39.8 us
    ppermute x46, waiting for transfers between devices: 72.2 us -> 57.7 us  [swap(): return lax.ppermute(v, axis, [(i, i ^ bits) for i in range(size)])]
    pallas_call x28 -> x31, Pallas kernels: 43.9 us -> 47 us  [call(): pl.pallas_call(run, out_shape=tuple(shapes), in_specs=(specs or [VMEM] *...]
    ppermute x46, starting transfers between devices: 38.1 us -> 39.8 us  [swap(): return lax.ppermute(v, axis, [(i, i ^ bits) for i in range(size)])]
  transfers between devices with their start and end apart: 46 -> 46, of which waited for: 22 -> 21; matrix products, arithmetic and copies ran while one was open for 0% -> 0% of each run, Pallas kernels for 25% -> 29%
where the time goes in v4:
time: 148 us; the launch traced here: 147 us
  waiting for transfers between devices  57.7 us (39%)
  Pallas kernels  47 us (32%)
  starting transfers between devices  39.8 us (27%)
    ppermute x46, waiting for transfers between devices, swap(): return lax.ppermute(v, axis, [(i, i ^ bits) for i in range(size)])  57.7 us
    pallas_call x31, Pallas kernels, call(): pl.pallas_call(run, out_shape=tuple(shapes), in_specs=(specs or [VMEM] *...  47 us
    ppermute x46, starting transfers between devices, swap(): return lax.ppermute(v, axis, [(i, i ^ bits) for i in range(size)])  39.8 us
  transfers between devices with their start and end apart: 46, of which 21 were waited for; matrix products, arithmetic and copies ran while one was open for 0% of the time, Pallas kernels for 29%

profile of v4, /device:TPU:0, one launch (start us, length us, event | category | flops | bytes accessed | tf_op | source)
XLA Modules:
  0.0 146.9 jit_solution(6687787796217112612)
XLA Ops:
  0.6 3.0 %collective-permute-start.1 = (s32[2,64]{1,0:T(2,128)}, s32[2,64]{1,0:T(2,128)S(1)}, u32[]{:S(2)}, u32[]{:S(2)}) collective-permute-start(s32[2,64]{1,0:T(2,128)} %refs_4_.1), channel_id=1, source_target_pairs={{0,2},{1,3},{2,0},{3,1},{4,6},{5,7},{6,4},{7,5},{8,10},{9,11},{10,... | collective-permute-start | bytes 1544 | tf_op jit(solution)/shard_map/ppermute | solution.py:451
  4.5 0.9 collective-permute-done.1.refs_2_
  5.4 1.4 collective-permute-done.2.refs_3_
  6.9 0.7 copy-done.9
  7.5 2.7 %select_kernel.1 = (bf16[256,768]{1,0:T(8,128)(2,1)S(1)}, bf16[256,768]{1,0:T(8,128)(2,1)S(1)}, bf16[256,512]{1,0:T(8,128)(2,1)S(1)}, bf16[256,512]{1,0:T(8,128)(2,1)S(1)}) custom-call(s32[11]{0:T(128)S(1)} %stack.44.refs_0_.refs_13_, s32[2,64]{1,0:T(2,128)S(1)} %collective-permute-done.refs_1_, s32[2,64]{1,0:T(2,128)S(1)} %collective-permute-done.1.refs_2_, ...), custom_call_target="tpu_custom_call" | custom-call | flops 8000000000 | bytes 1 | tf_op jit(solution)/shard_map/select_kernel/pallas_call | solution.py:55
  10.4 0.6 collective-permute-start.3
  10.9 1.1 select_again_kernel.1
  13.0 0.6 collective-permute-done.6
  14.0 1.1 collective-permute-start.8
  15.1 9.7 %collective-permute-done.4.refs_3_ = bf16[256,768]{1,0:T(8,128)(2,1)S(1)} collective-permute-done((bf16[256,768]{1,0:T(8,128)(2,1)S(1)}, bf16[256,768]{1,0:T(8,128)(2,1)S(1)}, u32[]{:S(2)}, u32[]{:S(2)}) %collective-permute-start.4) | collective-permute-done | bytes 393248 | tf_op jit(solution)/shard_map/ppermute | solution.py:451
  24.8 6.6 %attend_kernel.1 = (bf16[256,768]{1,0:T(8,128)(2,1)S(1)}, bf16[256,768]{1,0:T(8,128)(2,1)}, bf16[256,768]{1,0:T(8,128)(2,1)S(1)}, bf16[256,768]{1,0:T(8,128)(2,1...) custom-call(s32[11]{0:T(128)S(1)} %stack.44.refs_0_.refs_13_, ...), custom_call_target="tpu_custom_call" | custom-call | flops 600000000 | bytes 1 | tf_op jit(solution)/shard_map/attend_kernel/pallas_call | solution.py:55
  31.4 0.9 collective-permute-done.8.refs_2_.refs_7_.refs_4_
  32.4 1.8 %mlp_kernel.1 = (bf16[256,768]{1,0:T(8,128)(2,1)S(1)}, bf16[512,768]{1,0:T(8,128)(2,1)S(1)}, bf16[256,768]{1,0:T(8,128)(2,1)S(1)}) custom-call(f32[256,128]{1,0:T(8,128)S(1)} %get-tuple-element.111.refs_0_.refs_5_.refs_2_, bf16[256,768]{1,0:T(8,128)(2,1)S(1)} %maximum_add_fusion.refs_13_.refs_1_.refs_6_.refs_3_, ...), custom_call_target="tpu_custom_call" | custom-call | flops 4000000000 | bytes 1 | tf_op jit(solution)/shard_map/mlp_kernel/pallas_call | solution.py:55
  35.3 1.2 collective-permute-done.12.refs_6_
  36.5 1.1 collective-permute-done.11.refs_5_
  37.6 2.0 %mlp_grads_kernel.1 = (bf16[384,768]{1,0:T(8,128)(2,1)S(1)}, bf16[384,768]{1,0:T(8,128)(2,1)S(1)}, f32[384,768]{1,0:T(8,128)S(1)}, f32[384,768]{1,0:T(8,128)S(1)}) custom-call(s32[11]{0:T(128)S(1)} %stack.44.refs_0_.refs_13_, bf16[256,768]{1,0:T(8,128)(2,1)S(1)} %get-tuple-element.112.refs_1_.refs_0_, bf16[256,768]{1,0:T(8,128)(2,1)S(1)} %get-tuple-element.121.refs_2_, ...), custom_call_target="tpu_custom_call" | custom-call | flops 300000000 | bytes 1 | tf_op jit(solution)/shard_map/mlp_grads_kernel/pallas_call | solution.py:55
  39.6 1.6 %collective-permute-start.16 = (bf16[384,768]{1,0:T(8,128)(2,1)S(1)}, bf16[384,768]{1,0:T(8,128)(2,1)S(1)}, u32[]{:S(2)}, u32[]{:S(2)}) collective-permute-start(bf16[384,768]{1,0:T(8,128)(2,1)S(1)} %get-tuple-element.133), channel_id=1, source_target_pairs={{0,4},{4,0},{8,12},{12,8},{16,20},{20,16},{24,28},{28,24},{1,5},{5... | collective-permute-start | bytes 1769480 | tf_op jit(solution)/shard_map/ppermute | solution.py:451
  41.2 1.6 %collective-permute-start.17 = (bf16[384,768]{1,0:T(8,128)(2,1)S(1)}, bf16[384,768]{1,0:T(8,128)(2,1)S(1)}, u32[]{:S(2)}, u32[]{:S(2)}) collective-permute-start(bf16[384,768]{1,0:T(8,128)(2,1)S(1)} %get-tuple-element.134), channel_id=1, source_target_pairs={{0,8},{4,12},{8,0},{12,4},{16,24},{20,28},{24,16},{28,20},{1,9},{5... | collective-permute-start | bytes 1769480 | tf_op jit(solution)/shard_map/ppermute | solution.py:451
  42.8 3.1 %collective-permute-done.10.refs_4_ = bf16[256,768]{1,0:T(8,128)(2,1)S(1)} collective-permute-done((bf16[256,768]{1,0:T(8,128)(2,1)S(1)}, bf16[256,768]{1,0:T(8,128)(2,1)S(1)}, u32[]{:S(2)}, u32[]{:S(2)}) %collective-permute-start.10) | collective-permute-done | bytes 393248 | tf_op jit(solution)/shard_map/ppermute | solution.py:451
  45.8 5.5 %attend_back_kernel.1 = (bf16[512,768]{1,0:T(8,128)(2,1)S(1)}, bf16[512,768]{1,0:T(8,128)(2,1)S(1)}, bf16[256,768]{1,0:T(8,128)(2,1)S(1)}, bf16[256,768]{1,0:T(8...) custom-call(bf16[256,768]{1,0:T(8,128)(2,1)S(1)} %get-tuple-element.109.refs_0_, ...), custom_call_target="tpu_custom_call" | custom-call | flops 1 | bytes 1 | tf_op jit(solution)/shard_map/attend_back_kernel/pallas_call | solution.py:55
  51.4 0.8 moved_kernel.1.refs_3_.refs_5_
  52.2 0.6 collective-permute-start.13
  52.8 2.3 %collective-permute-done.16.refs_2_ = bf16[384,768]{1,0:T(8,128)(2,1)S(1)} collective-permute-done((bf16[384,768]{1,0:T(8,128)(2,1)S(1)}, bf16[384,768]{1,0:T(8,128)(2,1)S(1)}, u32[]{:S(2)}, u32[]{:S(2)}) %collective-permute-start.16) | collective-permute-done | bytes 589856 | tf_op jit(solution)/shard_map/ppermute | solution.py:451
  55.0 1.2 collective-permute-done.17.refs_4_.refs_2_
  56.3 0.6 reduce_kernel.2
  56.9 1.6 %collective-permute-start.22 = (bf16[192,768]{1,0:T(8,128)(2,1)S(1)}, bf16[192,768]{1,0:T(8,128)(2,1)S(1)}, u32[]{:S(2)}, u32[]{:S(2)}) collective-permute-start(bf16[192,768]{1,0:T(8,128)(2,1)S(1)} %get-tuple-element.142), channel_id=1, source_target_pairs={{0,8},{4,12},{8,0},{12,4},{16,24},{20,28},{24,16},{28,20},{1,9},{5... | collective-permute-start | bytes 884744 | tf_op jit(solution)/shard_map/ppermute | solution.py:451
  58.6 1.5 %attend_grads_kernel.1 = (bf16[192,768]{1,0:T(8,128)(2,1)S(1)}, bf16[192,768]{1,0:T(8,128)(2,1)S(1)}, f32[192,768]{1,0:T(8,128)S(1)}, f32[192,768]{1,0:T(8,128)S(1)}) custom-call(s32[11]{0:T(128)S(1)} %stack.44.refs_0_.refs_13_, bf16[512,768]{1,0:T(8,128)(2,1)S(1)} %get-tuple-element.130.refs_1_, bf16[512,768]{1,0:T(8,128)(2,1)S(1)} %collective-permute-done.14.refs_2_, ...), custom_call_target="tpu_custom_call" | custom-call | flops 1 | bytes 1 | tf_op jit(solution)/shard_map/attend_grads_kernel/pallas_call | solution.py:55
  60.1 0.6 collective-permute-start.20
  61.1 2.7 %collective-permute-done.13.refs_6_ = bf16[256,768]{1,0:T(8,128)(2,1)S(1)} collective-permute-done((bf16[256,768]{1,0:T(8,128)(2,1)S(1)}, bf16[256,768]{1,0:T(8,128)(2,1)S(1)}, u32[]{:S(2)}, u32[]{:S(2)}) %collective-permute-start.13) | collective-permute-done | bytes 393248 | tf_op jit(solution)/shard_map/ppermute | solution.py:451
  63.8 1.6 %slots_kernel.1 = (bf16[256,768]{1,0:T(8,128)(2,1)S(1)}, bf16[256,768]{1,0:T(8,128)(2,1)S(1)}, f32[8,768]{1,0:T(8,128)S(1)}) custom-call(bf16[256,768]{1,0:T(8,128)(2,1)S(1)} %get-tuple-element.109.refs_0_, f32[256,768]{1,0:T(8,128)S(1)} %get-tuple-element.110.refs_1_, f32[256,128]{1,0:T(8,128)S(1)} %get-tuple-element.111.refs_0_.refs_5_.refs_2_, ...), custom_call_target="tpu_custom_call" | custom-call | flops 1000000000 | bytes 1 | tf_op jit(solution)/shard_map/slots_kernel/pallas_call | solution.py:55
  66.0 1.0 collective-permute-done.22.refs_1_
  67.0 2.6 %collective-permute-start.26 = (bf16[192,768]{1,0:T(8,128)(2,1)S(1)}, bf16[192,768]{1,0:T(8,128)(2,1)S(1)}, u32[]{:S(2)}, u32[]{:S(2)}) collective-permute-start(bf16[192,768]{1,0:T(8,128)(2,1)S(1)} %round_kernel.2.refs_6_.refs_0_), channel_id=1, source_target_pairs={{0,16},{4,20},{8,24},{12,28},{16,0},{20,4},{24,8},{28,12},{1,17},{... | collective-permute-start | bytes 884744 | tf_op jit(solution)/shard_map/ppermute | solution.py:451
  69.7 5.4 %collective-permute-done.21.refs_5_ = bf16[192,768]{1,0:T(8,128)(2,1)S(1)} collective-permute-done((bf16[192,768]{1,0:T(8,128)(2,1)S(1)}, bf16[192,768]{1,0:T(8,128)(2,1)S(1)}, u32[]{:S(2)}, u32[]{:S(2)}) %collective-permute-start.21) | collective-permute-done | bytes 294944 | tf_op jit(solution)/shard_map/ppermute | solution.py:451
  75.1 0.7 reduce_small_kernel.1
  76.0 8.7 %collective-permute-done.23.refs_3_ = bf16[96,768]{1,0:T(8,128)(2,1)S(1)} collective-permute-done((bf16[96,768]{1,0:T(8,128)(2,1)S(1)}, bf16[96,768]{1,0:T(8,128)(2,1)S(1)}, u32[]{:S(2)}, u32[]{:S(2)}) %collective-permute-start.23) | collective-permute-done | bytes 147488 | tf_op jit(solution)/shard_map/ppermute | solution.py:451
  85.1 0.6 reduce_kernel.3
  85.7 2.0 %collective-permute-start.27 = (bf16[192,768]{1,0:T(8,128)(2,1)S(1)}, bf16[192,768]{1,0:T(8,128)(2,1)S(1)}, u32[]{:S(2)}, u32[]{:S(2)}) collective-permute-start(bf16[192,768]{1,0:T(8,128)(2,1)S(1)} %get-tuple-element.151), channel_id=1, source_target_pairs={{0,4},{4,0},{8,12},{12,8},{16,20},{20,16},{24,28},{28,24},{1,5},{5... | collective-permute-start | bytes 884744 | tf_op jit(solution)/shard_map/ppermute | solution.py:451
  87.7 2.5 %collective-permute-start.29 = (bf16[192,768]{1,0:T(8,128)(2,1)S(1)}, bf16[192,768]{1,0:T(8,128)(2,1)S(1)}, u32[]{:S(2)}, u32[]{:S(2)}) collective-permute-start(bf16[192,768]{1,0:T(8,128)(2,1)S(1)} %last_kernel.2.refs_3_.refs_1_), channel_id=1, source_target_pairs={{0,8},{4,12},{8,0},{12,4},{16,24},{20,28},{24,16},{28,20},{1,9},{5... | collective-permute-start | bytes 884744 | tf_op jit(solution)/shard_map/ppermute | solution.py:451
  90.2 2.3 %place_kernel.2 = (bf16[2,512,768]{2,1,0:T(8,128)(2,1)}, f32[8,128]{1,0:T(8,128)S(1)}) custom-call(s32[11]{0:T(128)S(1)} %stack.44.refs_0_.refs_13_, bf16[256,512]{1,0:T(8,128)(2,1)S(1)} %get-tuple-element.102.refs_1_, bf16[256,512]{1,0:T(8,128)(2,1)S(1)} %get-tuple-element.103.refs_2_, bf16[2,512,768]{2,1,0:T(8,128)(2,1)S(1)} %copy-done, ...), custom_call_target="tpu_custom_call" | custom-call | flops 100000000 | bytes 1 | tf_op jit(solution)/shard_map/place_kernel/pallas_call | solution.py:55
  92.5 7.5 %collective-permute-done.29.refs_3_.refs_2_ = bf16[192,768]{1,0:T(8,128)(2,1)S(1)} collective-permute-done((bf16[192,768]{1,0:T(8,128)(2,1)S(1)}, bf16[192,768]{1,0:T(8,128)(2,1)S(1)}, u32[]{:S(2)}, u32[]{:S(2)}) %collective-permute-start.29) | collective-permute-done | bytes 294944 | tf_op jit(solution)/shard_map/ppermute | solution.py:451
  100.1 5.7 %collective-permute-start.34 = (bf16[192,768]{1,0:T(8,128)(2,1)S(1)}, bf16[192,768]{1,0:T(8,128)(2,1)S(1)}, u32[]{:S(2)}, u32[]{:S(2)}) collective-permute-start(bf16[192,768]{1,0:T(8,128)(2,1)S(1)} %round_kernel.3.refs_3_.refs_0_), channel_id=1, source_target_pairs={{0,16},{4,20},{8,24},{12,28},{16,0},{20,4},{24,8},{28,12},{1,17},{... | collective-permute-start | bytes 884744 | tf_op jit(solution)/shard_map/ppermute | solution.py:451
  105.9 2.5 %collective-permute-start.30 = (bf16[112,768]{1,0:T(8,128)(2,1)S(1)}, bf16[112,768]{1,0:T(8,128)(2,1)S(1)}, u32[]{:S(2)}, u32[]{:S(2)}) collective-permute-start(bf16[112,768]{1,0:T(8,128)(2,1)S(1)} %get-tuple-element.154.refs_6_.refs_2_), channel_id=1, source_target_pairs={{0,8},{4,12},{8,0},{12,4},{16,24},{20,28},{24,16},{28,20},{1,9},{5... | collective-permute-start | bytes 516104 | tf_op jit(solution)/shard_map/ppermute | solution.py:451
  108.4 0.7 collective-permute-start.31
  109.6 2.3 %place_kernel.3 = (bf16[2,512,768]{2,1,0:T(8,128)(2,1)}, f32[8,128]{1,0:T(8,128)S(1)}) custom-call(s32[11]{0:T(128)S(1)} %stack.44.refs_0_.refs_13_, bf16[256,512]{1,0:T(8,128)(2,1)S(1)} %get-tuple-element.102.refs_1_, bf16[256,512]{1,0:T(8,128)(2,1)S(1)} %get-tuple-element.103.refs_2_, bf16[2,512,768]{2,1,0:T(8,128)(2,1)S(1)} %copy-done.7, ...), custom_call_target="tpu_custom_call" | custom-call | flops 1000000000 | bytes 1 | tf_op jit(solution)/shard_map/place_kernel/pallas_call | solution.py:55
  111.9 1.6 %collective-permute-done.31.refs_5_ = bf16[96,768]{1,0:T(8,128)(2,1)S(1)} collective-permute-done((bf16[96,768]{1,0:T(8,128)(2,1)S(1)}, bf16[96,768]{1,0:T(8,128)(2,1)S(1)}, u32[]{:S(2)}, u32[]{:S(2)}) %collective-permute-start.31) | collective-permute-done | bytes 147488 | tf_op jit(solution)/shard_map/ppermute | solution.py:451
  113.6 1.2 join_both_kernel.1
  114.7 1.4 collective-permute-start.32
  116.1 1.8 %collective-permute-start.33 = (bf16[192,768]{1,0:T(8,128)(2,1)S(1)}, bf16[192,768]{1,0:T(8,128)(2,1)S(1)}, u32[]{:S(2)}, u32[]{:S(2)}) collective-permute-start(bf16[192,768]{1,0:T(8,128)(2,1)S(1)} %get-tuple-element.164), channel_id=1, source_target_pairs={{0,8},{4,12},{8,0},{12,4},{16,24},{20,28},{24,16},{28,20},{1,9},{5... | collective-permute-start | bytes 884744 | tf_op jit(solution)/shard_map/ppermute | solution.py:451
  118.4 3.1 %collective-permute-done.32.refs_0_ = bf16[192,768]{1,0:T(8,128)(2,1)S(1)} collective-permute-done((bf16[192,768]{1,0:T(8,128)(2,1)S(1)}, bf16[192,768]{1,0:T(8,128)(2,1)S(1)}, u32[]{:S(2)}, u32[]{:S(2)}) %collective-permute-start.32) | collective-permute-done | bytes 294944 | tf_op jit(solution)/shard_map/ppermute | solution.py:451
  122.0 0.8 collective-permute-done.33.refs_1_
  123.0 0.7 collective-permute-start.35
  123.7 1.1 collective-permute-done.38.refs_2_
  124.8 0.6 join_kernel.2.refs_3_.refs_1_
  125.4 1.4 collective-permute-start.45
  126.7 0.6 join_kernel.3.refs_5_.refs_1_
  127.4 1.7 %collective-permute-start.44 = (bf16[384,768]{1,0:T(8,128)(2,1)S(1)}, bf16[384,768]{1,0:T(8,128)(2,1)S(1)}, u32[]{:S(2)}, u32[]{:S(2)}) collective-permute-start(bf16[384,768]{1,0:T(8,128)(2,1)S(1)} %join_kernel.3.refs_5_.refs_1_), channel_id=1, source_target_pairs={{0,4},{4,0},{8,12},{12,8},{16,20},{20,16},{24,28},{28,24},{1,5},{5... | collective-permute-start | bytes 1769480 | tf_op jit(solution)/shard_map/ppermute | solution.py:451
  129.1 2.8 %AT0.1 = (f32[768,768]{1,0:T(8,128)}, f32[768,768]{1,0:T(8,128)}, f32[768,768]{1,0:T(8,128)}, f32[768,768]{1,0:T(8,128)}, f32[8,128]{1,0:T(8,128)S(1)}) custom-call(s32[11]{0:T(128)S(1)} %stack.44.refs_0_.refs_13_, bf16[384,768]{1,0:T(8,128)(2,1)S(1)} %get-tuple-element.165.refs_2_.refs_1_, bf16[384,768]{1,0:T(8,128)(2,1)S(1)} %stack_kernel.1.refs_3_.refs_2_, ...), custom_call_target="tpu_custom_call" | custom-call | flops 4000000000 | bytes 1 | tf_op jit(solution)/shard_map/AT0/pallas_call | solution.py:55
  131.9 1.6 %half_kernel.4 = (f32[768,768]{1,0:T(8,128)}, f32[8,128]{1,0:T(8,128)S(1)}) custom-call(s32[11]{0:T(128)S(1)} %stack.44.refs_0_.refs_13_, bf16[384,768]{1,0:T(8,128)(2,1)S(1)} %join_kernel.2.refs_3_.refs_1_, f32[8,128]{1,0:T(8,128)S(1)} %get-tuple-element.168.refs_2_), custom_call_target="tpu_custom_call" | custom-call | flops 1 | bytes 1 | tf_op jit(solution)/shard_map/half_kernel/pallas_call | solution.py:55
  134.2 1.6 %half_kernel.5 = (f32[768,768]{1,0:T(8,128)}, f32[8,128]{1,0:T(8,128)S(1)}) custom-call(s32[11]{0:T(128)S(1)} %stack.44.refs_0_.refs_13_, bf16[384,768]{1,0:T(8,128)(2,1)S(1)} %join_kernel.3.refs_5_.refs_1_, f32[8,128]{1,0:T(8,128)S(1)} %get-tuple-element.169.refs_2_), custom_call_target="tpu_custom_call" | custom-call | flops 1 | bytes 1 | tf_op jit(solution)/shard_map/half_kernel/pallas_call | solution.py:55
  135.8 2.0 %ATE.1 = (f32[768,768]{1,0:T(8,128)}, f32[768,768]{1,0:T(8,128)}, f32[768,768]{1,0:T(8,128)}, f32[768,768]{1,0:T(8,128)}, f32[8,128]{1,0:T(8,128)S(1)}) custom-call(s32[11]{0:T(128)S(1)} %stack.44.refs_0_.refs_13_, ...), custom_call_target="tpu_custom_call", output_to_operand_aliasing={{0}: (5, {}), {1}: (6, {}), {2}: (7, {}), {3}: (8, {})} | custom-call | flops 100000000 | bytes 1 | tf_op jit(solution)/shard_map/ATE/pallas_call | solution.py:55
  137.9 3.0 %collective-permute-done.35.refs_1_ = bf16[384,768]{1,0:T(8,128)(2,1)S(1)} collective-permute-done((bf16[384,768]{1,0:T(8,128)(2,1)S(1)}, bf16[384,768]{1,0:T(8,128)(2,1)S(1)}, u32[]{:S(2)}, u32[]{:S(2)}) %collective-permute-start.35) | collective-permute-done | bytes 589856 | tf_op jit(solution)/shard_map/ppermute | solution.py:451
  140.8 1.6 %half_kernel.6 = (f32[768,768]{1,0:T(8,128)}, f32[8,128]{1,0:T(8,128)S(1)}) custom-call(s32[11]{0:T(128)S(1)} %stack.44.refs_0_.refs_13_, bf16[384,768]{1,0:T(8,128)(2,1)S(1)} %collective-permute-done.45.refs_1_, f32[768,768]{1,0:T(8,128)} %get-tuple-element.184.refs_2_, f32[8,128]{1,0:T(8,128)S(1)} %get-tuple-element.177.refs_3_), custom_call_target="tpu_custom_call", output_to_operand_aliasing={{0}: (2, {})} | custom-call | flops 100000000 | bytes 1 | tf_op jit(solution)/shard_map/half_kernel/pallas_call | solution.py:55
  142.5 1.6 %half_kernel.7 = (f32[768,768]{1,0:T(8,128)}, f32[8,128]{1,0:T(8,128)S(1)}) custom-call(s32[11]{0:T(128)S(1)} %stack.44.refs_0_.refs_13_, bf16[384,768]{1,0:T(8,128)(2,1)S(1)} %collective-permute-done.44.refs_1_, f32[768,768]{1,0:T(8,128)} %get-tuple-element.183.refs_2_, f32[8,128]{1,0:T(8,128)S(1)} %get-tuple-element.185.refs_3_), custom_call_target="tpu_custom_call", output_to_operand_aliasing={{0}: (2, {})} | custom-call | flops 4000000000 | bytes 1 | tf_op jit(solution)/shard_map/half_kernel/pallas_call | solution.py:55
  144.1 2.6 %ATL.1 = (f32[768,768]{1,0:T(8,128)}, f32[768,768]{1,0:T(8,128)}, f32[768,768]{1,0:T(8,128)}, f32[768,768]{1,0:T(8,128)}, f32[8,128]{1,0:T(8,128)}) custom-call(s32[11]{0:T(128)S(1)} %stack.44.refs_0_.refs_13_, bf16[384,768]{1,0:T(8,128)(2,1)S(1)} %collective-permute-done.35.refs_1_, ...), custom_call_target="tpu_custom_call", output_to_operand_aliasing={{0}: (3, {}), {1}: (4, {}), {2}: (5, {}), {3}: (6, {})} | custom-call | flops 8000000000 | bytes 1 | tf_op jit(solution)/shard_map/ATL/pallas_call | solution.py:55
  (92 shorter events, 7.4 us)
Async XLA Ops:
  0.6 4.8 %collective-permute-start.1 = (s32[2,64]{1,0:T(2,128)}, s32[2,64]{1,0:T(2,128)S(1)}, u32[]{:S(2)}, u32[]{:S(2)}) collective-permute-start(s32[2,64]{1,0:T(2,128)} %refs_4_.1), channel_id=1, source_target_pairs={{0,2},{1,3},{2,0},{3,1},{4,6},{5,7},{6,4},{7,5},{8,10},{9,11},{10,... | collective-permute-start | bytes 1544 | tf_op jit(solution)/shard_map/ppermute | solution.py:451
  3.6 1.8 %collective-permute-start = (s32[2,64]{1,0:T(2,128)}, s32[2,64]{1,0:T(2,128)S(1)}, u32[]{:S(2)}, u32[]{:S(2)}) collective-permute-start(s32[2,64]{1,0:T(2,128)} %refs_4_.1), channel_id=1, source_target_pairs={{0,1},{1,0},{2,3},{3,2},{4,5},{5,4},{6,7},{7,6},{8,9},{9,8},{10,11... | collective-permute-start | bytes 1544 | tf_op jit(solution)/shard_map/ppermute | solution.py:451
  3.6 3.2 %collective-permute-start.2 = (s32[2,64]{1,0:T(2,128)}, s32[2,64]{1,0:T(2,128)S(1)}, u32[]{:S(2)}, u32[]{:S(2)}) collective-permute-start(s32[2,64]{1,0:T(2,128)} %refs_4_.1), channel_id=1, source_target_pairs={{0,3},{1,2},{2,1},{3,0},{4,7},{5,6},{6,5},{7,4},{8,11},{9,10},{10,... | collective-permute-start | bytes 1544 | tf_op jit(solution)/shard_map/ppermute | solution.py:451
  3.9 20.9 %collective-permute-start.5 = (bf16[768,768]{1,0:T(8,128)(2,1)}, bf16[768,768]{1,0:T(8,128)(2,1)S(1)}, u32[]{:S(2)}, u32[]{:S(2)}) collective-permute-start(bf16[768,768]{1,0:T(8,128)(2,1)} %refs_5_.3), channel_id=1, source_target_pairs={{0,1},{1,0},{2,3},{3,2},{4,5},{5,4},{6,7},{7,6},{8,9},{9,8},{10,11... | collective-permute-start | bytes 3538952 | tf_op jit(solution)/shard_map/ppermute | solution.py:451
  4.2 28.2 %collective-permute-start.9 = (bf16[768,768]{1,0:T(8,128)(2,1)}, bf16[768,768]{1,0:T(8,128)(2,1)S(1)}, u32[]{:S(2)}, u32[]{:S(2)}) collective-permute-start(bf16[768,768]{1,0:T(8,128)(2,1)} %refs_2_.1), channel_id=1, source_target_pairs={{0,1},{1,0},{2,3},{3,2},{4,5},{5,4},{6,7},{7,6},{8,9},{9,8},{10,11... | collective-permute-start | bytes 3538952 | tf_op jit(solution)/shard_map/ppermute | solution.py:451
  4.5 6.5 %copy-start = (bf16[2,512,768]{2,1,0:T(8,128)(2,1)S(1)}, bf16[2,512,768]{2,1,0:T(8,128)(2,1)}, u32[]{:S(2)}) copy-start(bf16[2,512,768]{2,1,0:T(8,128)(2,1)} %refs_3_.4) | copy-start | bytes 4718596
  6.9 0.7 copy-start.9
  7.5 17.3 %copy-start.4 = (bf16[768,768]{1,0:T(8,128)(2,1)S(1)}, bf16[768,768]{1,0:T(8,128)(2,1)}, u32[]{:S(2)}) copy-start(bf16[768,768]{1,0:T(8,128)(2,1)} %refs_14_.1) | copy-start | bytes 3538948
  7.5 17.3 %copy-start.5 = (bf16[768,768]{1,0:T(8,128)(2,1)S(1)}, bf16[768,768]{1,0:T(8,128)(2,1)}, u32[]{:S(2)}) copy-start(bf16[768,768]{1,0:T(8,128)(2,1)} %refs_5_.3) | copy-start | bytes 3538948
  10.3 4.7 %copy-start.12 = (bf16[768]{0:T(1024)(128)(2,1)S(1)}, bf16[768]{0:T(1024)(128)(2,1)}, u32[]{:S(2)}) copy-start(bf16[768]{0:T(1024)(128)(2,1)} %param.16) | copy-start | bytes 4612
  10.3 4.7 %copy-start.10 = (f32[768]{0:T(1024)S(1)}, f32[768]{0:T(1024)}, u32[]{:S(2)}) copy-start(f32[768]{0:T(1024)} %param.17) | copy-start | bytes 9220
  10.3 4.7 %copy-start.11 = (f32[768]{0:T(1024)S(1)}, f32[768]{0:T(1024)}, u32[]{:S(2)}) copy-start(f32[768]{0:T(1024)} %param.18) | copy-start | bytes 9220
  10.3 14.5 %copy-start.1 = (bf16[768,768]{1,0:T(8,128)(2,1)S(1)}, bf16[768,768]{1,0:T(8,128)(2,1)}, u32[]{:S(2)}) copy-start(bf16[768,768]{1,0:T(8,128)(2,1)} %refs_12_.2) | copy-start | bytes 3538948
  10.3 14.5 %copy-start.2 = (bf16[768,768]{1,0:T(8,128)(2,1)S(1)}, bf16[768,768]{1,0:T(8,128)(2,1)}, u32[]{:S(2)}) copy-start(bf16[768,768]{1,0:T(8,128)(2,1)} %refs_12_.3) | copy-start | bytes 3538948
  10.3 14.5 %copy-start.3 = (bf16[768,768]{1,0:T(8,128)(2,1)S(1)}, bf16[768,768]{1,0:T(8,128)(2,1)}, u32[]{:S(2)}) copy-start(bf16[768,768]{1,0:T(8,128)(2,1)} %refs_13_.1) | copy-start | bytes 3538948
  10.4 14.5 %copy-start.6 = (s32[2]{0:T(128)S(1)}, s32[2]{0:T(128)}, u32[]{:S(2)}) copy-start(s32[2]{0:T(128)} %refs_1_.1) | copy-start | bytes 28
  10.4 2.3 %collective-permute-start.3 = (bf16[256,768]{1,0:T(8,128)(2,1)S(1)}, bf16[256,768]{1,0:T(8,128)(2,1)S(1)}, u32[]{:S(2)}, u32[]{:S(2)}) collective-permute-start(bf16[256,768]{1,0:T(8,128)(2,1)S(1)} %get-tuple-element.105), channel_id=1, source_target_pairs={{0,1},{1,0},{2,3},{3,2},{4,5},{5,4},{6,7},{7,6},{8,9},{9,8},{10,11... | collective-permute-start | bytes 1179656 | tf_op jit(solution)/shard_map/ppermute | solution.py:451
  12.1 1.5 %collective-permute-start.6 = (bf16[128,768]{1,0:T(8,128)(2,1)S(1)}, bf16[128,768]{1,0:T(8,128)(2,1)S(1)}, u32[]{:S(2)}, u32[]{:S(2)}) collective-permute-start(bf16[128,768]{1,0:T(8,128)(2,1)S(1)} %get-tuple-element.107), channel_id=1, source_target_pairs={{0,1},{1,0},{2,3},{3,2},{4,5},{5,4},{6,7},{7,6},{8,9},{9,8},{10,11... | collective-permute-start | bytes 589832 | tf_op jit(solution)/shard_map/ppermute | solution.py:451
  12.2 1.7 %collective-permute-start.7 = (bf16[128,768]{1,0:T(8,128)(2,1)S(1)}, bf16[128,768]{1,0:T(8,128)(2,1)S(1)}, u32[]{:S(2)}, u32[]{:S(2)}) collective-permute-start(bf16[128,768]{1,0:T(8,128)(2,1)S(1)} %get-tuple-element.108), channel_id=1, source_target_pairs={{0,1},{1,0},{2,3},{3,2},{4,5},{5,4},{6,7},{7,6},{8,9},{9,8},{10,11... | collective-permute-start | bytes 589832 | tf_op jit(solution)/shard_map/ppermute | solution.py:451
  12.8 12.0 %collective-permute-start.4 = (bf16[256,768]{1,0:T(8,128)(2,1)S(1)}, bf16[256,768]{1,0:T(8,128)(2,1)S(1)}, u32[]{:S(2)}, u32[]{:S(2)}) collective-permute-start(bf16[256,768]{1,0:T(8,128)(2,1)S(1)} %add.15.refs_2_), channel_id=1, source_target_pairs={{0,2},{1,3},{2,0},{3,1},{4,6},{5,7},{6,4},{7,5},{8,10},{9,11},{10,... | collective-permute-start | bytes 1179656 | tf_op jit(solution)/shard_map/ppermute | solution.py:451
  14.0 18.4 %collective-permute-start.8 = (bf16[256,768]{1,0:T(8,128)(2,1)S(1)}, bf16[256,768]{1,0:T(8,128)(2,1)S(1)}, u32[]{:S(2)}, u32[]{:S(2)}) collective-permute-start(bf16[256,768]{1,0:T(8,128)(2,1)S(1)} %maximum_add_fusion.refs_13_.refs_1_.refs_6_.refs_3_), channel_id=1, source_target_pairs={{0,2},{1,3},{2,0},{3,1},{4,6},{5,7},{6,4},{7,5},{8,10},{9,11},{10,... | collective-permute-start | bytes 1179656 | tf_op jit(solution)/shard_map/ppermute | solution.py:451
  15.1 17.3 %copy-start.8 = (bf16[768,768]{1,0:T(8,128)(2,1)S(1)}, bf16[768,768]{1,0:T(8,128)(2,1)}, u32[]{:S(2)}) copy-start(bf16[768,768]{1,0:T(8,128)(2,1)} %refs_2_.1) | copy-start | bytes 3538948
  34.1 2.4 %collective-permute-start.12 = (bf16[512,768]{1,0:T(8,128)(2,1)S(1)}, bf16[512,768]{1,0:T(8,128)(2,1)S(1)}, u32[]{:S(2)}, u32[]{:S(2)}) collective-permute-start(bf16[512,768]{1,0:T(8,128)(2,1)S(1)} %get-tuple-element.123.refs_4_), channel_id=1, source_target_pairs={{0,1},{1,0},{2,3},{3,2},{4,5},{5,4},{6,7},{7,6},{8,9},{9,8},{10,11... | collective-permute-start | bytes 2359304 | tf_op jit(solution)/shard_map/ppermute | solution.py:451
  34.2 3.4 %collective-permute-start.11 = (bf16[512,768]{1,0:T(8,128)(2,1)S(1)}, bf16[512,768]{1,0:T(8,128)(2,1)S(1)}, u32[]{:S(2)}, u32[]{:S(2)}) collective-permute-start(bf16[512,768]{1,0:T(8,128)(2,1)S(1)} %get-tuple-element.122.refs_3_), channel_id=1, source_target_pairs={{0,1},{1,0},{2,3},{3,2},{4,5},{5,4},{6,7},{7,6},{8,9},{9,8},{10,11... | collective-permute-start | bytes 2359304 | tf_op jit(solution)/shard_map/ppermute | solution.py:451
  34.7 11.1 %collective-permute-start.10 = (bf16[256,768]{1,0:T(8,128)(2,1)S(1)}, bf16[256,768]{1,0:T(8,128)(2,1)S(1)}, u32[]{:S(2)}, u32[]{:S(2)}) collective-permute-start(bf16[256,768]{1,0:T(8,128)(2,1)S(1)} %get-tuple-element.116.refs_3_), channel_id=1, source_target_pairs={{0,2},{1,3},{2,0},{3,1},{4,6},{5,7},{6,4},{7,5},{8,10},{9,11},{10,... | collective-permute-start | bytes 1179656 | tf_op jit(solution)/shard_map/ppermute | solution.py:451
  39.6 15.4 %collective-permute-start.16 = (bf16[384,768]{1,0:T(8,128)(2,1)S(1)}, bf16[384,768]{1,0:T(8,128)(2,1)S(1)}, u32[]{:S(2)}, u32[]{:S(2)}) collective-permute-start(bf16[384,768]{1,0:T(8,128)(2,1)S(1)} %get-tuple-element.133), channel_id=1, source_target_pairs={{0,4},{4,0},{8,12},{12,8},{16,20},{20,16},{24,28},{28,24},{1,5},{5... | collective-permute-start | bytes 1769480 | tf_op jit(solution)/shard_map/ppermute | solution.py:451
  41.2 15.1 %collective-permute-start.17 = (bf16[384,768]{1,0:T(8,128)(2,1)S(1)}, bf16[384,768]{1,0:T(8,128)(2,1)S(1)}, u32[]{:S(2)}, u32[]{:S(2)}) collective-permute-start(bf16[384,768]{1,0:T(8,128)(2,1)S(1)} %get-tuple-element.134), channel_id=1, source_target_pairs={{0,8},{4,12},{8,0},{12,4},{16,24},{20,28},{24,16},{28,20},{1,9},{5... | collective-permute-start | bytes 1769480 | tf_op jit(solution)/shard_map/ppermute | solution.py:451
  42.8 15.8 %collective-permute-start.14 = (bf16[512,768]{1,0:T(8,128)(2,1)S(1)}, bf16[512,768]{1,0:T(8,128)(2,1)S(1)}, u32[]{:S(2)}, u32[]{:S(2)}) collective-permute-start(bf16[512,768]{1,0:T(8,128)(2,1)S(1)} %get-tuple-element.130.refs_1_), channel_id=1, source_target_pairs={{0,1},{1,0},{2,3},{3,2},{4,5},{5,4},{6,7},{7,6},{8,9},{9,8},{10,11... | collective-permute-start | bytes 2359304 | tf_op jit(solution)/shard_map/ppermute | solution.py:451
  51.3 7.3 %collective-permute-start.15 = (bf16[512,768]{1,0:T(8,128)(2,1)S(1)}, bf16[512,768]{1,0:T(8,128)(2,1)S(1)}, u32[]{:S(2)}, u32[]{:S(2)}) collective-permute-start(bf16[512,768]{1,0:T(8,128)(2,1)S(1)} %get-tuple-element.132), channel_id=1, source_target_pairs={{0,1},{1,0},{2,3},{3,2},{4,5},{5,4},{6,7},{7,6},{8,9},{9,8},{10,11... | collective-permute-start | bytes 2359304 | tf_op jit(solution)/shard_map/ppermute | solution.py:451
  52.2 11.6 %collective-permute-start.13 = (bf16[256,768]{1,0:T(8,128)(2,1)S(1)}, bf16[256,768]{1,0:T(8,128)(2,1)S(1)}, u32[]{:S(2)}, u32[]{:S(2)}) collective-permute-start(bf16[256,768]{1,0:T(8,128)(2,1)S(1)} %moved_kernel.1.refs_3_.refs_5_), channel_id=1, source_target_pairs={{0,2},{1,3},{2,0},{3,1},{4,6},{5,7},{6,4},{7,5},{8,10},{9,11},{10,... | collective-permute-start | bytes 1179656 | tf_op jit(solution)/shard_map/ppermute | solution.py:451
  56.9 10.0 %collective-permute-start.22 = (bf16[192,768]{1,0:T(8,128)(2,1)S(1)}, bf16[192,768]{1,0:T(8,128)(2,1)S(1)}, u32[]{:S(2)}, u32[]{:S(2)}) collective-permute-start(bf16[192,768]{1,0:T(8,128)(2,1)S(1)} %get-tuple-element.142), channel_id=1, source_target_pairs={{0,8},{4,12},{8,0},{12,4},{16,24},{20,28},{24,16},{28,20},{1,9},{5... | collective-permute-start | bytes 884744 | tf_op jit(solution)/shard_map/ppermute | solution.py:451
  60.1 9.6 %collective-permute-start.20 = (bf16[192,768]{1,0:T(8,128)(2,1)S(1)}, bf16[192,768]{1,0:T(8,128)(2,1)S(1)}, u32[]{:S(2)}, u32[]{:S(2)}) collective-permute-start(bf16[192,768]{1,0:T(8,128)(2,1)S(1)} %get-tuple-element.140), channel_id=1, source_target_pairs={{0,4},{4,0},{8,12},{12,8},{16,20},{20,16},{24,28},{28,24},{1,5},{5... | collective-permute-start | bytes 884744 | tf_op jit(solution)/shard_map/ppermute | solution.py:451
  60.6 14.4 %collective-permute-start.21 = (bf16[192,768]{1,0:T(8,128)(2,1)S(1)}, bf16[192,768]{1,0:T(8,128)(2,1)S(1)}, u32[]{:S(2)}, u32[]{:S(2)}) collective-permute-start(bf16[192,768]{1,0:T(8,128)(2,1)S(1)} %get-tuple-element.141), channel_id=1, source_target_pairs={{0,8},{4,12},{8,0},{12,4},{16,24},{20,28},{24,16},{28,20},{1,9},{5... | collective-permute-start | bytes 884744 | tf_op jit(solution)/shard_map/ppermute | solution.py:451
  65.4 19.6 %collective-permute-start.18 = (bf16[256,768]{1,0:T(8,128)(2,1)S(1)}, bf16[256,768]{1,0:T(8,128)(2,1)S(1)}, u32[]{:S(2)}, u32[]{:S(2)}) collective-permute-start(bf16[256,768]{1,0:T(8,128)(2,1)S(1)} %get-tuple-element.137.refs_2_.refs_4_), channel_id=1, source_target_pairs={{0,1},{1,0},{2,3},{3,2},{4,5},{5,4},{6,7},{7,6},{8,9},{9,8},{10,11... | collective-permute-start | bytes 1179656 | tf_op jit(solution)/shard_map/ppermute | solution.py:451
  65.5 4.2 %collective-permute-start.19 = (f32[8,768]{1,0:T(8,128)S(1)}, f32[8,768]{1,0:T(8,128)S(1)}, u32[]{:S(2)}, u32[]{:S(2)}) collective-permute-start(f32[8,768]{1,0:T(8,128)S(1)} %get-tuple-element.138), channel_id=1, source_target_pairs={{0,1},{1,0},{2,3},{3,2},{4,5},{5,4},{6,7},{7,6},{8,9},{9,8},{10,11... | collective-permute-start | bytes 73736 | tf_op jit(solution)/shard_map/ppermute | solution.py:451
  67.0 18.0 %collective-permute-start.26 = (bf16[192,768]{1,0:T(8,128)(2,1)S(1)}, bf16[192,768]{1,0:T(8,128)(2,1)S(1)}, u32[]{:S(2)}, u32[]{:S(2)}) collective-permute-start(bf16[192,768]{1,0:T(8,128)(2,1)S(1)} %round_kernel.2.refs_6_.refs_0_), channel_id=1, source_target_pairs={{0,16},{4,20},{8,24},{12,28},{16,0},{20,4},{24,8},{28,12},{1,17},{... | collective-permute-start | bytes 884744 | tf_op jit(solution)/shard_map/ppermute | solution.py:451
  75.7 9.0 %collective-permute-start.24 = (bf16[112,768]{1,0:T(8,128)(2,1)S(1)}, bf16[112,768]{1,0:T(8,128)(2,1)S(1)}, u32[]{:S(2)}, u32[]{:S(2)}) collective-permute-start(bf16[112,768]{1,0:T(8,128)(2,1)S(1)} %get-tuple-element.146), channel_id=1, source_target_pairs={{0,4},{4,0},{8,12},{12,8},{16,20},{20,16},{24,28},{28,24},{1,5},{5... | collective-permute-start | bytes 516104 | tf_op jit(solution)/shard_map/ppermute | solution.py:451
  75.8 8.9 %collective-permute-start.23 = (bf16[96,768]{1,0:T(8,128)(2,1)S(1)}, bf16[96,768]{1,0:T(8,128)(2,1)S(1)}, u32[]{:S(2)}, u32[]{:S(2)}) collective-permute-start(bf16[96,768]{1,0:T(8,128)(2,1)S(1)} %get-tuple-element.145), channel_id=1, source_target_pairs={{0,8},{4,12},{8,0},{12,4},{16,24},{20,28},{24,16},{28,20},{1,9},{5... | collective-permute-start | bytes 442376 | tf_op jit(solution)/shard_map/ppermute | solution.py:451
  75.9 14.3 %collective-permute-start.28 = (bf16[256,768]{1,0:T(8,128)(2,1)S(1)}, bf16[256,768]{1,0:T(8,128)(2,1)S(1)}, u32[]{:S(2)}, u32[]{:S(2)}) collective-permute-start(bf16[256,768]{1,0:T(8,128)(2,1)S(1)} %get-tuple-element.152.refs_4_), channel_id=1, source_target_pairs={{0,1},{1,0},{2,3},{3,2},{4,5},{5,4},{6,7},{7,6},{8,9},{9,8},{10,11... | collective-permute-start | bytes 1179656 | tf_op jit(solution)/shard_map/ppermute | solution.py:451
  84.8 21.0 %collective-permute-start.25 = (bf16[208,768]{1,0:T(8,128)(2,1)S(1)}, bf16[208,768]{1,0:T(8,128)(2,1)S(1)}, u32[]{:S(2)}, u32[]{:S(2)}) collective-permute-start(bf16[208,768]{1,0:T(8,128)(2,1)S(1)} %get-tuple-element.148.refs_1_), channel_id=1, source_target_pairs={{0,16},{4,20},{8,24},{12,28},{16,0},{20,4},{24,8},{28,12},{1,17},{... | collective-permute-start | bytes 958472 | tf_op jit(solution)/shard_map/ppermute | solution.py:451
  85.7 6.8 %collective-permute-start.27 = (bf16[192,768]{1,0:T(8,128)(2,1)S(1)}, bf16[192,768]{1,0:T(8,128)(2,1)S(1)}, u32[]{:S(2)}, u32[]{:S(2)}) collective-permute-start(bf16[192,768]{1,0:T(8,128)(2,1)S(1)} %get-tuple-element.151), channel_id=1, source_target_pairs={{0,4},{4,0},{8,12},{12,8},{16,20},{20,16},{24,28},{28,24},{1,5},{5... | collective-permute-start | bytes 884744 | tf_op jit(solution)/shard_map/ppermute | solution.py:451
  87.7 12.3 %collective-permute-start.29 = (bf16[192,768]{1,0:T(8,128)(2,1)S(1)}, bf16[192,768]{1,0:T(8,128)(2,1)S(1)}, u32[]{:S(2)}, u32[]{:S(2)}) collective-permute-start(bf16[192,768]{1,0:T(8,128)(2,1)S(1)} %last_kernel.2.refs_3_.refs_1_), channel_id=1, source_target_pairs={{0,8},{4,12},{8,0},{12,4},{16,24},{20,28},{24,16},{28,20},{1,9},{5... | collective-permute-start | bytes 884744 | tf_op jit(solution)/shard_map/ppermute | solution.py:451
  100.0 9.5 %copy-start.7 = (bf16[2,512,768]{2,1,0:T(8,128)(2,1)S(1)}, bf16[2,512,768]{2,1,0:T(8,128)(2,1)}, u32[]{:S(2)}) copy-start(bf16[2,512,768]{2,1,0:T(8,128)(2,1)} %refs_3_.5) | copy-start | bytes 4718596
  100.1 17.8 %collective-permute-start.34 = (bf16[192,768]{1,0:T(8,128)(2,1)S(1)}, bf16[192,768]{1,0:T(8,128)(2,1)S(1)}, u32[]{:S(2)}, u32[]{:S(2)}) collective-permute-start(bf16[192,768]{1,0:T(8,128)(2,1)S(1)} %round_kernel.3.refs_3_.refs_0_), channel_id=1, source_target_pairs={{0,16},{4,20},{8,24},{12,28},{16,0},{20,4},{24,8},{28,12},{1,17},{... | collective-permute-start | bytes 884744 | tf_op jit(solution)/shard_map/ppermute | solution.py:451
  105.9 7.7 %collective-permute-start.30 = (bf16[112,768]{1,0:T(8,128)(2,1)S(1)}, bf16[112,768]{1,0:T(8,128)(2,1)S(1)}, u32[]{:S(2)}, u32[]{:S(2)}) collective-permute-start(bf16[112,768]{1,0:T(8,128)(2,1)S(1)} %get-tuple-element.154.refs_6_.refs_2_), channel_id=1, source_target_pairs={{0,8},{4,12},{8,0},{12,4},{16,24},{20,28},{24,16},{28,20},{1,9},{5... | collective-permute-start | bytes 516104 | tf_op jit(solution)/shard_map/ppermute | solution.py:451
  108.4 5.1 %collective-permute-start.31 = (bf16[96,768]{1,0:T(8,128)(2,1)S(1)}, bf16[96,768]{1,0:T(8,128)(2,1)S(1)}, u32[]{:S(2)}, u32[]{:S(2)}) collective-permute-start(bf16[96,768]{1,0:T(8,128)(2,1)S(1)} %get-tuple-element.158.refs_3_), channel_id=1, source_target_pairs={{0,4},{4,0},{8,12},{12,8},{16,20},{20,16},{24,28},{28,24},{1,5},{5... | collective-permute-start | bytes 442376 | tf_op jit(solution)/shard_map/ppermute | solution.py:451
  109.1 13.8 %collective-permute-start.36 = (bf16[192,768]{1,0:T(8,128)(2,1)S(1)}, bf16[192,768]{1,0:T(8,128)(2,1)S(1)}, u32[]{:S(2)}, u32[]{:S(2)}) collective-permute-start(bf16[192,768]{1,0:T(8,128)(2,1)S(1)} %get-tuple-element.166), channel_id=1, source_target_pairs={{0,2},{1,3},{2,0},{3,1},{4,6},{5,7},{6,4},{7,5},{8,10},{9,11},{10,... | collective-permute-start | bytes 884744 | tf_op jit(solution)/shard_map/ppermute | solution.py:451
  114.7 6.7 %collective-permute-start.32 = (bf16[192,768]{1,0:T(8,128)(2,1)S(1)}, bf16[192,768]{1,0:T(8,128)(2,1)S(1)}, u32[]{:S(2)}, u32[]{:S(2)}) collective-permute-start(bf16[192,768]{1,0:T(8,128)(2,1)S(1)} %get-tuple-element.163), channel_id=1, source_target_pairs={{0,4},{4,0},{8,12},{12,8},{16,20},{20,16},{24,28},{28,24},{1,5},{5... | collective-permute-start | bytes 884744 | tf_op jit(solution)/shard_map/ppermute | solution.py:451
  116.1 6.7 %collective-permute-start.33 = (bf16[192,768]{1,0:T(8,128)(2,1)S(1)}, bf16[192,768]{1,0:T(8,128)(2,1)S(1)}, u32[]{:S(2)}, u32[]{:S(2)}) collective-permute-start(bf16[192,768]{1,0:T(8,128)(2,1)S(1)} %get-tuple-element.164), channel_id=1, source_target_pairs={{0,8},{4,12},{8,0},{12,4},{16,24},{20,28},{24,16},{28,20},{1,9},{5... | collective-permute-start | bytes 884744 | tf_op jit(solution)/shard_map/ppermute | solution.py:451
  118.0 6.8 %collective-permute-start.38 = (bf16[192,768]{1,0:T(8,128)(2,1)S(1)}, bf16[192,768]{1,0:T(8,128)(2,1)S(1)}, u32[]{:S(2)}, u32[]{:S(2)}) collective-permute-start(bf16[192,768]{1,0:T(8,128)(2,1)S(1)} %last_kernel.3.refs_2_.refs_1_), channel_id=1, source_target_pairs={{0,4},{4,0},{8,12},{12,8},{16,20},{20,16},{24,28},{28,24},{1,5},{5... | collective-permute-start | bytes 884744 | tf_op jit(solution)/shard_map/ppermute | solution.py:451
  118.4 9.0 %collective-permute-start.39 = (bf16[384,768]{1,0:T(8,128)(2,1)S(1)}, bf16[384,768]{1,0:T(8,128)(2,1)S(1)}, u32[]{:S(2)}, u32[]{:S(2)}) collective-permute-start(bf16[384,768]{1,0:T(8,128)(2,1)S(1)} %get-tuple-element.165.refs_2_.refs_1_), channel_id=1, source_target_pairs={{0,1},{1,0},{2,3},{3,2},{4,5},{5,4},{6,7},{7,6},{8,9},{9,8},{10,11... | collective-permute-start | bytes 1769480 | tf_op jit(solution)/shard_map/ppermute | solution.py:451
  121.4 12.1 %collective-permute-start.37 = (bf16[192,768]{1,0:T(8,128)(2,1)S(1)}, bf16[192,768]{1,0:T(8,128)(2,1)S(1)}, u32[]{:S(2)}, u32[]{:S(2)}) collective-permute-start(bf16[192,768]{1,0:T(8,128)(2,1)S(1)} %get-tuple-element.167), channel_id=1, source_target_pairs={{0,2},{1,3},{2,0},{3,1},{4,6},{5,7},{6,4},{7,5},{8,10},{9,11},{10,... | collective-permute-start | bytes 884744 | tf_op jit(solution)/shard_map/ppermute | solution.py:451
  122.9 6.2 %collective-permute-start.40 = (bf16[384,768]{1,0:T(8,128)(2,1)S(1)}, bf16[384,768]{1,0:T(8,128)(2,1)S(1)}, u32[]{:S(2)}, u32[]{:S(2)}) collective-permute-start(bf16[384,768]{1,0:T(8,128)(2,1)S(1)} %stack_kernel.1.refs_3_.refs_2_), channel_id=1, source_target_pairs={{0,1},{1,0},{2,3},{3,2},{4,5},{5,4},{6,7},{7,6},{8,9},{9,8},{10,11... | collective-permute-start | bytes 1769480 | tf_op jit(solution)/shard_map/ppermute | solution.py:451
  123.0 17.9 %collective-permute-start.35 = (bf16[384,768]{1,0:T(8,128)(2,1)S(1)}, bf16[384,768]{1,0:T(8,128)(2,1)S(1)}, u32[]{:S(2)}, u32[]{:S(2)}) collective-permute-start(bf16[384,768]{1,0:T(8,128)(2,1)S(1)} %stack_kernel.1.refs_3_.refs_2_), channel_id=1, source_target_pairs={{0,2},{1,3},{2,0},{3,1},{4,6},{5,7},{6,4},{7,5},{8,10},{9,11},{10,... | collective-permute-start | bytes 1769480 | tf_op jit(solution)/shard_map/ppermute | solution.py:451
  125.4 15.5 %collective-permute-start.45 = (bf16[384,768]{1,0:T(8,128)(2,1)S(1)}, bf16[384,768]{1,0:T(8,128)(2,1)S(1)}, u32[]{:S(2)}, u32[]{:S(2)}) collective-permute-start(bf16[384,768]{1,0:T(8,128)(2,1)S(1)} %join_kernel.2.refs_3_.refs_1_), channel_id=1, source_target_pairs={{0,8},{4,12},{8,0},{12,4},{16,24},{20,28},{24,16},{28,20},{1,9},{5... | collective-permute-start | bytes 1769480 | tf_op jit(solution)/shard_map/ppermute | solution.py:451
  127.4 15.1 %collective-permute-start.44 = (bf16[384,768]{1,0:T(8,128)(2,1)S(1)}, bf16[384,768]{1,0:T(8,128)(2,1)S(1)}, u32[]{:S(2)}, u32[]{:S(2)}) collective-permute-start(bf16[384,768]{1,0:T(8,128)(2,1)S(1)} %join_kernel.3.refs_5_.refs_1_), channel_id=1, source_target_pairs={{0,4},{4,0},{8,12},{12,8},{16,20},{20,16},{24,28},{28,24},{1,5},{5... | collective-permute-start | bytes 1769480 | tf_op jit(solution)/shard_map/ppermute | solution.py:451
  133.6 2.2 %collective-permute-start.41 = (bf16[192,768]{1,0:T(8,128)(2,1)S(1)}, bf16[192,768]{1,0:T(8,128)(2,1)S(1)}, u32[]{:S(2)}, u32[]{:S(2)}) collective-permute-start(bf16[192,768]{1,0:T(8,128)(2,1)S(1)} %collective-permute-done.36.refs_4_.refs_1_), channel_id=1, source_target_pairs={{0,1},{1,0},{2,3},{3,2},{4,5},{5,4},{6,7},{7,6},{8,9},{9,8},{10,11... | collective-permute-start | bytes 884744 | tf_op jit(solution)/shard_map/ppermute | solution.py:451
  133.7 2.2 %collective-permute-start.42 = (bf16[192,768]{1,0:T(8,128)(2,1)S(1)}, bf16[192,768]{1,0:T(8,128)(2,1)S(1)}, u32[]{:S(2)}, u32[]{:S(2)}) collective-permute-start(bf16[192,768]{1,0:T(8,128)(2,1)S(1)} %collective-permute-done.37.refs_2_), channel_id=1, source_target_pairs={{0,1},{1,0},{2,3},{3,2},{4,5},{5,4},{6,7},{7,6},{8,9},{9,8},{10,11... | collective-permute-start | bytes 884744 | tf_op jit(solution)/shard_map/ppermute | solution.py:451
  140.8 3.3 %collective-permute-start.43 = (bf16[384,768]{1,0:T(8,128)(2,1)S(1)}, bf16[384,768]{1,0:T(8,128)(2,1)S(1)}, u32[]{:S(2)}, u32[]{:S(2)}) collective-permute-start(bf16[384,768]{1,0:T(8,128)(2,1)S(1)} %collective-permute-done.35.refs_1_), channel_id=1, source_target_pairs={{0,1},{1,0},{2,3},{3,2},{4,5},{5,4},{6,7},{7,6},{8,9},{9,8},{10,11... | collective-permute-start | bytes 1769480 | tf_op jit(solution)/shard_map/ppermute | solution.py:451

commit v5 on v4

--- a/solution.py
+++ b/solution.py
@@ -9,9 +9,9 @@
 
 NH = 12
 Y, Z0, Z1 = 8, 9, 10
-ORDER = ("F", "AB", "MV", "R2", "FA", "SL", "D3", "A2", "A3", "D4", "R2U", "P2", "U3", "A4", "P1", "A5", "U4", "A6", "U5", "D5", "AT0", "UH", "XE", "DH", "ATE", "XC", "UU", "DU", "ATL")
-WORK = {"P1": 1000, "D5": 600, "U5": 8000, "U4": 2000, "D3": 100, "SL": 1000, "UU": 100, "DU": 4000, "P2": 100, "R2": 4000, "AT0": 4000, "A6": 300, "A4": 1000, "A2": 300, "A3": 1000, "AT": 600, "ATE": 100, "R2U": 600, "ATL": 8000, "ML": 4000, "F": 300, "A5": 100, "D4": 300, "SE": 8000, "MV": 4000, "SA": 300}
-HOLD = {"U5": ["x1"], "U3": ["d5"], "R2": ["u1"], "D4": ["up"]}
+ORDER = ("F", "MV", "AB", "R2", "FA", "SL", "D3", "A2", "R2U", "A3", "D4", "P2", "A4", "U3", "P1", "A5", "U4", "A6", "D5", "U5", "XE", "MID", "XC", "FIN")
+WORK = {"P1": 600, "U5": 8000, "U4": 2000, "D3": 100, "SL": 300, "P2": 100, "R2": 4000, "A6": 2000, "A4": 1000, "A2": 4000, "AT": 600, "R2U": 2000, "ML": 4000, "F": 2000, "A5": 2000, "SE": 8000, "MV": 4000, "SA": 300, "D5": 300, "FA": 300, "FIN": 4000, "D4": 8000, "A3": 100}
+HOLD = {"R2": ["u1"], "D5": ["x2"], "R2U": ["gc"], "U4": ["a6", "x1"], "D3": ["a1"], "A4": ["u2"], "A5": ["d5"]}
 EPS = 1e-06
 F32 = jnp.float32
 BF16 = jnp.bfloat16
@@ -65,41 +65,33 @@
     )(*ins, *after)
 
 
-def select_kernel(meta, p1, p2, p3, picks, rows, own, other, hot_own, hot_other, local_rows, p0, sems):
+def select_kernel(meta, p0, p1, p2, p3, rows, other, hot_own, hot_other, local_rows, sem):
     core = meta[1]
-    copies = [
-        pltpu.make_async_copy(picks, p0, sems.at[0]),
-        pltpu.make_async_copy(rows.at[1 - core], local_rows.at[0], sems.at[1]),
-        pltpu.make_async_copy(rows.at[core], local_rows.at[1], sems.at[2]),
-    ]
-    for copy in copies:
-        copy.start()
+    copy = pltpu.make_async_copy(rows.at[1 - core], local_rows, sem)
+    copy.start()
     length = rows.shape[1]
     local = p1.shape[1]
     base = meta[0] * length
     down = lax.broadcasted_iota(jnp.int32, (local, local), 0)
     along = lax.broadcasted_iota(jnp.int32, (local, local), 1)
     places = lax.broadcasted_iota(jnp.int32, (local, length), 1)
-    for k, part in ((1, p1), (2, p2), (3, p3), (0, p0)):
-        if k == 0:
-            copies[0].wait()
-        at = pl.multiple_of(meta[4 + k] * local, local)
-        for seq, hot in ((1 - core, hot_other), (core, hot_own)):
+    for seq, hot in ((1 - core, hot_other), (core, hot_own)):
+        for k, part in enumerate((p0, p1, p2, p3)):
+            at = pl.multiple_of(meta[4 + k] * local, local)
             row = part[pl.ds(seq, 1), :]
             column = jnp.sum(jnp.where(down == along, row, 0), axis=1, keepdims=True)
             hot[pl.ds(at, local), :] = jnp.where(column - base == places, 1.0, 0.0).astype(BF16)
-    copies[1].wait()
-    other[...] = mm(hot_other[...], local_rows[0]).astype(BF16)
-    copies[2].wait()
-    own[...] = mm(hot_own[...], local_rows[1]).astype(BF16)
-
-
-def select_again_kernel(meta, hot_own, hot_other, rows, own, first, second):
+    copy.wait()
+    other[...] = mm(hot_other[...], local_rows[...]).astype(BF16)
+
+
+def select_again_kernel(meta, hot_own, hot_other, rows, more_rows, own, more_own, first, second):
     core = meta[1]
     half = first.shape[0]
-    first[...] = mm(hot_other[:half, :], rows[1 - core]).astype(BF16)
-    second[...] = mm(hot_other[half:, :], rows[1 - core]).astype(BF16)
     own[...] = mm(hot_own[...], rows[core]).astype(BF16)
+    first[...] = mm(hot_other[:half, :], more_rows[1 - core]).astype(BF16)
+    second[...] = mm(hot_other[half:, :], more_rows[1 - core]).astype(BF16)
+    more_own[...] = mm(hot_own[...], more_rows[core]).astype(BF16)
 
 
 def place_kernel(meta, hot_own, hot_other, rows, own, other, out):
@@ -409,8 +401,7 @@
     late[rows:, :] = got_b[...]
 
 
-def attention_kernel(far, parts, meta, *refs):
-    outs, (block, sems) = refs[-6:-2], refs[-2:]
+def start_attention(far, parts, meta, refs, outs, block, sems):
     core, side = meta[1], meta[3] ^ far
     rows = block.shape[1]
     count = sum(n for _, n in parts)
@@ -433,18 +424,36 @@
                         pltpu.make_async_copy(block.at[slot], out.at[at, :], sems.at[slot]).start()
 
                 copies.append(pltpu.make_async_copy(block.at[slot], outs[0].at[at, :], sems.at[slot]))
+    return copies
+
+
+def start_halves(theirs, meta, pieces, outs, block, sems):
+    copies = []
+    for n, (piece, bit) in enumerate(zip(pieces, (Y, Z0))):
+        rows = piece.shape[0]
+        block[n] = piece[...].astype(F32)
+        at = pl.ds(pl.multiple_of((meta[bit] ^ theirs) * rows, rows), rows)
+        copies.append(pltpu.make_async_copy(block.at[n], outs[n].at[at, :], sems.at[n]))
+        copies[-1].start()
+    return copies
+
+
+def middle_kernel(meta, *refs):
+    near, far, halves, outs = refs[:4], refs[4:8], refs[8:10], refs[10:16]
+    near_block, near_sems, far_block, far_sems, half_block, half_sems = refs[16:]
+    copies = start_halves(0, meta, halves, outs[4:], half_block, half_sems)
+    copies += start_attention(0, ((0, 1), (1, 1)), meta, near, outs[:4], near_block, near_sems)
+    copies += start_attention(1, ((0, 2),), meta, far, outs[:4], far_block, far_sems)
     for copy in copies:
         copy.wait()
 
 
-def half_kernel(bit, theirs, meta, piece, *refs):
-    out, block, sem = refs[-3:]
-    rows = piece.shape[0]
-    block[...] = piece[...].astype(F32)
-    at = pl.multiple_of((meta[bit] ^ theirs) * rows, rows)
-    copy = pltpu.make_async_copy(block, out.at[pl.ds(at, rows), :], sem)
-    copy.start()
-    copy.wait()
+def final_kernel(meta, side, side_core, d_got, u_got, *refs):
+    outs, (block, sems, half_block, half_sems) = refs[-10:-4], refs[-4:]
+    copies = start_halves(1, meta, (d_got, u_got), outs[4:], half_block, half_sems)
+    copies += start_attention(1, ((1, 1),), meta, (side, side_core), outs[:4], block, sems)
+    for copy in copies:
+        copy.wait()
 
 
 def swap(v, axis, size, bits):
@@ -476,23 +485,22 @@
     slope = ((slots, hidden_units), F32)
 
     got = [across(picks, bits=k) for k in (1, 2, 3)]
-    own, other, hot_own, hot_other = call(
-        "SE", select_kernel, [meta, *got, picks, tokens], [rows(slots)] * 2 + [hot] * 2,
-        specs=[SMEM] + [VMEM] * 3 + [HBM] * 2,
-        scratch=[
-            pltpu.VMEM((2, length, width), BF16), pltpu.VMEM(picks.shape, jnp.int32),
-            pltpu.SemaphoreType.DMA((3,)),
-        ],
+    own_picks = jnp.where(place < 4, picks, 0)
+    other, hot_own, hot_other = call(
+        "SE", select_kernel, [meta, own_picks, *got, tokens], [rows(slots)] + [hot] * 2,
+        specs=[SMEM] + [VMEM] * 4 + [HBM],
+        scratch=[pltpu.VMEM((length, width), BF16), pltpu.SemaphoreType.DMA],
         vmem=52,
     )
     up_other, down_other = across(w_up, bits=1), across(w_down, bits=1)
-    here = own + across(other, bits=1)
+    other = across(other, bits=1)
+    own, seen_here, *more = call(
+        "SA", select_again_kernel, [meta, hot_own, hot_other, tokens, cotangent],
+        [rows(slots)] * 2 + [rows(slots // 2)] * 2, specs=[SMEM] + [VMEM] * 4,
+    )
+    here = own + other
     there = across(here, bits=2)
-    own, *other = call(
-        "SA", select_again_kernel, [meta, hot_own, hot_other, cotangent], [rows(slots)] + [rows(slots // 2)] * 2,
-        specs=[SMEM] + [VMEM] * 3,
-    )
-    seen_here = own + jnp.concatenate([across(v, bits=1) for v in other], axis=0)
+    seen_here = seen_here + jnp.concatenate([across(v, bits=1) for v in more], axis=0)
     seen_there = across(seen_here, bits=2)
 
     (
@@ -592,22 +600,6 @@
             [((2 * count, width), dtype)], specs=[SMEM] + [VMEM] * 2, after=after, token=token,
         )
 
-    def attention(tag, far, parts, pieces, outs=(), after=()):
-        return call(
-            tag, functools.partial(attention_kernel, far, parts), [meta, *pieces, *outs], [wide(width)] * 4,
-            specs=[SMEM] + [VMEM] * len(pieces) + [HBM] * len(outs), out_specs=[HBM] * 4,
-            scratch=[pltpu.VMEM((4 * len(parts), half // 2, width), F32), pltpu.SemaphoreType.DMA((4 * len(parts),))],
-            aliases={1 + len(pieces) + m: m for m in range(len(outs))}, after=after, token=True, name=tag,
-        )
-
-    def write_half(tag, bit, theirs, piece, outs=(), after=()):
-        return call(
-            tag, functools.partial(half_kernel, bit, theirs), [meta, piece, *outs], [wide(width)],
-            specs=[SMEM, VMEM] + [HBM] * len(outs), out_specs=[HBM],
-            scratch=[pltpu.VMEM(piece.shape, F32), pltpu.SemaphoreType.DMA],
-            aliases={2: 0} if outs else {}, after=after, token=True,
-        )
-
     v, moved = {}, {}
 
     def kept(name, value):
@@ -720,15 +712,6 @@
 
         return step
 
-    def halves(tag, key, bit, theirs):
-        def step(after):
-            outs = [v["grad_" + key]] if theirs else []
-            piece = v[key] if theirs else v[key + "_all"]
-            v["grad_" + key], token = write_half(tag, bit, theirs, piece, outs, after)
-            return token
-
-        return step
-
     def place(tag, name, values, mine, core):
         def step(after):
             v[name], token = placed(tag, values, v[mine], v[core], after)
@@ -736,18 +719,22 @@
 
         return step
 
-    def step_at0(after):
-        pieces = [v["early"], v["late"], v["early_core"], v["late_core"]]
-        *v["grads"], token = attention("AT0", 0, ((0, 1), (1, 1)), pieces, after=after)
-        return token
-
     def step_xe(after):
         near, far, *_ = lax.optimization_barrier((v["near"], v["far"], *after))
         v["side_early"] = [near, far, kept("g1", across(near, bits=1)), kept("g2", across(far, bits=1))]
         return after[0]
 
-    def step_ate(after):
-        *v["grads"], token = attention("ATE", 1, ((0, 2),), v["side_early"], v["grads"], after)
+    def blocks(parts):
+        return [pltpu.VMEM((4 * parts, half // 2, width), F32), pltpu.SemaphoreType.DMA((4 * parts,))]
+
+    half_blocks = [pltpu.VMEM((2, half, width), F32), pltpu.SemaphoreType.DMA((2,))]
+
+    def step_mid(after):
+        pieces = [v["early"], v["late"], v["early_core"], v["late_core"], *v["side_early"], v["d_all"], v["u_all"]]
+        *v["grads"], token = call(
+            "MID", middle_kernel, [meta, *pieces], [wide(width)] * 6, specs=[SMEM] + [VMEM] * 10, out_specs=[HBM] * 6,
+            scratch=blocks(2) + blocks(1) + half_blocks, vmem=14, after=after, token=True,
+        )
         return token
 
     def step_xc(after):
@@ -755,23 +742,25 @@
         v["side_late"] = [side, across(side, bits=1)]
         return after[0]
 
-    def step_atl(after):
-        *v["grads"], token = attention("ATL", 1, ((1, 1),), v["side_late"], v["grads"], after)
-        return token
+    def step_fin(after):
+        ins = [meta, *v["side_late"], v["d"], v["u"], *v["grads"]]
+        v["grads"] = call(
+            "FIN", final_kernel, ins, [wide(width)] * 6, specs=[SMEM] + [VMEM] * 4 + [HBM] * 6, out_specs=[HBM] * 6,
+            scratch=blocks(1) + half_blocks, aliases={5 + m: m for m in range(6)}, after=after,
+        )
 
     steps = dict(
         F=step_f, AB=step_ab, SL=step_sl, FA=step_fa, R2=step_r2, R2U=step_r2u, A2=step_a2, A3=step_a3,
         D3=third("D3", "d"), U3=third("U3", "u"), D4=fourth("D4", "d", 1), U4=fourth("U4", "u", 0), A4=step_a4,
-        A5=step_a5, A6=step_a6, D5=fifth("D5", "d", Z0, 0), U5=fifth("U5", "u", Y, 1), DH=halves("DH", "d", Y, 0),
-        DU=halves("DU", "d", Y, 1), UH=halves("UH", "u", Z0, 0), UU=halves("UU", "u", Z0, 1), MV=step_mv, XE=step_xe,
-        ATE=step_ate, ATL=step_atl, P1=place("P1", "output", tokens, "update", "update_core"),
-        P2=place("P2", "grad_tokens", cotangent, "grad_chosen", "chosen_core"), AT0=step_at0, XC=step_xc,
+        A5=step_a5, A6=step_a6, D5=fifth("D5", "d", Z0, 0), U5=fifth("U5", "u", Y, 1), MV=step_mv, XE=step_xe,
+        MID=step_mid, FIN=step_fin, P1=place("P1", "output", tokens, "update", "update_core"),
+        P2=place("P2", "grad_tokens", cotangent, "grad_chosen", "chosen_core"), XC=step_xc,
     )
     after = []
     for name in ORDER:
         after = [steps[name](after + [moved[key] for key in HOLD.get(name, ())])]
     return (
-        v["output"], v["grad_tokens"], *v["vectors"], *v["grads"], v["grad_u"], v["grad_d"],
+        v["output"], v["grad_tokens"], *v["vectors"], *v["grads"][:4], v["grads"][5], v["grads"][4],
     )
 
 

time: 148 us -> 143 us (0.966)
  waiting for transfers between devices: 57.7 us -> 65.1 us
  Pallas kernels: 47 us -> 39.9 us
  starting transfers between devices: 39.8 us -> 35.5 us
    ppermute x46, waiting for transfers between devices: 57.7 us -> 65.1 us  [swap(): return lax.ppermute(v, axis, [(i, i ^ bits) for i in range(size)])]
    pallas_call x31 -> x26, Pallas kernels: 47 us -> 39.9 us  [call(): pl.pallas_call(run, out_shape=tuple(shapes), in_specs=(specs or [VMEM] *...]
    ppermute x46, starting transfers between devices: 39.8 us -> 35.5 us  [swap(): return lax.ppermute(v, axis, [(i, i ^ bits) for i in range(size)])]
  transfers between devices with their start and end apart: 46 -> 46, of which waited for: 21 -> 26; matrix products, arithmetic and copies ran while one was open for 0% -> 1% of each run, Pallas kernels for 29% -> 25%
where the time goes in v5:
time: 143 us
  waiting for transfers between devices  65.1 us (46%)
  Pallas kernels  39.9 us (28%)
  starting transfers between devices  35.5 us (25%)
    ppermute x46, waiting for transfers between devices, swap(): return lax.ppermute(v, axis, [(i, i ^ bits) for i in range(size)])  65.1 us
    pallas_call x26, Pallas kernels, call(): pl.pallas_call(run, out_shape=tuple(shapes), in_specs=(specs or [VMEM] *...  39.9 us
    ppermute x46, starting transfers between devices, swap(): return lax.ppermute(v, axis, [(i, i ^ bits) for i in range(size)])  35.5 us
  transfers between devices with their start and end apart: 46, of which 26 were waited for; matrix products, arithmetic and copies ran while one was open for 1% of the time, Pallas kernels for 25%

profile of v5, /device:TPU:0, one launch (start us, length us, event | category | flops | bytes accessed | tf_op | source)
XLA Modules:
  0.0 142.9 jit_solution(9320765456502122419)
XLA Ops:
  0.6 0.5 collective-permute-start
  1.2 2.6 %collective-permute-start.2 = (s32[2,64]{1,0:T(2,128)}, s32[2,64]{1,0:T(2,128)S(1)}, u32[]{:S(2)}, u32[]{:S(2)}) collective-permute-start(s32[2,64]{1,0:T(2,128)} %param.15), channel_id=1, source_target_pairs={{0,3},{1,2},{2,1},{3,0},{4,7},{5,6},{6,5},{7,4},{8,11},{9,10},{10,... | collective-permute-start | bytes 1544 | tf_op jit(solution)/shard_map/ppermute | solution.py:460
  4.3 0.7 broadcast_select_fusion.refs_1_
  5.3 2.3 %collective-permute-done.1.refs_3_ = s32[2,64]{1,0:T(2,128)S(1)} collective-permute-done((s32[2,64]{1,0:T(2,128)}, s32[2,64]{1,0:T(2,128)S(1)}, u32[]{:S(2)}, u32[]{:S(2)}) %collective-permute-start.1) | collective-permute-done | bytes 544 | tf_op jit(solution)/shard_map/ppermute | solution.py:460
  7.6 2.2 %select_kernel.1 = (bf16[256,768]{1,0:T(8,128)(2,1)S(1)}, bf16[256,512]{1,0:T(8,128)(2,1)S(1)}, bf16[256,512]{1,0:T(8,128)(2,1)S(1)}) custom-call(s32[11]{0:T(128)S(1)} %stack.44.refs_0_.refs_13_, s32[2,64]{1,0:T(2,128)S(1)} %broadcast_select_fusion.refs_1_, s32[2,64]{1,0:T(2,128)S(1)} %collective-permute-done.refs_2_, ...), custom_call_target="tpu_custom_call" | custom-call | flops 8000000000 | bytes 1 | tf_op jit(solution)/shard_map/select_kernel/pallas_call | solution.py:55
  9.9 1.3 select_again_kernel.1
  11.3 0.5 collective-permute-start.6
  12.1 0.7 collective-permute-done.6
  13.4 0.9 collective-permute-start.8
  14.3 9.7 %collective-permute-done.4.refs_3_ = bf16[256,768]{1,0:T(8,128)(2,1)S(1)} collective-permute-done((bf16[256,768]{1,0:T(8,128)(2,1)S(1)}, bf16[256,768]{1,0:T(8,128)(2,1)S(1)}, u32[]{:S(2)}, u32[]{:S(2)}) %collective-permute-start.4) | collective-permute-done | bytes 393248 | tf_op jit(solution)/shard_map/ppermute | solution.py:460
  24.0 6.6 %attend_kernel.1 = (bf16[256,768]{1,0:T(8,128)(2,1)S(1)}, bf16[256,768]{1,0:T(8,128)(2,1)}, bf16[256,768]{1,0:T(8,128)(2,1)S(1)}, bf16[256,768]{1,0:T(8,128)(2,1...) custom-call(s32[11]{0:T(128)S(1)} %stack.44.refs_0_.refs_13_, ...), custom_call_target="tpu_custom_call" | custom-call | flops 600000000 | bytes 1 | tf_op jit(solution)/shard_map/attend_kernel/pallas_call | solution.py:55
  30.6 1.4 collective-permute-done.8.refs_2_.refs_7_.refs_4_
  32.0 1.8 %mlp_kernel.1 = (bf16[256,768]{1,0:T(8,128)(2,1)S(1)}, bf16[512,768]{1,0:T(8,128)(2,1)S(1)}, bf16[256,768]{1,0:T(8,128)(2,1)S(1)}) custom-call(f32[256,128]{1,0:T(8,128)S(1)} %get-tuple-element.102.refs_0_.refs_5_.refs_2_, bf16[256,768]{1,0:T(8,128)(2,1)S(1)} %maximum_add_fusion.refs_13_.refs_1_.refs_6_.refs_3_, ...), custom_call_target="tpu_custom_call" | custom-call | flops 4000000000 | bytes 1 | tf_op jit(solution)/shard_map/mlp_kernel/pallas_call | solution.py:55
  33.9 0.5 collective-permute-start.10
  34.6 1.5 %collective-permute-done.11.refs_6_ = bf16[512,768]{1,0:T(8,128)(2,1)S(1)} collective-permute-done((bf16[512,768]{1,0:T(8,128)(2,1)S(1)}, bf16[512,768]{1,0:T(8,128)(2,1)S(1)}, u32[]{:S(2)}, u32[]{:S(2)}) %collective-permute-start.11) | collective-permute-done | bytes 786464 | tf_op jit(solution)/shard_map/ppermute | solution.py:460
  36.1 1.1 collective-permute-done.10.refs_5_
  37.3 2.0 %mlp_grads_kernel.1 = (bf16[384,768]{1,0:T(8,128)(2,1)S(1)}, bf16[384,768]{1,0:T(8,128)(2,1)S(1)}, f32[384,768]{1,0:T(8,128)S(1)}, f32[384,768]{1,0:T(8,128)S(1)}) custom-call(s32[11]{0:T(128)S(1)} %stack.44.refs_0_.refs_13_, bf16[256,768]{1,0:T(8,128)(2,1)S(1)} %get-tuple-element.103.refs_1_.refs_0_, bf16[256,768]{1,0:T(8,128)(2,1)S(1)} %get-tuple-element.107.refs_2_, ...), custom_call_target="tpu_custom_call" | custom-call | flops 2000000000 | bytes 1 | tf_op jit(solution)/shard_map/mlp_grads_kernel/pallas_call | solution.py:55
  39.2 1.6 %collective-permute-start.16 = (bf16[384,768]{1,0:T(8,128)(2,1)S(1)}, bf16[384,768]{1,0:T(8,128)(2,1)S(1)}, u32[]{:S(2)}, u32[]{:S(2)}) collective-permute-start(bf16[384,768]{1,0:T(8,128)(2,1)S(1)} %get-tuple-element.124), channel_id=1, source_target_pairs={{0,4},{4,0},{8,12},{12,8},{16,20},{20,16},{24,28},{28,24},{1,5},{5... | collective-permute-start | bytes 1769480 | tf_op jit(solution)/shard_map/ppermute | solution.py:460
  40.8 1.6 %collective-permute-start.17 = (bf16[384,768]{1,0:T(8,128)(2,1)S(1)}, bf16[384,768]{1,0:T(8,128)(2,1)S(1)}, u32[]{:S(2)}, u32[]{:S(2)}) collective-permute-start(bf16[384,768]{1,0:T(8,128)(2,1)S(1)} %get-tuple-element.125), channel_id=1, source_target_pairs={{0,8},{4,12},{8,0},{12,4},{16,24},{20,28},{24,16},{28,20},{1,9},{5... | collective-permute-start | bytes 1769480 | tf_op jit(solution)/shard_map/ppermute | solution.py:460
  42.4 0.8 moved_kernel.1.refs_14_.refs_5_
  43.2 2.3 %collective-permute-done.13.refs_4_ = bf16[256,768]{1,0:T(8,128)(2,1)S(1)} collective-permute-done((bf16[256,768]{1,0:T(8,128)(2,1)S(1)}, bf16[256,768]{1,0:T(8,128)(2,1)S(1)}, u32[]{:S(2)}, u32[]{:S(2)}) %collective-permute-start.13) | collective-permute-done | bytes 393248 | tf_op jit(solution)/shard_map/ppermute | solution.py:460
  45.5 5.5 %attend_back_kernel.1 = (bf16[512,768]{1,0:T(8,128)(2,1)S(1)}, bf16[512,768]{1,0:T(8,128)(2,1)S(1)}, bf16[256,768]{1,0:T(8,128)(2,1)S(1)}, bf16[256,768]{1,0:T(8...) custom-call(bf16[256,768]{1,0:T(8,128)(2,1)S(1)} %get-tuple-element.100.refs_0_, ...), custom_call_target="tpu_custom_call" | custom-call | flops 1 | bytes 1 | tf_op jit(solution)/shard_map/attend_back_kernel/pallas_call | solution.py:55
  51.4 3.3 %collective-permute-done.16.refs_2_ = bf16[384,768]{1,0:T(8,128)(2,1)S(1)} collective-permute-done((bf16[384,768]{1,0:T(8,128)(2,1)S(1)}, bf16[384,768]{1,0:T(8,128)(2,1)S(1)}, u32[]{:S(2)}, u32[]{:S(2)}) %collective-permute-start.16) | collective-permute-done | bytes 589856 | tf_op jit(solution)/shard_map/ppermute | solution.py:460
  54.7 1.2 collective-permute-done.17.refs_4_.refs_2_
  55.9 0.7 reduce_kernel.2
  56.6 1.6 %collective-permute-start.22 = (bf16[192,768]{1,0:T(8,128)(2,1)S(1)}, bf16[192,768]{1,0:T(8,128)(2,1)S(1)}, u32[]{:S(2)}, u32[]{:S(2)}) collective-permute-start(bf16[192,768]{1,0:T(8,128)(2,1)S(1)} %get-tuple-element.134), channel_id=1, source_target_pairs={{0,8},{4,12},{8,0},{12,4},{16,24},{20,28},{24,16},{28,20},{1,9},{5... | collective-permute-start | bytes 884744 | tf_op jit(solution)/shard_map/ppermute | solution.py:460
  58.2 1.5 %attend_grads_kernel.1 = (bf16[192,768]{1,0:T(8,128)(2,1)S(1)}, bf16[192,768]{1,0:T(8,128)(2,1)S(1)}, f32[192,768]{1,0:T(8,128)S(1)}, f32[192,768]{1,0:T(8,128)S(1)}) custom-call(s32[11]{0:T(128)S(1)} %stack.44.refs_0_.refs_13_, bf16[512,768]{1,0:T(8,128)(2,1)S(1)} %get-tuple-element.121.refs_1_, bf16[512,768]{1,0:T(8,128)(2,1)S(1)} %collective-permute-done.14.refs_2_, ...), custom_call_target="tpu_custom_call" | custom-call | flops 300000000 | bytes 1 | tf_op jit(solution)/shard_map/attend_grads_kernel/pallas_call | solution.py:55
  59.7 0.6 collective-permute-start.20
  60.8 1.8 %collective-permute-done.12.refs_6_ = bf16[256,768]{1,0:T(8,128)(2,1)S(1)} collective-permute-done((bf16[256,768]{1,0:T(8,128)(2,1)S(1)}, bf16[256,768]{1,0:T(8,128)(2,1)S(1)}, u32[]{:S(2)}, u32[]{:S(2)}) %collective-permute-start.12) | collective-permute-done | bytes 393248 | tf_op jit(solution)/shard_map/ppermute | solution.py:460
  62.6 1.6 %slots_kernel.1 = (bf16[256,768]{1,0:T(8,128)(2,1)S(1)}, bf16[256,768]{1,0:T(8,128)(2,1)S(1)}, f32[8,768]{1,0:T(8,128)S(1)}) custom-call(bf16[256,768]{1,0:T(8,128)(2,1)S(1)} %get-tuple-element.100.refs_0_, f32[256,768]{1,0:T(8,128)S(1)} %get-tuple-element.101.refs_1_, f32[256,128]{1,0:T(8,128)S(1)} %get-tuple-element.102.refs_0_.refs_5_.refs_2_, ...), custom_call_target="tpu_custom_call" | custom-call | flops 300000000 | bytes 1 | tf_op jit(solution)/shard_map/slots_kernel/pallas_call | solution.py:55
  64.3 0.5 collective-permute-start.23
  64.8 0.7 collective-permute-done.19
  65.6 0.9 collective-permute-done.22.refs_1_
  66.6 0.8 collective-permute-done.20.refs_3_.refs_4_
  67.5 2.7 %collective-permute-start.28 = (bf16[192,768]{1,0:T(8,128)(2,1)S(1)}, bf16[192,768]{1,0:T(8,128)(2,1)S(1)}, u32[]{:S(2)}, u32[]{:S(2)}) collective-permute-start(bf16[192,768]{1,0:T(8,128)(2,1)S(1)} %round_kernel.2.refs_6_.refs_0_), channel_id=1, source_target_pairs={{0,16},{4,20},{8,24},{12,28},{16,0},{20,4},{24,8},{28,12},{1,17},{... | collective-permute-start | bytes 884744 | tf_op jit(solution)/shard_map/ppermute | solution.py:460
  70.1 3.9 %collective-permute-done.21.refs_5_ = bf16[192,768]{1,0:T(8,128)(2,1)S(1)} collective-permute-done((bf16[192,768]{1,0:T(8,128)(2,1)S(1)}, bf16[192,768]{1,0:T(8,128)(2,1)S(1)}, u32[]{:S(2)}, u32[]{:S(2)}) %collective-permute-start.21) | collective-permute-done | bytes 294944 | tf_op jit(solution)/shard_map/ppermute | solution.py:460
  74.1 0.7 reduce_small_kernel.1
  74.9 0.7 reduce_kernel.3
  75.6 2.1 %collective-permute-start.24 = (bf16[192,768]{1,0:T(8,128)(2,1)S(1)}, bf16[192,768]{1,0:T(8,128)(2,1)S(1)}, u32[]{:S(2)}, u32[]{:S(2)}) collective-permute-start(bf16[192,768]{1,0:T(8,128)(2,1)S(1)} %get-tuple-element.138), channel_id=1, source_target_pairs={{0,4},{4,0},{8,12},{12,8},{16,20},{20,16},{24,28},{28,24},{1,5},{5... | collective-permute-start | bytes 884744 | tf_op jit(solution)/shard_map/ppermute | solution.py:460
  77.7 3.3 %collective-permute-done.25.refs_3_ = bf16[96,768]{1,0:T(8,128)(2,1)S(1)} collective-permute-done((bf16[96,768]{1,0:T(8,128)(2,1)S(1)}, bf16[96,768]{1,0:T(8,128)(2,1)S(1)}, u32[]{:S(2)}, u32[]{:S(2)}) %collective-permute-start.25) | collective-permute-done | bytes 147488 | tf_op jit(solution)/shard_map/ppermute | solution.py:460
  81.0 3.4 %collective-permute-start.27 = (bf16[208,768]{1,0:T(8,128)(2,1)S(1)}, bf16[208,768]{1,0:T(8,128)(2,1)S(1)}, u32[]{:S(2)}, u32[]{:S(2)}) collective-permute-start(bf16[208,768]{1,0:T(8,128)(2,1)S(1)} %get-tuple-element.143.refs_1_), channel_id=1, source_target_pairs={{0,16},{4,20},{8,24},{12,28},{16,0},{20,4},{24,8},{28,12},{1,17},{... | collective-permute-start | bytes 958472 | tf_op jit(solution)/shard_map/ppermute | solution.py:460
  84.6 2.9 %collective-permute-start.31 = (bf16[192,768]{1,0:T(8,128)(2,1)S(1)}, bf16[192,768]{1,0:T(8,128)(2,1)S(1)}, u32[]{:S(2)}, u32[]{:S(2)}) collective-permute-start(bf16[192,768]{1,0:T(8,128)(2,1)S(1)} %last_kernel.2.refs_6_.refs_1_), channel_id=1, source_target_pairs={{0,8},{4,12},{8,0},{12,4},{16,24},{20,28},{24,16},{28,20},{1,9},{5... | collective-permute-start | bytes 884744 | tf_op jit(solution)/shard_map/ppermute | solution.py:460
  87.4 2.3 %place_kernel.2 = (bf16[2,512,768]{2,1,0:T(8,128)(2,1)}, f32[8,128]{1,0:T(8,128)S(1)}) custom-call(s32[11]{0:T(128)S(1)} %stack.44.refs_0_.refs_13_, bf16[256,512]{1,0:T(8,128)(2,1)S(1)} %get-tuple-element.93.refs_1_, bf16[256,512]{1,0:T(8,128)(2,1)S(1)} %get-tuple-element.94.refs_2_, bf16[2,512,768]{2,1,0:T(8,128)(2,1)S(1)} %copy-done, ...), custom_call_target="tpu_custom_call" | custom-call | flops 100000000 | bytes 1 | tf_op jit(solution)/shard_map/place_kernel/pallas_call | solution.py:55
  89.8 6.4 %collective-permute-done.27.refs_2_ = bf16[208,768]{1,0:T(8,128)(2,1)S(1)} collective-permute-done((bf16[208,768]{1,0:T(8,128)(2,1)S(1)}, bf16[208,768]{1,0:T(8,128)(2,1)S(1)}, u32[]{:S(2)}, u32[]{:S(2)}) %collective-permute-start.27) | collective-permute-done | bytes 319520 | tf_op jit(solution)/shard_map/ppermute | solution.py:460
  96.3 0.7 collective-permute-start.29
  97.0 1.5 %collective-permute-start.30 = (bf16[96,768]{1,0:T(8,128)(2,1)S(1)}, bf16[96,768]{1,0:T(8,128)(2,1)S(1)}, u32[]{:S(2)}, u32[]{:S(2)}) collective-permute-start(bf16[96,768]{1,0:T(8,128)(2,1)S(1)} %get-tuple-element.149.refs_3_), channel_id=1, source_target_pairs={{0,4},{4,0},{8,12},{12,8},{16,20},{20,16},{24,28},{28,24},{1,5},{5... | collective-permute-start | bytes 442376 | tf_op jit(solution)/shard_map/ppermute | solution.py:460
  98.5 0.5 collective-permute-start.35
  99.1 3.5 %collective-permute-start.34 = (bf16[192,768]{1,0:T(8,128)(2,1)S(1)}, bf16[192,768]{1,0:T(8,128)(2,1)S(1)}, u32[]{:S(2)}, u32[]{:S(2)}) collective-permute-start(bf16[192,768]{1,0:T(8,128)(2,1)S(1)} %round_kernel.3.refs_6_.refs_0_), channel_id=1, source_target_pairs={{0,16},{4,20},{8,24},{12,28},{16,0},{20,4},{24,8},{28,12},{1,17},{... | collective-permute-start | bytes 884744 | tf_op jit(solution)/shard_map/ppermute | solution.py:460
  102.6 2.3 %place_kernel.3 = (bf16[2,512,768]{2,1,0:T(8,128)(2,1)}, f32[8,128]{1,0:T(8,128)S(1)}) custom-call(s32[11]{0:T(128)S(1)} %stack.44.refs_0_.refs_13_, bf16[256,512]{1,0:T(8,128)(2,1)S(1)} %get-tuple-element.93.refs_1_, bf16[256,512]{1,0:T(8,128)(2,1)S(1)} %get-tuple-element.94.refs_2_, bf16[2,512,768]{2,1,0:T(8,128)(2,1)S(1)} %copy-done.1, ...), custom_call_target="tpu_custom_call" | custom-call | flops 600000000 | bytes 1 | tf_op jit(solution)/shard_map/place_kernel/pallas_call | solution.py:55
  104.9 1.2 join_both_kernel.1
  106.1 2.1 %collective-permute-start.32 = (bf16[192,768]{1,0:T(8,128)(2,1)S(1)}, bf16[192,768]{1,0:T(8,128)(2,1)S(1)}, u32[]{:S(2)}, u32[]{:S(2)}) collective-permute-start(bf16[192,768]{1,0:T(8,128)(2,1)S(1)} %get-tuple-element.154), channel_id=1, source_target_pairs={{0,4},{4,0},{8,12},{12,8},{16,20},{20,16},{24,28},{28,24},{1,5},{5... | collective-permute-start | bytes 884744 | tf_op jit(solution)/shard_map/ppermute | solution.py:460
  108.3 6.8 %collective-permute-done.34.refs_1_ = bf16[192,768]{1,0:T(8,128)(2,1)S(1)} collective-permute-done((bf16[192,768]{1,0:T(8,128)(2,1)S(1)}, bf16[192,768]{1,0:T(8,128)(2,1)S(1)}, u32[]{:S(2)}, u32[]{:S(2)}) %collective-permute-start.34) | collective-permute-done | bytes 294944 | tf_op jit(solution)/shard_map/ppermute | solution.py:460
  115.2 0.5 collective-permute-start.40
  115.7 4.6 %collective-permute-done.33.refs_1_ = bf16[192,768]{1,0:T(8,128)(2,1)S(1)} collective-permute-done((bf16[192,768]{1,0:T(8,128)(2,1)S(1)}, bf16[192,768]{1,0:T(8,128)(2,1)S(1)}, u32[]{:S(2)}, u32[]{:S(2)}) %collective-permute-start.33) | collective-permute-done | bytes 294944 | tf_op jit(solution)/shard_map/ppermute | solution.py:460
  120.4 1.2 collective-permute-start.36
  121.6 0.6 join_kernel.2.refs_3_.refs_9_
  122.2 1.1 collective-permute-done.40.refs_2_
  123.3 0.6 join_kernel.3.refs_10_.refs_11_
  124.0 0.5 collective-permute-start.42
  124.8 0.8 collective-permute-done.41.refs_7_
  126.0 4.4 %middle_kernel.1 = (f32[768,768]{1,0:T(8,128)}, f32[768,768]{1,0:T(8,128)}, f32[768,768]{1,0:T(8,128)}, f32[768,768]{1,0:T(8,128)}, f32[768,768]{1,0:T(8,128)}, ...) custom-call(s32[11]{0:T(128)S(1)} %stack.44.refs_0_.refs_13_, bf16[384,768]{1,0:T(8,128)(2,1)S(1)} %get-tuple-element.156.refs_2_.refs_1_, ...), custom_call_target="tpu_custom_call" | custom-call | flops 1 | bytes 1 | tf_op jit(solution)/shard_map/middle_kernel/pallas_call | solution.py:55
  130.3 5.8 %collective-permute-done.36.refs_1_ = bf16[384,768]{1,0:T(8,128)(2,1)S(1)} collective-permute-done((bf16[384,768]{1,0:T(8,128)(2,1)S(1)}, bf16[384,768]{1,0:T(8,128)(2,1)S(1)}, u32[]{:S(2)}, u32[]{:S(2)}) %collective-permute-start.36) | collective-permute-done | bytes 589856 | tf_op jit(solution)/shard_map/ppermute | solution.py:460
  136.1 3.6 %collective-permute-done.44.refs_3_ = bf16[384,768]{1,0:T(8,128)(2,1)S(1)} collective-permute-done((bf16[384,768]{1,0:T(8,128)(2,1)S(1)}, bf16[384,768]{1,0:T(8,128)(2,1)S(1)}, u32[]{:S(2)}, u32[]{:S(2)}) %collective-permute-start.44) | collective-permute-done | bytes 589856 | tf_op jit(solution)/shard_map/ppermute | solution.py:460
  139.9 2.8 %final_kernel.1 = (f32[768,768]{1,0:T(8,128)}, f32[768,768]{1,0:T(8,128)}, f32[768,768]{1,0:T(8,128)}, f32[768,768]{1,0:T(8,128)}, f32[768,768]{1,0:T(8,128)}, /*index=5*/f32[768,768]{1,0:T(8,128)}) custom-call(s32[11]{0:T(128)S(1)} %stack.44.refs_0_.refs_13_, ...), custom_call_target="tpu_custom_call", output_to_operand_aliasing={{0}: (5, {}), {1}: (6, {}), {2}: (7, {}), {3}: (8, {}), {4}... | custom-call | flops 4000000000 | bytes 1 | tf_op jit(solution)/shard_map/final_kernel/pallas_call | solution.py:55
  (86 shorter events, 4.8 us)
Async XLA Ops:
  0.6 4.5 %collective-permute-start = (s32[2,64]{1,0:T(2,128)}, s32[2,64]{1,0:T(2,128)S(1)}, u32[]{:S(2)}, u32[]{:S(2)}) collective-permute-start(s32[2,64]{1,0:T(2,128)} %param.15), channel_id=1, source_target_pairs={{0,1},{1,0},{2,3},{3,2},{4,5},{5,4},{6,7},{7,6},{8,9},{9,8},{10,11... | collective-permute-start | bytes 1544 | tf_op jit(solution)/shard_map/ppermute | solution.py:460
  1.2 4.1 %collective-permute-start.2 = (s32[2,64]{1,0:T(2,128)}, s32[2,64]{1,0:T(2,128)S(1)}, u32[]{:S(2)}, u32[]{:S(2)}) collective-permute-start(s32[2,64]{1,0:T(2,128)} %param.15), channel_id=1, source_target_pairs={{0,3},{1,2},{2,1},{3,0},{4,7},{5,6},{6,5},{7,4},{8,11},{9,10},{10,... | collective-permute-start | bytes 1544 | tf_op jit(solution)/shard_map/ppermute | solution.py:460
  3.8 3.8 %collective-permute-start.1 = (s32[2,64]{1,0:T(2,128)}, s32[2,64]{1,0:T(2,128)S(1)}, u32[]{:S(2)}, u32[]{:S(2)}) collective-permute-start(s32[2,64]{1,0:T(2,128)} %param.15), channel_id=1, source_target_pairs={{0,2},{1,3},{2,0},{3,1},{4,6},{5,7},{6,4},{7,5},{8,10},{9,11},{10,... | collective-permute-start | bytes 1544 | tf_op jit(solution)/shard_map/ppermute | solution.py:460
  3.8 20.2 %collective-permute-start.5 = (bf16[768,768]{1,0:T(8,128)(2,1)}, bf16[768,768]{1,0:T(8,128)(2,1)S(1)}, u32[]{:S(2)}, u32[]{:S(2)}) collective-permute-start(bf16[768,768]{1,0:T(8,128)(2,1)} %refs_5_.3), channel_id=1, source_target_pairs={{0,1},{1,0},{2,3},{3,2},{4,5},{5,4},{6,7},{7,6},{8,9},{9,8},{10,11... | collective-permute-start | bytes 3538952 | tf_op jit(solution)/shard_map/ppermute | solution.py:460
  3.9 28.1 %collective-permute-start.9 = (bf16[768,768]{1,0:T(8,128)(2,1)}, bf16[768,768]{1,0:T(8,128)(2,1)S(1)}, u32[]{:S(2)}, u32[]{:S(2)}) collective-permute-start(bf16[768,768]{1,0:T(8,128)(2,1)} %refs_2_.1), channel_id=1, source_target_pairs={{0,1},{1,0},{2,3},{3,2},{4,5},{5,4},{6,7},{7,6},{8,9},{9,8},{10,11... | collective-permute-start | bytes 3538952 | tf_op jit(solution)/shard_map/ppermute | solution.py:460
  5.1 4.7 %copy-start = (bf16[2,512,768]{2,1,0:T(8,128)(2,1)S(1)}, bf16[2,512,768]{2,1,0:T(8,128)(2,1)}, u32[]{:S(2)}) copy-start(bf16[2,512,768]{2,1,0:T(8,128)(2,1)} %refs_3_.4) | copy-start | bytes 4718596
  5.1 4.7 %copy-start.1 = (bf16[2,512,768]{2,1,0:T(8,128)(2,1)S(1)}, bf16[2,512,768]{2,1,0:T(8,128)(2,1)}, u32[]{:S(2)}) copy-start(bf16[2,512,768]{2,1,0:T(8,128)(2,1)} %refs_3_.5) | copy-start | bytes 4718596
  9.7 2.2 %collective-permute-start.3 = (bf16[256,768]{1,0:T(8,128)(2,1)S(1)}, bf16[256,768]{1,0:T(8,128)(2,1)S(1)}, u32[]{:S(2)}, u32[]{:S(2)}) collective-permute-start(bf16[256,768]{1,0:T(8,128)(2,1)S(1)} %get-tuple-element.96), channel_id=1, source_target_pairs={{0,1},{1,0},{2,3},{3,2},{4,5},{5,4},{6,7},{7,6},{8,9},{9,8},{10,11... | collective-permute-start | bytes 1179656 | tf_op jit(solution)/shard_map/ppermute | solution.py:460
  9.8 4.4 %copy-start.11 = (bf16[768]{0:T(1024)(128)(2,1)S(1)}, bf16[768]{0:T(1024)(128)(2,1)}, u32[]{:S(2)}) copy-start(bf16[768]{0:T(1024)(128)(2,1)} %param.16) | copy-start | bytes 4612
  9.9 14.1 %copy-start.4 = (bf16[768,768]{1,0:T(8,128)(2,1)S(1)}, bf16[768,768]{1,0:T(8,128)(2,1)}, u32[]{:S(2)}) copy-start(bf16[768,768]{1,0:T(8,128)(2,1)} %refs_13_.1) | copy-start | bytes 3538948
  9.9 14.1 %copy-start.5 = (bf16[768,768]{1,0:T(8,128)(2,1)S(1)}, bf16[768,768]{1,0:T(8,128)(2,1)}, u32[]{:S(2)}) copy-start(bf16[768,768]{1,0:T(8,128)(2,1)} %refs_14_.1) | copy-start | bytes 3538948
  9.9 14.1 %copy-start.6 = (bf16[768,768]{1,0:T(8,128)(2,1)S(1)}, bf16[768,768]{1,0:T(8,128)(2,1)}, u32[]{:S(2)}) copy-start(bf16[768,768]{1,0:T(8,128)(2,1)} %refs_5_.3) | copy-start | bytes 3538948
  11.2 3.0 %copy-start.9 = (f32[768]{0:T(1024)S(1)}, f32[768]{0:T(1024)}, u32[]{:S(2)}) copy-start(f32[768]{0:T(1024)} %param.17) | copy-start | bytes 9220
  11.2 3.1 %copy-start.10 = (f32[768]{0:T(1024)S(1)}, f32[768]{0:T(1024)}, u32[]{:S(2)}) copy-start(f32[768]{0:T(1024)} %param.18) | copy-start | bytes 9220
  11.3 12.8 %copy-start.2 = (bf16[768,768]{1,0:T(8,128)(2,1)S(1)}, bf16[768,768]{1,0:T(8,128)(2,1)}, u32[]{:S(2)}) copy-start(bf16[768,768]{1,0:T(8,128)(2,1)} %refs_12_.2) | copy-start | bytes 3538948
  11.3 12.8 %copy-start.3 = (bf16[768,768]{1,0:T(8,128)(2,1)S(1)}, bf16[768,768]{1,0:T(8,128)(2,1)}, u32[]{:S(2)}) copy-start(bf16[768,768]{1,0:T(8,128)(2,1)} %refs_12_.3) | copy-start | bytes 3538948
  11.3 12.8 %copy-start.7 = (s32[2]{0:T(128)S(1)}, s32[2]{0:T(128)}, u32[]{:S(2)}) copy-start(s32[2]{0:T(128)} %refs_1_.1) | copy-start | bytes 28
  11.3 1.6 %collective-permute-start.6 = (bf16[128,768]{1,0:T(8,128)(2,1)S(1)}, bf16[128,768]{1,0:T(8,128)(2,1)S(1)}, u32[]{:S(2)}, u32[]{:S(2)}) collective-permute-start(bf16[128,768]{1,0:T(8,128)(2,1)S(1)} %get-tuple-element.98), channel_id=1, source_target_pairs={{0,1},{1,0},{2,3},{3,2},{4,5},{5,4},{6,7},{7,6},{8,9},{9,8},{10,11... | collective-permute-start | bytes 589832 | tf_op jit(solution)/shard_map/ppermute | solution.py:460
  11.8 1.4 %collective-permute-start.7 = (bf16[128,768]{1,0:T(8,128)(2,1)S(1)}, bf16[128,768]{1,0:T(8,128)(2,1)S(1)}, u32[]{:S(2)}, u32[]{:S(2)}) collective-permute-start(bf16[128,768]{1,0:T(8,128)(2,1)S(1)} %get-tuple-element.99), channel_id=1, source_target_pairs={{0,1},{1,0},{2,3},{3,2},{4,5},{5,4},{6,7},{7,6},{8,9},{9,8},{10,11... | collective-permute-start | bytes 589832 | tf_op jit(solution)/shard_map/ppermute | solution.py:460
  12.0 12.0 %collective-permute-start.4 = (bf16[256,768]{1,0:T(8,128)(2,1)S(1)}, bf16[256,768]{1,0:T(8,128)(2,1)S(1)}, u32[]{:S(2)}, u32[]{:S(2)}) collective-permute-start(bf16[256,768]{1,0:T(8,128)(2,1)S(1)} %add.15.refs_2_), channel_id=1, source_target_pairs={{0,2},{1,3},{2,0},{3,1},{4,6},{5,7},{6,4},{7,5},{8,10},{9,11},{10,... | collective-permute-start | bytes 1179656 | tf_op jit(solution)/shard_map/ppermute | solution.py:460
  13.4 18.6 %collective-permute-start.8 = (bf16[256,768]{1,0:T(8,128)(2,1)S(1)}, bf16[256,768]{1,0:T(8,128)(2,1)S(1)}, u32[]{:S(2)}, u32[]{:S(2)}) collective-permute-start(bf16[256,768]{1,0:T(8,128)(2,1)S(1)} %maximum_add_fusion.refs_13_.refs_1_.refs_6_.refs_3_), channel_id=1, source_target_pairs={{0,2},{1,3},{2,0},{3,1},{4,6},{5,7},{6,4},{7,5},{8,10},{9,11},{10,... | collective-permute-start | bytes 1179656 | tf_op jit(solution)/shard_map/ppermute | solution.py:460
  14.3 17.7 %copy-start.8 = (bf16[768,768]{1,0:T(8,128)(2,1)S(1)}, bf16[768,768]{1,0:T(8,128)(2,1)}, u32[]{:S(2)}) copy-start(bf16[768,768]{1,0:T(8,128)(2,1)} %refs_2_.1) | copy-start | bytes 3538948
  33.8 2.4 %collective-permute-start.11 = (bf16[512,768]{1,0:T(8,128)(2,1)S(1)}, bf16[512,768]{1,0:T(8,128)(2,1)S(1)}, u32[]{:S(2)}, u32[]{:S(2)}) collective-permute-start(bf16[512,768]{1,0:T(8,128)(2,1)S(1)} %get-tuple-element.109.refs_4_), channel_id=1, source_target_pairs={{0,1},{1,0},{2,3},{3,2},{4,5},{5,4},{6,7},{7,6},{8,9},{9,8},{10,11... | collective-permute-start | bytes 2359304 | tf_op jit(solution)/shard_map/ppermute | solution.py:460
  33.9 3.4 %collective-permute-start.10 = (bf16[512,768]{1,0:T(8,128)(2,1)S(1)}, bf16[512,768]{1,0:T(8,128)(2,1)S(1)}, u32[]{:S(2)}, u32[]{:S(2)}) collective-permute-start(bf16[512,768]{1,0:T(8,128)(2,1)S(1)} %get-tuple-element.108.refs_3_), channel_id=1, source_target_pairs={{0,1},{1,0},{2,3},{3,2},{4,5},{5,4},{6,7},{7,6},{8,9},{9,8},{10,11... | collective-permute-start | bytes 2359304 | tf_op jit(solution)/shard_map/ppermute | solution.py:460
  34.4 11.1 %collective-permute-start.13 = (bf16[256,768]{1,0:T(8,128)(2,1)S(1)}, bf16[256,768]{1,0:T(8,128)(2,1)S(1)}, u32[]{:S(2)}, u32[]{:S(2)}) collective-permute-start(bf16[256,768]{1,0:T(8,128)(2,1)S(1)} %get-tuple-element.111.refs_3_), channel_id=1, source_target_pairs={{0,2},{1,3},{2,0},{3,1},{4,6},{5,7},{6,4},{7,5},{8,10},{9,11},{10,... | collective-permute-start | bytes 1179656 | tf_op jit(solution)/shard_map/ppermute | solution.py:460
  34.6 23.6 %collective-permute-start.14 = (bf16[512,768]{1,0:T(8,128)(2,1)S(1)}, bf16[512,768]{1,0:T(8,128)(2,1)S(1)}, u32[]{:S(2)}, u32[]{:S(2)}) collective-permute-start(bf16[512,768]{1,0:T(8,128)(2,1)S(1)} %get-tuple-element.121.refs_1_), channel_id=1, source_target_pairs={{0,1},{1,0},{2,3},{3,2},{4,5},{5,4},{6,7},{7,6},{8,9},{9,8},{10,11... | collective-permute-start | bytes 2359304 | tf_op jit(solution)/shard_map/ppermute | solution.py:460
  39.2 15.4 %collective-permute-start.16 = (bf16[384,768]{1,0:T(8,128)(2,1)S(1)}, bf16[384,768]{1,0:T(8,128)(2,1)S(1)}, u32[]{:S(2)}, u32[]{:S(2)}) collective-permute-start(bf16[384,768]{1,0:T(8,128)(2,1)S(1)} %get-tuple-element.124), channel_id=1, source_target_pairs={{0,4},{4,0},{8,12},{12,8},{16,20},{20,16},{24,28},{28,24},{1,5},{5... | collective-permute-start | bytes 1769480 | tf_op jit(solution)/shard_map/ppermute | solution.py:460
  40.8 15.1 %collective-permute-start.17 = (bf16[384,768]{1,0:T(8,128)(2,1)S(1)}, bf16[384,768]{1,0:T(8,128)(2,1)S(1)}, u32[]{:S(2)}, u32[]{:S(2)}) collective-permute-start(bf16[384,768]{1,0:T(8,128)(2,1)S(1)} %get-tuple-element.125), channel_id=1, source_target_pairs={{0,8},{4,12},{8,0},{12,4},{16,24},{20,28},{24,16},{28,20},{1,9},{5... | collective-permute-start | bytes 1769480 | tf_op jit(solution)/shard_map/ppermute | solution.py:460
  51.0 7.3 %collective-permute-start.15 = (bf16[512,768]{1,0:T(8,128)(2,1)S(1)}, bf16[512,768]{1,0:T(8,128)(2,1)S(1)}, u32[]{:S(2)}, u32[]{:S(2)}) collective-permute-start(bf16[512,768]{1,0:T(8,128)(2,1)S(1)} %get-tuple-element.123), channel_id=1, source_target_pairs={{0,1},{1,0},{2,3},{3,2},{4,5},{5,4},{6,7},{7,6},{8,9},{9,8},{10,11... | collective-permute-start | bytes 2359304 | tf_op jit(solution)/shard_map/ppermute | solution.py:460
  51.0 11.5 %collective-permute-start.12 = (bf16[256,768]{1,0:T(8,128)(2,1)S(1)}, bf16[256,768]{1,0:T(8,128)(2,1)S(1)}, u32[]{:S(2)}, u32[]{:S(2)}) collective-permute-start(bf16[256,768]{1,0:T(8,128)(2,1)S(1)} %moved_kernel.1.refs_14_.refs_5_), channel_id=1, source_target_pairs={{0,2},{1,3},{2,0},{3,1},{4,6},{5,7},{6,4},{7,5},{8,10},{9,11},{10,... | collective-permute-start | bytes 1179656 | tf_op jit(solution)/shard_map/ppermute | solution.py:460
  56.6 10.0 %collective-permute-start.22 = (bf16[192,768]{1,0:T(8,128)(2,1)S(1)}, bf16[192,768]{1,0:T(8,128)(2,1)S(1)}, u32[]{:S(2)}, u32[]{:S(2)}) collective-permute-start(bf16[192,768]{1,0:T(8,128)(2,1)S(1)} %get-tuple-element.134), channel_id=1, source_target_pairs={{0,8},{4,12},{8,0},{12,4},{16,24},{20,28},{24,16},{28,20},{1,9},{5... | collective-permute-start | bytes 884744 | tf_op jit(solution)/shard_map/ppermute | solution.py:460
  59.7 7.7 %collective-permute-start.20 = (bf16[192,768]{1,0:T(8,128)(2,1)S(1)}, bf16[192,768]{1,0:T(8,128)(2,1)S(1)}, u32[]{:S(2)}, u32[]{:S(2)}) collective-permute-start(bf16[192,768]{1,0:T(8,128)(2,1)S(1)} %get-tuple-element.132), channel_id=1, source_target_pairs={{0,4},{4,0},{8,12},{12,8},{16,20},{20,16},{24,28},{28,24},{1,5},{5... | collective-permute-start | bytes 884744 | tf_op jit(solution)/shard_map/ppermute | solution.py:460
  60.3 13.8 %collective-permute-start.21 = (bf16[192,768]{1,0:T(8,128)(2,1)S(1)}, bf16[192,768]{1,0:T(8,128)(2,1)S(1)}, u32[]{:S(2)}, u32[]{:S(2)}) collective-permute-start(bf16[192,768]{1,0:T(8,128)(2,1)S(1)} %get-tuple-element.133), channel_id=1, source_target_pairs={{0,8},{4,12},{8,0},{12,4},{16,24},{20,28},{24,16},{28,20},{1,9},{5... | collective-permute-start | bytes 884744 | tf_op jit(solution)/shard_map/ppermute | solution.py:460
  64.2 1.3 collective-permute-start.19
  64.3 10.6 %collective-permute-start.23 = (bf16[256,768]{1,0:T(8,128)(2,1)S(1)}, bf16[256,768]{1,0:T(8,128)(2,1)S(1)}, u32[]{:S(2)}, u32[]{:S(2)}) collective-permute-start(bf16[256,768]{1,0:T(8,128)(2,1)S(1)} %get-tuple-element.136.refs_4_), channel_id=1, source_target_pairs={{0,1},{1,0},{2,3},{3,2},{4,5},{5,4},{6,7},{7,6},{8,9},{9,8},{10,11... | collective-permute-start | bytes 1179656 | tf_op jit(solution)/shard_map/ppermute | solution.py:460
  65.5 33.6 %collective-permute-start.18 = (bf16[256,768]{1,0:T(8,128)(2,1)S(1)}, bf16[256,768]{1,0:T(8,128)(2,1)S(1)}, u32[]{:S(2)}, u32[]{:S(2)}) collective-permute-start(bf16[256,768]{1,0:T(8,128)(2,1)S(1)} %get-tuple-element.128.refs_2_.refs_4_), channel_id=1, source_target_pairs={{0,1},{1,0},{2,3},{3,2},{4,5},{5,4},{6,7},{7,6},{8,9},{9,8},{10,11... | collective-permute-start | bytes 1179656 | tf_op jit(solution)/shard_map/ppermute | solution.py:460
  67.5 17.0 %collective-permute-start.28 = (bf16[192,768]{1,0:T(8,128)(2,1)S(1)}, bf16[192,768]{1,0:T(8,128)(2,1)S(1)}, u32[]{:S(2)}, u32[]{:S(2)}) collective-permute-start(bf16[192,768]{1,0:T(8,128)(2,1)S(1)} %round_kernel.2.refs_6_.refs_0_), channel_id=1, source_target_pairs={{0,16},{4,20},{8,24},{12,28},{16,0},{20,4},{24,8},{28,12},{1,17},{... | collective-permute-start | bytes 884744 | tf_op jit(solution)/shard_map/ppermute | solution.py:460
  74.7 6.2 %collective-permute-start.25 = (bf16[96,768]{1,0:T(8,128)(2,1)S(1)}, bf16[96,768]{1,0:T(8,128)(2,1)S(1)}, u32[]{:S(2)}, u32[]{:S(2)}) collective-permute-start(bf16[96,768]{1,0:T(8,128)(2,1)S(1)} %get-tuple-element.140), channel_id=1, source_target_pairs={{0,8},{4,12},{8,0},{12,4},{16,24},{20,28},{24,16},{28,20},{1,9},{5... | collective-permute-start | bytes 442376 | tf_op jit(solution)/shard_map/ppermute | solution.py:460
  74.8 6.2 %collective-permute-start.26 = (bf16[112,768]{1,0:T(8,128)(2,1)S(1)}, bf16[112,768]{1,0:T(8,128)(2,1)S(1)}, u32[]{:S(2)}, u32[]{:S(2)}) collective-permute-start(bf16[112,768]{1,0:T(8,128)(2,1)S(1)} %get-tuple-element.141), channel_id=1, source_target_pairs={{0,4},{4,0},{8,12},{12,8},{16,20},{20,16},{24,28},{28,24},{1,5},{5... | collective-permute-start | bytes 516104 | tf_op jit(solution)/shard_map/ppermute | solution.py:460
  75.6 14.2 %collective-permute-start.24 = (bf16[192,768]{1,0:T(8,128)(2,1)S(1)}, bf16[192,768]{1,0:T(8,128)(2,1)S(1)}, u32[]{:S(2)}, u32[]{:S(2)}) collective-permute-start(bf16[192,768]{1,0:T(8,128)(2,1)S(1)} %get-tuple-element.138), channel_id=1, source_target_pairs={{0,4},{4,0},{8,12},{12,8},{16,20},{20,16},{24,28},{28,24},{1,5},{5... | collective-permute-start | bytes 884744 | tf_op jit(solution)/shard_map/ppermute | solution.py:460
  81.0 15.1 %collective-permute-start.27 = (bf16[208,768]{1,0:T(8,128)(2,1)S(1)}, bf16[208,768]{1,0:T(8,128)(2,1)S(1)}, u32[]{:S(2)}, u32[]{:S(2)}) collective-permute-start(bf16[208,768]{1,0:T(8,128)(2,1)S(1)} %get-tuple-element.143.refs_1_), channel_id=1, source_target_pairs={{0,16},{4,20},{8,24},{12,28},{16,0},{20,4},{24,8},{28,12},{1,17},{... | collective-permute-start | bytes 958472 | tf_op jit(solution)/shard_map/ppermute | solution.py:460
  84.6 20.4 %collective-permute-start.31 = (bf16[192,768]{1,0:T(8,128)(2,1)S(1)}, bf16[192,768]{1,0:T(8,128)(2,1)S(1)}, u32[]{:S(2)}, u32[]{:S(2)}) collective-permute-start(bf16[192,768]{1,0:T(8,128)(2,1)S(1)} %last_kernel.2.refs_6_.refs_1_), channel_id=1, source_target_pairs={{0,8},{4,12},{8,0},{12,4},{16,24},{20,28},{24,16},{28,20},{1,9},{5... | collective-permute-start | bytes 884744 | tf_op jit(solution)/shard_map/ppermute | solution.py:460
  96.3 8.6 %collective-permute-start.29 = (bf16[112,768]{1,0:T(8,128)(2,1)S(1)}, bf16[112,768]{1,0:T(8,128)(2,1)S(1)}, u32[]{:S(2)}, u32[]{:S(2)}) collective-permute-start(bf16[112,768]{1,0:T(8,128)(2,1)S(1)} %get-tuple-element.145.refs_2_), channel_id=1, source_target_pairs={{0,8},{4,12},{8,0},{12,4},{16,24},{20,28},{24,16},{28,20},{1,9},{5... | collective-permute-start | bytes 516104 | tf_op jit(solution)/shard_map/ppermute | solution.py:460
  97.0 7.9 %collective-permute-start.30 = (bf16[96,768]{1,0:T(8,128)(2,1)S(1)}, bf16[96,768]{1,0:T(8,128)(2,1)S(1)}, u32[]{:S(2)}, u32[]{:S(2)}) collective-permute-start(bf16[96,768]{1,0:T(8,128)(2,1)S(1)} %get-tuple-element.149.refs_3_), channel_id=1, source_target_pairs={{0,4},{4,0},{8,12},{12,8},{16,20},{20,16},{24,28},{28,24},{1,5},{5... | collective-permute-start | bytes 442376 | tf_op jit(solution)/shard_map/ppermute | solution.py:460
  98.5 9.8 %collective-permute-start.35 = (bf16[192,768]{1,0:T(8,128)(2,1)S(1)}, bf16[192,768]{1,0:T(8,128)(2,1)S(1)}, u32[]{:S(2)}, u32[]{:S(2)}) collective-permute-start(bf16[192,768]{1,0:T(8,128)(2,1)S(1)} %get-tuple-element.157), channel_id=1, source_target_pairs={{0,2},{1,3},{2,0},{3,1},{4,6},{5,7},{6,4},{7,5},{8,10},{9,11},{10,... | collective-permute-start | bytes 884744 | tf_op jit(solution)/shard_map/ppermute | solution.py:460
  99.1 16.0 %collective-permute-start.34 = (bf16[192,768]{1,0:T(8,128)(2,1)S(1)}, bf16[192,768]{1,0:T(8,128)(2,1)S(1)}, u32[]{:S(2)}, u32[]{:S(2)}) collective-permute-start(bf16[192,768]{1,0:T(8,128)(2,1)S(1)} %round_kernel.3.refs_6_.refs_0_), channel_id=1, source_target_pairs={{0,16},{4,20},{8,24},{12,28},{16,0},{20,4},{24,8},{28,12},{1,17},{... | collective-permute-start | bytes 884744 | tf_op jit(solution)/shard_map/ppermute | solution.py:460
  106.1 9.0 %collective-permute-start.32 = (bf16[192,768]{1,0:T(8,128)(2,1)S(1)}, bf16[192,768]{1,0:T(8,128)(2,1)S(1)}, u32[]{:S(2)}, u32[]{:S(2)}) collective-permute-start(bf16[192,768]{1,0:T(8,128)(2,1)S(1)} %get-tuple-element.154), channel_id=1, source_target_pairs={{0,4},{4,0},{8,12},{12,8},{16,20},{20,16},{24,28},{28,24},{1,5},{5... | collective-permute-start | bytes 884744 | tf_op jit(solution)/shard_map/ppermute | solution.py:460
  108.2 12.0 %collective-permute-start.33 = (bf16[192,768]{1,0:T(8,128)(2,1)S(1)}, bf16[192,768]{1,0:T(8,128)(2,1)S(1)}, u32[]{:S(2)}, u32[]{:S(2)}) collective-permute-start(bf16[192,768]{1,0:T(8,128)(2,1)S(1)} %get-tuple-element.155), channel_id=1, source_target_pairs={{0,8},{4,12},{8,0},{12,4},{16,24},{20,28},{24,16},{28,20},{1,9},{5... | collective-permute-start | bytes 884744 | tf_op jit(solution)/shard_map/ppermute | solution.py:460
  108.3 13.4 %collective-permute-start.39 = (bf16[192,768]{1,0:T(8,128)(2,1)S(1)}, bf16[192,768]{1,0:T(8,128)(2,1)S(1)}, u32[]{:S(2)}, u32[]{:S(2)}) collective-permute-start(bf16[192,768]{1,0:T(8,128)(2,1)S(1)} %get-tuple-element.158), channel_id=1, source_target_pairs={{0,2},{1,3},{2,0},{3,1},{4,6},{5,7},{6,4},{7,5},{8,10},{9,11},{10,... | collective-permute-start | bytes 884744 | tf_op jit(solution)/shard_map/ppermute | solution.py:460
  115.2 8.1 %collective-permute-start.40 = (bf16[192,768]{1,0:T(8,128)(2,1)S(1)}, bf16[192,768]{1,0:T(8,128)(2,1)S(1)}, u32[]{:S(2)}, u32[]{:S(2)}) collective-permute-start(bf16[192,768]{1,0:T(8,128)(2,1)S(1)} %last_kernel.3.refs_2_.refs_1_), channel_id=1, source_target_pairs={{0,4},{4,0},{8,12},{12,8},{16,20},{20,16},{24,28},{28,24},{1,5},{5... | collective-permute-start | bytes 884744 | tf_op jit(solution)/shard_map/ppermute | solution.py:460
  115.7 8.8 %collective-permute-start.37 = (bf16[384,768]{1,0:T(8,128)(2,1)S(1)}, bf16[384,768]{1,0:T(8,128)(2,1)S(1)}, u32[]{:S(2)}, u32[]{:S(2)}) collective-permute-start(bf16[384,768]{1,0:T(8,128)(2,1)S(1)} %get-tuple-element.156.refs_2_.refs_1_), channel_id=1, source_target_pairs={{0,1},{1,0},{2,3},{3,2},{4,5},{5,4},{6,7},{7,6},{8,9},{9,8},{10,11... | collective-permute-start | bytes 1769480 | tf_op jit(solution)/shard_map/ppermute | solution.py:460
  120.3 4.4 %collective-permute-start.38 = (bf16[384,768]{1,0:T(8,128)(2,1)S(1)}, bf16[384,768]{1,0:T(8,128)(2,1)S(1)}, u32[]{:S(2)}, u32[]{:S(2)}) collective-permute-start(bf16[384,768]{1,0:T(8,128)(2,1)S(1)} %stack_kernel.1.refs_3_.refs_2_), channel_id=1, source_target_pairs={{0,1},{1,0},{2,3},{3,2},{4,5},{5,4},{6,7},{7,6},{8,9},{9,8},{10,11... | collective-permute-start | bytes 1769480 | tf_op jit(solution)/shard_map/ppermute | solution.py:460
  120.4 15.7 %collective-permute-start.36 = (bf16[384,768]{1,0:T(8,128)(2,1)S(1)}, bf16[384,768]{1,0:T(8,128)(2,1)S(1)}, u32[]{:S(2)}, u32[]{:S(2)}) collective-permute-start(bf16[384,768]{1,0:T(8,128)(2,1)S(1)} %stack_kernel.1.refs_3_.refs_2_), channel_id=1, source_target_pairs={{0,2},{1,3},{2,0},{3,1},{4,6},{5,7},{6,4},{7,5},{8,10},{9,11},{10,... | collective-permute-start | bytes 1769480 | tf_op jit(solution)/shard_map/ppermute | solution.py:460
  123.9 1.6 %collective-permute-start.41 = (bf16[192,768]{1,0:T(8,128)(2,1)S(1)}, bf16[192,768]{1,0:T(8,128)(2,1)S(1)}, u32[]{:S(2)}, u32[]{:S(2)}) collective-permute-start(bf16[192,768]{1,0:T(8,128)(2,1)S(1)} %collective-permute-done.35.refs_4_.refs_5_), channel_id=1, source_target_pairs={{0,1},{1,0},{2,3},{3,2},{4,5},{5,4},{6,7},{7,6},{8,9},{9,8},{10,11... | collective-permute-start | bytes 884744 | tf_op jit(solution)/shard_map/ppermute | solution.py:460
  124.0 2.0 %collective-permute-start.42 = (bf16[192,768]{1,0:T(8,128)(2,1)S(1)}, bf16[192,768]{1,0:T(8,128)(2,1)S(1)}, u32[]{:S(2)}, u32[]{:S(2)}) collective-permute-start(bf16[192,768]{1,0:T(8,128)(2,1)S(1)} %collective-permute-done.39.refs_4_.refs_6_), channel_id=1, source_target_pairs={{0,1},{1,0},{2,3},{3,2},{4,5},{5,4},{6,7},{7,6},{8,9},{9,8},{10,11... | collective-permute-start | bytes 884744 | tf_op jit(solution)/shard_map/ppermute | solution.py:460
  124.5 15.3 %collective-permute-start.44 = (bf16[384,768]{1,0:T(8,128)(2,1)S(1)}, bf16[384,768]{1,0:T(8,128)(2,1)S(1)}, u32[]{:S(2)}, u32[]{:S(2)}) collective-permute-start(bf16[384,768]{1,0:T(8,128)(2,1)S(1)} %join_kernel.2.refs_3_.refs_9_), channel_id=1, source_target_pairs={{0,4},{4,0},{8,12},{12,8},{16,20},{20,16},{24,28},{28,24},{1,5},{5... | collective-permute-start | bytes 1769480 | tf_op jit(solution)/shard_map/ppermute | solution.py:460
  124.8 15.1 %collective-permute-start.45 = (bf16[384,768]{1,0:T(8,128)(2,1)S(1)}, bf16[384,768]{1,0:T(8,128)(2,1)S(1)}, u32[]{:S(2)}, u32[]{:S(2)}) collective-permute-start(bf16[384,768]{1,0:T(8,128)(2,1)S(1)} %join_kernel.3.refs_10_.refs_11_), channel_id=1, source_target_pairs={{0,8},{4,12},{8,0},{12,4},{16,24},{20,28},{24,16},{28,20},{1,9},{5... | collective-permute-start | bytes 1769480 | tf_op jit(solution)/shard_map/ppermute | solution.py:460
  136.1 3.7 %collective-permute-start.43 = (bf16[384,768]{1,0:T(8,128)(2,1)S(1)}, bf16[384,768]{1,0:T(8,128)(2,1)S(1)}, u32[]{:S(2)}, u32[]{:S(2)}) collective-permute-start(bf16[384,768]{1,0:T(8,128)(2,1)S(1)} %collective-permute-done.36.refs_1_), channel_id=1, source_target_pairs={{0,1},{1,0},{2,3},{3,2},{4,5},{5,4},{6,7},{7,6},{8,9},{9,8},{10,11... | collective-permute-start | bytes 1769480 | tf_op jit(solution)/shard_map/ppermute | solution.py:460
